TPU v7x, 128 devices: a whole 4x4x4 slice. The times are simulated.
128 devices in a mesh: ctx: 8 (over y, z_lo), fsdp: 16 (over x, z_hi, core).
Axes of the slice: x: 4, y: 4, z: 4 (z_hi: 2, z_lo: 2; z = z_hi * 2 + z_lo), core: 2. Of those that a mesh axis runs over, the one named last changes fastest.
Arguments:
- tokens: bfloat16 [16, 1024, 2048], P('fsdp', 'ctx'), may hold values from -6 to 6
- block_deal: int32 [16, 8, 2], replicated, may hold values from 0 to 15, as said below
- attn_gain: bfloat16 [2048], P('fsdp'), may hold values from 0.5 to 1.5
- query_weight: bfloat16 [2048, 2048], P('fsdp'), may hold values from -0.125 to 0.125
- key_weight: bfloat16 [2048, 256], P('fsdp'), may hold values from -0.125 to 0.125
- value_weight: bfloat16 [2048, 256], P('fsdp'), may hold values from -0.125 to 0.125
- output_weight: bfloat16 [2048, 2048], P('fsdp'), may hold values from -2 to 2
- mlp_gain: bfloat16 [2048], P('fsdp'), may hold values from 0.5 to 1.5
- gate_weight: bfloat16 [2048, 5632], P('fsdp'), may hold values from -0.125 to 0.125
- up_weight: bfloat16 [2048, 5632], P('fsdp'), may hold values from -0.125 to 0.125
- down_weight: bfloat16 [5632, 2048], P('fsdp'), may hold values from -0.078125 to 0.078125
- cotangent: bfloat16 [16, 1024, 2048], P('fsdp', 'ctx'), may hold values from -6 to 6
Outputs:
- mixed: bfloat16 [16, 1024, 2048], P('fsdp', 'ctx')
- tokens_grad: bfloat16 [16, 1024, 2048], P('fsdp', 'ctx')
- attn_gain_grad: float32 [2048], P('fsdp')
- query_grad: float32 [2048, 2048], P('fsdp')
- key_grad: float32 [2048, 256], P('fsdp')
- value_grad: float32 [2048, 256], P('fsdp')
- output_grad: float32 [2048, 2048], P('fsdp')
- mlp_gain_grad: float32 [2048], P('fsdp')
- gate_grad: float32 [2048, 5632], P('fsdp')
- up_grad: float32 [2048, 5632], P('fsdp')
- down_grad: float32 [5632, 2048], P('fsdp')
Inputs may be any that keep to these rules, and one draw needn't show every extreme that they name: In each group, block_deal[g, :, 0] is a permutation of 0 to 8 - 1 (prompt blocks) and block_deal[g, :, 1] one of 8 to 2 * 8 - 1 (continuation blocks).
All inputs are finite; a program needn't handle non-finite values.
Results may differ from a plain program's by a relative error of at most 0.025.
Values may be sent and summed in bfloat16 or wider, within the bound.
A program may use at most 320 MiB of HBM per device.

v0:
```python
import jax
import jax.numpy as jnp
from jax import lax
from jax.sharding import PartitionSpec as P

HEADS = 32
KV_HEADS = 4
HEAD_DIM = 64
GROUP_HEADS = 8


EPS = 1e-05
SCALE = 0.125
BASE = 10000.0


def mult(left, right):
    return jnp.dot(left, right, preferred_element_type=jnp.float32)


def mult_back(left, right):
    return lax.dot_general(
        left, right, (((1,), (1,)), ((), ())), preferred_element_type=jnp.float32
    )


def mult_rows(left, right):
    return lax.dot_general(
        left, right, (((0,), (0,)), ((), ())), preferred_element_type=jnp.float32
    )


def rms_norm(values, gain):
    return values * lax.rsqrt(jnp.mean(values * values, axis=-1, keepdims=True) + EPS) * gain


def tables(position):
    freq = BASE ** (-(jnp.arange(HEAD_DIM // 2, dtype=jnp.float32) * 2.0) / HEAD_DIM)
    angle = position.astype(jnp.float32)[:, None] * freq[None, :]
    angle = jnp.concatenate([angle, angle], axis=-1)
    return (jnp.cos(angle), jnp.sin(angle))


def rotate(values, cosine, sine):
    half_dim = values.shape[-1] // 2
    turned = jnp.concatenate([-values[..., half_dim:], values[..., :half_dim]], axis=-1)
    return values * cosine[:, None, :] + turned * sine[:, None, :]


def unrotate(values, cosine, sine):
    half_dim = values.shape[-1] // 2
    scaled = values * sine[:, None, :]
    turned = jnp.concatenate([scaled[..., half_dim:], -scaled[..., :half_dim]], axis=-1)
    return values * cosine[:, None, :] + turned


def timeline(table_flat, total_len, row_count):
    everywhere = jnp.arange(total_len, dtype=jnp.int32)
    half_len = row_count // 2
    slot = everywhere // row_count * 2 + everywhere % row_count // half_len
    moment = jnp.take(table_flat, slot) * half_len + everywhere % half_len
    prompt_len = total_len // 2
    cont_len = total_len // 8
    later = moment >= prompt_len
    segment = jnp.where(later, 1 + (moment - prompt_len) // cont_len, 0)
    position = jnp.where(later, prompt_len + (moment - prompt_len) % cont_len, moment)
    return (segment, position)


def fetch_attention(attn_gain, mlp_gain, query_weight, key_weight, value_weight, output_weight):
    return (
        lax.all_gather(attn_gain, "fsdp", axis=0, tiled=True),
        lax.all_gather(mlp_gain, "fsdp", axis=0, tiled=True),
        lax.all_gather(query_weight, "fsdp", axis=0, tiled=True),
        lax.all_gather(key_weight, "fsdp", axis=0, tiled=True),
        lax.all_gather(value_weight, "fsdp", axis=0, tiled=True),
        lax.all_gather(output_weight, "fsdp", axis=0, tiled=True),
    )


def fetch_mlp(gate_weight, up_weight, down_weight):
    return (
        lax.all_gather(gate_weight, "fsdp", axis=0, tiled=True),
        lax.all_gather(up_weight, "fsdp", axis=0, tiled=True),
        lax.all_gather(down_weight, "fsdp", axis=0, tiled=True),
    )


def weight_share(left, right):
    return lax.psum_scatter(
        mult_rows(left, right).astype(jnp.bfloat16), "fsdp", scatter_dimension=0, tiled=True
    ).astype(jnp.float32)


def softmax_parts(masked):
    peak = jnp.max(masked, axis=-1, keepdims=True)
    unscaled = jnp.exp(masked - peak)
    total = jnp.sum(unscaled, axis=-1, keepdims=True)
    return ((unscaled / total).astype(jnp.bfloat16), peak + jnp.log(total))


def on_device(
    tokens,
    block_deal,
    attn_gain,
    query_weight,
    key_weight,
    value_weight,
    output_weight,
    mlp_gain,
    gate_weight,
    up_weight,
    down_weight,
    cotangent,
):
    inputs = tokens[0].astype(jnp.float32)
    grad_out = cotangent[0].astype(jnp.float32)
    row_count = inputs.shape[0]
    ctx_index = lax.axis_index("ctx")
    group_index = lax.axis_index("fsdp")
    full_len = row_count * lax.axis_size("ctx")
    seg_all, pos_all = jax.vmap(lambda table: timeline(table.reshape(-1), full_len, row_count))(
        block_deal
    )
    own_seg_all = lax.dynamic_slice_in_dim(seg_all, ctx_index * row_count, row_count, 1)
    own_pos_all = lax.dynamic_slice_in_dim(pos_all, ctx_index * row_count, row_count, 1)
    own_position = lax.dynamic_index_in_dim(own_pos_all, group_index, 0, keepdims=False)
    cosine, sine = tables(own_position)
    segment = lax.dynamic_index_in_dim(seg_all, group_index, 0, keepdims=False)
    position = lax.dynamic_index_in_dim(pos_all, group_index, 0, keepdims=False)
    own_segment = lax.dynamic_index_in_dim(own_seg_all, group_index, 0, keepdims=False)
    same = (segment[None, :] == 0) | (segment[None, :] == own_segment[:, None])
    visible = same & (position[None, :] <= own_position[:, None])
    gain_one, gain_two, query_full, key_full, value_full, output_full = fetch_attention(
        attn_gain, mlp_gain, query_weight, key_weight, value_weight, output_weight
    )
    gain_first = gain_one.astype(jnp.float32)
    gain_second = gain_two.astype(jnp.float32)
    normed = rms_norm(inputs, gain_first).astype(jnp.bfloat16)
    query_raw = mult(normed, query_full).reshape(row_count, HEADS, HEAD_DIM)
    key_raw = mult(normed, key_full).reshape(row_count, KV_HEADS, HEAD_DIM)
    queries = rotate(query_raw, cosine, sine).astype(jnp.bfloat16)
    queries = queries.reshape(row_count, KV_HEADS, GROUP_HEADS, HEAD_DIM)
    keys_own = (
        rotate(key_raw, cosine, sine).astype(jnp.bfloat16).reshape(row_count, KV_HEADS * HEAD_DIM)
    )
    values_own = mult(normed, value_full).astype(jnp.bfloat16)
    keys_flat, values_flat = (
        lax.all_gather(keys_own, "ctx", axis=0, tiled=True),
        lax.all_gather(values_own, "ctx", axis=0, tiled=True),
    )
    keys_all = keys_flat.reshape(full_len, KV_HEADS, HEAD_DIM)
    values_all = values_flat.reshape(full_len, KV_HEADS, HEAD_DIM)
    scores = (
        jnp.einsum("qcgd,kcd->cgqk", queries, keys_all, preferred_element_type=jnp.float32) * SCALE
    )
    probs_low, log_total = softmax_parts(jnp.where(visible, scores, -1e30))
    heads_out = jnp.einsum(
        "cgqk,kcd->qcgd", probs_low, values_all, preferred_element_type=jnp.float32
    )
    attended = heads_out.astype(jnp.bfloat16).reshape(row_count, HEADS * HEAD_DIM)
    hidden_state = inputs + mult(attended, output_full)
    gate_full, up_full, down_full = fetch_mlp(gate_weight, up_weight, down_weight)
    normed_two = rms_norm(hidden_state, gain_second).astype(jnp.bfloat16)
    gate_act = mult(normed_two, gate_full)
    up_act = mult(normed_two, up_full)
    inner = (jax.nn.silu(gate_act) * up_act).astype(jnp.bfloat16)
    mixed = (hidden_state + mult(inner, down_full)).astype(jnp.bfloat16)
    gain_one, gain_two, query_full, key_full, value_full, output_full = fetch_attention(
        attn_gain, mlp_gain, query_weight, key_weight, value_weight, output_weight
    )
    gate_full, up_full, down_full = fetch_mlp(gate_weight, up_weight, down_weight)
    grad_mlp = cotangent[0]
    grad_inner = mult_back(grad_mlp, down_full)
    _, swiglu_back = jax.vjp(lambda first, second: jax.nn.silu(first) * second, gate_act, up_act)
    grad_gate, grad_up = swiglu_back(grad_inner)
    grad_gate = grad_gate.astype(jnp.bfloat16)
    grad_up = grad_up.astype(jnp.bfloat16)
    grad_normed_two = mult_back(grad_gate, gate_full) + mult_back(grad_up, up_full)
    _, norm_two_back = jax.vjp(rms_norm, hidden_state, gain_second)
    grad_hidden_norm, grad_gain_two = norm_two_back(grad_normed_two)
    grad_hidden = grad_out + grad_hidden_norm
    grad_att = grad_hidden.astype(jnp.bfloat16)
    grad_heads = mult_back(grad_att, output_full).astype(jnp.bfloat16)
    grad_heads = grad_heads.reshape(row_count, KV_HEADS, GROUP_HEADS, HEAD_DIM)
    scores_again = (
        jnp.einsum("qcgd,kcd->cgqk", queries, keys_all, preferred_element_type=jnp.float32) * SCALE
    )
    probs = jnp.exp(jnp.where(visible, scores_again, -1e30) - log_total)
    probs_again = probs.astype(jnp.bfloat16)
    grad_probs = jnp.einsum(
        "qcgd,kcd->cgqk", grad_heads, values_all, preferred_element_type=jnp.float32
    )
    grad_values_all = jnp.einsum(
        "cgqk,qcgd->kcd", probs_again, grad_heads, preferred_element_type=jnp.float32
    )
    grad_scores = probs * (grad_probs - jnp.sum(probs * grad_probs, axis=-1, keepdims=True))
    grad_scores = grad_scores.astype(jnp.bfloat16)
    grad_queries = (
        jnp.einsum("cgqk,kcd->qcgd", grad_scores, keys_all, preferred_element_type=jnp.float32)
        * SCALE
    )
    grad_keys_all = (
        jnp.einsum("cgqk,qcgd->kcd", grad_scores, queries, preferred_element_type=jnp.float32)
        * SCALE
    )
    grad_keys_own, grad_values_own = (
        lax.psum_scatter(
            grad_keys_all.reshape(full_len, KV_HEADS * HEAD_DIM).astype(jnp.bfloat16),
            "ctx",
            scatter_dimension=0,
            tiled=True,
        ).astype(jnp.float32),
        lax.psum_scatter(
            grad_values_all.reshape(full_len, KV_HEADS * HEAD_DIM).astype(jnp.bfloat16),
            "ctx",
            scatter_dimension=0,
            tiled=True,
        ).astype(jnp.float32),
    )
    grad_query_raw = unrotate(grad_queries.reshape(row_count, HEADS, HEAD_DIM), cosine, sine)
    grad_query_raw = grad_query_raw.reshape(row_count, HEADS * HEAD_DIM).astype(jnp.bfloat16)
    grad_key_raw = unrotate(grad_keys_own.reshape(row_count, KV_HEADS, HEAD_DIM), cosine, sine)
    grad_key_raw = grad_key_raw.reshape(row_count, KV_HEADS * HEAD_DIM).astype(jnp.bfloat16)
    grad_value_raw = grad_values_own.astype(jnp.bfloat16)
    grad_normed = (
        mult_back(grad_query_raw, query_full)
        + mult_back(grad_key_raw, key_full)
        + mult_back(grad_value_raw, value_full)
    )
    _, norm_one_back = jax.vjp(rms_norm, inputs, gain_first)
    grad_inputs_norm, grad_gain_one = norm_one_back(grad_normed)
    tokens_grad = (grad_hidden + grad_inputs_norm).astype(jnp.bfloat16)
    query_part = weight_share(normed, grad_query_raw)
    key_part = weight_share(normed, grad_key_raw)
    value_part = weight_share(normed, grad_value_raw)
    output_part = weight_share(attended, grad_att)
    gate_part = weight_share(normed_two, grad_gate)
    up_part = weight_share(normed_two, grad_up)
    down_part = weight_share(inner, grad_mlp)
    gain_one_part, gain_two_part = (
        lax.psum_scatter(grad_gain_one, "fsdp", scatter_dimension=0, tiled=True),
        lax.psum_scatter(grad_gain_two, "fsdp", scatter_dimension=0, tiled=True),
    )
    summed = (
        lax.psum(gain_one_part.astype(jnp.bfloat16), "ctx").astype(jnp.float32),
        lax.psum(query_part.astype(jnp.bfloat16), "ctx").astype(jnp.float32),
        lax.psum(key_part.astype(jnp.bfloat16), "ctx").astype(jnp.float32),
        lax.psum(value_part.astype(jnp.bfloat16), "ctx").astype(jnp.float32),
        lax.psum(output_part.astype(jnp.bfloat16), "ctx").astype(jnp.float32),
        lax.psum(gain_two_part.astype(jnp.bfloat16), "ctx").astype(jnp.float32),
        lax.psum(gate_part.astype(jnp.bfloat16), "ctx").astype(jnp.float32),
        lax.psum(up_part.astype(jnp.bfloat16), "ctx").astype(jnp.float32),
        lax.psum(down_part.astype(jnp.bfloat16), "ctx").astype(jnp.float32),
    )
    return (
        mixed[None],
        tokens_grad[None],
        summed[0],
        summed[1],
        summed[2],
        summed[3],
        summed[4],
        summed[5],
        summed[6],
        summed[7],
        summed[8],
    )


def solution(mesh):
    return jax.shard_map(
        on_device,
        mesh=mesh,
        in_specs=(
            P("fsdp", "ctx", None),
            P(),
            P("fsdp"),
            P("fsdp", None),
            P("fsdp", None),
            P("fsdp", None),
            P("fsdp", None),
            P("fsdp"),
            P("fsdp", None),
            P("fsdp", None),
            P("fsdp", None),
            P("fsdp", "ctx", None),
        ),
        out_specs=(
            P("fsdp", "ctx", None),
            P("fsdp", "ctx", None),
            P("fsdp"),
            P("fsdp", None),
            P("fsdp", None),
            P("fsdp", None),
            P("fsdp", None),
            P("fsdp"),
            P("fsdp", None),
            P("fsdp", None),
            P("fsdp", None),
        ),
        check_vma=False,
    )
```

profile of v0, /device:TPU:0, one launch (start us, length us, event | category | flops | bytes accessed | tf_op | source)
XLA Modules:
  0.0 1975.7 jit_solution(17718080086583564125)
XLA Ops:
  12.0 25.1 %all-gather = bf16[16,1,128]{2,1,0:T(2,128)(2,1)S(1)} all-gather(bf16[1,1,128]{2,1,0:T(2,128)(2,1)} %bitcast.244), channel_id=1, replica_groups=mesh['ctx'=8,'fsdp'=16] {'fsdp'}, dimensions={0}, use_global_device_ids=true | all-gather | bytes 4352 | tf_op jit(solution)/shard_map/all_gather | solution.py:72
  37.1 19.3 all-gather.1
  56.5 2.8 gather_fusion
  63.1 1.6 convolution_convert_fusion.8
  64.7 29.5 %all_gather.42 = bf16[1024,256]{1,0:T(8,128)(2,1)S(1)} all-gather(bf16[128,256]{1,0:T(8,128)(2,1)S(1)} %convolution_convert_fusion.8), channel_id=1, replica_groups=mesh['ctx'=8,'fsdp'=16] {'ctx'}, dimensions={0}, use_global_device_ids=true | all-gather | bytes 589824 | tf_op jit(solution)/shard_map/all_gather | solution.py:150
  94.5 10.2 all-gather.12.cloned.1.call-done
  106.7 27.0 %all_gather.44 = bf16[1024,256]{0,1:T(8,128)(2,1)S(1)} all-gather(bf16[128,256]{0,1:T(8,128)(2,1)S(1)} %bitcast.239), channel_id=1, replica_groups=mesh['ctx'=8,'fsdp'=16] {'ctx'}, dimensions={0}, use_global_device_ids=true | all-gather | bytes 589824 | tf_op jit(solution)/shard_map/all_gather | solution.py:149
  133.7 47.0 %all-gather.14.cloned.1.call-done = bf16[2048,2048]{1,0:T(8,128)(2,1)} async-done(((bf16[128,2048]{1,0:T(8,128)(2,1)}), bf16[2048,2048]{1,0:T(8,128)(2,1)}) %all-gather.14.cloned.1.call-update) | async-done | bytes 8388624 | tf_op jit(solution)/shard_map/all_gather | solution.py:74
  180.7 12.3 copy.43
  193.0 5.9 fusion.51
  199.2 7.3 fusion.95
  206.5 8.4 fusion.3
  214.9 7.9 fusion.27
  222.8 30.6 %all-gather.16.cloned.1.call-done = bf16[2048,2048]{1,0:T(8,128)(2,1)} async-done(((bf16[128,2048]{1,0:T(8,128)(2,1)}), bf16[2048,2048]{1,0:T(8,128)(2,1)}) %all-gather.16.cloned.1.call-update) | async-done | bytes 8388624 | tf_op jit(solution)/shard_map/all_gather | solution.py:77
  253.4 4.8 multiply_reduce_fusion.2
  258.4 134.3 %all-gather.20.cloned.1.call-done = bf16[2048,5632]{1,0:T(8,128)(2,1)} async-done(((bf16[128,5632]{1,0:T(8,128)(2,1)}), bf16[2048,5632]{1,0:T(8,128)(2,1)}) %all-gather.20.cloned.1.call-update) | async-done | bytes 23068688 | tf_op jit(solution)/shard_map/all_gather | solution.py:84
  392.7 12.3 fusion.97
  405.0 126.8 %all-gather.18.cloned.1.call-done = bf16[2048,5632]{1,0:T(8,128)(2,1)} async-done(((bf16[128,5632]{1,0:T(8,128)(2,1)}), bf16[2048,5632]{1,0:T(8,128)(2,1)}) %all-gather.18.cloned.1.call-update) | async-done | bytes 23068688 | tf_op jit(solution)/shard_map/all_gather | solution.py:83
  531.8 12.3 fusion.96
  544.1 126.9 %all-gather.22.cloned.1.call-done = bf16[5632,2048]{1,0:T(8,128)(2,1)} async-done(((bf16[352,2048]{1,0:T(8,128)(2,1)}), bf16[5632,2048]{1,0:T(8,128)(2,1)}) %all-gather.22.cloned.1.call-update) | async-done | bytes 23068688 | tf_op jit(solution)/shard_map/all_gather | solution.py:85
  671.0 14.9 multiply_convert_fusion
  685.9 12.6 fusion.98
  698.5 13.3 multiply_reduce_fusion
  711.8 1.7 fusion.36
  713.5 7.1 convolution_convert_fusion.7
  720.6 2.0 copy.45
  722.7 9.5 fusion.23
  732.2 10.7 fusion
  742.9 2.0 copy.59
  745.0 12.0 fusion.2
  757.0 3.3 copy-done.2
  760.3 3.4 fusion.26
  763.7 2.0 copy.57
  765.8 14.6 reduce-scatter.30.cloned.1.call-done
  780.5 2.4 convolution_convert_fusion.5
  782.9 37.3 %reduce-scatter.28.cloned.1.call-done = bf16[128,256]{1,0:T(8,128)(2,1)} async-done(((bf16[1024,256]{1,0:T(8,128)(2,1)}), bf16[128,256]{1,0:T(8,128)(2,1)}) %reduce-scatter.28.cloned.1.call-update) | async-done | bytes 65552
  821.3 1.5 convolution_convert_fusion.6
  822.9 6.7 convolution_convert_fusion.3
  829.6 5.2 convolution_multiply_fusion
  837.0 5.7 convolution_convert_fusion.4
  842.7 12.4 convolution_convert_fusion
  855.2 12.3 convolution_convert_fusion.1
  867.5 12.2 convolution_convert_fusion.2
  880.1 9.5 reduce-scatter.18.cloned.1.call-done
  889.6 70.6 %reduce-scatter.16.cloned.1.call-done = bf16[128,256]{1,0:T(8,128)(2,1)} async-done(((bf16[2048,256]{1,0:T(8,128)(2,1)}), bf16[128,256]{1,0:T(8,128)(2,1)}) %reduce-scatter.16.cloned.1.call-update) | async-done | bytes 65552 | tf_op jit(solution)/shard_map/reduce_scatter | solution.py:90
  960.2 105.9 %reduce-scatter.20.cloned.1.call-done = bf16[128,2048]{1,0:T(8,128)(2,1)} async-done(((bf16[2048,2048]{1,0:T(8,128)(2,1)}), bf16[128,2048]{1,0:T(8,128)(2,1)}) %reduce-scatter.20.cloned.1.call-update) | async-done | bytes 524304 | tf_op jit(solution)/shard_map/reduce_scatter | solution.py:90
  1066.1 105.7 %reduce-scatter.14.cloned.1.call-done = bf16[128,2048]{1,0:T(8,128)(2,1)} async-done(((bf16[2048,2048]{1,0:T(8,128)(2,1)}), bf16[128,2048]{1,0:T(8,128)(2,1)}) %reduce-scatter.14.cloned.1.call-update) | async-done | bytes 524304 | tf_op jit(solution)/shard_map/reduce_scatter | solution.py:90
  1171.8 181.8 %reduce-scatter.26.cloned.1.call-done = bf16[352,2048]{1,0:T(8,128)(2,1)} async-done(((bf16[5632,2048]{1,0:T(8,128)(2,1)}), bf16[352,2048]{1,0:T(8,128)(2,1)}) %reduce-scatter.26.cloned.1.call-update) | async-done | bytes 1441808 | tf_op jit(solution)/shard_map/reduce_scatter | solution.py:90
  1353.7 181.5 %reduce-scatter.24.cloned.1.call-done = bf16[128,5632]{1,0:T(8,128)(2,1)} async-done(((bf16[2048,5632]{1,0:T(8,128)(2,1)}), bf16[128,5632]{1,0:T(8,128)(2,1)}) %reduce-scatter.24.cloned.1.call-update) | async-done | bytes 1441808 | tf_op jit(solution)/shard_map/reduce_scatter | solution.py:90
  1535.2 180.9 %reduce-scatter.22.cloned.1.call-done = bf16[128,5632]{1,0:T(8,128)(2,1)} async-done(((bf16[2048,5632]{1,0:T(8,128)(2,1)}), bf16[128,5632]{1,0:T(8,128)(2,1)}) %reduce-scatter.22.cloned.1.call-update) | async-done | bytes 1441808 | tf_op jit(solution)/shard_map/reduce_scatter | solution.py:90
  1717.4 1.8 fusion.42
  1719.1 6.3 fusion.99
  1725.5 12.0 fusion.14
  1738.1 1.6 fusion.31
  1739.6 66.7 %all-reduce.2 = (bf16[2048]{0:T(1024)(128)(2,1)S(1)}, bf16[2048]{0:T(1024)(128)(2,1)S(1)}) all-reduce(f32[2048]{0:T(1024)S(1)} %get-tuple-element.13, f32[2048]{0:T(1024)S(1)} %get-tuple-element.11), channel_id=4, replica_groups=mesh['ctx'=8,'fsdp'=16] {'fsdp'}, use_global_device_ids=true, to_apply=%region_10.11.clone | all-reduce | flops 4096 | bytes 24576
  1806.5 21.1 %all-reduce.3 = (bf16[128]{0:T(256)(128)(2,1)S(1)}, bf16[128]{0:T(256)(128)(2,1)S(1)}) all-reduce(bf16[128]{0:T(256)(128)(2,1)S(1)} %dynamic-slice.7, bf16[128]{0:T(256)(128)(2,1)S(1)} %dynamic-slice.6), channel_id=1, replica_groups=mesh['ctx'=8,'fsdp'=16] {'ctx'}, use_global_device_ids=true, to_apply=%region_11.12 | all-reduce | flops 256 | bytes 1024 | tf_op jit(solution)/shard_map/psum | solution.py:246
  1828.6 2.4 fusion.47
  1831.0 123.6 %all-reduce.7.cloned.1.call-done = (bf16[128,2048]{1,0:T(8,128)(2,1)}, bf16[128,256]{1,0:T(8,128)(2,1)}, bf16[128,256]{1,0:T(8,128)(2,1)}, bf16[128,2048]{1,0:T(...) async-done(((bf16[128,2048]{1,0:T(8,128)(2,1)}, bf16[128,256]{1,0:T(8,128)(2,1)}, bf16[128,256]{1,0:T(8,128)(2,1)}, ...) | async-done | bytes 5505040 | tf_op jit(solution)/shard_map/psum | solution.py:247
  1954.5 1.7 convert_element_type.235
  1957.7 2.1 convert_element_type.233
  1959.8 2.1 convert_element_type.239
  1961.9 3.2 convert_element_type.243
  1965.1 1.9 convert_element_type.245
  1967.0 1.9 convert_element_type.247
  (125 shorter events, 18.9 us)
Async XLA Ops:
  7.2 49.3 %copy-start = (s32[16,8,2]{0,2,1:T(2,128)S(1)}, s32[16,8,2]{0,2,1:T(2,128)}, u32[]{:S(2)}) copy-start(s32[16,8,2]{0,2,1:T(2,128)} %param.13) | copy-start | bytes 3076
  7.2 54.8 %copy-start.3 = (bf16[1,128,2048]{2,1,0:T(8,128)(2,1)S(1)}, bf16[1,128,2048]{2,1,0:T(8,128)(2,1)}, u32[]{:S(2)}) copy-start(bf16[1,128,2048]{2,1,0:T(8,128)(2,1)} %param.12) | copy-start | bytes 1572868
  7.2 55.9 %all-gather.10.cloned.1.call-start = ((), (), s32[]{:S(2)}) async-start(), calls=%async_computation.9 | async-start | bytes 1114112 | tf_op jit(solution)/shard_map/all_gather | solution.py:76
  7.9 96.7 %all-gather.12.cloned.1.call-start = ((), (), s32[]{:S(2)}) async-start(), calls=%async_computation.10 | async-start | bytes 1114112 | tf_op jit(solution)/shard_map/all_gather | solution.py:75
  8.7 172.0 %all-gather.14.cloned.1.call-start = ((), (), s32[]{:S(2)}) async-start(), calls=%async_computation.11 | async-start | bytes 8912896 | tf_op jit(solution)/shard_map/all_gather | solution.py:74
  9.4 244.0 %all-gather.16.cloned.1.call-start = ((), (), s32[]{:S(2)}) async-start(), calls=%async_computation.12 | async-start | bytes 8912896 | tf_op jit(solution)/shard_map/all_gather | solution.py:77
  10.0 382.7 %all-gather.20.cloned.1.call-start = ((), (), s32[]{:S(2)}) async-start(), calls=%async_computation.14 | async-start | bytes 24510464 | tf_op jit(solution)/shard_map/all_gather | solution.py:84
  10.6 521.2 %all-gather.18.cloned.1.call-start = ((), (), s32[]{:S(2)}) async-start(), calls=%async_computation.13 | async-start | bytes 24510464 | tf_op jit(solution)/shard_map/all_gather | solution.py:83
  11.2 659.8 %all-gather.22.cloned.1.call-start = ((), (), s32[]{:S(2)}) async-start(), calls=%async_computation.15 | async-start | bytes 24510464 | tf_op jit(solution)/shard_map/all_gather | solution.py:85
  11.9 768.6 %reduce-scatter.30.cloned.1.call-start = ((), (), s32[]{:S(2)}) async-start(), calls=%async_computation.24 | async-start | bytes 589824
  62.2 130.8 %copy-start.20 = (f32[128]{0:T(128)}, f32[128]{0:T(128)S(1)}, u32[]{:S(2)}) copy-start(f32[128]{0:T(128)S(1)} %fusion.32) | copy-start | bytes 1540
  94.5 120.5 %copy-start.13 = (bf16[1024,256]{0,1:T(8,128)(2,1)}, bf16[1024,256]{0,1:T(8,128)(2,1)S(1)}, u32[]{:S(2)}) copy-start(bf16[1024,256]{0,1:T(8,128)(2,1)S(1)} %copy.41) | copy-start | bytes 1572868
  133.7 65.5 %copy-start.9 = (bf16[1024,256]{0,1:T(8,128)(2,1)}, bf16[1024,256]{0,1:T(8,128)(2,1)S(1)}, u32[]{:S(2)}) copy-start(bf16[1024,256]{0,1:T(8,128)(2,1)S(1)} %all_gather.44) | copy-start | bytes 1572868
  199.2 7.3 copy-start.10
  222.8 35.3 %copy-start.8 = (bf16[4,64,8,128]{3,1,2,0:T(8,128)(2,1)}, bf16[4,64,8,128]{3,1,2,0:T(8,128)(2,1)S(1)}, u32[]{:S(2)}) copy-start(bf16[4,64,8,128]{3,1,2,0:T(8,128)(2,1)S(1)} %fusion.27) | copy-start | bytes 1572868
  405.0 266.0 %copy-start.15 = (bf16[1,128,2048]{2,1,0:T(8,128)(2,1)S(1)}, bf16[1,128,2048]{2,1,0:T(8,128)(2,1)}, u32[]{:S(2)}) copy-start(bf16[1,128,2048]{2,1,0:T(8,128)(2,1)} %param.23) | copy-start | bytes 1572868
  685.9 12.6 copy-start.5
  722.7 9.5 copy-start.7
  722.7 9.5 copy-start.14
  745.0 75.3 %reduce-scatter.28.cloned.1.call-start = ((), (), s32[]{:S(2)}) async-start(), calls=%async_computation.23 | async-start | bytes 589824
  745.0 15.3 copy-start.11
  757.0 3.3 copy-start.2
  765.8 123.8 %reduce-scatter.18.cloned.1.call-start = ((), (), s32[]{:S(2)}) async-start(), calls=%async_computation.18 | async-start | bytes 1114112 | tf_op jit(solution)/shard_map/reduce_scatter | solution.py:90
  782.9 177.4 %reduce-scatter.16.cloned.1.call-start = ((), (), s32[]{:S(2)}) async-start(), calls=%async_computation.17 | async-start | bytes 1114112 | tf_op jit(solution)/shard_map/reduce_scatter | solution.py:90
  822.8 243.3 %reduce-scatter.20.cloned.1.call-start = ((), (), s32[]{:S(2)}) async-start(), calls=%async_computation.19 | async-start | bytes 8912896 | tf_op jit(solution)/shard_map/reduce_scatter | solution.py:90
  829.6 342.3 %reduce-scatter.14.cloned.1.call-start = ((), (), s32[]{:S(2)}) async-start(), calls=%async_computation.16 | async-start | bytes 8912896 | tf_op jit(solution)/shard_map/reduce_scatter | solution.py:90
  834.8 1.0 copy-start.4
  842.7 511.0 %reduce-scatter.26.cloned.1.call-start = ((), (), s32[]{:S(2)}) async-start(), calls=%async_computation.22 | async-start | bytes 24510464 | tf_op jit(solution)/shard_map/reduce_scatter | solution.py:90
  855.1 680.1 %reduce-scatter.24.cloned.1.call-start = ((), (), s32[]{:S(2)}) async-start(), calls=%async_computation.21 | async-start | bytes 24510464 | tf_op jit(solution)/shard_map/reduce_scatter | solution.py:90
  867.5 848.6 %reduce-scatter.22.cloned.1.call-start = ((), (), s32[]{:S(2)}) async-start(), calls=%async_computation.20 | async-start | bytes 24510464 | tf_op jit(solution)/shard_map/reduce_scatter | solution.py:90
  879.8 836.3 %copy-start.22 = (u32[128]{0:T(128)S(1)}, u32[128]{0:T(128)}, u32[]{:S(2)}) copy-start(u32[128]{0:T(128)} %constant.179) | copy-start | bytes 1540
  879.8 1074.7 %all-reduce.7.cloned.1.call-start = ((), (), s32[]{:S(2)}) async-start(), calls=%async_computation.25 | async-start | bytes 11010048 | tf_op jit(solution)/shard_map/psum | solution.py:247
  1717.4 8.1 copy-start.6
  1725.5 12.1 copy-start.12
  1725.5 12.5 copy-start.18
  1725.5 12.5 copy-start.19
  1725.5 103.1 %copy-start.21 = (f32[128]{0:T(128)S(1)}, f32[128]{0:T(128)}, u32[]{:S(2)}) copy-start(f32[128]{0:T(128)} %copy-done.20) | copy-start | bytes 1540
  1828.6 140.3 %copy-start.1 = (s32[16,8,2]{0,2,1:T(2,128)S(1)}, s32[16,8,2]{0,2,1:T(2,128)}, u32[]{:S(2)}) copy-start(s32[16,8,2]{0,2,1:T(2,128)} %param.13) | copy-start | bytes 3076
  1954.5 10.6 copy-start.17
  1954.5 12.5 copy-start.16
Sparse Core Ops, SparseCore 0:
  10.4 47.5 all-gather.9
  60.4 44.1 all-gather.11
  107.0 73.6 all-gather.13
  183.0 70.3 all-gather.15
  255.7 136.9 all-gather.19
  394.9 136.7 all-gather.17
  534.2 136.7 all-gather.21
  745.1 35.3 reduce-scatter.29
  783.5 36.6 reduce-scatter.27
  824.5 65.0 reduce-scatter.17
  894.5 65.6 reduce-scatter.15
  964.4 101.6 reduce-scatter.19
  1070.5 101.3 reduce-scatter.13
  1176.1 177.5 reduce-scatter.25
  1358.6 176.6 reduce-scatter.23
  1539.5 176.5 reduce-scatter.21
  1719.3 235.1 all-reduce.6
where the time goes:
time: 1980 us
  waiting for transfers between devices  1490 us (75%)
  matrix products  203 us (10%)
  blocking collectives  189 us (10%)
  other arithmetic  46.3 us (2%)
  local copies, waits for them, and re-layouts  29.8 us (2%)
    reduce_scatter x7, waiting for transfers between devices, weight_share(): lax.psum_scatter(mult_rows(left, right).astype(jnp.bfloat16), 'fsdp', sca...  836 us
    all_gather x1, waiting for transfers between devices, fetch_mlp(): lax.all_gather(up_weight, 'fsdp', axis=0, tiled=True)  134 us
    all_gather x1, waiting for transfers between devices, fetch_mlp(): lax.all_gather(down_weight, 'fsdp', axis=0, tiled=True)  127 us
    all_gather x1, waiting for transfers between devices, fetch_mlp(): lax.all_gather(gate_weight, 'fsdp', axis=0, tiled=True)  127 us
    psum x1, waiting for transfers between devices, on_device(): lax.psum(query_part.astype(jnp.bfloat16), 'ctx').astype(jnp.float32)  124 us
    unnamed x1, blocking collectives  66.7 us
    unnamed x19, waiting for transfers between devices  56.5 us
    dot_general x7, matrix products, mult_back(): lax.dot_general(left, right, (((1,), (1,)), ((), ())), preferred_element_...  56.3 us
  transfers between devices with their start and end apart: 17, of which 16 were waited for; matrix products, arithmetic and copies ran while one was open for 9% of the time, Pallas kernels for 0%

commit v1 on v0

--- a/solution.py
+++ b/solution.py
@@ -78,12 +78,44 @@
     )
 
 
+def swap_pairs():
+    pairs = []
+    for c in range(8):
+        for f in range(16):
+            pairs.append((c * 16 + f, (f // 2) * 16 + 2 * c + f % 2))
+    return pairs
+
+
 def fetch_mlp(gate_weight, up_weight, down_weight):
+    c = lax.axis_index("ctx")
+    width = gate_weight.shape[1] // 8
+    gate_own = lax.dynamic_slice_in_dim(gate_weight, c * width, width, 1)
+    up_own = lax.dynamic_slice_in_dim(up_weight, c * width, width, 1)
+    span = down_weight.shape[1] // 8
+    rows = down_weight.shape[0]
+    down_own = lax.dynamic_slice_in_dim(down_weight, c * span, span, 1)
+    down_own = lax.ppermute(down_own, ("ctx", "fsdp"), swap_pairs())
+    down_all = lax.all_gather(down_own, "fsdp", axis=0, tiled=False)
+    down_all = down_all.reshape(8, 2, rows, span).transpose(1, 2, 0, 3).reshape(2 * rows, 8 * span)
     return (
-        lax.all_gather(gate_weight, "fsdp", axis=0, tiled=True),
-        lax.all_gather(up_weight, "fsdp", axis=0, tiled=True),
-        lax.all_gather(down_weight, "fsdp", axis=0, tiled=True),
-    )
+        lax.all_gather(gate_own, "fsdp", axis=0, tiled=True),
+        lax.all_gather(up_own, "fsdp", axis=0, tiled=True),
+        down_all,
+    )
+
+
+def sliced_share(grad):
+    part = lax.psum_scatter(grad.astype(jnp.bfloat16), "fsdp", scatter_dimension=0, tiled=True)
+    return lax.all_gather(part, "ctx", axis=1, tiled=True).astype(jnp.float32)
+
+
+def down_share(grad):
+    rows, span = grad.shape[0] // 2, grad.shape[1] // 8
+    grad = grad.astype(jnp.bfloat16).reshape(2, rows, 8, span).transpose(2, 0, 1, 3)
+    grad = grad.reshape(16, rows, span)
+    part = lax.psum_scatter(grad, "fsdp", scatter_dimension=0, tiled=False)
+    part = lax.ppermute(part, ("ctx", "fsdp"), swap_pairs())
+    return lax.all_gather(part, "ctx", axis=1, tiled=True).astype(jnp.float32)
 
 
 def weight_share(left, right):
@@ -160,23 +192,30 @@
     )
     attended = heads_out.astype(jnp.bfloat16).reshape(row_count, HEADS * HEAD_DIM)
     hidden_state = inputs + mult(attended, output_full)
-    gate_full, up_full, down_full = fetch_mlp(gate_weight, up_weight, down_weight)
+    gate_part, up_part, down_part = fetch_mlp(gate_weight, up_weight, down_weight)
     normed_two = rms_norm(hidden_state, gain_second).astype(jnp.bfloat16)
-    gate_act = mult(normed_two, gate_full)
-    up_act = mult(normed_two, up_full)
+    normed_two_all = lax.all_gather(normed_two, "ctx", axis=0, tiled=True)
+    grad_mlp_all = lax.all_gather(cotangent[0], "ctx", axis=0, tiled=True)
+    gate_act = mult(normed_two_all, gate_part)
+    up_act = mult(normed_two_all, up_part)
     inner = (jax.nn.silu(gate_act) * up_act).astype(jnp.bfloat16)
-    mixed = (hidden_state + mult(inner, down_full)).astype(jnp.bfloat16)
-    gain_one, gain_two, query_full, key_full, value_full, output_full = fetch_attention(
-        attn_gain, mlp_gain, query_weight, key_weight, value_weight, output_weight
-    )
-    gate_full, up_full, down_full = fetch_mlp(gate_weight, up_weight, down_weight)
-    grad_mlp = cotangent[0]
-    grad_inner = mult_back(grad_mlp, down_full)
+    mixed = (
+        hidden_state
+        + lax.psum_scatter(
+            mult(inner, down_part).astype(jnp.bfloat16), "ctx", scatter_dimension=0, tiled=True
+        ).astype(jnp.float32)
+    ).astype(jnp.bfloat16)
+    grad_inner = mult_back(grad_mlp_all, down_part)
     _, swiglu_back = jax.vjp(lambda first, second: jax.nn.silu(first) * second, gate_act, up_act)
     grad_gate, grad_up = swiglu_back(grad_inner)
     grad_gate = grad_gate.astype(jnp.bfloat16)
     grad_up = grad_up.astype(jnp.bfloat16)
-    grad_normed_two = mult_back(grad_gate, gate_full) + mult_back(grad_up, up_full)
+    grad_normed_two = lax.psum_scatter(
+        (mult_back(grad_gate, gate_part) + mult_back(grad_up, up_part)).astype(jnp.bfloat16),
+        "ctx",
+        scatter_dimension=0,
+        tiled=True,
+    ).astype(jnp.float32)
     _, norm_two_back = jax.vjp(rms_norm, hidden_state, gain_second)
     grad_hidden_norm, grad_gain_two = norm_two_back(grad_normed_two)
     grad_hidden = grad_out + grad_hidden_norm
@@ -235,9 +274,9 @@
     key_part = weight_share(normed, grad_key_raw)
     value_part = weight_share(normed, grad_value_raw)
     output_part = weight_share(attended, grad_att)
-    gate_part = weight_share(normed_two, grad_gate)
-    up_part = weight_share(normed_two, grad_up)
-    down_part = weight_share(inner, grad_mlp)
+    gate_part = sliced_share(mult_rows(normed_two_all, grad_gate))
+    up_part = sliced_share(mult_rows(normed_two_all, grad_up))
+    down_part = down_share(mult_rows(inner, grad_mlp_all))
     gain_one_part, gain_two_part = (
         lax.psum_scatter(grad_gain_one, "fsdp", scatter_dimension=0, tiled=True),
         lax.psum_scatter(grad_gain_two, "fsdp", scatter_dimension=0, tiled=True),
@@ -249,9 +288,9 @@
         lax.psum(value_part.astype(jnp.bfloat16), "ctx").astype(jnp.float32),
         lax.psum(output_part.astype(jnp.bfloat16), "ctx").astype(jnp.float32),
         lax.psum(gain_two_part.astype(jnp.bfloat16), "ctx").astype(jnp.float32),
-        lax.psum(gate_part.astype(jnp.bfloat16), "ctx").astype(jnp.float32),
-        lax.psum(up_part.astype(jnp.bfloat16), "ctx").astype(jnp.float32),
-        lax.psum(down_part.astype(jnp.bfloat16), "ctx").astype(jnp.float32),
+        gate_part,
+        up_part,
+        down_part,
     )
     return (
         mixed[None],

time: 1980 us -> 1730 us (0.87)
  waiting for transfers between devices: 1490 us -> 1240 us
  matrix products: 203 us -> 152 us
  local copies, waits for them, and re-layouts: 29.8 us -> 58.9 us
    reduce_scatter x7 -> x4, waiting for transfers between devices: 836 us -> 344 us  [weight_share(): lax.psum_scatter(mult_rows(left, right).astype(jnp.bfloat16), 'fsdp', sca...]
    reduce_scatter x0 -> x3, waiting for transfers between devices: none -> 219 us  [the longest x1 92.3 us: on_device(): lax.psum_scatter(mult(inner, down_part).astype(jnp.bfloat16), 'ctx', scat...]
    unnamed x19 -> x28, waiting for transfers between devices: 56.5 us -> 185 us
    psum x1, waiting for transfers between devices: 124 us -> 0.01 us  [on_device(): lax.psum(query_part.astype(jnp.bfloat16), 'ctx').astype(jnp.float32)]
    all_gather x3 -> x8, waiting for transfers between devices: 388 us -> 422 us  [the longest x1 90.6 us: on_device(): normed_two_all = lax.all_gather(normed_two, 'ctx', axis=0, tiled=True)]
    unnamed x52 -> x80, local copies, waits for them, and re-layouts: 9.92 us -> 30.6 us
  transfers between devices with their start and end apart: 17 -> 26, of which waited for: 16 -> 21; matrix products, arithmetic and copies ran while one was open for 9% -> 13% of each run, Pallas kernels for 0% -> 0%
where the time goes in v1:
time: 1730 us; the launch traced here: 1720 us
  waiting for transfers between devices  1240 us (72%)
  blocking collectives  200 us (12%)
  matrix products  152 us (9%)
  local copies, waits for them, and re-layouts  58.9 us (3%)
  other arithmetic  44 us (3%)
    reduce_scatter x4, waiting for transfers between devices, weight_share(): lax.psum_scatter(mult_rows(left, right).astype(jnp.bfloat16), 'fsdp', sca...  344 us
    unnamed x28, waiting for transfers between devices  185 us
    reduce_scatter x1, waiting for transfers between devices, on_device(): lax.psum_scatter(mult(inner, down_part).astype(jnp.bfloat16), 'ctx', scat...  92.3 us
    all_gather x1, waiting for transfers between devices, on_device(): normed_two_all = lax.all_gather(normed_two, 'ctx', axis=0, tiled=True)  90.6 us
    all_gather x1, waiting for transfers between devices, on_device(): grad_mlp_all = lax.all_gather(cotangent[0], 'ctx', axis=0, tiled=True)  82.1 us
    reduce_scatter x1, waiting for transfers between devices, down_share(): part = lax.psum_scatter(grad, 'fsdp', scatter_dimension=0, tiled=False)  75.6 us
    unnamed x1, blocking collectives  65.3 us
    all_gather x2, waiting for transfers between devices, sliced_share(): return lax.all_gather(part, 'ctx', axis=1, tiled=True).astype(jnp.float32)  60 us
  transfers between devices with their start and end apart: 26, of which 21 were waited for; matrix products, arithmetic and copies ran while one was open for 13% of the time, Pallas kernels for 0%

profile of v1, /device:TPU:0, one launch (start us, length us, event | category | flops | bytes accessed | tf_op | source)
XLA Modules:
  0.0 1719.7 jit_solution(10038083252428583648)
XLA Ops:
  13.5 3.5 gather_fusion
  19.7 40.9 %all-gather.2 = bf16[16,1,128]{2,1,0:T(2,128)(2,1)S(1)} all-gather(bf16[1,1,128]{2,1,0:T(2,128)(2,1)S(1)} %bitcast.278), channel_id=1, replica_groups=mesh['ctx'=8,'fsdp'=16] {'fsdp'}, dimensions={0}, use_global_device_ids=true | all-gather | bytes 4352 | tf_op jit(solution)/shard_map/all_gather | solution.py:72
  60.6 19.1 %all-gather.3 = bf16[16,1,128]{2,1,0:T(2,128)(2,1)S(1)} all-gather(bf16[1,1,128]{2,1,0:T(2,128)(2,1)S(1)} %bitcast.279), channel_id=1, replica_groups=mesh['ctx'=8,'fsdp'=16] {'fsdp'}, dimensions={0}, use_global_device_ids=true | all-gather | bytes 4352 | tf_op jit(solution)/shard_map/all_gather | solution.py:73
  82.5 29.3 %all_gather.53 = bf16[1024,256]{1,0:T(8,128)(2,1)S(1)} all-gather(bf16[128,256]{1,0:T(8,128)(2,1)S(1)} %convolution_convert_fusion.8), channel_id=1, replica_groups=mesh['ctx'=8,'fsdp'=16] {'ctx'}, dimensions={0}, use_global_device_ids=true | all-gather | bytes 589824 | tf_op jit(solution)/shard_map/all_gather | solution.py:182
  114.2 26.0 %all_gather.55 = bf16[1024,256]{0,1:T(8,128)(2,1)S(1)} all-gather(bf16[128,256]{0,1:T(8,128)(2,1)S(1)} %bitcast.273), channel_id=1, replica_groups=mesh['ctx'=8,'fsdp'=16] {'ctx'}, dimensions={0}, use_global_device_ids=true | all-gather | bytes 589824 | tf_op jit(solution)/shard_map/all_gather | solution.py:181
  140.3 43.2 %all-gather.21.cloned.1.call-done = bf16[2048,2048]{1,0:T(8,128)(2,1)} async-done(((bf16[128,2048]{1,0:T(8,128)(2,1)}), bf16[2048,2048]{1,0:T(8,128)(2,1)}) %all-gather.21.cloned.1.call-update) | async-done | bytes 8388624 | tf_op jit(solution)/shard_map/all_gather | solution.py:74
  183.5 12.3 copy.50
  195.8 5.8 fusion.59
  202.0 7.2 fusion.103
  209.1 8.3 fusion.3
  217.4 8.0 fusion.33
  225.4 30.8 %all-gather.23.cloned.1.call-done = bf16[2048,2048]{1,0:T(8,128)(2,1)} async-done(((bf16[128,2048]{1,0:T(8,128)(2,1)}), bf16[2048,2048]{1,0:T(8,128)(2,1)}) %all-gather.23.cloned.1.call-update) | async-done | bytes 8388624 | tf_op jit(solution)/shard_map/all_gather | solution.py:77
  256.2 4.7 multiply_reduce_fusion
  264.7 43.3 %all-gather.37.cloned.1.call-done = bf16[5632,256]{1,0:T(8,128)(2,1)} async-done(((bf16[352,256]{1,0:T(8,128)(2,1)}), bf16[5632,256]{1,0:T(8,128)(2,1)}) %all-gather.37.cloned.1.call-update) | async-done | bytes 2883600 | tf_op jit(solution)/shard_map/all_gather | solution.py:98
  308.1 3.4 copy.52
  311.5 2.6 copy.76
  314.1 47.8 %all-gather.29.cloned.1.call-done = bf16[2048,704]{1,0:T(8,128)(2,1)} async-done(((bf16[128,704]{1,0:T(8,128)(2,1)}), bf16[2048,704]{1,0:T(8,128)(2,1)}) %all-gather.29.cloned.1.call-update) | async-done | bytes 2883600 | tf_op jit(solution)/shard_map/all_gather | solution.py:102
  361.8 90.6 %all-gather.25.cloned.1.call-done = bf16[1024,2048]{1,0:T(8,128)(2,1)} async-done(((bf16[128,2048]{1,0:T(8,128)(2,1)}), bf16[1024,2048]{1,0:T(8,128)(2,1)}) %all-gather.25.cloned.1.call-update) | async-done | bytes 4194320 | tf_op jit(solution)/shard_map/all_gather | solution.py:197
  452.5 7.9 fusion.105
  460.4 49.9 %all-gather.27.cloned.1.call-done = bf16[2048,704]{1,0:T(8,128)(2,1)} async-done(((bf16[128,704]{1,0:T(8,128)(2,1)}), bf16[2048,704]{1,0:T(8,128)(2,1)}) %all-gather.27.cloned.1.call-update) | async-done | bytes 2883600 | tf_op jit(solution)/shard_map/all_gather | solution.py:101
  510.3 7.9 fusion.104
  518.2 82.1 %all-gather.39.cloned.1.call-done = bf16[1,1024,2048]{2,1,0:T(8,128)(2,1)} async-done(((bf16[1,128,2048]{2,1,0:T(8,128)(2,1)}), bf16[1,1024,2048]{2,1,0:T(8,128)(2,1)}) %all-gather.39.cloned.1.call-update) | async-done | bytes 4194320 | tf_op jit(solution)/shard_map/all_gather | solution.py:198
  600.3 10.6 fusion.19
  611.0 3.5 fusion.106
  614.5 5.2 add_convert_fusion
  619.8 7.7 convolution_convert_fusion.2
  627.6 7.4 convolution_convert_fusion.3
  634.9 4.6 copy.74
  639.8 7.4 convolution_convert_fusion.4
  647.2 4.6 copy.72
  651.9 5.8 fusion.13
  658.9 2.2 copy.57
  661.4 51.2 %reduce-scatter.22.cloned.1.call-done = bf16[128,2048]{1,0:T(8,128)(2,1)} async-done(((bf16[1024,2048]{1,0:T(8,128)(2,1)}), bf16[128,2048]{1,0:T(8,128)(2,1)}) %reduce-scatter.22.cloned.1.call-update) | async-done | bytes 524304 | tf_op jit(solution)/shard_map/reduce_scatter | solution.py:213
  714.0 92.3 %reduce-scatter.20.cloned.1.call-done = bf16[128,2048]{1,0:T(8,128)(2,1)} async-done(((bf16[1024,2048]{1,0:T(8,128)(2,1)}), bf16[128,2048]{1,0:T(8,128)(2,1)}) %reduce-scatter.20.cloned.1.call-update) | async-done | bytes 524304 | tf_op jit(solution)/shard_map/reduce_scatter | solution.py:204
  806.3 2.5 fusion.46
  808.8 6.3 convolution_convert_fusion.7
  815.4 9.6 fusion.29
  827.0 11.5 fusion
  838.6 12.2 fusion.2
  850.9 2.6 fusion.32
  855.2 31.3 %reduce-scatter.40.cloned.1.call-done = bf16[128,704]{1,0:T(8,128)(2,1)} async-done(((bf16[2048,704]{1,0:T(8,128)(2,1)}), bf16[128,704]{1,0:T(8,128)(2,1)}) %reduce-scatter.40.cloned.1.call-update) | async-done | bytes 180240
  888.3 76.3 %reduce-scatter.38.cloned.1.call-done = bf16[128,704]{1,0:T(8,128)(2,1)} async-done(((bf16[2048,704]{1,0:T(8,128)(2,1)}), bf16[128,704]{1,0:T(8,128)(2,1)}) %reduce-scatter.38.cloned.1.call-update) | async-done | bytes 180240
  966.5 75.6 %reduce-scatter.32.cloned.1.call-done = bf16[1,352,256]{2,1,0:T(8,128)(2,1)} async-done(((bf16[16,352,256]{2,1,0:T(8,128)(2,1)}), bf16[1,352,256]{2,1,0:T(8,128)(2,1)}) %reduce-scatter.32.cloned.1.call-update) | async-done | bytes 180240 | tf_op jit(solution)/shard_map/reduce_scatter | solution.py:116
  1044.3 37.3 %reduce-scatter.36.cloned.1.call-done = bf16[128,256]{1,0:T(8,128)(2,1)} async-done(((bf16[1024,256]{1,0:T(8,128)(2,1)}), bf16[128,256]{1,0:T(8,128)(2,1)}) %reduce-scatter.36.cloned.1.call-update) | async-done | bytes 65552
  1081.7 2.3 convolution_convert_fusion.5
  1084.1 36.7 %reduce-scatter.34.cloned.1.call-done = bf16[128,256]{1,0:T(8,128)(2,1)} async-done(((bf16[1024,256]{1,0:T(8,128)(2,1)}), bf16[128,256]{1,0:T(8,128)(2,1)}) %reduce-scatter.34.cloned.1.call-update) | async-done | bytes 65552
  1123.8 5.6 convolution_convert_fusion
  1130.4 4.9 convolution_multiply_fusion
  1136.7 5.7 convolution_convert_fusion.1
  1144.4 18.5 %all-gather.33.cloned.1.call-done = bf16[128,5632]{0,1:T(8,128)(2,1)} async-done(((bf16[128,704]{0,1:T(8,128)(2,1)}), bf16[128,5632]{0,1:T(8,128)(2,1)}) %all-gather.33.cloned.1.call-update) | async-done | bytes 1441808 | tf_op jit(solution)/shard_map/all_gather | solution.py:109
  1162.9 3.0 copy.59
  1165.9 41.4 %all-gather.31.cloned.1.call-done = bf16[128,5632]{0,1:T(8,128)(2,1)} async-done(((bf16[128,704]{0,1:T(8,128)(2,1)}), bf16[128,5632]{0,1:T(8,128)(2,1)}) %all-gather.31.cloned.1.call-update) | async-done | bytes 1441808 | tf_op jit(solution)/shard_map/all_gather | solution.py:109
  1207.3 3.0 copy.58
  1210.2 48.4 %all-gather.35.cloned.1.call-done = bf16[352,2048]{1,0:T(8,128)(2,1)} async-done(((bf16[352,256]{1,0:T(8,128)(2,1)}), bf16[352,2048]{1,0:T(8,128)(2,1)}) %all-gather.35.cloned.1.call-update) | async-done | bytes 1441808 | tf_op jit(solution)/shard_map/all_gather | solution.py:118
  1258.7 3.4 convert_element_type.257
  1262.2 6.3 fusion.107
  1268.5 60.7 %reduce-scatter.28.cloned.1.call-done = bf16[128,256]{1,0:T(8,128)(2,1)} async-done(((bf16[2048,256]{1,0:T(8,128)(2,1)}), bf16[128,256]{1,0:T(8,128)(2,1)}) %reduce-scatter.28.cloned.1.call-update) | async-done | bytes 65552 | tf_op jit(solution)/shard_map/reduce_scatter | solution.py:122
  1329.2 70.2 %reduce-scatter.26.cloned.1.call-done = bf16[128,256]{1,0:T(8,128)(2,1)} async-done(((bf16[2048,256]{1,0:T(8,128)(2,1)}), bf16[128,256]{1,0:T(8,128)(2,1)}) %reduce-scatter.26.cloned.1.call-update) | async-done | bytes 65552 | tf_op jit(solution)/shard_map/reduce_scatter | solution.py:122
  1399.4 106.5 %reduce-scatter.30.cloned.1.call-done = bf16[128,2048]{1,0:T(8,128)(2,1)} async-done(((bf16[2048,2048]{1,0:T(8,128)(2,1)}), bf16[128,2048]{1,0:T(8,128)(2,1)}) %reduce-scatter.30.cloned.1.call-update) | async-done | bytes 524304 | tf_op jit(solution)/shard_map/reduce_scatter | solution.py:122
  1506.0 106.2 %reduce-scatter.24.cloned.1.call-done = bf16[128,2048]{1,0:T(8,128)(2,1)} async-done(((bf16[2048,2048]{1,0:T(8,128)(2,1)}), bf16[128,2048]{1,0:T(8,128)(2,1)}) %reduce-scatter.24.cloned.1.call-update) | async-done | bytes 524304 | tf_op jit(solution)/shard_map/reduce_scatter | solution.py:122
  1614.0 2.9 fusion.39
  1616.8 65.3 %all-reduce.2 = (bf16[2048]{0:T(1024)(128)(2,1)S(1)}, bf16[2048]{0:T(1024)(128)(2,1)S(1)}) all-reduce(f32[2048]{0:T(1024)S(1)} %get-tuple-element.46, f32[2048]{0:T(1024)S(1)} %get-tuple-element.44), channel_id=8, replica_groups=mesh['ctx'=8,'fsdp'=16] {'fsdp'}, use_global_device_ids=true, to_apply=%region_12.13.clone | all-reduce | flops 4096 | bytes 24576
  1682.3 19.6 %all-reduce.3 = (bf16[128]{0:T(256)(128)(2,1)S(1)}, bf16[128]{0:T(256)(128)(2,1)S(1)}) all-reduce(bf16[128]{0:T(256)(128)(2,1)S(1)} %dynamic-slice.7, bf16[128]{0:T(256)(128)(2,1)S(1)} %dynamic-slice.6), channel_id=1, replica_groups=mesh['ctx'=8,'fsdp'=16] {'ctx'}, use_global_device_ids=true, to_apply=%region_13.14 | all-reduce | flops 256 | bytes 1024 | tf_op jit(solution)/shard_map/psum | solution.py:285
  1702.9 2.3 fusion.58
  (183 shorter events, 48.0 us)
Async XLA Ops:
  7.2 2.9 copy-start
  7.2 12.3 copy-start.3
  7.2 12.5 copy-start.26
  7.2 53.4 %copy-start.27 = (bf16[128]{0:T(256)(128)(2,1)S(1)}, bf16[128]{0:T(256)(128)(2,1)}, u32[]{:S(2)}) copy-start(bf16[128]{0:T(256)(128)(2,1)} %param.19) | copy-start | bytes 772
  7.2 73.6 %all-gather.17.cloned.1.call-start = ((), (), s32[]{:S(2)}) async-start(), calls=%async_computation.11 | async-start | bytes 1114112 | tf_op jit(solution)/shard_map/all_gather | solution.py:76
  8.0 104.0 %all-gather.19.cloned.1.call-start = ((), (), s32[]{:S(2)}) async-start(), calls=%async_computation.12 | async-start | bytes 1114112 | tf_op jit(solution)/shard_map/all_gather | solution.py:75
  8.7 174.8 %all-gather.21.cloned.1.call-start = ((), (), s32[]{:S(2)}) async-start(), calls=%async_computation.13 | async-start | bytes 8912896 | tf_op jit(solution)/shard_map/all_gather | solution.py:74
  9.4 246.7 %all-gather.23.cloned.1.call-start = ((), (), s32[]{:S(2)}) async-start(), calls=%async_computation.14 | async-start | bytes 8912896 | tf_op jit(solution)/shard_map/all_gather | solution.py:77
  10.0 298.0 %all-gather.37.cloned.1.call-start = ((), (), s32[]{:S(2)}) async-start(), calls=%async_computation.28 | async-start | bytes 3063808 | tf_op jit(solution)/shard_map/all_gather | solution.py:98
  10.1 0.7 collective-permute-start
  10.8 0.7 copy-start.18
  11.5 350.3 %all-gather.29.cloned.1.call-start = ((), (), s32[]{:S(2)}) async-start(), calls=%async_computation.17 | async-start | bytes 3342336 | tf_op jit(solution)/shard_map/all_gather | solution.py:102
  13.3 439.1 %all-gather.25.cloned.1.call-start = ((), (), s32[]{:S(2)}) async-start(), calls=%async_computation.15 | async-start | bytes 4718592 | tf_op jit(solution)/shard_map/all_gather | solution.py:197
  19.7 94.6 %copy-start.24 = (f32[128]{0:T(128)}, f32[128]{0:T(128)S(1)}, u32[]{:S(2)}) copy-start(f32[128]{0:T(128)S(1)} %fusion.42) | copy-start | bytes 1540
  19.7 176.1 %copy-start.20 = (f32[128]{0:T(128)}, f32[128]{0:T(128)S(1)}, u32[]{:S(2)}) copy-start(f32[128]{0:T(128)S(1)} %fusion.93) | copy-start | bytes 1540
  60.6 135.2 %copy-start.15 = (f32[16,1,128]{2,1,0:T(1,128)}, f32[16,1,128]{2,1,0:T(1,128)S(1)}, u32[]{:S(2)}) copy-start(f32[16,1,128]{2,1,0:T(1,128)S(1)} %convert_element_type.260) | copy-start | bytes 24580
  79.9 121.8 %copy-start.11 = (f32[128,64]{0,1:T(8,128)}, f32[128,64]{0,1:T(8,128)S(1)}, u32[]{:S(2)}) copy-start(f32[128,64]{0,1:T(8,128)S(1)} %get-tuple-element.73) | copy-start | bytes 98308
  79.9 121.8 %copy-start.13 = (f32[128,64]{0,1:T(8,128)}, f32[128,64]{0,1:T(8,128)S(1)}, u32[]{:S(2)}) copy-start(f32[128,64]{0,1:T(8,128)S(1)} %get-tuple-element.74) | copy-start | bytes 98308
  111.9 105.4 %copy-start.9 = (bf16[1024,256]{0,1:T(8,128)(2,1)}, bf16[1024,256]{0,1:T(8,128)(2,1)S(1)}, u32[]{:S(2)}) copy-start(bf16[1024,256]{0,1:T(8,128)(2,1)S(1)} %copy.48) | copy-start | bytes 1572868
  140.3 61.7 %copy-start.4 = (bf16[1024,256]{0,1:T(8,128)(2,1)}, bf16[1024,256]{0,1:T(8,128)(2,1)S(1)}, u32[]{:S(2)}) copy-start(bf16[1024,256]{0,1:T(8,128)(2,1)S(1)} %all_gather.55) | copy-start | bytes 1572868
  201.9 7.2 copy-start.6
  261.9 248.3 %all-gather.27.cloned.1.call-start = ((), (), s32[]{:S(2)}) async-start(), calls=%async_computation.16 | async-start | bytes 3342336 | tf_op jit(solution)/shard_map/all_gather | solution.py:101
  263.7 336.6 %all-gather.39.cloned.1.call-start = ((), (), s32[]{:S(2)}) async-start(), calls=%async_computation.29 | async-start | bytes 4718592 | tf_op jit(solution)/shard_map/all_gather | solution.py:198
  264.5 448.2 %reduce-scatter.22.cloned.1.call-start = ((), (), s32[]{:S(2)}) async-start(), calls=%async_computation.19 | async-start | bytes 4718592 | tf_op jit(solution)/shard_map/reduce_scatter | solution.py:213
  600.3 10.6 copy-start.29
  610.9 3.5 copy-start.31
  610.9 3.5 copy-start.32
  610.9 3.6 copy-start.28
  619.7 186.6 %reduce-scatter.20.cloned.1.call-start = ((), (), s32[]{:S(2)}) async-start(), calls=%async_computation.18 | async-start | bytes 4718592 | tf_op jit(solution)/shard_map/reduce_scatter | solution.py:204
  627.5 259.0 %reduce-scatter.40.cloned.1.call-start = ((), (), s32[]{:S(2)}) async-start(), calls=%async_computation.33 | async-start | bytes 3342336
  639.6 325.0 %reduce-scatter.38.cloned.1.call-start = ((), (), s32[]{:S(2)}) async-start(), calls=%async_computation.32 | async-start | bytes 3342336
  651.9 390.2 %reduce-scatter.32.cloned.1.call-start = ((), (), s32[]{:S(2)}) async-start(), calls=%async_computation.26 | async-start | bytes 3063808 | tf_op jit(solution)/shard_map/reduce_scatter | solution.py:116
  661.2 420.5 %reduce-scatter.36.cloned.1.call-start = ((), (), s32[]{:S(2)}) async-start(), calls=%async_computation.31 | async-start | bytes 589824
  815.4 11.6 copy-start.10
  838.6 282.3 %reduce-scatter.34.cloned.1.call-start = ((), (), s32[]{:S(2)}) async-start(), calls=%async_computation.30 | async-start | bytes 589824
  838.6 12.2 copy-start.7
  850.8 3.3 copy-start.2
  850.8 230.8 %copy-start.16 = (f32[16,1,128]{2,1,0:T(1,128)S(1)}, f32[16,1,128]{2,1,0:T(1,128)}, u32[]{:S(2)}) copy-start(f32[16,1,128]{2,1,0:T(1,128)} %copy-done.15) | copy-start | bytes 24580
  850.9 230.8 %copy-start.21 = (f32[128]{0:T(128)S(1)}, f32[128]{0:T(128)}, u32[]{:S(2)}) copy-start(f32[128]{0:T(128)} %copy-done.20) | copy-start | bytes 1540
  854.1 267.7 %copy-start.14 = (f32[128,64]{0,1:T(8,128)S(1)}, f32[128,64]{0,1:T(8,128)}, u32[]{:S(2)}) copy-start(f32[128,64]{0,1:T(8,128)} %copy-done.13) | copy-start | bytes 98308
  854.1 267.7 %copy-start.12 = (f32[128,64]{0,1:T(8,128)S(1)}, f32[128,64]{0,1:T(8,128)}, u32[]{:S(2)}) copy-start(f32[128,64]{0,1:T(8,128)} %copy-done.11) | copy-start | bytes 98308
  854.1 267.8 %copy-start.22 = (f32[128]{0:T(128)S(1)}, f32[128]{0:T(128)}, u32[]{:S(2)}) copy-start(f32[128]{0:T(128)} %copy-done.20) | copy-start | bytes 1540
  855.1 307.8 %all-gather.33.cloned.1.call-start = ((), (), s32[]{:S(2)}) async-start(), calls=%async_computation.25 | async-start | bytes 1622016 | tf_op jit(solution)/shard_map/all_gather | solution.py:109
  888.3 319.0 %all-gather.31.cloned.1.call-start = ((), (), s32[]{:S(2)}) async-start(), calls=%async_computation.24 | async-start | bytes 1622016 | tf_op jit(solution)/shard_map/all_gather | solution.py:109
  966.4 292.3 %all-gather.35.cloned.1.call-start = ((), (), s32[]{:S(2)}) async-start(), calls=%async_computation.27 | async-start | bytes 1622016 | tf_op jit(solution)/shard_map/all_gather | solution.py:118
  1042.0 1.6 collective-permute-start.1
  1043.6 0.7 copy-start.19
  1044.3 284.9 %reduce-scatter.28.cloned.1.call-start = ((), (), s32[]{:S(2)}) async-start(), calls=%async_computation.22 | async-start | bytes 1114112 | tf_op jit(solution)/shard_map/reduce_scatter | solution.py:122
  1084.0 315.4 %reduce-scatter.26.cloned.1.call-start = ((), (), s32[]{:S(2)}) async-start(), calls=%async_computation.21 | async-start | bytes 1114112 | tf_op jit(solution)/shard_map/reduce_scatter | solution.py:122
  1123.4 382.5 %reduce-scatter.30.cloned.1.call-start = ((), (), s32[]{:S(2)}) async-start(), calls=%async_computation.23 | async-start | bytes 8912896 | tf_op jit(solution)/shard_map/reduce_scatter | solution.py:122
  1129.3 1.0 copy-start.5
  1129.4 482.8 %reduce-scatter.24.cloned.1.call-start = ((), (), s32[]{:S(2)}) async-start(), calls=%async_computation.20 | async-start | bytes 8912896 | tf_op jit(solution)/shard_map/reduce_scatter | solution.py:122
  1135.3 1.4 copy-start.23
  1142.5 0.7 copy-start.30
  1142.5 562.8 %all-reduce.7.cloned.1.call-start = ((), (), s32[]{:S(2)}) async-start(), calls=%async_computation.34 | async-start | bytes 2359296 | tf_op jit(solution)/shard_map/psum | solution.py:286
  1258.7 3.4 copy-start.8
  1268.5 345.4 %copy-start.17 = (bf16[128,256]{1,0:T(8,128)(2,1)S(1)}, bf16[128,256]{1,0:T(8,128)(2,1)}, u32[]{:S(2)}) copy-start(bf16[128,256]{1,0:T(8,128)(2,1)} %reduce-scatter.36.cloned.1.call-done) | copy-start | bytes 196612
  1268.5 434.4 %copy-start.25 = (f32[128]{0:T(128)S(1)}, f32[128]{0:T(128)}, u32[]{:S(2)}) copy-start(f32[128]{0:T(128)} %copy-done.24) | copy-start | bytes 1540
  1614.0 98.6 %copy-start.1 = (bf16[352,2048]{1,0:T(8,128)(2,1)S(1)}, bf16[352,2048]{1,0:T(8,128)(2,1)}, u32[]{:S(2)}) copy-start(bf16[352,2048]{1,0:T(8,128)(2,1)} %param.22) | copy-start | bytes 4325380
Sparse Core Ops, SparseCore 0:
  10.5 47.5 all-gather.16
  60.5 45.7 all-gather.18
  108.6 74.8 all-gather.20
  185.7 70.3 all-gather.22
  259.0 49.0 all-gather.36
  310.9 50.9 all-gather.28
  364.0 88.3 all-gather.24
  455.4 54.7 all-gather.26
  511.9 88.3 all-gather.38
  619.9 92.7 reduce-scatter.21
  715.1 91.2 reduce-scatter.19
  810.2 76.2 reduce-scatter.39
  890.5 74.0 reduce-scatter.37
  969.1 72.8 reduce-scatter.31
  1044.9 36.7 reduce-scatter.35
  1084.5 36.3 reduce-scatter.33
  1122.4 40.4 all-gather.32
  1165.1 42.1 all-gather.30
  1209.5 49.1 all-gather.34
  1262.8 66.3 reduce-scatter.27
  1333.6 65.7 reduce-scatter.25
  1404.4 101.5 reduce-scatter.29
  1510.9 101.2 reduce-scatter.23
  1615.0 78.9 all-reduce.6

commit v2 on v0

v2 whole, which is shorter than its diff:
```python
import functools

import jax
import jax.numpy as jnp
from jax import lax
from jax.experimental import pallas as pl
from jax.experimental.pallas import tpu as pltpu
from jax.sharding import PartitionSpec as P

MESH = pl.DeviceIdType.MESH
BF = jnp.bfloat16
F32 = jnp.float32
ANY = pl.BlockSpec(memory_space=pl.ANY)
VMEM = pl.BlockSpec(memory_space=pltpu.VMEM)

SLOT = {(0, 0): 0, (0, 1): 1, (1, 0): 2, (3, 0): 3, (1, 1): 4, (3, 1): 5, (2, 0): 6, (2, 1): 7}
STEPS = (0, 0, 1, 3, 1, 3, 2, 2)
PAIRS = (0, 1, 0, 0, 1, 1, 0, 1)


def slot_of(dr, dp):
    return SLOT[(dr % 4, dp % 2)]


class Place:
    def __init__(self):
        self.c = lax.axis_index("ctx")
        self.f = lax.axis_index("fsdp")
        self.y, self.zl = lax.div(self.c, 2), lax.rem(self.c, 2)
        self.j, self.co = lax.div(self.f, 2), lax.rem(self.f, 2)
        self.x, self.zh = lax.div(self.j, 2), lax.rem(self.j, 2)

    def ctx_at(self, dr, dp):
        return lax.rem(self.y + dr % 4, 4) * 2 + lax.rem(self.zl + dp, 2)

    def chip_at(self, dr, dp):
        return lax.rem(self.x + dr % 4, 4) * 2 + lax.rem(self.zh + dp, 2)

    def fsdp_at(self, dr, dp):
        return self.chip_at(dr, dp) * 2 + self.co

    def across_y(self, dr, dp):
        return {"ctx": self.ctx_at(dr, dp), "fsdp": self.f}

    def across_x(self, dr, dp):
        return {"ctx": self.c, "fsdp": self.fsdp_at(dr, dp)}

    def sibling(self):
        return {"ctx": self.c, "fsdp": self.f + 1 - 2 * self.co}


def greet(devices):
    barrier = pltpu.get_barrier_semaphore()
    for device in devices:
        pl.semaphore_signal(barrier, 1, device_id=device, device_id_type=MESH)
    pl.semaphore_wait(barrier, len(devices))


def near(dev):
    return [dev(1, 0), dev(-1, 0), dev(0, 1)]


def send(src, dst, sems, index, device):
    return pltpu.make_async_remote_copy(
        src, dst, sems[0].at[index], sems[1].at[index], device_id=device, device_id_type=MESH
    )


class Gather:
    MOVES = (
        ((0, 0), (0, 1), None),
        ((0, 0), (1, 0), None),
        ((0, 0), (-1, 0), None),
        ((0, 1), (1, 0), None),
        ((0, 1), (-1, 0), None),
        ((-1, 0), (1, 0), 0),
        ((-1, 1), (1, 0), 0),
        ((1, 0), (-1, 0), 1),
        ((1, 1), (-1, 0), 1),
    )

    def __init__(self, dev, own, loc, sems, row, sibling=None, sibling_sems=None):
        self.loc = loc
        self.copies = []
        for index, (block, to, half) in enumerate(self.MOVES):
            src = own if block == (0, 0) else loc(*block, 0, 0, half)
            dst = loc(*block, *to, half)
            self.copies.append(send(src, dst, sems, (row, index), dev(*to)))
        self.passed = []
        self.sibling = sibling
        self.sibling_sems = sibling_sems
        self.row = row
        self.own = own

    def _pass(self, index, src, dst):
        if self.sibling is not None:
            copy = send(src, dst, self.sibling_sems, (self.row, index), self.sibling)
            copy.start()
            self.passed.append(copy)

    def _got(self, index):
        self.copies[index].wait_recv()
        (dr, dp), (er, ep), half = self.MOVES[index]
        ref = self.loc(dr - er, dp + ep, 0, 0, half)
        self._pass(index, ref, ref)

    def start(self):
        for index in (0, 1, 2):
            self.copies[index].start()
        self._pass(9, self.own, self.loc(0, 0, 0, 0, None))

    def pair(self):
        self._got(0)
        self.copies[3].start()
        self.copies[4].start()

    def turn(self, dp):
        for got, on in (((1, 5), (2, 7)) if dp == 0 else ((3, 6), (4, 8))):
            self._got(got)
            self.copies[on].start()

    def last(self, dp):
        for got in ((5, 7) if dp == 0 else (6, 8)):
            self._got(got)

    def end(self):
        for copy in self.copies:
            copy.wait_send()
        for copy in self.passed:
            copy.wait()

    def all(self):
        self.start()
        self.pair()
        self.turn(0)
        self.turn(1)
        self.last(0)
        self.last(1)
        self.end()


def row_half(half, rows):
    return pl.ds(0, rows) if half is None else pl.ds(half * (rows // 2), rows // 2)


def add_into(ref, rows, others, step=16):
    step = min(step, rows)

    @pl.loop(0, rows // step)
    def _(i):
        at = pl.ds(pl.multiple_of(i * step, step), step)
        total = ref[at].astype(F32)
        for other in others:
            total = total + other[at].astype(F32)
        ref[at] = total.astype(ref.dtype)


class Scatter:
    def __init__(self, dev, part, rows, halves, fulls, paired, sems, row, cut=None):
        self.part, self.rows, self.cut = part, rows, cut
        self.halves, self.fulls, self.paired = halves, fulls, paired
        self.first, self.second = {}, {}
        for dp in (0, 1):
            for way, sign in ((0, 1), (1, -1)):
                self.first[way, dp] = send(
                    self._half(part(slot_of(2, dp)), way), halves.at[way, dp], sems, (row, way * 2 + dp), dev(sign, 0)
                )
                self.second[way, dp] = send(
                    part(slot_of(sign, dp)), fulls.at[way, dp], sems, (row, 4 + way * 2 + dp), dev(sign, 0)
                )
        self.third = send(part(slot_of(0, 1)), paired, sems, (row, 8), dev(0, 1))

    def _half(self, ref, way):
        if self.cut is None:
            return ref.at[pl.ds(way * (self.rows // 2), self.rows // 2)]
        return ref.at[:, pl.ds(way * (self.cut // 2), self.cut // 2)]

    def start(self):
        for dp in (1, 0):
            for way in (0, 1):
                self.first[way, dp].start()

    def turn(self, dp):
        for way, sign in ((0, 1), (1, -1)):
            self.first[way, dp].wait_recv()
            block = self._half(self.part(slot_of(sign, dp)), way)
            add_into(block, block.shape[0], [self.halves.at[way, dp]])
            self.second[way, dp].start()

    def pair(self):
        for way in (0, 1):
            self.second[way, 1].wait_recv()
        add_into(self.part(slot_of(0, 1)), self.rows, [self.fulls.at[0, 1], self.fulls.at[1, 1]])
        self.third.start()

    def finish(self, out, extra=()):
        for way in (0, 1):
            self.second[way, 0].wait_recv()
        self.third.wait_recv()
        own = self.part(0)
        terms = [own, self.fulls.at[0, 0], self.fulls.at[1, 0], self.paired, *extra]

        @pl.loop(0, self.rows // 16)
        def _(i):
            at = pl.ds(pl.multiple_of(i * 16, 16), 16)
            total = terms[0][at].astype(F32)
            for term in terms[1:]:
                total = total + term[at].astype(F32)
            out[at] = total.astype(out.dtype)

    def end(self):
        for copy in (*self.first.values(), *self.second.values(), self.third):
            copy.wait_send()


def scatter_buffers(rows, columns, dtype=BF, cut=False):
    half = (rows, columns // 2) if cut else (rows // 2, columns)
    return [
        pltpu.VMEM((2, 2, *half), dtype),
        pltpu.VMEM((2, 2, rows, columns), dtype),
        pltpu.VMEM((rows, columns), dtype),
    ]


def dma_sems(rows, count):
    return [pltpu.SemaphoreType.DMA((rows, count)), pltpu.SemaphoreType.DMA((rows, count))]


def params(collective_id, vmem=56):
    return pltpu.CompilerParams(
        collective_id=collective_id, has_side_effects=True, vmem_limit_bytes=vmem << 20
    )


def dot_in(left, right):
    return jnp.dot(left, right, preferred_element_type=F32)


def dot_back(left, right):
    return lax.dot_general(left, right, (((1,), (1,)), ((), ())), preferred_element_type=F32)


def dot_rows(left, right):
    return lax.dot_general(left, right, (((0,), (0,)), ((), ())), preferred_element_type=F32)


def weights_kernel(
    gains, qkv, wo, gu, dn, dy, gains_all, qkv_all, wo_all, gu_all, dn_all, dy_all, s0, s1, t0, t1, y0, y1, local
):
    me = Place()
    greet(near(me.across_x) + near(me.across_y) + [me.sibling()])

    def rows_at(ref, rows):
        def loc(dr, dp, er, ep, half):
            size = rows if half is None else rows // 2
            first = me.fsdp_at(dr, dp) * rows + (0 if half is None else half * size)
            return ref.at[pl.ds(pl.multiple_of(first, size), size)]

        return loc

    def gains_at(dr, dp, er, ep, half):
        return gains_all.at[me.fsdp_at(dr, dp), row_half(half, 16)]

    def dn_at(dr, dp, er, ep, half):
        size = 352 if half is None else 176
        first = me.co * 352 + (0 if half is None else half * size)
        return dn_all.at[
            pl.ds(pl.multiple_of(first, 16), size),
            pl.ds(pl.multiple_of(me.chip_at(dr, dp) * 256, 256), 256),
        ]

    def dy_at(dr, dp, er, ep, half):
        return dy_all.at[slot_of(dr - er, dp + ep), row_half(half, 128)]

    def over_x(own, loc, row):
        return Gather(me.across_x, own, loc, (s0, s1), row, me.sibling(), (t0, t1))

    tasks = [
        over_x(gains, gains_at, 0),
        over_x(qkv, rows_at(qkv_all, 128), 1),
        over_x(wo, rows_at(wo_all, 128), 2),
        over_x(gu, rows_at(gu_all, 128), 3),
        over_x(dn, dn_at, 4),
    ]
    grad = Gather(me.across_y, dy, dy_at, (y0, y1), 0)
    kept = []
    for index, task in enumerate([*tasks, grad]):
        copy = pltpu.make_async_copy(task.own, task.loc(0, 0, 0, 0, None), local.at[index])
        copy.start()
        kept.append(copy)
    g, q, o, m, d = tasks
    g.start()
    q.start()
    grad.start()
    g.pair()
    q.pair()
    grad.pair()
    g.turn(0)
    q.turn(0)
    grad.turn(0)
    o.start()
    g.turn(1)
    q.turn(1)
    grad.turn(1)
    o.pair()
    o.turn(0)
    m.start()
    d.start()
    for task in (g, q, grad):
        task.last(0)
        task.last(1)
    o.turn(1)
    m.pair()
    d.pair()
    m.turn(0)
    d.turn(0)
    o.last(0)
    o.last(1)
    m.turn(1)
    d.turn(1)
    for task in (m, d):
        task.last(0)
        task.last(1)
    for task in [*tasks, grad]:
        task.end()
    for copy in kept:
        copy.wait()


def gather_weights(gains, qkv, wo, gu, dn, dy):
    return pl.pallas_call(
        weights_kernel,
        out_shape=(
            jax.ShapeDtypeStruct((16, 16, 128), F32),
            jax.ShapeDtypeStruct((2048, 2560), BF),
            jax.ShapeDtypeStruct((2048, 2048), BF),
            jax.ShapeDtypeStruct((2048, 1536), BF),
            jax.ShapeDtypeStruct((704, 2048), BF),
            jax.ShapeDtypeStruct((8, 128, 2048), BF),
        ),
        in_specs=[ANY] * 6,
        out_specs=[ANY] * 6,
        scratch_shapes=dma_sems(5, 9) + dma_sems(5, 10) + dma_sems(1, 9) + [pltpu.SemaphoreType.DMA((6,))],
        compiler_params=params(1),
        name="gather_weights",
    )(gains, qkv, wo, gu, dn, dy)


def kv_kernel(own, everyone, y0, y1, local):
    me = Place()
    greet(near(me.across_y))

    def loc(dr, dp, er, ep, half):
        return everyone.at[me.ctx_at(dr, dp), row_half(half, 128)]

    task = Gather(me.across_y, own, loc, (y0, y1), 0)
    copy = pltpu.make_async_copy(own, loc(0, 0, 0, 0, None), local)
    copy.start()
    task.all()
    copy.wait()


def gather_kv(own):
    rows, columns = own.shape
    return pl.pallas_call(
        kv_kernel,
        out_shape=jax.ShapeDtypeStruct((8, rows, columns), BF),
        in_specs=[VMEM],
        out_specs=VMEM,
        scratch_shapes=dma_sems(1, 9) + [pltpu.SemaphoreType.DMA],
        compiler_params=params(2),
        name="gather_kv",
    )(own)


def kv_back_kernel(parts, out, halves, fulls, paired, work, y0, y1):
    me = Place()
    greet(near(me.across_y))
    for slot in range(8):
        work[slot] = parts[me.ctx_at(STEPS[slot], PAIRS[slot])]
    task = Scatter(me.across_y, lambda slot: work.at[slot], 128, halves, fulls, paired, (y0, y1), 0)
    task.start()
    task.turn(1)
    task.turn(0)
    task.pair()
    task.finish(out)
    task.end()


def scatter_kv(parts):
    return pl.pallas_call(
        kv_back_kernel,
        out_shape=jax.ShapeDtypeStruct((128, 512), F32),
        in_specs=[VMEM],
        out_specs=VMEM,
        scratch_shapes=scatter_buffers(128, 512) + [pltpu.VMEM((8, 128, 512), BF)] + dma_sems(1, 9),
        compiler_params=params(3),
        name="scatter_kv",
    )(parts)


def mlp_kernel(
    a2, gu_in, dn_in, dy_in,
    da2_out, mpart, gu_out, dn_out,
    acts, gu, wd, dy, hid, dgu, dpart,
    d_half, d_full, d_pair,
    gsib, grecv, gown, gd, gdrecv, gdown,
    g_half, g_full, g_pair, n_half, n_full, n_pair,
    ag0, ag1, rs0, rs1, sib0, sib1, local,
):
    me = Place()
    greet(near(me.across_x) + near(me.across_y) + [me.sibling()])

    def acts_at(dr, dp, er, ep, half):
        return acts.at[slot_of(dr - er, dp + ep), row_half(half, 128)]

    task = Gather(me.across_y, a2, acts_at, (ag0, ag1), 0)
    task.start()
    loads = [
        pltpu.make_async_copy(gu_in, gu, local.at[0]),
        pltpu.make_async_copy(dn_in, wd.at[pl.ds(0, 704)], local.at[1]),
        pltpu.make_async_copy(dy_in, dy, local.at[2]),
    ]
    for load in loads:
        load.start()
    acts[0] = a2[...]
    wd[pl.ds(704, 64)] = jnp.zeros((64, 2048), BF)
    for load in loads:
        load.wait()

    def group(g):
        at = pl.ds(2 * g, 2)
        rows = pl.ds(pl.multiple_of(256 * g, 256), 256)
        for h in range(3):
            first, second = pl.ds(256 * h, 256), pl.ds(768 + 256 * h, 256)
            here = acts[at].reshape(256, 2048)
            gate = dot_in(here, gu[:, first])
            up = dot_in(here, gu[:, second])
            back = dot_back(dy[at].reshape(256, 2048), wd[first, :])
            curve = 1.0 / (1.0 + jnp.exp(-gate))
            silu = gate * curve
            hid[rows, first] = (silu * up).astype(BF)
            dgu[rows, first] = (back * up * (curve + silu * (1.0 - curve))).astype(BF)
            dgu[rows, second] = (back * silu).astype(BF)
        for n in range(4):
            wide = pl.ds(512 * n, 512)
            mpart[at, :, wide] = dot_in(hid[rows, :], wd[:, wide]).astype(BF).reshape(2, 128, 512)
            dpart[at, :, wide] = dot_back(dgu[rows, :], gu[wide, :]).astype(BF).reshape(2, 128, 512)

    @pl.loop(0, 4)
    def _(g):
        @pl.when(g == 0)
        def _():
            task.pair()

        @pl.when(g == 1)
        def _():
            task.turn(0)

        @pl.when(g == 2)
        def _():
            task.turn(1)

        @pl.when(g == 3)
        def _():
            task.last(0)
            task.last(1)

        group(g)

    grad = Scatter(me.across_y, lambda slot: dpart.at[slot], 128, d_half, d_full, d_pair, (rs0, rs1), 0)
    grad.start()

    def chip_of(t):
        dr = jnp.where(t < 2, 0, jnp.where(t >= 6, 2, 1 + 2 * lax.rem(t, 2)))
        dp = jnp.where(t < 2, t, jnp.where(t >= 6, t - 6, lax.div(t, 4)))
        return lax.rem(me.x + dr, 4) * 2 + lax.rem(me.zh + dp, 2)

    def weight_terms(t, core, out):
        first = pl.multiple_of((chip_of(t) * 2 + core) * 128, 128)
        left = acts[:, :, pl.ds(first, 128)].reshape(1024, 128)
        out[t] = dot_rows(left, dgu[...]).astype(BF)

    down_to = [
        send(gd.at[t, pl.ds(pl.multiple_of((1 - me.co) * 352, 16), 352)], gdrecv.at[t], (sib0, sib1), t, me.sibling())
        for t in range(8)
    ]
    gu_to = [send(gsib.at[t], grecv.at[t], (sib0, sib1), 8 + t, me.sibling()) for t in range(8)]

    @pl.loop(0, 8)
    def _(t):
        first = pl.multiple_of(chip_of(t) * 256, 256)
        gd[t] = dot_rows(hid[...], dy[:, :, pl.ds(first, 256)].reshape(1024, 256)).astype(BF)

    for copy in down_to:
        copy.start()

    @pl.loop(0, 8)
    def _(t):
        weight_terms(t, 1 - me.co, gsib)

    for copy in gu_to:
        copy.start()
    grad.turn(1)
    grad.turn(0)

    @pl.loop(0, 8)
    def _(t):
        weight_terms(t, me.co, gown)

    for copy in down_to:
        copy.wait_recv()

    @pl.loop(0, 8 * 22)
    def _(i):
        t, row = lax.div(i, 22), lax.rem(i, 22) * 16
        mine = gd[t, pl.ds(pl.multiple_of(me.co * 352 + row, 16), 16)].astype(F32)
        at = pl.ds(pl.multiple_of(row, 16), 16)
        gdown[t, at] = (mine + gdrecv[t, at].astype(F32)).astype(BF)

    for copy in gu_to:
        copy.wait_recv()

    @pl.loop(0, 8 * 8)
    def _(i):
        t, at = lax.div(i, 8), pl.ds(pl.multiple_of(lax.rem(i, 8) * 16, 16), 16)
        gown[t, at] = (gown[t, at].astype(F32) + grecv[t, at].astype(F32)).astype(BF)

    first = Scatter(me.across_x, lambda slot: gown.at[slot], 128, g_half, g_full, g_pair, (rs0, rs1), 1)
    second = Scatter(me.across_x, lambda slot: gdown.at[slot], 352, n_half, n_full, n_pair, (rs0, rs1), 2)
    first.start()
    second.start()
    grad.pair()
    for dp in (1, 0):
        first.turn(dp)
        second.turn(dp)
    grad.finish(da2_out)
    first.pair()
    second.pair()
    first.finish(gu_out)
    second.finish(dn_out)
    for job in (task, grad, first, second):
        job.end()
    for copy in (*down_to, *gu_to):
        copy.wait_send()


def feed_forward(a2, gu, dn, dy):
    scratch = [
        pltpu.VMEM((8, 128, 2048), BF),
        pltpu.VMEM((2048, 1536), BF),
        pltpu.VMEM((768, 2048), BF),
        pltpu.VMEM((8, 128, 2048), BF),
        pltpu.VMEM((1024, 768), BF),
        pltpu.VMEM((1024, 1536), BF),
        pltpu.VMEM((8, 128, 2048), BF),
        *scatter_buffers(128, 2048),
        pltpu.VMEM((8, 128, 1536), BF),
        pltpu.VMEM((8, 128, 1536), BF),
        pltpu.VMEM((8, 128, 1536), BF),
        pltpu.VMEM((8, 768, 256), BF),
        pltpu.VMEM((8, 352, 256), BF),
        pltpu.VMEM((8, 352, 256), BF),
        *scatter_buffers(128, 1536),
        *scatter_buffers(352, 256),
        *dma_sems(1, 9),
        *dma_sems(3, 9),
        pltpu.SemaphoreType.DMA((16,)),
        pltpu.SemaphoreType.DMA((16,)),
        pltpu.SemaphoreType.DMA((3,)),
    ]
    return pl.pallas_call(
        mlp_kernel,
        out_shape=(
            jax.ShapeDtypeStruct((128, 2048), F32),
            jax.ShapeDtypeStruct((8, 128, 2048), BF),
            jax.ShapeDtypeStruct((128, 1536), BF),
            jax.ShapeDtypeStruct((352, 256), BF),
        ),
        in_specs=[VMEM, ANY, ANY, ANY],
        out_specs=[VMEM] * 4,
        scratch_shapes=scratch,
        compiler_params=params(4, 62),
        name="feed_forward",
    )(a2, gu, dn, dy)


def grads_kernel(
    a1, att, dqkv, datt, gains, mpart_in, h1, gu, dn,
    mixed, q_out, o_out, gains_out, gu_all, dn_all,
    a1s, atts, dqkvs, datts, gsib, mpart,
    qp, op, gp, ggot,
    q_half, q_full, q_pair, o_half, o_full, o_pair, e_half, e_full, e_pair,
    m_half, m_full, m_pair,
    q_sum, o_sum, g_sum,
    qr_half, qr_full, qr_pair, or_half, or_full, or_pair,
    sib0, sib1, x0, x1, y0, y1, ag0, ag1, local,
):
    me = Place()
    greet(near(me.across_x) + near(me.across_y) + [me.sibling()])
    swaps = []
    for index, (own, both) in enumerate(((att, atts), (datt, datts), (a1, a1s), (dqkv, dqkvs))):
        swaps.append(send(own, both.at[pl.ds(128, 128)], (sib0, sib1), index, me.sibling()))
    swaps.append(send(gains, gsib, (sib0, sib1), 4, me.sibling()))
    for copy in swaps:
        copy.start()
    load = pltpu.make_async_copy(mpart_in, mpart, local.at[0])
    load.start()

    def at_ctx(ref):
        def loc(dr, dp, er, ep, half):
            rows = ref.shape[1]
            return ref.at[me.ctx_at(dr, dp), row_half(half, rows)]

        return loc

    gu_task = Gather(me.across_y, gu, at_ctx(gu_all), (ag0, ag1), 0)
    dn_task = Gather(me.across_y, dn, at_ctx(dn_all), (ag0, ag1), 1)
    kept = [
        pltpu.make_async_copy(gu, gu_all.at[me.c], local.at[1]),
        pltpu.make_async_copy(dn, dn_all.at[me.c], local.at[2]),
    ]
    for copy in kept:
        copy.start()
    gu_task.start()
    dn_task.start()
    for own, both in ((att, atts), (datt, datts), (a1, a1s), (dqkv, dqkvs)):
        both[pl.ds(0, 128)] = own[...]

    def chip_of(t):
        dr = jnp.where(t < 2, 0, jnp.where(t >= 6, 2, 1 + 2 * lax.rem(t, 2)))
        dp = jnp.where(t < 2, t, jnp.where(t >= 6, t - 6, lax.div(t, 4)))
        return lax.rem(me.x + dr, 4) * 2 + lax.rem(me.zh + dp, 2)

    swaps[0].wait_recv()
    swaps[1].wait_recv()

    def terms(left, right, out):
        @pl.loop(0, 8)
        def _(i):
            t = 7 - i
            first = pl.multiple_of((chip_of(t) * 2 + me.co) * 128, 128)
            out[t] = dot_rows(left[:, pl.ds(first, 128)], right[...]).astype(BF)

    over_x = (x0, x1)
    over_y = (y0, y1)
    o_job = Scatter(me.across_x, lambda slot: op.at[slot], 128, o_half, o_full, o_pair, over_x, 0)
    q_job = Scatter(me.across_x, lambda slot: qp.at[slot], 128, q_half, q_full, q_pair, over_x, 1)
    e_job = Scatter(me.across_x, lambda slot: gp.at[slot], 16, e_half, e_full, e_pair, over_x, 2)
    m_job = Scatter(me.across_y, lambda slot: mpart.at[slot], 128, m_half, m_full, m_pair, over_y, 0)
    terms(atts, datts, op)
    o_job.start()
    swaps[4].wait_recv()
    for slot in range(8):
        block = me.fsdp_at(STEPS[slot], PAIRS[slot])
        gp[slot] = gains[block] + gsib[block]
    e_job.start()
    swaps[2].wait_recv()
    swaps[3].wait_recv()
    terms(a1s, dqkvs, qp)
    gu_task.pair()
    dn_task.pair()
    for dp in (1, 0):
        o_job.turn(dp)
        e_job.turn(dp)
    q_job.start()
    gu_task.turn(0)
    dn_task.turn(0)
    gu_task.turn(1)
    dn_task.turn(1)
    load.wait()
    m_job.start()
    o_job.pair()
    e_job.pair()
    o_job.finish(o_sum)
    e_job.finish(g_sum)
    for dp in (1, 0):
        q_job.turn(dp)
        m_job.turn(dp)

    def sum_over_ctx(total, columns, halves, fulls, paired, row):
        def part(slot):
            first = pl.multiple_of(me.ctx_at(STEPS[slot], PAIRS[slot]) * 16, 16)
            return total.at[pl.ds(first, 16)]

        return Scatter(me.across_y, part, 16, halves, fulls, paired, over_y, row, cut=columns)

    def spread(out, columns, row):
        def loc(dr, dp, er, ep, half):
            first = pl.multiple_of(me.ctx_at(dr, dp) * 16, 16)
            if half is None:
                return out.at[pl.ds(first, 16)]
            return out.at[pl.ds(first, 16), pl.ds(half * (columns // 2), columns // 2)]

        return Gather(me.across_y, loc(0, 0, 0, 0, None), loc, (ag0, ag1), row)

    e_task = Gather(me.across_y, g_sum, at_ctx(ggot), (ag0, ag1), 2)
    e_task.start()
    o_sums = sum_over_ctx(o_sum, 2048, or_half, or_full, or_pair, 1)
    o_sums.start()
    o_spread = spread(o_out, 2048, 3)
    q_spread = spread(q_out, 2560, 4)
    ggot[me.c] = g_sum[...]
    e_task.pair()
    e_task.turn(0)
    e_task.turn(1)
    o_sums.turn(1)
    o_sums.turn(0)
    m_job.pair()
    o_sums.pair()
    m_job.finish(mixed, (h1,))
    own_rows = pl.ds(pl.multiple_of(me.c * 16, 16), 16)
    o_sums.finish(o_out.at[own_rows])
    o_spread.start()
    for task in (gu_task, dn_task, e_task):
        task.last(0)
        task.last(1)
    total = ggot[0]
    for index in range(1, 8):
        total = total + ggot[index]
    gains_out[...] = total
    q_job.pair()
    q_job.finish(q_sum)
    q_sums = sum_over_ctx(q_sum, 2560, qr_half, qr_full, qr_pair, 2)
    q_sums.start()
    o_spread.pair()
    o_spread.turn(0)
    o_spread.turn(1)
    q_sums.turn(1)
    q_sums.turn(0)
    q_sums.pair()
    q_sums.finish(q_out.at[own_rows])
    q_spread.start()
    q_spread.pair()
    q_spread.turn(0)
    q_spread.turn(1)
    for task in (o_spread, q_spread):
        task.last(0)
        task.last(1)
    for job in (o_job, q_job, e_job, m_job, o_sums, q_sums, gu_task, dn_task, e_task, o_spread, q_spread):
        job.end()
    for copy in swaps:
        copy.wait_send()
    for copy in kept:
        copy.wait()


def weight_grads(a1, att, dqkv, datt, gains, mpart, h1, gu, dn):
    scratch = [
        pltpu.VMEM((256, 2048), BF),
        pltpu.VMEM((256, 2048), BF),
        pltpu.VMEM((256, 2560), BF),
        pltpu.VMEM((256, 2048), BF),
        pltpu.VMEM((16, 16, 128), F32),
        pltpu.VMEM((8, 128, 2048), BF),
        pltpu.VMEM((8, 128, 2560), BF),
        pltpu.VMEM((8, 128, 2048), BF),
        pltpu.VMEM((8, 16, 128), F32),
        pltpu.VMEM((8, 16, 128), F32),
        *scatter_buffers(128, 2560),
        *scatter_buffers(128, 2048),
        *scatter_buffers(16, 128, F32),
        *scatter_buffers(128, 2048),
        pltpu.VMEM((128, 2560), BF),
        pltpu.VMEM((128, 2048), BF),
        pltpu.VMEM((16, 128), F32),
        *scatter_buffers(16, 2560, cut=True),
        *scatter_buffers(16, 2048, cut=True),
        pltpu.SemaphoreType.DMA((5,)),
        pltpu.SemaphoreType.DMA((5,)),
        *dma_sems(3, 9),
        *dma_sems(3, 9),
        *dma_sems(5, 9),
        pltpu.SemaphoreType.DMA((3,)),
    ]
    return pl.pallas_call(
        grads_kernel,
        out_shape=(
            jax.ShapeDtypeStruct((128, 2048), BF),
            jax.ShapeDtypeStruct((128, 2560), BF),
            jax.ShapeDtypeStruct((128, 2048), BF),
            jax.ShapeDtypeStruct((16, 128), F32),
            jax.ShapeDtypeStruct((8, 128, 1536), BF),
            jax.ShapeDtypeStruct((8, 352, 256), BF),
        ),
        in_specs=[VMEM] * 5 + [ANY, VMEM, ANY, ANY],
        out_specs=[VMEM] * 4 + [ANY, ANY],
        scratch_shapes=scratch,
        compiler_params=params(5, 60),
        name="weight_grads",
    )(a1, att, dqkv, datt, gains, mpart, h1, gu, dn)


HEADS = 32
KV_HEADS = 4
HEAD_DIM = 64
GROUP_HEADS = 8
EPS = 1e-05
SCALE = 0.125
BASE = 10000.0


def rms_norm(values, gain):
    return values * lax.rsqrt(jnp.mean(values * values, axis=-1, keepdims=True) + EPS) * gain


def tables(position):
    freq = BASE ** (-(jnp.arange(HEAD_DIM // 2, dtype=jnp.float32) * 2.0) / HEAD_DIM)
    angle = position.astype(jnp.float32)[:, None] * freq[None, :]
    angle = jnp.concatenate([angle, angle], axis=-1)
    return (jnp.cos(angle), jnp.sin(angle))


def rotate(values, cosine, sine):
    half_dim = values.shape[-1] // 2
    turned = jnp.concatenate([-values[..., half_dim:], values[..., :half_dim]], axis=-1)
    return values * cosine[:, None, :] + turned * sine[:, None, :]


def unrotate(values, cosine, sine):
    half_dim = values.shape[-1] // 2
    scaled = values * sine[:, None, :]
    turned = jnp.concatenate([scaled[..., half_dim:], -scaled[..., :half_dim]], axis=-1)
    return values * cosine[:, None, :] + turned


def timeline(table_flat, total_len, row_count):
    everywhere = jnp.arange(total_len, dtype=jnp.int32)
    half_len = row_count // 2
    moment = jnp.repeat(table_flat, half_len) * half_len + everywhere % half_len
    prompt_len = total_len // 2
    cont_len = total_len // 8
    later = moment >= prompt_len
    segment = jnp.where(later, 1 + (moment - prompt_len) // cont_len, 0)
    position = jnp.where(later, prompt_len + (moment - prompt_len) % cont_len, moment)
    return (segment, position)


def swap_pairs():
    pairs = []
    for c in range(8):
        for f in range(16):
            pairs.append((c * 16 + f, (f // 2) * 16 + 2 * c + f % 2))
    return pairs


def softmax_parts(masked):
    peak = jnp.max(masked, axis=-1, keepdims=True)
    unscaled = jnp.exp(masked - peak)
    total = jnp.sum(unscaled, axis=-1, keepdims=True)
    return ((unscaled / total).astype(jnp.bfloat16), peak + jnp.log(total))


def on_device(
    tokens,
    block_deal,
    attn_gain,
    query_weight,
    key_weight,
    value_weight,
    output_weight,
    mlp_gain,
    gate_weight,
    up_weight,
    down_weight,
    cotangent,
):
    inputs = tokens[0].astype(F32)
    grad_out = cotangent[0].astype(F32)
    row_count = inputs.shape[0]
    c = lax.axis_index("ctx")
    f = lax.axis_index("fsdp")
    full_len = row_count * 8

    def sliced(weight):
        return jnp.pad(lax.dynamic_slice_in_dim(weight, c * 704, 704, 1), ((0, 0), (0, 64)))

    none = jnp.zeros((7, 128), F32)
    gains = jnp.concatenate([attn_gain.astype(F32)[None], none, mlp_gain.astype(F32)[None], none])
    qkv = jnp.concatenate([query_weight, key_weight, value_weight], axis=1)
    gu = jnp.concatenate([sliced(gate_weight), sliced(up_weight)], axis=1)
    dn = lax.dynamic_slice_in_dim(down_weight, c * 256, 256, 1)
    dn = lax.ppermute(dn, ("ctx", "fsdp"), swap_pairs())
    gains_all, qkv_all, wo_all, gu_all, dn_all, dy_all = gather_weights(
        gains, qkv, output_weight, gu, dn, cotangent[0]
    )
    gain_first = gains_all[:, 0].reshape(2048)
    gain_second = gains_all[:, 8].reshape(2048)

    deal = lax.dynamic_index_in_dim(block_deal, f, 0, keepdims=False)
    segment, position = timeline(deal.reshape(-1), full_len, row_count)
    own_segment = lax.dynamic_slice_in_dim(segment, c * row_count, row_count, 0)
    own_position = lax.dynamic_slice_in_dim(position, c * row_count, row_count, 0)
    cosine, sine = tables(own_position)
    same = (segment[None, :] == 0) | (segment[None, :] == own_segment[:, None])
    visible = same & (position[None, :] <= own_position[:, None])

    normed = rms_norm(inputs, gain_first).astype(BF)
    raw = dot_in(normed, qkv_all)
    query_raw = raw[:, :2048].reshape(row_count, HEADS, HEAD_DIM)
    key_raw = raw[:, 2048:2304].reshape(row_count, KV_HEADS, HEAD_DIM)
    queries = rotate(query_raw, cosine, sine).astype(BF)
    queries = queries.reshape(row_count, KV_HEADS, GROUP_HEADS, HEAD_DIM)
    keys_own = rotate(key_raw, cosine, sine).astype(BF).reshape(row_count, KV_HEADS * HEAD_DIM)
    values_own = raw[:, 2304:].astype(BF)
    kv_all = gather_kv(jnp.concatenate([keys_own, values_own], axis=1)).reshape(full_len, 512)
    keys_all = kv_all[:, :256].reshape(full_len, KV_HEADS, HEAD_DIM)
    values_all = kv_all[:, 256:].reshape(full_len, KV_HEADS, HEAD_DIM)
    scores = jnp.einsum("qcgd,kcd->cgqk", queries, keys_all, preferred_element_type=F32) * SCALE
    probs_low, log_total = softmax_parts(jnp.where(visible, scores, -1e30))
    heads_out = jnp.einsum("cgqk,kcd->qcgd", probs_low, values_all, preferred_element_type=F32)
    attended = heads_out.astype(BF).reshape(row_count, HEADS * HEAD_DIM)
    hidden_state = inputs + dot_in(attended, wo_all)

    normed_two = rms_norm(hidden_state, gain_second).astype(BF)
    grad_normed_two, mixed_parts, gu_sum, dn_sum = feed_forward(normed_two, gu_all, dn_all, dy_all)
    dn_sum = lax.ppermute(dn_sum, ("ctx", "fsdp"), swap_pairs())
    _, norm_two_back = jax.vjp(rms_norm, hidden_state, gain_second)
    grad_hidden_norm, grad_gain_two = norm_two_back(grad_normed_two)
    grad_hidden = grad_out + grad_hidden_norm
    grad_att = grad_hidden.astype(BF)

    grad_heads = dot_back(grad_att, wo_all).astype(BF)
    grad_heads = grad_heads.reshape(row_count, KV_HEADS, GROUP_HEADS, HEAD_DIM)
    scores_again = jnp.einsum("qcgd,kcd->cgqk", queries, keys_all, preferred_element_type=F32) * SCALE
    probs = jnp.exp(jnp.where(visible, scores_again, -1e30) - log_total)
    probs_again = probs.astype(BF)
    grad_probs = jnp.einsum("qcgd,kcd->cgqk", grad_heads, values_all, preferred_element_type=F32)
    grad_values_all = jnp.einsum("cgqk,qcgd->kcd", probs_again, grad_heads, preferred_element_type=F32)
    grad_scores = probs * (grad_probs - jnp.sum(probs * grad_probs, axis=-1, keepdims=True))
    grad_scores = grad_scores.astype(BF)
    grad_queries = jnp.einsum("cgqk,kcd->qcgd", grad_scores, keys_all, preferred_element_type=F32) * SCALE
    grad_keys_all = jnp.einsum("cgqk,qcgd->kcd", grad_scores, queries, preferred_element_type=F32) * SCALE
    kv_parts = jnp.concatenate(
        [grad_keys_all.reshape(full_len, 256), grad_values_all.reshape(full_len, 256)], axis=1
    ).astype(BF)
    grad_kv = scatter_kv(kv_parts.reshape(8, 128, 512))
    grad_query_raw = unrotate(grad_queries.reshape(row_count, HEADS, HEAD_DIM), cosine, sine)
    grad_query_raw = grad_query_raw.reshape(row_count, HEADS * HEAD_DIM).astype(BF)
    grad_key_raw = unrotate(grad_kv[:, :256].reshape(row_count, KV_HEADS, HEAD_DIM), cosine, sine)
    grad_key_raw = grad_key_raw.reshape(row_count, KV_HEADS * HEAD_DIM).astype(BF)
    grad_raw = jnp.concatenate([grad_query_raw, grad_key_raw, grad_kv[:, 256:].astype(BF)], axis=1)
    grad_normed = dot_back(grad_raw, qkv_all)
    _, norm_one_back = jax.vjp(rms_norm, inputs, gain_first)
    grad_inputs_norm, grad_gain_one = norm_one_back(grad_normed)
    tokens_grad = (grad_hidden + grad_inputs_norm).astype(BF)

    gain_terms = jnp.zeros((16, 16, 128), F32)
    gain_terms = gain_terms.at[:, 0].set(grad_gain_one.reshape(16, 128))
    gain_terms = gain_terms.at[:, 8].set(grad_gain_two.reshape(16, 128))
    mixed, qkv_grad, o_grad, gain_grads, gu_grads, dn_grads = weight_grads(
        normed, attended, grad_raw, grad_att, gain_terms, mixed_parts, hidden_state, gu_sum, dn_sum
    )

    def joined(parts):
        return parts.transpose(1, 0, 2).reshape(parts.shape[1], -1).astype(F32)

    return (
        mixed[None],
        tokens_grad[None],
        gain_grads[0],
        qkv_grad[:, :2048].astype(F32),
        qkv_grad[:, 2048:2304].astype(F32),
        qkv_grad[:, 2304:].astype(F32),
        o_grad.astype(F32),
        gain_grads[8],
        joined(gu_grads[:, :, :704]),
        joined(gu_grads[:, :, 768:1472]),
        joined(dn_grads),
    )


def solution(mesh):
    held = P("fsdp", "ctx", None)
    rows = P("fsdp", None)
    return jax.shard_map(
        on_device,
        mesh=mesh,
        in_specs=(held, P(), P("fsdp"), rows, rows, rows, rows, P("fsdp"), rows, rows, rows, held),
        out_specs=(held, held, P("fsdp"), rows, rows, rows, rows, P("fsdp"), rows, rows, rows),
        check_vma=False,
    )
```

time: 1980 us -> 589 us (0.30)
  waiting for transfers between devices: 1490 us -> 0.01 us
  Pallas kernels: 0 us -> 418 us
  blocking collectives: 189 us -> 0 us
  matrix products: 203 us -> 63.6 us
    reduce_scatter x7 -> x0, waiting for transfers between devices: 836 us -> none  [weight_share(): lax.psum_scatter(mult_rows(left, right).astype(jnp.bfloat16), 'fsdp', sca...]
    all_gather x7 -> x0, waiting for transfers between devices: 476 us -> none  [the longest x1 134 us: fetch_mlp(): lax.all_gather(up_weight, 'fsdp', axis=0, tiled=True)]
    pallas_call x0 -> x5, Pallas kernels: none -> 418 us  [the longest x1 150 us: weight_grads(): pl.pallas_call(grads_kernel, out_shape=(jax.ShapeDtypeStruct((128, 2048),...]
    dot_general x22 -> x5, matrix products: 166 us -> 31.6 us  [the longest x2 13.9 us: dot_back(): lax.dot_general(left, right, (((1,), (1,)), ((), ())), preferred_element_...]
    psum x1 -> x0, waiting for transfers between devices: 124 us -> none  [on_device(): lax.psum(query_part.astype(jnp.bfloat16), 'ctx').astype(jnp.float32)]
    all_gather x4 -> x0, blocking collectives: 101 us -> none  [the longest x1 29.5 us: on_device(): lax.all_gather(values_own, 'ctx', axis=0, tiled=True)]
    unnamed x1 -> x0, blocking collectives: 66.7 us -> none
    unnamed x19 -> x0, waiting for transfers between devices: 56.5 us -> none
  transfers between devices with their start and end apart: 17 -> 2, of which waited for: 16 -> 0; matrix products, arithmetic and copies ran while one was open for 9% -> 2% of each run, Pallas kernels for 0% -> 0%
where the time goes in v2:
time: 589 us; the launch traced here: 578 us
  Pallas kernels  418 us (71%)
  matrix products  63.6 us (11%)
  other arithmetic  50.4 us (9%)
  local copies, waits for them, and re-layouts  42.6 us (7%)
    pallas_call x1, Pallas kernels, weight_grads(): pl.pallas_call(grads_kernel, out_shape=(jax.ShapeDtypeStruct((128, 2048),...  150 us
    pallas_call x1, Pallas kernels, gather_weights(): pl.pallas_call(weights_kernel, out_shape=(jax.ShapeDtypeStruct((16, 16, 1...  130 us
    pallas_call x1, Pallas kernels, feed_forward(): pl.pallas_call(mlp_kernel, out_shape=(jax.ShapeDtypeStruct((128, 2048), F...  104 us
    pallas_call x1, Pallas kernels, gather_kv(): pl.pallas_call(kv_kernel, out_shape=jax.ShapeDtypeStruct((8, rows, column...  17 us
    pallas_call x1, Pallas kernels, scatter_kv(): pl.pallas_call(kv_back_kernel, out_shape=jax.ShapeDtypeStruct((128, 512),...  16.7 us
    dot_general x1, matrix products, on_device(): jnp.einsum('qcgd,kcd->cgqk', grad_heads, values_all, preferred_element_ty...  15.4 us
    dot_general x2, matrix products, dot_back(): lax.dot_general(left, right, (((1,), (1,)), ((), ())), preferred_element_...  13.9 us
    unnamed x77, local copies, waits for them, and re-layouts  13.8 us
  transfers between devices with their start and end apart: 2, of which 0 were waited for; matrix products, arithmetic and copies ran while one was open for 2% of the time, Pallas kernels for 0%

profile of v2, /device:TPU:0, one launch (start us, length us, event | category | flops | bytes accessed | tf_op | source)
XLA Modules:
  0.0 578.2 jit_solution(15669537578979200834)
XLA Ops:
  0.7 1.3 copy-done
  2.0 0.7 collective-permute-start
  2.7 1.0 multiply_reduce_fusion.3
  4.0 1.2 fusion.25
  5.8 1.3 copy.54
  7.1 1.2 constant_dynamic-slice_fusion.1
  8.3 0.8 fusion.32.gu
  9.1 0.7 bitcast_convert_fusion
  10.4 2.0 pad_maximum_fusion.2.qkv
  12.4 0.9 compare_and_fusion
  14.0 130.1 %gather_weights.1 = (f32[16,16,128]{2,1,0:T(8,128)}, bf16[2048,2560]{1,0:T(8,128)(2,1)}, bf16[2048,2048]{1,0:T(8,128)(2,1)}, bf16[2048,1536]{1,0:T(8,128)(2,1)},...) custom-call(f32[16,128]{1,0:T(8,128)} %pad_maximum_fusion.7.gains, bf16[128,2560]{1,0:T(8,128)(2,1)} %pad_maximum_fusion.2.qkv, ...), custom_call_target="tpu_custom_call" | custom-call | tf_op jit(solution)/shard_map/gather_weights/pallas_call | solution.py:331
  144.1 0.9 fusion.51
  145.2 5.7 fusion.53
  150.9 1.0 slice.143
  152.6 1.5 copy.48
  154.2 1.1 slice_negate_fusion.1
  155.5 1.5 pad_maximum_fusion.4.own
  157.0 17.0 %gather_kv.1 = bf16[8,128,512]{2,1,0:T(8,128)(2,1)} custom-call(bf16[128,512]{1,0:T(8,128)(2,1)} %pad_maximum_fusion.4.own), custom_call_target="tpu_custom_call" | custom-call | tf_op jit(solution)/shard_map/gather_kv/pallas_call | solution.py:365
  174.1 1.3 fusion.49
  175.6 1.6 fusion.28
  177.2 7.1 %fusion.52 = (f32[4,8,128]{2,1,0:T(8,128)S(1)}, f32[4,8,128,1024]{2,3,1,0:T(8,128)}) fusion(bf16[1024,4,64,1]{0,2,3,1:T(8,128)(2,1)S(1)} %bitcast.134, bf16[128,4,8,64]{0,3,2,1:T(8,128)(2,1)S(1)} %fusion.28, pred[128,1024]{0,1:T(8,128)(4,1)S(1)} %compare_and_fusion), kind=kOutput, calls=%fused_computation.124 | convolution fusion | flops 549449728 | bytes 17973248 | tf_op jit(solution)/shard_map/qcgd,kcd->cgqk/dot_general | solution.py:909
  184.3 8.3 %fusion.3 = f32[4,8,128]{2,1,0:T(8,128)S(1)} fusion(f32[4,8,128,1024]{2,3,1,0:T(8,128)} %get-tuple-element.107, f32[4,8,128]{2,1,0:T(8,128)S(1)} %get-tuple-element.106), kind=kLoop, calls=%fused_computation.9 | loop fusion | flops 8384512 | bytes 16809984 | tf_op jit(solution)/shard_map/reduce_sum | solution.py:850
  192.8 7.8 %fusion.17 = bf16[4,64,8,128]{3,1,2,0:T(8,128)(2,1)S(1)} fusion(bf16[1024,4,64,1]{0,2,3,1:T(8,128)(2,1)S(1)} %bitcast.142, f32[4,8,128,1024]{2,3,1,0:T(8,128)} %get-tuple-element.107, f32[4,8,128]{2,1,0:T(8,128)S(1)} %fusion.3, f32[4,8,128]{2,1,0:T(8,128)S(1)} %get-tuple-element.106), kind=kOutput, calls=%fused_computation.31 | convolution fusion | flops 549715968 | bytes 17858560 | tf_op jit(solution)/shard_map/cgqk,kcd->qcgd/dot_general | solution.py:911
  200.6 4.9 multiply_reduce_fusion.2
  205.6 1.1 multiply_convert_fusion.a2
  206.7 104.3 %feed_forward.1 = (f32[128,2048]{1,0:T(8,128)}, bf16[8,128,2048]{2,1,0:T(8,128)(2,1)}, bf16[128,1536]{1,0:T(8,128)(2,1)}, bf16[352,256]{1,0:T(8,128)(2,1)}) custom-call(bf16[128,2048]{1,0:T(8,128)(2,1)} %multiply_convert_fusion.a2, bf16[2048,1536]{1,0:T(8,128)(2,1)} %get-tuple-element.54.gu_in, bf16[704,2048]{1,0:T(8,128)(2,1)} %get-tuple-element.55.dn_in, ...), custom_call_target="tpu_custom_call" | custom-call | tf_op jit(solution)/shard_map/feed_forward/pallas_call | solution.py:572
  311.0 1.5 multiply_reduce_fusion
  312.4 1.6 fusion.46.datt
  314.0 0.8 copy-done.11
  314.8 6.3 %convolution_convert_fusion = bf16[128,2048]{1,0:T(8,128)(2,1)S(1)} fusion(bf16[128,2048]{1,0:T(8,128)(2,1)S(1)} %fusion.46.datt, bf16[2048,2048]{1,0:T(8,128)(2,1)} %get-tuple-element.53), kind=kOutput, calls=%fused_computation.18 | convolution fusion | flops 1074003968 | bytes 9437184 | tf_op jit(solution)/shard_map/dot_general | solution.py:240
  321.5 15.4 %fusion = (f32[4,8,128]{2,1,0:T(8,128)S(1)}, f32[4,1024,128,8]{2,1,3,0:T(8,128)}) fusion(f32[4,8,128,1024]{2,3,1,0:T(8,128)} %get-tuple-element.107, f32[4,8,128]{2,1,0:T(8,128)S(1)} %log_add_fusion, bf16[1024,4,64,1]{0,2,3,1:T(8,128)(2,1)S(1)} %bitcast.143, bf16[128,4,8,64]{0,3,2,1:T(8,128)(2,1)S(1)} %bitcast.132), kind=kOutput, calls=%fused_computation.2 | convolution fusion | flops 549449728 | bytes 34635776 | tf_op jit(solution)/shard_map/qcgd,kcd->cgqk/dot_general | solution.py:928
  336.9 1.1 slice-done.3
  338.1 7.7 %fusion.2 = bf16[4,8,128,1024]{2,3,1,0:T(8,128)(2,1)S(1)} fusion(f32[4,1024,128,8]{2,1,3,0:T(8,128)} %get-tuple-element.111, f32[4,8,128,1024]{2,3,1,0:T(8,128)S(1)} %bitcast.126, f32[4,8,128]{2,1,0:T(8,128)S(1)} %get-tuple-element.110, f32[4,8,128]{2,1,0:T(8,128)S(1)} %log_add_fusion), kind=kLoop, calls=%fused_computation.4 | loop fusion | flops 16777216 | bytes 41975808 | tf_op jit(solution)/shard_map/convert_element_type | solution.py:931
  345.8 1.5 convolution_multiply_fusion
  347.3 3.7 fusion.16
  351.0 3.6 fusion.13
  354.7 1.1 copy.58
  355.8 1.1 copy.79
  357.0 1.1 copy.59
  358.1 2.2 pad_maximum_fusion.1.parts
  360.3 16.7 %scatter_kv.1 = f32[128,512]{1,0:T(8,128)} custom-call(bf16[8,128,512]{2,1,0:T(8,128)(2,1)} %pad_maximum_fusion.1.parts), custom_call_target="tpu_custom_call" | custom-call | tf_op jit(solution)/shard_map/scatter_kv/pallas_call | solution.py:391
  377.1 1.0 slice.166
  378.1 2.1 copy.63.att
  380.4 1.1 pad_maximum_fusion
  381.5 2.5 copy.55
  384.0 1.3 copy.53
  385.6 2.2 add_convert_fusion
  387.8 7.6 %fusion.26 = (f32[128]{0:T(128)S(1)}, f32[2048]{0:T(1024)S(1)}, f32[128,2048]{1,0:T(8,128)S(1)}) fusion(bf16[1,128,2048]{2,1,0:T(8,128)(2,1)S(1)} %copy-done.5, f32[2048]{0:T(1024)S(1)} %bitcast.162, f32[128]{0:T(128)S(1)} %copy-done.28, bf16[2048,2560]{1,0:T(8,128)(2,1)} %get-tuple-element.52, bf16[128,256]{1,0:T(8,128)(2,1)S(1)} %slice.166, ...), kind=kOutput, calls=%fused_computation.40 | convolution fusion | flops 1345976192 | bytes 12731392 | tf_op jit(solution)/shard_map/dot_general | solution.py:240
  395.4 0.7 collective-permute-start.1
  396.2 1.5 fusion.31
  397.7 0.9 pad_maximum_fusion.3.dqkv
  398.6 0.7 copy-done.26
  399.2 150.3 %weight_grads.1 = (bf16[128,2048]{1,0:T(8,128)(2,1)}, bf16[128,2560]{1,0:T(8,128)(2,1)}, bf16[128,2048]{1,0:T(8,128)(2,1)}, f32[16,128]{1,0:T(8,128)}, bf16[8,12...) custom-call(bf16[128,2048]{1,0:T(8,128)(2,1)} %copy-done.6, bf16[128,2048]{1,0:T(8,128)(2,1)} %copy.63.att, ...), custom_call_target="tpu_custom_call" | custom-call | tf_op jit(solution)/shard_map/weight_grads/pallas_call | solution.py:776
  549.5 2.1 slice_convert_fusion
  551.6 1.6 slice_convert_fusion.3
  553.2 5.3 convert_bitcast_fusion
  558.5 3.5 copy.64
  562.0 3.5 copy.67
  565.5 3.5 copy.65
  568.9 3.5 copy.68
  572.7 2.0 copy.77
  574.7 1.1 convert_element_type.125
  575.8 1.2 slice_bitcast_fusion
  577.0 0.8 copy.82
  (117 shorter events, 4.9 us)
Async XLA Ops:
  0.6 1.4 copy-start
  0.7 144.3 %copy-start.4 = (bf16[1,128,2048]{2,1,0:T(8,128)(2,1)S(1)}, bf16[1,128,2048]{2,1,0:T(8,128)(2,1)}, u32[]{:S(2)}) copy-start(bf16[1,128,2048]{2,1,0:T(8,128)(2,1)} %param.16) | copy-start | bytes 1572868
  2.0 11.2 %collective-permute-start = (bf16[352,256]{1,0:T(8,128)(2,1)S(1)}, bf16[352,256]{1,0:T(8,128)(2,1)S(1)}, u32[]{:S(2)}, u32[]{:S(2)}) collective-permute-start(bf16[352,256]{1,0:T(8,128)(2,1)S(1)} %constant_dynamic-slice_fusion), channel_id=1, source_target_pairs={{0,0},{1,1},{2,16},{3,17},{4,32},{5,33},{6,48},{7,49},{8,64},{9,65... | collective-permute-start | bytes 540680 | tf_op jit(solution)/shard_map/ppermute | solution.py:883
  5.2 145.7 %copy-start.29 = (f32[128]{0:T(128)}, f32[128]{0:T(128)S(1)}, u32[]{:S(2)}) copy-start(f32[128]{0:T(128)S(1)} %fusion.25) | copy-start | bytes 1540
  5.5 170.1 %copy-start.20 = (f32[128,64]{0,1:T(8,128)}, f32[128,64]{0,1:T(8,128)S(1)}, u32[]{:S(2)}) copy-start(f32[128,64]{0,1:T(8,128)S(1)} %get-tuple-element.103) | copy-start | bytes 98308
  13.3 137.6 %copy-start.27 = (f32[128]{0:T(128)}, f32[128]{0:T(128)S(1)}, u32[]{:S(2)}) copy-start(f32[128]{0:T(128)S(1)} %fusion.43) | copy-start | bytes 1540
  13.3 0.7 copy-start.25
  145.2 5.7 copy-start.6
  175.5 8.7 %copy-start.9 = (bf16[1024,256]{0,1:T(8,128)(2,1)}, bf16[1024,256]{0,1:T(8,128)(2,1)S(1)}, u32[]{:S(2)}) copy-start(bf16[1024,256]{0,1:T(8,128)(2,1)S(1)} %copy.47) | copy-start | bytes 1572868
  177.2 7.1 %copy-start.12 = (bf16[128,4,8,64]{0,3,2,1:T(8,128)(2,1)}, bf16[128,4,8,64]{0,3,2,1:T(8,128)(2,1)S(1)}, u32[]{:S(2)}) copy-start(bf16[128,4,8,64]{0,3,2,1:T(8,128)(2,1)S(1)} %fusion.28) | copy-start | bytes 1572868
  192.8 7.8 %copy-start.16 = (bf16[1024,256]{0,1:T(8,128)(2,1)}, bf16[1024,256]{0,1:T(8,128)(2,1)S(1)}, u32[]{:S(2)}) copy-start(bf16[1024,256]{0,1:T(8,128)(2,1)S(1)} %copy.46) | copy-start | bytes 1572868
  200.6 5.0 copy-start.15
  205.5 190.6 %copy-start.2 = (f32[128,2048]{1,0:T(8,128)}, f32[128,2048]{1,0:T(8,128)S(1)}, u32[]{:S(2)}) copy-start(f32[128,2048]{1,0:T(8,128)S(1)} %get-tuple-element.109.h1) | copy-start | bytes 3145732
  206.7 105.8 %copy-start.13 = (bf16[1,128,2048]{2,1,0:T(8,128)(2,1)S(1)}, bf16[1,128,2048]{2,1,0:T(8,128)(2,1)}, u32[]{:S(2)}) copy-start(bf16[1,128,2048]{2,1,0:T(8,128)(2,1)} %param.27) | copy-start | bytes 1572868
  314.0 0.8 copy-start.11
  314.8 6.7 %copy-start.17 = (bf16[1024,256]{0,1:T(8,128)(2,1)S(1)}, bf16[1024,256]{0,1:T(8,128)(2,1)}, u32[]{:S(2)}) copy-start(bf16[1024,256]{0,1:T(8,128)(2,1)} %copy-done.16) | copy-start | bytes 1572868
  321.4 15.5 %copy-start.7 = (bf16[128,2048]{0,1:T(8,128)(2,1)}, bf16[128,2048]{0,1:T(8,128)(2,1)S(1)}, u32[]{:S(2)}) copy-start(bf16[128,2048]{0,1:T(8,128)(2,1)S(1)} %copy.51) | copy-start | bytes 1572868
  321.5 15.5 %slice-start = ((s8[16777216]{0:T(1024)(128)(4,1)}), s8[4194304]{0:T(1024)(128)(4,1)S(1)}, s32[]{:S(2)}) async-start(s8[16777216]{0:T(1024)(128)(4,1)} %bitcast.125), calls=%async_computation | async-start | bytes 8388608
  321.5 15.5 %slice-start.1 = ((s8[16777216]{0:T(1024)(128)(4,1)}), s8[4194304]{0:T(1024)(128)(4,1)S(1)}, s32[]{:S(2)}) async-start(s8[16777216]{0:T(1024)(128)(4,1)} %bitcast.125), calls=%async_computation.1 | async-start | bytes 8388608
  321.5 15.4 %slice-start.2 = ((s8[16777216]{0:T(1024)(128)(4,1)}), s8[4194304]{0:T(1024)(128)(4,1)S(1)}, s32[]{:S(2)}) async-start(s8[16777216]{0:T(1024)(128)(4,1)} %bitcast.125), calls=%async_computation.2 | async-start | bytes 8388608
  321.5 16.6 %slice-start.3 = ((s8[16777216]{0:T(1024)(128)(4,1)}), s8[4194304]{0:T(1024)(128)(4,1)S(1)}, s32[]{:S(2)}) async-start(s8[16777216]{0:T(1024)(128)(4,1)} %bitcast.125), calls=%async_computation.3 | async-start | bytes 8388608
  338.1 7.7 %copy-start.10 = (bf16[1024,256]{0,1:T(8,128)(2,1)S(1)}, bf16[1024,256]{0,1:T(8,128)(2,1)}, u32[]{:S(2)}) copy-start(bf16[1024,256]{0,1:T(8,128)(2,1)} %copy-done.9) | copy-start | bytes 1572868
  345.8 5.3 copy-start.8
  354.6 25.6 %copy-start.21 = (f32[128,64]{0,1:T(8,128)S(1)}, f32[128,64]{0,1:T(8,128)}, u32[]{:S(2)}) copy-start(f32[128,64]{0,1:T(8,128)} %copy-done.20) | copy-start | bytes 98308
  377.0 8.3 %slice-start.4 = ((f32[128,512]{1,0:T(8,128)}), f32[128,256]{1,0:T(8,128)S(1)}, s32[]{:S(2)}) async-start(f32[128,512]{1,0:T(8,128)} %scatter_kv.1), calls=%async_computation.4 | async-start | bytes 262144 | tf_op jit(solution)/shard_map/slice | solution.py:940
  377.1 8.5 %copy-start.19 = (f32[128,512]{1,0:T(8,128)S(1)}, f32[128,512]{1,0:T(8,128)}, u32[]{:S(2)}) copy-start(f32[128,512]{1,0:T(8,128)} %scatter_kv.1) | copy-start | bytes 786436
  378.0 9.8 %copy-start.5 = (bf16[1,128,2048]{2,1,0:T(8,128)(2,1)S(1)}, bf16[1,128,2048]{2,1,0:T(8,128)(2,1)}, u32[]{:S(2)}) copy-start(bf16[1,128,2048]{2,1,0:T(8,128)(2,1)} %param.16) | copy-start | bytes 1572868
  378.1 9.8 %copy-start.28 = (f32[128]{0:T(128)S(1)}, f32[128]{0:T(128)}, u32[]{:S(2)}) copy-start(f32[128]{0:T(128)} %copy-done.27) | copy-start | bytes 1540
  385.6 9.8 %copy-start.31 = (bf16[352,256]{1,0:T(8,128)(2,1)S(1)}, bf16[352,256]{1,0:T(8,128)(2,1)}, u32[]{:S(2)}) copy-start(bf16[352,256]{1,0:T(8,128)(2,1)} %get-tuple-element.60) | copy-start | bytes 540676
  385.6 10.5 %copy-start.30 = (f32[128]{0:T(128)S(1)}, f32[128]{0:T(128)}, u32[]{:S(2)}) copy-start(f32[128]{0:T(128)} %copy-done.29) | copy-start | bytes 1540
  385.6 10.5 %copy-start.3 = (f32[128,2048]{1,0:T(8,128)S(1)}, f32[128,2048]{1,0:T(8,128)}, u32[]{:S(2)}) copy-start(f32[128,2048]{1,0:T(8,128)} %get-tuple-element.57) | copy-start | bytes 3145732
  385.6 10.5 %copy-start.14 = (bf16[1,128,2048]{2,1,0:T(8,128)(2,1)S(1)}, bf16[1,128,2048]{2,1,0:T(8,128)(2,1)}, u32[]{:S(2)}) copy-start(bf16[1,128,2048]{2,1,0:T(8,128)(2,1)} %param.27) | copy-start | bytes 1572868
  395.4 3.1 collective-permute-start.1
  397.7 0.9 copy-start.22
  398.6 0.7 copy-start.26
  562.0 10.5 %copy-start.18 = (bf16[8,352,256]{2,1,0:T(8,128)(2,1)S(1)}, bf16[8,352,256]{2,1,0:T(8,128)(2,1)}, u32[]{:S(2)}) copy-start(bf16[8,352,256]{2,1,0:T(8,128)(2,1)} %get-tuple-element.66) | copy-start | bytes 4325380
  568.9 5.8 copy-start.23
  568.9 8.8 %copy-start.1 = (bf16[352,2048]{1,0:T(8,128)(2,1)S(1)}, bf16[352,2048]{1,0:T(8,128)(2,1)}, u32[]{:S(2)}) copy-start(bf16[352,2048]{1,0:T(8,128)(2,1)} %param.26) | copy-start | bytes 4325380
  572.4 4.5 copy-start.24

commit v3 on v2

v3 whole, which is shorter than its diff:
```python
import functools

import jax
import jax.numpy as jnp
from jax import lax
from jax.experimental import pallas as pl
from jax.experimental.pallas import tpu as pltpu
from jax.sharding import PartitionSpec as P

MESH = pl.DeviceIdType.MESH
BF = jnp.bfloat16
F32 = jnp.float32
ANY = pl.BlockSpec(memory_space=pl.ANY)
VMEM = pl.BlockSpec(memory_space=pltpu.VMEM)

HEAD_DIM = 64
EPS = 1e-05
SCALE = 0.125
BASE = 10000.0

SLOT = {(0, 0): 0, (0, 1): 1, (1, 0): 2, (3, 0): 3, (1, 1): 4, (3, 1): 5, (2, 0): 6, (2, 1): 7}
STEPS = (0, 0, 1, 3, 1, 3, 2, 2)
PAIRS = (0, 1, 0, 0, 1, 1, 0, 1)


def slot_of(dr, dp):
    return SLOT[(dr % 4, dp % 2)]


class Place:
    def __init__(self):
        self.c = lax.axis_index("ctx")
        self.f = lax.axis_index("fsdp")
        self.y, self.zl = lax.div(self.c, 2), lax.rem(self.c, 2)
        self.j, self.co = lax.div(self.f, 2), lax.rem(self.f, 2)
        self.x, self.zh = lax.div(self.j, 2), lax.rem(self.j, 2)

    def ctx_at(self, dr, dp):
        return lax.rem(self.y + dr % 4, 4) * 2 + lax.rem(self.zl + dp, 2)

    def chip_at(self, dr, dp):
        return lax.rem(self.x + dr % 4, 4) * 2 + lax.rem(self.zh + dp, 2)

    def fsdp_at(self, dr, dp):
        return self.chip_at(dr, dp) * 2 + self.co

    def across_y(self, dr, dp):
        return {"ctx": self.ctx_at(dr, dp), "fsdp": self.f}

    def across_x(self, dr, dp):
        return {"ctx": self.c, "fsdp": self.fsdp_at(dr, dp)}

    def sibling(self):
        return {"ctx": self.c, "fsdp": self.f + 1 - 2 * self.co}


def greet(devices):
    barrier = pltpu.get_barrier_semaphore()
    for device in devices:
        pl.semaphore_signal(barrier, 1, device_id=device, device_id_type=MESH)
    pl.semaphore_wait(barrier, len(devices))


def near(dev):
    return [dev(1, 0), dev(-1, 0), dev(0, 1)]


def send(src, dst, sems, index, device):
    return pltpu.make_async_remote_copy(
        src, dst, sems[0].at[index], sems[1].at[index], device_id=device, device_id_type=MESH
    )


class Gather:
    MOVES = (
        ((0, 0), (0, 1), None),
        ((0, 0), (1, 0), None),
        ((0, 0), (-1, 0), None),
        ((0, 1), (1, 0), None),
        ((0, 1), (-1, 0), None),
        ((-1, 0), (1, 0), 0),
        ((-1, 1), (1, 0), 0),
        ((1, 0), (-1, 0), 1),
        ((1, 1), (-1, 0), 1),
    )

    def __init__(self, dev, own, loc, sems, row, sibling=None, sibling_sems=None):
        self.loc = loc
        self.copies = []
        for index, (block, to, half) in enumerate(self.MOVES):
            src = own if block == (0, 0) else loc(*block, 0, 0, half)
            dst = loc(*block, *to, half)
            self.copies.append(send(src, dst, sems, (row, index), dev(*to)))
        self.passed = {}
        if sibling is not None:
            self.passed[9] = send(own, loc(0, 0, 0, 0, None), sibling_sems, (row, 9), sibling)
            for index, ((dr, dp), (er, ep), half) in enumerate(self.MOVES):
                ref = loc(dr - er, dp + ep, 0, 0, half)
                self.passed[index] = send(ref, ref, sibling_sems, (row, index), sibling)
        self.own = own

    def _pass(self, index):
        if self.passed:
            self.passed[index].start()

    def _got(self, index):
        self.copies[index].wait_recv()
        self._pass(index)

    def start(self):
        for index in (0, 1, 2):
            self.copies[index].start()
        self._pass(9)

    def pair(self):
        self._got(0)
        self.copies[3].start()
        self.copies[4].start()

    def turn(self, dp):
        for got, on in (((1, 5), (2, 7)) if dp == 0 else ((3, 6), (4, 8))):
            self._got(got)
            self.copies[on].start()

    def last(self, dp):
        for got in ((5, 7) if dp == 0 else (6, 8)):
            self._got(got)

    def end(self):
        for copy in self.copies:
            copy.wait_send()
        for copy in self.passed.values():
            copy.wait()

    def all(self):
        self.start()
        self.pair()
        self.turn(0)
        self.turn(1)
        self.last(0)
        self.last(1)
        self.end()


def row_half(half, rows):
    return pl.ds(0, rows) if half is None else pl.ds(half * (rows // 2), rows // 2)


def add_into(ref, rows, others, step=16):
    step = min(step, rows)

    @pl.loop(0, rows // step)
    def _(i):
        at = pl.ds(pl.multiple_of(i * step, step), step)
        total = ref[at].astype(F32)
        for other in others:
            total = total + other[at].astype(F32)
        ref[at] = total.astype(ref.dtype)


class Scatter:
    def __init__(self, dev, part, rows, halves, fulls, paired, sems, row, cut=None):
        self.part, self.rows, self.cut = part, rows, cut
        self.halves, self.fulls, self.paired = halves, fulls, paired
        self.first, self.second = {}, {}
        for dp in (0, 1):
            for way, sign in ((0, 1), (1, -1)):
                self.first[way, dp] = send(
                    self._half(part(slot_of(2, dp)), way), halves.at[way, dp], sems, (row, way * 2 + dp), dev(sign, 0)
                )
                self.second[way, dp] = send(
                    part(slot_of(sign, dp)), fulls.at[way, dp], sems, (row, 4 + way * 2 + dp), dev(sign, 0)
                )
        self.third = send(part(slot_of(0, 1)), paired, sems, (row, 8), dev(0, 1))

    def _half(self, ref, way):
        if self.cut is None:
            return ref.at[pl.ds(way * (self.rows // 2), self.rows // 2)]
        return ref.at[:, pl.ds(way * (self.cut // 2), self.cut // 2)]

    def start(self):
        for dp in (1, 0):
            for way in (0, 1):
                self.first[way, dp].start()

    def turn(self, dp):
        for way, sign in ((0, 1), (1, -1)):
            self.first[way, dp].wait_recv()
            block = self._half(self.part(slot_of(sign, dp)), way)
            add_into(block, block.shape[0], [self.halves.at[way, dp]])
            self.second[way, dp].start()

    def pair(self):
        for way in (0, 1):
            self.second[way, 1].wait_recv()
        add_into(self.part(slot_of(0, 1)), self.rows, [self.fulls.at[0, 1], self.fulls.at[1, 1]])
        self.third.start()

    def finish(self, out, extra=()):
        for way in (0, 1):
            self.second[way, 0].wait_recv()
        self.third.wait_recv()
        own = self.part(0)
        terms = [own, self.fulls.at[0, 0], self.fulls.at[1, 0], self.paired, *extra]

        @pl.loop(0, self.rows // 16)
        def _(i):
            at = pl.ds(pl.multiple_of(i * 16, 16), 16)
            total = terms[0][at].astype(F32)
            for term in terms[1:]:
                total = total + term[at].astype(F32)
            out[at] = total.astype(out.dtype)

    def end(self):
        for copy in (*self.first.values(), *self.second.values(), self.third):
            copy.wait_send()


def scatter_buffers(rows, columns, dtype=BF, cut=False):
    half = (rows, columns // 2) if cut else (rows // 2, columns)
    return [
        pltpu.VMEM((2, 2, *half), dtype),
        pltpu.VMEM((2, 2, rows, columns), dtype),
        pltpu.VMEM((rows, columns), dtype),
    ]


def dma_sems(rows, count):
    return [pltpu.SemaphoreType.DMA((rows, count)), pltpu.SemaphoreType.DMA((rows, count))]


def params(collective_id, vmem=56):
    return pltpu.CompilerParams(
        collective_id=collective_id, has_side_effects=True, vmem_limit_bytes=vmem << 20
    )


def dot_in(left, right):
    return jnp.dot(left, right, preferred_element_type=F32)


def dot_back(left, right):
    return lax.dot_general(left, right, (((1,), (1,)), ((), ())), preferred_element_type=F32)


def dot_rows(left, right):
    return lax.dot_general(left, right, (((0,), (0,)), ((), ())), preferred_element_type=F32)


def mlp_kernel(
    a2, gu_in, dn_in, dy_in,
    da2_out, mpart, gu_out, dn_out,
    acts, gu, wd, dy, hid, dgu, dpart,
    d_half, d_full, d_pair,
    gsib, grecv, gown, gd, gdrecv, gdown,
    g_half, g_full, g_pair, n_half, n_full, n_pair,
    ag0, ag1, rs0, rs1, sib0, sib1, local,
):
    me = Place()
    greet(near(me.across_x) + near(me.across_y) + [me.sibling()])

    def acts_at(dr, dp, er, ep, half):
        return acts.at[slot_of(dr - er, dp + ep), row_half(half, 128)]

    task = Gather(me.across_y, a2, acts_at, (ag0, ag1), 0)
    task.start()
    loads = [
        pltpu.make_async_copy(gu_in, gu, local.at[0]),
        pltpu.make_async_copy(dn_in, wd.at[pl.ds(0, 704)], local.at[1]),
        pltpu.make_async_copy(dy_in, dy, local.at[2]),
    ]
    for load in loads:
        load.start()
    acts[0] = a2[...]
    wd[pl.ds(704, 64)] = jnp.zeros((64, 2048), BF)
    for load in loads:
        load.wait()

    def group(g):
        at = pl.ds(2 * g, 2)
        rows = pl.ds(pl.multiple_of(256 * g, 256), 256)
        for h in range(3):
            first, second = pl.ds(256 * h, 256), pl.ds(768 + 256 * h, 256)
            here = acts[at].reshape(256, 2048)
            gate = dot_in(here, gu[:, first])
            up = dot_in(here, gu[:, second])
            back = dot_back(dy[at].reshape(256, 2048), wd[first, :])
            curve = 1.0 / (1.0 + jnp.exp(-gate))
            silu = gate * curve
            hid[rows, first] = (silu * up).astype(BF)
            dgu[rows, first] = (back * up * (curve + silu * (1.0 - curve))).astype(BF)
            dgu[rows, second] = (back * silu).astype(BF)
        for n in range(4):
            wide = pl.ds(512 * n, 512)
            mpart[at, :, wide] = dot_in(hid[rows, :], wd[:, wide]).astype(BF).reshape(2, 128, 512)
            dpart[at, :, wide] = dot_back(dgu[rows, :], gu[wide, :]).astype(BF).reshape(2, 128, 512)

    @pl.loop(0, 4)
    def _(g):
        @pl.when(g == 0)
        def _():
            task.pair()

        @pl.when(g == 1)
        def _():
            task.turn(0)

        @pl.when(g == 2)
        def _():
            task.turn(1)

        @pl.when(g == 3)
        def _():
            task.last(0)
            task.last(1)

        group(g)

    grad = Scatter(me.across_y, lambda slot: dpart.at[slot], 128, d_half, d_full, d_pair, (rs0, rs1), 0)
    grad.start()

    def chip_of(t):
        dr = jnp.where(t < 2, 0, jnp.where(t >= 6, 2, 1 + 2 * lax.rem(t, 2)))
        dp = jnp.where(t < 2, t, jnp.where(t >= 6, t - 6, lax.div(t, 4)))
        return lax.rem(me.x + dr, 4) * 2 + lax.rem(me.zh + dp, 2)

    def weight_terms(t, core, out):
        first = pl.multiple_of((chip_of(t) * 2 + core) * 128, 128)
        left = acts[:, :, pl.ds(first, 128)].reshape(1024, 128)
        out[t] = dot_rows(left, dgu[...]).astype(BF)

    down_to = [
        send(gd.at[t, pl.ds(pl.multiple_of((1 - me.co) * 352, 16), 352)], gdrecv.at[t], (sib0, sib1), t, me.sibling())
        for t in range(8)
    ]
    gu_to = [send(gsib.at[t], grecv.at[t], (sib0, sib1), 8 + t, me.sibling()) for t in range(8)]

    @pl.loop(0, 8)
    def _(t):
        first = pl.multiple_of(chip_of(t) * 256, 256)
        gd[t] = dot_rows(hid[...], dy[:, :, pl.ds(first, 256)].reshape(1024, 256)).astype(BF)

    for copy in down_to:
        copy.start()

    @pl.loop(0, 8)
    def _(t):
        weight_terms(t, 1 - me.co, gsib)

    for copy in gu_to:
        copy.start()
    grad.turn(1)
    grad.turn(0)

    @pl.loop(0, 8)
    def _(t):
        weight_terms(t, me.co, gown)

    for copy in down_to:
        copy.wait_recv()

    @pl.loop(0, 8 * 22)
    def _(i):
        t, row = lax.div(i, 22), lax.rem(i, 22) * 16
        mine = gd[t, pl.ds(pl.multiple_of(me.co * 352 + row, 16), 16)].astype(F32)
        at = pl.ds(pl.multiple_of(row, 16), 16)
        gdown[t, at] = (mine + gdrecv[t, at].astype(F32)).astype(BF)

    for copy in gu_to:
        copy.wait_recv()

    @pl.loop(0, 8 * 8)
    def _(i):
        t, at = lax.div(i, 8), pl.ds(pl.multiple_of(lax.rem(i, 8) * 16, 16), 16)
        gown[t, at] = (gown[t, at].astype(F32) + grecv[t, at].astype(F32)).astype(BF)

    first = Scatter(me.across_x, lambda slot: gown.at[slot], 128, g_half, g_full, g_pair, (rs0, rs1), 1)
    second = Scatter(me.across_x, lambda slot: gdown.at[slot], 352, n_half, n_full, n_pair, (rs0, rs1), 2)
    first.start()
    second.start()
    grad.pair()
    for dp in (1, 0):
        first.turn(dp)
        second.turn(dp)
    grad.finish(da2_out)
    first.pair()
    second.pair()
    first.finish(gu_out)
    second.finish(dn_out)
    for job in (task, grad, first, second):
        job.end()
    for copy in (*down_to, *gu_to):
        copy.wait_send()


def feed_forward(a2, gu, dn, dy):
    scratch = [
        pltpu.VMEM((8, 128, 2048), BF),
        pltpu.VMEM((2048, 1536), BF),
        pltpu.VMEM((768, 2048), BF),
        pltpu.VMEM((8, 128, 2048), BF),
        pltpu.VMEM((1024, 768), BF),
        pltpu.VMEM((1024, 1536), BF),
        pltpu.VMEM((8, 128, 2048), BF),
        *scatter_buffers(128, 2048),
        pltpu.VMEM((8, 128, 1536), BF),
        pltpu.VMEM((8, 128, 1536), BF),
        pltpu.VMEM((8, 128, 1536), BF),
        pltpu.VMEM((8, 768, 256), BF),
        pltpu.VMEM((8, 352, 256), BF),
        pltpu.VMEM((8, 352, 256), BF),
        *scatter_buffers(128, 1536),
        *scatter_buffers(352, 256),
        *dma_sems(1, 9),
        *dma_sems(3, 9),
        pltpu.SemaphoreType.DMA((16,)),
        pltpu.SemaphoreType.DMA((16,)),
        pltpu.SemaphoreType.DMA((3,)),
    ]
    return pl.pallas_call(
        mlp_kernel,
        out_shape=(
            jax.ShapeDtypeStruct((128, 2048), F32),
            jax.ShapeDtypeStruct((8, 128, 2048), BF),
            jax.ShapeDtypeStruct((128, 1536), BF),
            jax.ShapeDtypeStruct((352, 256), BF),
        ),
        in_specs=[VMEM, ANY, ANY, ANY],
        out_specs=[VMEM] * 4,
        scratch_shapes=scratch,
        compiler_params=params(4, 62),
        name="feed_forward",
    )(a2, gu, dn, dy)


def load(src, dst, sem):
    copy = pltpu.make_async_copy(src, dst, sem)
    copy.start()
    return copy


def turned(values):
    lane = lax.broadcasted_iota(jnp.int32, values.shape, 1)
    low = lax.rem(lane, 64) < 32
    return jnp.where(low, pltpu.roll(values, 96, 1), pltpu.roll(values, 32, 1))


def pile(out, values, half):
    for h in range(8):
        out[pl.ds(64 * h, 64), :] = values[64 * half : 64 * half + 64, 64 * h : 64 * h + 64]


def unpile(values):
    flat = values.T
    return [
        jnp.concatenate([flat[128 * m : 128 * m + 64], flat[128 * m + 64 : 128 * m + 128]], axis=1)
        for m in range(4)
    ]


def norm_scale(ref, out):
    values = ref[...].astype(F32)
    out[...] = lax.rsqrt(jnp.mean(values * values, axis=1, keepdims=True) + EPS)


def front_kernel(
    x, gains_in, qkv_in, wo_in, gu_in, dn_in, dy_in, cosine, sine, bias_p, bias_c, partner,
    gains, qkv_out, wo_out, gu_all, dn_all, dy_all, a1, qst, kst, vst, att, lse, h1, a2,
    qkv, wo, kv_own, kv, sT, pT, scale,
    s0, s1, t0, t1, y0, y1, u0, u1, local,
):
    me = Place()
    greet(near(me.across_x) + near(me.across_y) + [me.sibling()])

    def rows_at(ref, rows):
        def loc(dr, dp, er, ep, half):
            size = rows if half is None else rows // 2
            first = me.fsdp_at(dr, dp) * rows + (0 if half is None else half * size)
            return ref.at[pl.ds(pl.multiple_of(first, size), size)]

        return loc

    def gains_at(dr, dp, er, ep, half):
        return gains.at[me.fsdp_at(dr, dp), row_half(half, 16)]

    def dn_at(dr, dp, er, ep, half):
        size = 352 if half is None else 176
        first = me.co * 352 + (0 if half is None else half * size)
        return dn_all.at[
            pl.ds(pl.multiple_of(first, 16), size),
            pl.ds(pl.multiple_of(me.chip_at(dr, dp) * 256, 256), 256),
        ]

    def slot_at(ref, rows):
        def loc(dr, dp, er, ep, half):
            return ref.at[slot_of(dr - er, dp + ep), row_half(half, rows)]

        return loc

    def columns(index):
        return pl.ds(pl.multiple_of(index * 256, 256), 256)

    def wo_x_at(dr, dp, er, ep, half):
        return wo.at[me.chip_at(dr, dp), me.co, row_half(half, 128), columns(me.c)]

    def wo_y_at(dr, dp, er, ep, half):
        chips = pl.ds(0, 8) if half is None else pl.ds(4 * half, 4)
        return wo.at[chips, me.co, :, columns(me.ctx_at(dr, dp))]

    def over_x(own, loc, row, both=True):
        return Gather(me.across_x, own, loc, (s0, s1), row, me.sibling() if both else None, (t0, t1))

    wo_own = wo_in.at[:, columns(me.c)]
    g = over_x(gains_in, gains_at, 0)
    q = over_x(qkv_in, rows_at(qkv, 128), 1)
    o = over_x(wo_own, wo_x_at, 2, both=False)
    m = over_x(gu_in, rows_at(gu_all, 128), 3)
    d = over_x(dn_in, dn_at, 4)
    dy = Gather(me.across_y, dy_in, slot_at(dy_all, 128), (y0, y1), 0)
    oy = Gather(me.across_y, wo_y_at(0, 0, 0, 0, None), wo_y_at, (y0, y1), 1, me.sibling(), (u0, u1))
    kv_task = Gather(me.across_y, kv_own, slot_at(kv, 128), (y0, y1), 2)
    kept = [load(task.own, task.loc(0, 0, 0, 0, None), local.at[i]) for i, task in enumerate((g, q, o, m, d, dy))]

    g.start()
    q.start()
    o.start()
    norm_scale(x, scale)
    g.pair()
    o.pair()
    q.pair()
    for task in (g, o, q):
        task.turn(0)
    for task in (g, o, q):
        task.turn(1)
    m.start()
    d.start()
    for task in (g, o):
        task.last(0)
        task.last(1)
    kept[2].wait()
    oy.start()
    kept[0].wait()
    g.end()

    @pl.loop(0, 16)
    def _(i):
        at = pl.ds(pl.multiple_of(i * 128, 128), 128)
        a1[:, at] = (x[:, at].astype(F32) * scale[...] * gains[i, pl.ds(0, 1), :]).astype(BF)

    q.last(0)
    q.last(1)
    oy.pair()
    kept[1].wait()
    q.end()
    saved = [load(qkv, qkv_out, local.at[6])]

    @pl.loop(0, 4)
    def _(n):
        raw = dot_in(a1[...], qkv[:, pl.ds(pl.multiple_of(512 * n, 512), 512)])
        for i in range(4):
            part = raw[:, 128 * i : 128 * i + 128]
            part = ((part * cosine[...] + turned(part) * sine[...]) .astype(BF).astype(F32) * SCALE).astype(BF)
            for half in (0, 1):
                for e in (0, 1):
                    qst[n, half, pl.ds(64 * (2 * i + e), 64), :] = part[64 * half : 64 * half + 64, 64 * e : 64 * e + 64]

    raw = dot_in(a1[...], qkv[:, pl.ds(2048, 512)])
    for i in range(2):
        part = raw[:, 128 * i : 128 * i + 128]
        kv_own[:, 128 * i : 128 * i + 128] = (part * cosine[...] + turned(part) * sine[...]).astype(BF)
    kv_own[:, 256:] = raw[:, 256:].astype(BF)
    kv_task.start()
    kv[0] = kv_own[...]
    m.pair()
    d.pair()
    kv_task.pair()
    kv_task.turn(0)
    kv_task.turn(1)
    m.turn(0)
    d.turn(0)
    oy.turn(0)
    kv_task.last(0)
    kv_task.last(1)
    kv_task.end()
    dy.start()
    oy.turn(1)

    mate = partner[0]
    beside = kv[mate]
    for out, base in ((kst, 0), (vst, 256)):
        for n in range(4):
            first = base + 64 * n
            for slot in range(8):
                out[n, pl.ds(64 * slot, 64), :] = kv[slot, 0:64, first : first + 64]
            out[n, pl.ds(512, 64), :] = beside[64:128, first : first + 64]
            out[n, pl.ds(576, 64), :] = kv_own[64:128, first : first + 64]

    def attend(n, half):
        count = 512 if half == 0 else 640
        keys = pl.ds(0, count)
        sT[keys] = dot_back(kst[n, keys, :], qst[n, half])
        for i in range(4):
            at = pl.ds(128 * i, 128)
            if half == 0:
                scores = sT[keys, at] + bias_p[...]
                peak = jnp.max(scores, axis=0, keepdims=True)
                raised = jnp.exp(scores - peak)
                total = jnp.sum(raised, axis=0, keepdims=True)
                pT[keys, at] = (raised * (1.0 / total)).astype(BF)
            else:
                first = sT[0:512, at]
                rest = sT[512:640, at] + bias_c[...]
                peak = jnp.maximum(
                    jnp.max(first, axis=0, keepdims=True), jnp.max(rest, axis=0, keepdims=True)
                )
                first = jnp.exp(first - peak)
                rest = jnp.exp(rest - peak)
                total = jnp.sum(first, axis=0, keepdims=True) + jnp.sum(rest, axis=0, keepdims=True)
                pT[0:512, at] = (first * (1.0 / total)).astype(BF)
                pT[512:640, at] = (rest * (1.0 / total)).astype(BF)
            lse[2 * n + half, :, at] = peak + jnp.log(total)
        for i, block in enumerate(unpile(dot_rows(vst[n, keys, :], pT[keys]))):
            first = pl.multiple_of(512 * n + 128 * i, 128)
            att[pl.ds(64 * half, 64), pl.ds(first, 128)] = block.astype(BF)

    @pl.loop(0, 4)
    def _(n):
        attend(n, 0)
        attend(n, 1)

        @pl.when(n == 0)
        def _():
            m.turn(1)
            d.turn(1)
            dy.pair()

        @pl.when(n == 1)
        def _():
            oy.last(0)
            dy.turn(0)

        @pl.when(n == 2)
        def _():
            oy.last(1)
            dy.turn(1)

    o.end()
    oy.end()
    saved.append(load(wo, wo_out, local.at[7]))

    @pl.loop(0, 4)
    def _(n):
        at = pl.ds(pl.multiple_of(512 * n, 512), 512)
        h1[:, at] = x[:, at].astype(F32) + dot_in(att[...], wo[:, :, :, at].reshape(2048, 512))

    norm_scale(h1, scale)

    @pl.loop(0, 16)
    def _(i):
        at = pl.ds(pl.multiple_of(i * 128, 128), 128)
        a2[:, at] = (h1[:, at] * scale[...] * gains[i, pl.ds(8, 1), :]).astype(BF)

    for task in (m, d, dy):
        task.last(0)
        task.last(1)
        task.end()
    for copy in (*kept[3:], *saved):
        copy.wait()


def front(x, gains, qkv, wo, gu, dn, dy, cosine, sine, bias_p, bias_c, partner):
    return pl.pallas_call(
        front_kernel,
        out_shape=(
            jax.ShapeDtypeStruct((16, 16, 128), F32),
            jax.ShapeDtypeStruct((2048, 2560), BF),
            jax.ShapeDtypeStruct((8, 2, 128, 2048), BF),
            jax.ShapeDtypeStruct((2048, 1536), BF),
            jax.ShapeDtypeStruct((704, 2048), BF),
            jax.ShapeDtypeStruct((8, 128, 2048), BF),
            jax.ShapeDtypeStruct((128, 2048), BF),
            jax.ShapeDtypeStruct((4, 2, 512, 64), BF),
            jax.ShapeDtypeStruct((4, 640, 64), BF),
            jax.ShapeDtypeStruct((4, 640, 64), BF),
            jax.ShapeDtypeStruct((128, 2048), BF),
            jax.ShapeDtypeStruct((8, 1, 512), F32),
            jax.ShapeDtypeStruct((128, 2048), F32),
            jax.ShapeDtypeStruct((128, 2048), BF),
        ),
        in_specs=[VMEM] + [ANY] * 6 + [VMEM] * 4 + [pl.BlockSpec(memory_space=pltpu.SMEM)],
        out_specs=[VMEM] + [ANY] * 5 + [VMEM] * 8,
        scratch_shapes=[
            pltpu.VMEM((2048, 2560), BF),
            pltpu.VMEM((8, 2, 128, 2048), BF),
            pltpu.VMEM((128, 512), BF),
            pltpu.VMEM((8, 128, 512), BF),
            pltpu.VMEM((640, 512), F32),
            pltpu.VMEM((640, 512), BF),
            pltpu.VMEM((128, 1), F32),
            *dma_sems(5, 9),
            *dma_sems(5, 10),
            *dma_sems(3, 9),
            *dma_sems(2, 10),
            pltpu.SemaphoreType.DMA((8,)),
        ],
        compiler_params=params(1, 50),
        name="front",
    )(x, gains, qkv, wo, gu, dn, dy, cosine, sine, bias_p, bias_c, partner)


def back_kernel(
    da2, h1, dy, x, gains, wo_in, qkv_in, qst, kst, vst, lse, cosine, sine, bias_p, bias_c, partner,
    a1_in, att_in, mpart_in, gu, dn,
    mixed, tokens_grad, q_out, kv_out, o_out, gains_out, gu_all, dn_all,
    a1s, atts, dqkvs, datts, grow, dh1, gown, gsib, mpart, stream, dost, sT, dT, pT, dsT,
    kgrad, vgrad, kvp, dkv, da1, dnp,
    qp, op, kp, gp, ggot, q_sum, o_sum, kv_sum, g_sum,
    q_half, q_full, q_pair, o_half, o_full, o_pair, k_half, k_full, k_pair, e_half, e_full, e_pair,
    m_half, m_full, m_pair, d_half, d_full, d_pair,
    or_half, or_full, or_pair, qr_half, qr_full, qr_pair, kr_half, kr_full, kr_pair,
    sib0, sib1, x0, x1, y0, y1, ag0, ag1, swap0, swap1, local,
):
    me = Place()
    moved = me.c != me.j
    swapped = {"ctx": me.j, "fsdp": 2 * me.c + me.co}
    barrier = pltpu.get_barrier_semaphore()
    others = near(me.across_x) + near(me.across_y) + [me.sibling()]
    for device in others:
        pl.semaphore_signal(barrier, 1, device_id=device, device_id_type=MESH)

    @pl.when(moved)
    def _():
        pl.semaphore_signal(barrier, 1, device_id=swapped, device_id_type=MESH)

    pl.semaphore_wait(barrier, len(others) + jnp.where(moved, 1, 0))

    dn_move = pltpu.make_async_remote_copy(dn, dnp, swap0, swap1, device_id=swapped, device_id_type=MESH)
    dn_keep = pltpu.make_async_copy(dn, dnp, local.at[0])

    @pl.when(moved)
    def _():
        dn_move.start()

    @pl.when(jnp.logical_not(moved))
    def _():
        dn_keep.start()

    own, other = pl.ds(0, 128), pl.ds(128, 128)
    mload = load(mpart_in, mpart, local.at[1])
    a1load = load(a1_in, a1s.at[own], local.at[2])
    attload = load(att_in, atts.at[own], local.at[3])

    def wo_load(n):
        return pltpu.make_async_copy(
            wo_in.at[pl.ds(512 * n, 512)], stream.at[n % 2, :, pl.ds(0, 2048)], local.at[4 + n % 2]
        )

    def qkv_load(n):
        return pltpu.make_async_copy(qkv_in.at[pl.ds(512 * n, 512)], stream.at[n % 2], local.at[4 + n % 2])

    wo_load(0).start()
    wo_load(1).start()

    over_x, over_y, over_ag = (x0, x1), (y0, y1), (ag0, ag1)
    o_job = Scatter(me.across_x, lambda slot: op.at[slot], 128, o_half, o_full, o_pair, over_x, 0)
    q_job = Scatter(me.across_x, lambda slot: qp.at[slot], 128, q_half, q_full, q_pair, over_x, 1)
    k_job = Scatter(me.across_x, lambda slot: kp.at[slot], 128, k_half, k_full, k_pair, over_x, 2)
    e_job = Scatter(me.across_x, lambda slot: gp.at[slot], 16, e_half, e_full, e_pair, over_x, 3)
    m_job = Scatter(me.across_y, lambda slot: mpart.at[slot], 128, m_half, m_full, m_pair, over_y, 0)
    d_job = Scatter(me.across_y, lambda slot: kvp.at[slot], 128, d_half, d_full, d_pair, over_y, 1)

    def at_ctx(ref):
        def loc(dr, dp, er, ep, half):
            return ref.at[me.ctx_at(dr, dp), row_half(half, ref.shape[1])]

        return loc

    def dn_at(dr, dp, er, ep, half):
        first = pl.multiple_of(me.ctx_at(dr, dp) * 256, 256)
        return dn_all.at[row_half(half, 352), pl.ds(first, 256)]

    gu_task = Gather(me.across_y, gu, at_ctx(gu_all), over_ag, 0)
    dn_task = Gather(me.across_y, dnp, dn_at, over_ag, 1)
    e_task = Gather(me.across_y, g_sum, at_ctx(ggot), over_ag, 2)

    def sum_over_ctx(total, columns, halves, fulls, paired, row):
        def part(slot):
            first = pl.multiple_of(me.ctx_at(STEPS[slot], PAIRS[slot]) * 16, 16)
            return total.at[pl.ds(first, 16)]

        return Scatter(me.across_y, part, 16, halves, fulls, paired, over_y, row, cut=columns)

    def spread(out, columns, row):
        def loc(dr, dp, er, ep, half):
            first = pl.multiple_of(me.ctx_at(dr, dp) * 16, 16)
            if half is None:
                return out.at[pl.ds(first, 16)]
            return out.at[pl.ds(first, 16), pl.ds(half * (columns // 2), columns // 2)]

        return Gather(me.across_y, loc(0, 0, 0, 0, None), loc, over_ag, row)

    o_sums = sum_over_ctx(o_sum, 2048, or_half, or_full, or_pair, 2)
    q_sums = sum_over_ctx(q_sum, 2048, qr_half, qr_full, qr_pair, 3)
    kv_sums = sum_over_ctx(kv_sum, 512, kr_half, kr_full, kr_pair, 4)
    o_spread = spread(o_out, 2048, 3)
    q_spread = spread(q_out, 2048, 4)
    kv_spread = spread(kv_out, 512, 5)
    own_rows = pl.ds(pl.multiple_of(me.c * 16, 16), 16)

    swap = lambda src, dst, index: send(src, dst, (sib0, sib1), index, me.sibling())
    att_swap = swap(atts.at[own], atts.at[other], 0)
    datt_swap = swap(datts.at[own], datts.at[other], 1)
    a1_swap = swap(a1s.at[own], a1s.at[other], 2)
    queries = pl.ds(0, 2048)
    dq_swap = swap(dqkvs.at[own, queries], dqkvs.at[other, queries], 3)
    rest = pl.ds(2048, 512)
    dkv_swap = swap(dqkvs.at[own, rest], dqkvs.at[other, rest], 4)
    gain_swap = swap(gown, gsib, 5)

    attload.wait()
    att_swap.start()
    a1load.wait()
    a1_swap.start()
    mload.wait()
    m_job.start()

    gown[...] = jnp.zeros((16, 16, 128), F32)
    for i in range(16):
        grow[0, :, 128 * i : 128 * i + 128] = gains[i, 0:1, :]
        grow[1, :, 128 * i : 128 * i + 128] = gains[i, 8:9, :]
    grow[2] = jnp.zeros((1, 2048), F32)
    grow[3] = jnp.zeros((1, 2048), F32)

    @pl.loop(0, 8)
    def _(i):
        at = pl.ds(pl.multiple_of(16 * i, 16), 16)
        values, grad = h1[at], da2[at]
        scale = lax.rsqrt(jnp.mean(values * values, axis=1, keepdims=True) + EPS)
        grow[3] += jnp.sum(grad * values * scale, axis=0, keepdims=True)
        grad = grad * grow[1]
        level = jnp.mean(grad * values, axis=1, keepdims=True) * scale * scale * scale
        total = dy[at].astype(F32) + scale * grad - values * level
        dh1[at] = total
        datts[at] = total.astype(BF)

    datt_swap.start()
    for n in range(4):
        wo_load(n).wait()
        part = dot_back(datts[own], stream[n % 2, :, 0:2048]).astype(BF)
        for half in (0, 1):
            pile(dost.at[n, half], part, half)
        if n < 2:
            wo_load(n + 2).start()
    qkv_load(0).start()
    qkv_load(1).start()

    def chip_of(t):
        dr = jnp.where(t < 2, 0, jnp.where(t >= 6, 2, 1 + 2 * lax.rem(t, 2)))
        dp = jnp.where(t < 2, t, jnp.where(t >= 6, t - 6, lax.div(t, 4)))
        return lax.rem(me.x + dr, 4) * 2 + lax.rem(me.zh + dp, 2)

    def terms(left, right, out):
        @pl.loop(0, 8)
        def _(i):
            t = 7 - i
            first = pl.multiple_of((chip_of(t) * 2 + me.co) * 128, 128)
            out[t] = dot_rows(left[:, pl.ds(first, 128)], right).astype(BF)

    att_swap.wait_recv()
    datt_swap.wait_recv()
    terms(atts, datts[...], op)
    o_job.start()
    m_job.turn(1)
    m_job.turn(0)

    def attend(n, half):
        count = 512 if half == 0 else 640
        keys = pl.ds(0, count)
        key, query, out = kst[n, keys, :], qst[n, half], dost[n, half]
        sT[keys] = dot_back(key, query)
        dT[keys] = dot_back(vst[n, keys, :], out)
        for i in range(4):
            at = pl.ds(128 * i, 128)
            parts = []
            for first, size in ((0, 512), (512, 128))[: 1 + half]:
                scores = sT[first : first + size, at]
                if half == 0:
                    scores = scores + bias_p[...]
                elif first:
                    scores = scores + bias_c[...]
                probs = jnp.exp(scores - lse[2 * n + half, :, at])
                grad = dT[first : first + size, at]
                parts.append((first, size, probs, grad))
            level = sum(jnp.sum(probs * grad, axis=0, keepdims=True) for _, _, probs, grad in parts)
            for first, size, probs, grad in parts:
                pT[first : first + size, at] = probs.astype(BF)
                dsT[first : first + size, at] = (probs * (grad - level)).astype(BF)
        rows = slice(64 * half, 64 * half + 64)
        for i, block in enumerate(unpile(dot_rows(key, dsT[keys]) * SCALE)):
            block = block * cosine[rows] - turned(block) * sine[rows]
            first = pl.multiple_of(512 * n + 128 * i, 128)
            dqkvs[rows, pl.ds(first, 128)] = block.astype(BF)
        return dot_in(dsT[keys], query), dot_in(pT[keys], out)

    @pl.loop(0, 4)
    def _(n):
        key_one, value_one = attend(n, 0)
        key_two, value_two = attend(n, 1)
        for out, one, two in ((kgrad, key_one, key_two), (vgrad, value_one, value_two)):
            out[n, 0:512] = (one + two[0:512]).astype(BF)
            out[n, 512:640] = two[512:640].astype(BF)

        @pl.when(n == 0)
        def _():
            o_job.turn(1)
            o_job.turn(0)

        @pl.when(n == 1)
        def _():
            m_job.pair()

        @pl.when(n == 2)
        def _():
            o_job.pair()

    dq_swap.start()
    mate = partner[0]
    for out, base in ((kgrad, 0), (vgrad, 256)):
        for n in range(4):
            first = base + 64 * n
            for slot in range(8):
                kvp[slot, 0:64, first : first + 64] = out[n, 64 * slot : 64 * slot + 64, :]
                if slot == 0:
                    late = out[n, 576:640, :]
                else:
                    late = jnp.where(mate == slot, out[n, 512:576, :], jnp.zeros((64, 64), BF))
                kvp[slot, 64:128, first : first + 64] = late
    d_job.start()
    a1_swap.wait_recv()
    dq_swap.wait_recv()
    terms(a1s, dqkvs[:, 0:2048], qp)
    q_job.start()
    d_job.turn(1)
    d_job.turn(0)
    m_job.finish(mixed, (h1,))
    o_job.finish(o_sum)
    d_job.pair()
    d_job.finish(dkv)
    for i in range(2):
        at = slice(128 * i, 128 * i + 128)
        block = dkv[:, at]
        dqkvs[own, 2048 + 128 * i : 2176 + 128 * i] = (block * cosine[...] - turned(block) * sine[...]).astype(BF)
    dqkvs[own, 2304:2560] = dkv[:, 256:512].astype(BF)
    dkv_swap.start()
    o_sums.start()
    kept = [load(gu, gu_all.at[me.c], local.at[6])]
    gu_task.start()

    @pl.when(moved)
    def _():
        dn_move.wait()

    @pl.when(jnp.logical_not(moved))
    def _():
        dn_keep.wait()

    dn_task.start()
    kept.append(load(dnp, dn_at(0, 0, 0, 0, None), local.at[7]))
    dkv_swap.wait_recv()
    terms(a1s, dqkvs[:, 2048:2560], kp)
    k_job.start()
    q_job.turn(1)
    q_job.turn(0)

    for n in range(4):
        qkv_load(n).wait()
        da1[:, 512 * n : 512 * n + 512] = dot_back(dqkvs[own], stream[n % 2])
        if n < 2:
            qkv_load(n + 2).start()

    @pl.loop(0, 8)
    def _(i):
        at = pl.ds(pl.multiple_of(16 * i, 16), 16)
        values, grad = x[at].astype(F32), da1[at]
        scale = lax.rsqrt(jnp.mean(values * values, axis=1, keepdims=True) + EPS)
        grow[2] += jnp.sum(grad * values * scale, axis=0, keepdims=True)
        grad = grad * grow[0]
        level = jnp.mean(grad * values, axis=1, keepdims=True) * scale * scale * scale
        tokens_grad[at] = (dh1[at] + scale * grad - values * level).astype(BF)

    for i in range(16):
        gown[i, 0:1, :] = grow[2, :, 128 * i : 128 * i + 128]
        gown[i, 8:9, :] = grow[3, :, 128 * i : 128 * i + 128]
    gain_swap.start()
    o_sums.turn(1)
    o_sums.turn(0)
    gain_swap.wait_recv()
    for slot in range(8):
        block = me.fsdp_at(STEPS[slot], PAIRS[slot])
        gp[slot] = gown[block] + gsib[block]
    e_job.start()
    gu_task.pair()
    dn_task.pair()
    o_sums.pair()
    o_sums.finish(o_out.at[own_rows])
    o_spread.start()
    gu_task.turn(0)
    dn_task.turn(0)
    k_job.turn(1)
    k_job.turn(0)
    q_job.pair()
    e_job.turn(1)
    e_job.turn(0)
    gu_task.turn(1)
    dn_task.turn(1)
    o_spread.pair()
    o_spread.turn(0)
    o_spread.turn(1)
    k_job.pair()
    e_job.pair()
    q_job.finish(q_sum)
    q_sums.start()
    k_job.finish(kv_sum)
    kv_sums.start()
    e_job.finish(g_sum)
    e_task.start()
    ggot[me.c] = g_sum[...]
    for job in (q_sums, kv_sums):
        job.turn(1)
        job.turn(0)
    e_task.pair()
    e_task.turn(0)
    e_task.turn(1)
    for job, out, task in ((q_sums, q_out, q_spread), (kv_sums, kv_out, kv_spread)):
        job.pair()
        job.finish(out.at[own_rows])
        task.start()
    for task in (q_spread, kv_spread):
        task.pair()
    for task in (q_spread, kv_spread):
        task.turn(0)
        task.turn(1)
    e_task.last(0)
    e_task.last(1)
    total = ggot[0]
    for index in range(1, 8):
        total = total + ggot[index]
    gains_out[...] = total
    for task in (gu_task, dn_task, o_spread, q_spread, kv_spread):
        task.last(0)
        task.last(1)
    jobs = (o_job, q_job, k_job, e_job, m_job, d_job, o_sums, q_sums, kv_sums)
    for job in (*jobs, gu_task, dn_task, e_task, o_spread, q_spread, kv_spread):
        job.end()
    for copy in (att_swap, datt_swap, a1_swap, dq_swap, dkv_swap, gain_swap):
        copy.wait_send()
    for copy in kept:
        copy.wait()


def back(da2, h1, dy, x, gains, wo, qkv, qst, kst, vst, lse, cosine, sine, bias_p, bias_c, partner, a1, att, mpart, gu, dn):
    scratch = [
        pltpu.VMEM((256, 2048), BF),
        pltpu.VMEM((256, 2048), BF),
        pltpu.VMEM((256, 2560), BF),
        pltpu.VMEM((256, 2048), BF),
        pltpu.VMEM((4, 1, 2048), F32),
        pltpu.VMEM((128, 2048), F32),
        pltpu.VMEM((16, 16, 128), F32),
        pltpu.VMEM((16, 16, 128), F32),
        pltpu.VMEM((8, 128, 2048), BF),
        pltpu.VMEM((2, 512, 2560), BF),
        pltpu.VMEM((4, 2, 512, 64), BF),
        pltpu.VMEM((640, 512), F32),
        pltpu.VMEM((640, 512), F32),
        pltpu.VMEM((640, 512), BF),
        pltpu.VMEM((640, 512), BF),
        pltpu.VMEM((4, 640, 64), BF),
        pltpu.VMEM((4, 640, 64), BF),
        pltpu.VMEM((8, 128, 512), BF),
        pltpu.VMEM((128, 512), F32),
        pltpu.VMEM((128, 2048), F32),
        pltpu.VMEM((352, 256), BF),
        pltpu.VMEM((8, 128, 2048), BF),
        pltpu.VMEM((8, 128, 2048), BF),
        pltpu.VMEM((8, 128, 512), BF),
        pltpu.VMEM((8, 16, 128), F32),
        pltpu.VMEM((8, 16, 128), F32),
        pltpu.VMEM((128, 2048), BF),
        pltpu.VMEM((128, 2048), BF),
        pltpu.VMEM((128, 512), BF),
        pltpu.VMEM((16, 128), F32),
        *scatter_buffers(128, 2048),
        *scatter_buffers(128, 2048),
        *scatter_buffers(128, 512),
        *scatter_buffers(16, 128, F32),
        *scatter_buffers(128, 2048),
        *scatter_buffers(128, 512),
        *scatter_buffers(16, 2048, cut=True),
        *scatter_buffers(16, 2048, cut=True),
        *scatter_buffers(16, 512, cut=True),
        pltpu.SemaphoreType.DMA((6,)),
        pltpu.SemaphoreType.DMA((6,)),
        *dma_sems(4, 9),
        *dma_sems(5, 9),
        *dma_sems(6, 9),
        pltpu.SemaphoreType.DMA,
        pltpu.SemaphoreType.DMA,
        pltpu.SemaphoreType.DMA((8,)),
    ]
    return pl.pallas_call(
        back_kernel,
        out_shape=(
            jax.ShapeDtypeStruct((128, 2048), BF),
            jax.ShapeDtypeStruct((128, 2048), BF),
            jax.ShapeDtypeStruct((128, 2048), BF),
            jax.ShapeDtypeStruct((128, 512), BF),
            jax.ShapeDtypeStruct((128, 2048), BF),
            jax.ShapeDtypeStruct((16, 128), F32),
            jax.ShapeDtypeStruct((8, 128, 1536), BF),
            jax.ShapeDtypeStruct((352, 2048), BF),
        ),
        in_specs=[VMEM] * 5 + [ANY] * 2 + [VMEM] * 8 + [pl.BlockSpec(memory_space=pltpu.SMEM)] + [ANY] * 5,
        out_specs=[VMEM] * 6 + [ANY] * 2,
        scratch_shapes=scratch,
        compiler_params=params(5, 62),
        name="back",
    )(da2, h1, dy, x, gains, wo, qkv, qst, kst, vst, lse, cosine, sine, bias_p, bias_c, partner, a1, att, mpart, gu, dn)


def tables(position):
    freq = BASE ** (-(jnp.arange(HEAD_DIM // 2, dtype=jnp.float32) * 2.0) / HEAD_DIM)
    angle = position.astype(jnp.float32)[:, None] * freq[None, :]
    angle = jnp.concatenate([angle, angle], axis=-1)
    return (jnp.cos(angle), jnp.sin(angle))


def timeline(table_flat, total_len, row_count):
    everywhere = jnp.arange(total_len, dtype=jnp.int32)
    half_len = row_count // 2
    moment = jnp.repeat(table_flat, half_len) * half_len + everywhere % half_len
    prompt_len = total_len // 2
    cont_len = total_len // 8
    later = moment >= prompt_len
    segment = jnp.where(later, 1 + (moment - prompt_len) // cont_len, 0)
    position = jnp.where(later, prompt_len + (moment - prompt_len) % cont_len, moment)
    return (segment, position)


def swap_pairs():
    pairs = []
    for c in range(8):
        for f in range(16):
            pairs.append((c * 16 + f, (f // 2) * 16 + 2 * c + f % 2))
    return pairs


def on_device(
    tokens,
    block_deal,
    attn_gain,
    query_weight,
    key_weight,
    value_weight,
    output_weight,
    mlp_gain,
    gate_weight,
    up_weight,
    down_weight,
    cotangent,
):
    row_count = tokens.shape[1]
    c = lax.axis_index("ctx")
    f = lax.axis_index("fsdp")
    full_len = row_count * 8

    def sliced(weight):
        return jnp.pad(lax.dynamic_slice_in_dim(weight, c * 704, 704, 1), ((0, 0), (0, 64)))

    none = jnp.zeros((7, 128), F32)
    gains = jnp.concatenate([attn_gain.astype(F32)[None], none, mlp_gain.astype(F32)[None], none])
    qkv = jnp.concatenate([query_weight, key_weight, value_weight], axis=1)
    gu = jnp.concatenate([sliced(gate_weight), sliced(up_weight)], axis=1)
    dn = lax.dynamic_slice_in_dim(down_weight, c * 256, 256, 1)
    dn = lax.ppermute(dn, ("ctx", "fsdp"), swap_pairs())

    y, zl = c // 2, c % 2
    order = jnp.stack([((y + STEPS[s]) % 4) * 2 + (zl + PAIRS[s]) % 2 for s in range(8)])
    deal = jnp.take(lax.dynamic_index_in_dim(block_deal, f, 0, keepdims=False), order, axis=0)
    mate_block = 8 + (deal[0, 1] - 8 + 1 - 2 * ((deal[0, 1] - 8) % 2))
    mate = jnp.argmax((deal[:, 1] == mate_block).astype(jnp.int32)).astype(jnp.int32)
    segment, position = timeline(deal.reshape(-1), full_len, row_count)
    own_segment, own_position = segment[:row_count], position[:row_count]
    cosine, sine = tables(own_position)
    sign = jnp.where(jnp.arange(HEAD_DIM) < 32, -1.0, 1.0)
    cosine_two = jnp.concatenate([cosine, cosine], axis=1)
    sine_two = jnp.concatenate([sine * sign, sine * sign], axis=1)
    prompt_position = position.reshape(8, 2, 64)[:, 0].reshape(512)
    bias_p = jnp.where(prompt_position[:, None] <= own_position[None, :64], 0.0, -1e30)
    mate_seen = deal[0, 1] > mate_block
    step = jnp.arange(64)
    bias_c = jnp.concatenate(
        [
            jnp.broadcast_to(jnp.where(mate_seen, 0.0, -1e30), (64, 64)),
            jnp.where(step[:, None] <= step[None, :], 0.0, -1e30),
        ]
    )
    bias_p = jnp.concatenate([bias_p, bias_p], axis=1).astype(F32)
    bias_c = jnp.concatenate([bias_c, bias_c], axis=1).astype(F32)

    gains_all, qkv_all, wo_all, gu_all, dn_all, dy_all, normed, qst, kst, vst, attended, lse, hidden_state, normed_two = front(
        tokens[0], gains, qkv, output_weight, gu, dn, cotangent[0], cosine_two, sine_two, bias_p, bias_c, mate[None]
    )
    wo_all = wo_all.reshape(2048, 2048)

    grad_normed_two, mixed_parts, gu_sum, dn_sum = feed_forward(normed_two, gu_all, dn_all, dy_all)

    mixed, tokens_grad, query_grad, kv_grad, o_grad, gain_grads, gu_grads, dn_grad = back(
        grad_normed_two, hidden_state, cotangent[0], tokens[0], gains_all, wo_all, qkv_all, qst, kst, vst, lse,
        cosine_two, sine_two, bias_p, bias_c, mate[None], normed, attended, mixed_parts, gu_sum, dn_sum,
    )

    def joined(parts):
        return parts.transpose(1, 0, 2).reshape(parts.shape[1], -1).astype(F32)

    return (
        mixed[None],
        tokens_grad[None],
        gain_grads[0],
        query_grad.astype(F32),
        kv_grad[:, :256].astype(F32),
        kv_grad[:, 256:].astype(F32),
        o_grad.astype(F32),
        gain_grads[8],
        joined(gu_grads[:, :, :704]),
        joined(gu_grads[:, :, 768:1472]),
        dn_grad.astype(F32),
    )


def solution(mesh):
    held = P("fsdp", "ctx", None)
    rows = P("fsdp", None)
    return jax.shard_map(
        on_device,
        mesh=mesh,
        in_specs=(held, P(), P("fsdp"), rows, rows, rows, rows, P("fsdp"), rows, rows, rows, held),
        out_specs=(held, held, P("fsdp"), rows, rows, rows, rows, P("fsdp"), rows, rows, rows),
        check_vma=False,
    )
```

time: 589 us -> 433 us (0.74); the launches traced: 578 us -> 432 us
  matrix products: 63.6 us -> 0 us
  other arithmetic: 50.4 us -> 13.9 us
  Pallas kernels: 418 us -> 392 us
  local copies, waits for them, and re-layouts: 42.6 us -> 22.4 us
    dot_general x10 -> x0, matrix products: 63.6 us -> none  [the longest x1 15.4 us: on_device(): jnp.einsum('qcgd,kcd->cgqk', grad_heads, values_all, preferred_element_ty...]
    pallas_call x4 -> x2, Pallas kernels: 314 us -> 281 us  [the longest x1 142 us: back(): pl.pallas_call(back_kernel, out_shape=(jax.ShapeDtypeStruct((128, 2048),...]
    convert_element_type x10 -> x4, other arithmetic: 18.1 us -> 5.81 us  [the longest x1 2.12 us: on_device(): query_grad.astype(F32)]
    reduce_sum x3 -> x0, other arithmetic: 11 us -> none  [the longest x1 8.26 us: softmax_parts(): total = jnp.sum(unscaled, axis=-1, keepdims=True)]
    pallas_call x1, Pallas kernels: 104 us -> 111 us  [feed_forward(): pl.pallas_call(mlp_kernel, out_shape=(jax.ShapeDtypeStruct((128, 2048), F...]
    slice x13 -> x2, local copies, waits for them, and re-layouts: 6.96 us -> 0.59 us  [the longest x1 0.58 us: on_device(): mate_seen = deal[0, 1] > mate_block]
    unnamed x77 -> x44, local copies, waits for them, and re-layouts: 13.8 us -> 11.4 us
  transfers between devices with their start and end apart: 2 -> 1, of which waited for: 0 -> 0; matrix products, arithmetic and copies ran while one was open for 2% -> 2% of each run, Pallas kernels for 0% -> 0%
where the time goes in v3:
time: 433 us; the launch traced here: 432 us
  Pallas kernels  392 us (91%)
  local copies, waits for them, and re-layouts  22.4 us (5%)
  other arithmetic  13.9 us (3%)
    pallas_call x1, Pallas kernels, back(): pl.pallas_call(back_kernel, out_shape=(jax.ShapeDtypeStruct((128, 2048),...  142 us
    pallas_call x1, Pallas kernels, front(): pl.pallas_call(front_kernel, out_shape=(jax.ShapeDtypeStruct((16, 16, 128...  139 us
    pallas_call x1, Pallas kernels, feed_forward(): pl.pallas_call(mlp_kernel, out_shape=(jax.ShapeDtypeStruct((128, 2048), F...  111 us
    unnamed x44, local copies, waits for them, and re-layouts  11.4 us
  transfers between devices with their start and end apart: 1, of which 0 were waited for; matrix products, arithmetic and copies ran while one was open for 2% of the time, Pallas kernels for 0%

profile of v3, /device:TPU:0, one launch (start us, length us, event | category | flops | bytes accessed | tf_op | source)
XLA Modules:
  0.0 432.0 jit_solution(17936240458052445127)
XLA Ops:
  0.6 0.0 copy-start
  0.7 0.0 copy-start.18
  0.7 0.0 copy-start.19
  0.7 0.0 copy-start.15
  0.7 0.0 copy-start.9
  0.7 0.0 copy-start.3
  0.7 1.3 copy-done
  2.0 0.7 collective-permute-start
  2.9 0.1 stack.53
  3.0 0.1 stack.62
  3.1 0.8 constant_dynamic-slice_fusion
  3.9 0.1 copy.25
  4.0 0.1 copy.26
  4.0 0.6 gather_fusion
  4.6 0.1 broadcast_multiply_fusion.1
  4.7 0.6 slice.39
  7.2 0.2 convert_reduce_fusion
  7.4 0.1 mul.86
  7.5 0.1 add_compare_fusion
  7.6 0.1 broadcast_in_dim.74
  7.6 0.1 mul.87
  7.8 0.1 fusion.6
  7.9 0.1 le.36
  8.0 0.1 pad_maximum_fusion.5.bias_c
  8.1 0.0 copy-start.4
  8.1 0.1 compare_select_fusion
  8.2 0.1 pad_maximum_fusion.1.bias_p
  8.4 0.0 copy-start.2
  8.4 0.7 bitcast_convert_fusion
  9.1 0.1 broadcast_multiply_fusion
  9.2 0.3 sine_multiply_fusion
  9.5 0.1 pad_maximum_fusion.3
  9.6 0.0 copy-start.5
  9.6 0.0 copy-start.6
  9.7 1.3 constant_dynamic-slice_fusion.2
  11.0 0.0 copy-done.18
  11.0 0.0 copy-done.19
  11.0 0.0 copy-done.15
  11.0 0.9 pad_maximum_fusion.qkv_in
  11.9 0.7 iota_reduce_fusion
  12.6 0.0 collective-permute-done.dn_in
  12.6 0.0 copy-done.9
  12.6 0.0 copy-done.3
  12.6 139.0 %front.1 = (f32[16,16,128]{2,1,0:T(8,128)S(1)}, bf16[2048,2560]{1,0:T(8,128)(2,1)}, bf16[8,2,128,2048]{3,2,1,0:T(8,128)(2,1)}, bf16[2048,1536]{1,0:T(8,128)(2,1)...) custom-call(bf16[128,2048]{1,0:T(8,128)(2,1)S(1)} %bitcast.43, ...), custom_call_target="tpu_custom_call" | custom-call | tf_op jit(solution)/shard_map/front/pallas_call | solution.py:672
  151.6 0.0 copy-start.7
  151.6 0.8 copy-done.7
  152.4 0.8 copy-done.10
  153.2 110.9 %feed_forward.1 = (f32[128,2048]{1,0:T(8,128)}, bf16[8,128,2048]{2,1,0:T(8,128)(2,1)}, bf16[128,1536]{1,0:T(8,128)(2,1)}, bf16[352,256]{1,0:T(8,128)(2,1)}) custom-call(bf16[128,2048]{1,0:T(8,128)(2,1)} %copy-done.10, bf16[2048,1536]{1,0:T(8,128)(2,1)} %get-tuple-element.40.gu_in, bf16[704,2048]{1,0:T(8,128)(2,1)} %get-tuple-element.41.dn_in, ...), custom_call_target="tpu_custom_call" | custom-call | tf_op jit(solution)/shard_map/feed_forward/pallas_call | solution.py:420
  264.1 0.0 copy-done.8
  264.1 0.0 copy-done.11
  264.1 0.0 copy-done.12
  264.1 142.1 %back.1 = (bf16[128,2048]{1,0:T(8,128)(2,1)}, bf16[128,2048]{1,0:T(8,128)(2,1)}, bf16[128,2048]{1,0:T(8,128)(2,1)}, bf16[128,512]{1,0:T(8,128)(2,1)}, bf16[128,2...) custom-call(f32[128,2048]{1,0:T(8,128)} %get-tuple-element.43.da2, ...), custom_call_target="tpu_custom_call" | custom-call | tf_op jit(solution)/shard_map/back/pallas_call | solution.py:1111
  406.2 1.3 slice_bitcast_fusion
  407.6 1.6 slice_convert_fusion
  409.1 2.1 convert_element_type.50
  411.3 2.3 convert_element_type.53
  413.5 1.9 convert_element_type.60
  415.5 2.3 convert_bitcast_fusion
  417.8 3.5 copy.28
  421.2 3.4 copy.30
  424.6 2.3 copy.27
  426.9 3.5 copy.29
  430.4 0.8 copy.33
  431.2 0.8 copy.34
  (33 shorter events, 0.2 us)
Async XLA Ops:
  0.6 1.4 copy-start
  0.7 10.3 %copy-start.18 = (bf16[128,256]{1,0:T(8,128)(2,1)S(1)}, bf16[128,256]{1,0:T(8,128)(2,1)}, u32[]{:S(2)}) copy-start(bf16[128,256]{1,0:T(8,128)(2,1)} %param.17) | copy-start | bytes 196612
  0.7 10.3 %copy-start.19 = (bf16[128,256]{1,0:T(8,128)(2,1)S(1)}, bf16[128,256]{1,0:T(8,128)(2,1)}, u32[]{:S(2)}) copy-start(bf16[128,256]{1,0:T(8,128)(2,1)} %param.16) | copy-start | bytes 196612
  0.7 10.3 %copy-start.15 = (bf16[128,2048]{1,0:T(8,128)(2,1)S(1)}, bf16[128,2048]{1,0:T(8,128)(2,1)}, u32[]{:S(2)}) copy-start(bf16[128,2048]{1,0:T(8,128)(2,1)} %param.15) | copy-start | bytes 1572868
  0.7 11.9 %copy-start.9 = (bf16[128,2048]{1,0:T(8,128)(2,1)S(1)}, bf16[128,2048]{1,0:T(8,128)(2,1)}, u32[]{:S(2)}) copy-start(bf16[128,2048]{1,0:T(8,128)(2,1)} %wo_in.1) | copy-start | bytes 1572868
  0.7 11.9 %copy-start.3 = (bf16[1,128,2048]{2,1,0:T(8,128)(2,1)S(1)}, bf16[1,128,2048]{2,1,0:T(8,128)(2,1)}, u32[]{:S(2)}) copy-start(bf16[1,128,2048]{2,1,0:T(8,128)(2,1)} %param.12) | copy-start | bytes 1572868
  2.0 10.5 %collective-permute-start = (bf16[352,256]{1,0:T(8,128)(2,1)S(1)}, bf16[352,256]{1,0:T(8,128)(2,1)S(1)}, u32[]{:S(2)}, u32[]{:S(2)}) collective-permute-start(bf16[352,256]{1,0:T(8,128)(2,1)S(1)} %constant_dynamic-slice_fusion.1), channel_id=1, source_target_pairs={{0,0},{1,1},{2,16},{3,17},{4,32},{5,33},{6,48},{7,49},{8,64},{9,65... | collective-permute-start | bytes 540680 | tf_op jit(solution)/shard_map/ppermute | solution.py:1185
  8.1 143.5 %copy-start.4 = (f32[128,128]{1,0:T(8,128)}, f32[128,128]{1,0:T(8,128)S(1)}, u32[]{:S(2)}) copy-start(f32[128,128]{1,0:T(8,128)S(1)} %pad_maximum_fusion.5.bias_c) | copy-start | bytes 196612
  8.4 143.2 %copy-start.2 = (f32[512,128]{1,0:T(8,128)}, f32[512,128]{1,0:T(8,128)S(1)}, u32[]{:S(2)}) copy-start(f32[512,128]{1,0:T(8,128)S(1)} %pad_maximum_fusion.1.bias_p) | copy-start | bytes 786436
  9.6 141.9 %copy-start.5 = (f32[128,128]{1,0:T(8,128)}, f32[128,128]{1,0:T(8,128)S(1)}, u32[]{:S(2)}) copy-start(f32[128,128]{1,0:T(8,128)S(1)} %get-tuple-element.93.cosine) | copy-start | bytes 196612
  9.6 141.9 %copy-start.6 = (f32[128,128]{1,0:T(8,128)}, f32[128,128]{1,0:T(8,128)S(1)}, u32[]{:S(2)}) copy-start(f32[128,128]{1,0:T(8,128)S(1)} %get-tuple-element.94.sine) | copy-start | bytes 196612
  151.6 0.8 copy-start.7
  152.4 0.8 copy-start.10
  153.2 110.9 %copy-start.8 = (bf16[128,2048]{1,0:T(8,128)(2,1)}, bf16[128,2048]{1,0:T(8,128)(2,1)S(1)}, u32[]{:S(2)}) copy-start(bf16[128,2048]{1,0:T(8,128)(2,1)S(1)} %get-tuple-element.53.att_in) | copy-start | bytes 1572868
  153.2 110.9 %copy-start.11 = (f32[16,16,128]{2,1,0:T(8,128)}, f32[16,16,128]{2,1,0:T(8,128)S(1)}, u32[]{:S(2)}) copy-start(f32[16,16,128]{2,1,0:T(8,128)S(1)} %get-tuple-element.45.gains) | copy-start | bytes 393220
  153.2 110.9 %copy-start.12 = (f32[8,1,512]{2,1,0:T(1,128)}, f32[8,1,512]{2,1,0:T(1,128)S(1)}, u32[]{:S(2)}) copy-start(f32[8,1,512]{2,1,0:T(1,128)S(1)} %get-tuple-element.51.lse) | copy-start | bytes 49156
  406.2 7.3 %copy-start.14 = (bf16[352,2048]{1,0:T(8,128)(2,1)S(1)}, bf16[352,2048]{1,0:T(8,128)(2,1)}, u32[]{:S(2)}) copy-start(bf16[352,2048]{1,0:T(8,128)(2,1)} %get-tuple-element.64) | copy-start | bytes 4325380
  411.3 4.2 copy-start.13
  426.9 5.1 %copy-start.1 = (bf16[352,2048]{1,0:T(8,128)(2,1)S(1)}, bf16[352,2048]{1,0:T(8,128)(2,1)}, u32[]{:S(2)}) copy-start(bf16[352,2048]{1,0:T(8,128)(2,1)} %param.22) | copy-start | bytes 4325380
  426.9 3.5 copy-start.17
  426.9 4.3 %copy-start.16 = (bf16[128,2048]{1,0:T(8,128)(2,1)S(1)}, bf16[128,2048]{1,0:T(8,128)(2,1)}, u32[]{:S(2)}) copy-start(bf16[128,2048]{1,0:T(8,128)(2,1)} %get-tuple-element.58) | copy-start | bytes 1572868

commit v4 on v3

--- a/solution.py
+++ b/solution.py
@@ -54,11 +54,50 @@
         return {"ctx": self.c, "fsdp": self.f + 1 - 2 * self.co}
 
 
+def chip_of(me, t):
+    dr = jnp.where(t < 2, 0, jnp.where(t >= 6, 2, 1 + 2 * lax.rem(t, 2)))
+    dp = jnp.where(t < 2, t, jnp.where(t >= 6, t - 6, lax.div(t, 4)))
+    return lax.rem(me.x + dr, 4) * 2 + lax.rem(me.zh + dp, 2)
+
+
 def greet(devices):
     barrier = pltpu.get_barrier_semaphore()
     for device in devices:
         pl.semaphore_signal(barrier, 1, device_id=device, device_id_type=MESH)
     pl.semaphore_wait(barrier, len(devices))
+
+
+class Swap:
+    def __init__(self, me, src, dst, sems, local):
+        self.moved = me.c != me.j
+        self.to = {"ctx": me.j, "fsdp": 2 * me.c + me.co}
+        self.copy = pltpu.make_async_remote_copy(
+            src, dst, sems[0], sems[1], device_id=self.to, device_id_type=MESH
+        )
+        self.keep = pltpu.make_async_copy(src, dst, local)
+
+    def start(self):
+        pl.when(self.moved)(self.copy.start)
+        pl.when(jnp.logical_not(self.moved))(self.keep.start)
+
+    def wait(self):
+        pl.when(self.moved)(self.copy.wait)
+        pl.when(jnp.logical_not(self.moved))(self.keep.wait)
+
+
+def greet_all(me):
+    barrier = pltpu.get_barrier_semaphore()
+    others = near(me.across_x) + near(me.across_y) + [me.sibling()]
+    for device in others:
+        pl.semaphore_signal(barrier, 1, device_id=device, device_id_type=MESH)
+    moved = me.c != me.j
+
+    @pl.when(moved)
+    def _():
+        to = {"ctx": me.j, "fsdp": 2 * me.c + me.co}
+        pl.semaphore_signal(barrier, 1, device_id=to, device_id_type=MESH)
+
+    pl.semaphore_wait(barrier, len(others) + jnp.where(moved, 1, 0))
 
 
 def near(dev):
@@ -249,11 +288,11 @@
 
 def mlp_kernel(
     a2, gu_in, dn_in, dy_in,
-    da2_out, mpart, gu_out, dn_out,
+    da2_out, mpart, gu_out, gdown,
     acts, gu, wd, dy, hid, dgu, dpart,
     d_half, d_full, d_pair,
-    gsib, grecv, gown, gd, gdrecv, gdown,
-    g_half, g_full, g_pair, n_half, n_full, n_pair,
+    gsib, grecv, gown, gd, gdrecv,
+    g_half, g_full, g_pair,
     ag0, ag1, rs0, rs1, sib0, sib1, local,
 ):
     me = Place()
@@ -317,80 +356,69 @@
         group(g)
 
     grad = Scatter(me.across_y, lambda slot: dpart.at[slot], 128, d_half, d_full, d_pair, (rs0, rs1), 0)
+    first = Scatter(me.across_x, lambda slot: gown.at[slot], 128, g_half, g_full, g_pair, (rs0, rs1), 1)
     grad.start()
 
-    def chip_of(t):
-        dr = jnp.where(t < 2, 0, jnp.where(t >= 6, 2, 1 + 2 * lax.rem(t, 2)))
-        dp = jnp.where(t < 2, t, jnp.where(t >= 6, t - 6, lax.div(t, 4)))
-        return lax.rem(me.x + dr, 4) * 2 + lax.rem(me.zh + dp, 2)
-
-    def weight_terms(t, core, out):
-        first = pl.multiple_of((chip_of(t) * 2 + core) * 128, 128)
-        left = acts[:, :, pl.ds(first, 128)].reshape(1024, 128)
-        out[t] = dot_rows(left, dgu[...]).astype(BF)
-
-    down_to = [
-        send(gd.at[t, pl.ds(pl.multiple_of((1 - me.co) * 352, 16), 352)], gdrecv.at[t], (sib0, sib1), t, me.sibling())
-        for t in range(8)
-    ]
-    gu_to = [send(gsib.at[t], grecv.at[t], (sib0, sib1), 8 + t, me.sibling()) for t in range(8)]
+    def weight_terms(t, core):
+        at = pl.multiple_of((chip_of(me, t) * 2 + core) * 128, 128)
+        left = acts[:, :, pl.ds(at, 128)].reshape(1024, 128)
+        return dot_rows(left, dgu[...])
+
+    def gu_to(t):
+        return send(gsib.at[t], grecv.at[t], (sib0, sib1), 8 + t, me.sibling())
+
+    @pl.loop(0, 8)
+    def _(i):
+        gsib[7 - i] = weight_terms(7 - i, 1 - me.co).astype(BF)
+        gu_to(7 - i).start()
+
+    grad.turn(1)
+
+    @pl.loop(0, 8)
+    def _(i):
+        gu_to(7 - i).wait_recv()
+        gown[7 - i] = (weight_terms(7 - i, me.co) + grecv[7 - i].astype(F32)).astype(BF)
+
+        @pl.when(i == 1)
+        def _():
+            first.start()
+
+    grad.turn(0)
+    first.turn(1)
+
+    def down_to(t):
+        mine = pl.ds(pl.multiple_of((1 - me.co) * 352, 16), 352)
+        return send(gd.at[t, mine], gdrecv.at[t], (sib0, sib1), t, me.sibling())
 
     @pl.loop(0, 8)
     def _(t):
-        first = pl.multiple_of(chip_of(t) * 256, 256)
-        gd[t] = dot_rows(hid[...], dy[:, :, pl.ds(first, 256)].reshape(1024, 256)).astype(BF)
-
-    for copy in down_to:
-        copy.start()
+        at = pl.multiple_of(chip_of(me, t) * 256, 256)
+        gd[t] = dot_rows(hid[...], dy[:, :, pl.ds(at, 256)].reshape(1024, 256)).astype(BF)
+        down_to(t).start()
+
+    first.turn(0)
+    grad.pair()
+    first.pair()
 
     @pl.loop(0, 8)
     def _(t):
-        weight_terms(t, 1 - me.co, gsib)
-
-    for copy in gu_to:
-        copy.start()
-    grad.turn(1)
-    grad.turn(0)
+        down_to(t).wait_recv()
+
+        @pl.loop(0, 22)
+        def _(i):
+            mine = gd[t, pl.ds(pl.multiple_of(me.co * 352 + i * 16, 16), 16)].astype(F32)
+            at = pl.ds(pl.multiple_of(i * 16, 16), 16)
+            gdown[t, at] = (mine + gdrecv[t, at].astype(F32)).astype(BF)
+
+    first.finish(gu_out)
+    grad.finish(da2_out)
+    for job in (task, grad, first):
+        job.end()
 
     @pl.loop(0, 8)
     def _(t):
-        weight_terms(t, me.co, gown)
-
-    for copy in down_to:
-        copy.wait_recv()
-
-    @pl.loop(0, 8 * 22)
-    def _(i):
-        t, row = lax.div(i, 22), lax.rem(i, 22) * 16
-        mine = gd[t, pl.ds(pl.multiple_of(me.co * 352 + row, 16), 16)].astype(F32)
-        at = pl.ds(pl.multiple_of(row, 16), 16)
-        gdown[t, at] = (mine + gdrecv[t, at].astype(F32)).astype(BF)
-
-    for copy in gu_to:
-        copy.wait_recv()
-
-    @pl.loop(0, 8 * 8)
-    def _(i):
-        t, at = lax.div(i, 8), pl.ds(pl.multiple_of(lax.rem(i, 8) * 16, 16), 16)
-        gown[t, at] = (gown[t, at].astype(F32) + grecv[t, at].astype(F32)).astype(BF)
-
-    first = Scatter(me.across_x, lambda slot: gown.at[slot], 128, g_half, g_full, g_pair, (rs0, rs1), 1)
-    second = Scatter(me.across_x, lambda slot: gdown.at[slot], 352, n_half, n_full, n_pair, (rs0, rs1), 2)
-    first.start()
-    second.start()
-    grad.pair()
-    for dp in (1, 0):
-        first.turn(dp)
-        second.turn(dp)
-    grad.finish(da2_out)
-    first.pair()
-    second.pair()
-    first.finish(gu_out)
-    second.finish(dn_out)
-    for job in (task, grad, first, second):
-        job.end()
-    for copy in (*down_to, *gu_to):
-        copy.wait_send()
+        gu_to(t).wait_send()
+        down_to(t).wait_send()
 
 
 def feed_forward(a2, gu, dn, dy):
@@ -408,11 +436,9 @@
         pltpu.VMEM((8, 128, 1536), BF),
         pltpu.VMEM((8, 768, 256), BF),
         pltpu.VMEM((8, 352, 256), BF),
-        pltpu.VMEM((8, 352, 256), BF),
         *scatter_buffers(128, 1536),
-        *scatter_buffers(352, 256),
         *dma_sems(1, 9),
-        *dma_sems(3, 9),
+        *dma_sems(2, 9),
         pltpu.SemaphoreType.DMA((16,)),
         pltpu.SemaphoreType.DMA((16,)),
         pltpu.SemaphoreType.DMA((3,)),
@@ -423,7 +449,7 @@
             jax.ShapeDtypeStruct((128, 2048), F32),
             jax.ShapeDtypeStruct((8, 128, 2048), BF),
             jax.ShapeDtypeStruct((128, 1536), BF),
-            jax.ShapeDtypeStruct((352, 256), BF),
+            jax.ShapeDtypeStruct((8, 352, 256), BF),
         ),
         in_specs=[VMEM, ANY, ANY, ANY],
         out_specs=[VMEM] * 4,
@@ -466,11 +492,13 @@
 def front_kernel(
     x, gains_in, qkv_in, wo_in, gu_in, dn_in, dy_in, cosine, sine, bias_p, bias_c, partner,
     gains, qkv_out, wo_out, gu_all, dn_all, dy_all, a1, qst, kst, vst, att, lse, h1, a2,
-    qkv, wo, kv_own, kv, sT, pT, scale,
-    s0, s1, t0, t1, y0, y1, u0, u1, local,
+    qkv, wo, kv_own, kv, sT, pT, scale, dnp,
+    s0, s1, t0, t1, y0, y1, u0, u1, w0, w1, local,
 ):
     me = Place()
-    greet(near(me.across_x) + near(me.across_y) + [me.sibling()])
+    greet_all(me)
+    swap = Swap(me, dn_in.at[:, pl.ds(pl.multiple_of(me.c * 256, 256), 256)], dnp, (w0, w1), local.at[8])
+    swap.start()
 
     def rows_at(ref, rows):
         def loc(dr, dp, er, ep, half):
@@ -515,23 +543,30 @@
     q = over_x(qkv_in, rows_at(qkv, 128), 1)
     o = over_x(wo_own, wo_x_at, 2, both=False)
     m = over_x(gu_in, rows_at(gu_all, 128), 3)
-    d = over_x(dn_in, dn_at, 4)
+    d = over_x(dnp, dn_at, 4)
     dy = Gather(me.across_y, dy_in, slot_at(dy_all, 128), (y0, y1), 0)
     oy = Gather(me.across_y, wo_y_at(0, 0, 0, 0, None), wo_y_at, (y0, y1), 1, me.sibling(), (u0, u1))
     kv_task = Gather(me.across_y, kv_own, slot_at(kv, 128), (y0, y1), 2)
-    kept = [load(task.own, task.loc(0, 0, 0, 0, None), local.at[i]) for i, task in enumerate((g, q, o, m, d, dy))]
+    kept = [load(task.own, task.loc(0, 0, 0, 0, None), local.at[i]) for i, task in enumerate((g, q, o, m, dy))]
 
     g.start()
+    o.start()
     q.start()
-    o.start()
+    dy.start()
     norm_scale(x, scale)
-    g.pair()
-    o.pair()
+    swap.wait()
+    kept.append(load(dnp, d.loc(0, 0, 0, 0, None), local.at[5]))
+    for task in (g, o):
+        task.pair()
+        task.turn(0)
+    dy.pair()
+    dy.turn(0)
     q.pair()
-    for task in (g, o, q):
-        task.turn(0)
-    for task in (g, o, q):
-        task.turn(1)
+    g.turn(1)
+    o.turn(1)
+    q.turn(0)
+    dy.turn(1)
+    q.turn(1)
     m.start()
     d.start()
     for task in (g, o):
@@ -539,6 +574,8 @@
         task.last(1)
     kept[2].wait()
     oy.start()
+    dy.last(0)
+    dy.last(1)
     kept[0].wait()
     g.end()
 
@@ -549,6 +586,8 @@
 
     q.last(0)
     q.last(1)
+    m.pair()
+    d.pair()
     oy.pair()
     kept[1].wait()
     q.end()
@@ -571,19 +610,15 @@
     kv_own[:, 256:] = raw[:, 256:].astype(BF)
     kv_task.start()
     kv[0] = kv_own[...]
-    m.pair()
-    d.pair()
+    m.turn(0)
     kv_task.pair()
     kv_task.turn(0)
+    d.turn(0)
     kv_task.turn(1)
-    m.turn(0)
-    d.turn(0)
     oy.turn(0)
     kv_task.last(0)
     kv_task.last(1)
     kv_task.end()
-    dy.start()
-    oy.turn(1)
 
     mate = partner[0]
     beside = kv[mate]
@@ -630,20 +665,15 @@
 
         @pl.when(n == 0)
         def _():
+            oy.turn(1)
             m.turn(1)
-            d.turn(1)
-            dy.pair()
 
         @pl.when(n == 1)
         def _():
-            oy.last(0)
-            dy.turn(0)
-
-        @pl.when(n == 2)
-        def _():
-            oy.last(1)
-            dy.turn(1)
-
+            d.turn(1)
+
+    oy.last(0)
+    oy.last(1)
     o.end()
     oy.end()
     saved.append(load(wo, wo_out, local.at[7]))
@@ -660,9 +690,10 @@
         at = pl.ds(pl.multiple_of(i * 128, 128), 128)
         a2[:, at] = (h1[:, at] * scale[...] * gains[i, pl.ds(8, 1), :]).astype(BF)
 
-    for task in (m, d, dy):
+    for task in (m, d):
         task.last(0)
         task.last(1)
+    for task in (m, d, dy):
         task.end()
     for copy in (*kept[3:], *saved):
         copy.wait()
@@ -697,11 +728,14 @@
             pltpu.VMEM((640, 512), F32),
             pltpu.VMEM((640, 512), BF),
             pltpu.VMEM((128, 1), F32),
+            pltpu.VMEM((352, 256), BF),
             *dma_sems(5, 9),
             *dma_sems(5, 10),
             *dma_sems(3, 9),
             *dma_sems(2, 10),
-            pltpu.SemaphoreType.DMA((8,)),
+            pltpu.SemaphoreType.DMA,
+            pltpu.SemaphoreType.DMA,
+            pltpu.SemaphoreType.DMA((9,)),
         ],
         compiler_params=params(1, 50),
         name="front",
@@ -710,41 +744,19 @@
 
 def back_kernel(
     da2, h1, dy, x, gains, wo_in, qkv_in, qst, kst, vst, lse, cosine, sine, bias_p, bias_c, partner,
-    a1_in, att_in, mpart_in, gu, dn,
+    a1_in, att_in, mpart_in, gu, gdown_in,
     mixed, tokens_grad, q_out, kv_out, o_out, gains_out, gu_all, dn_all,
     a1s, atts, dqkvs, datts, grow, dh1, gown, gsib, mpart, stream, dost, sT, dT, pT, dsT,
-    kgrad, vgrad, kvp, dkv, da1, dnp,
+    kgrad, vgrad, kvp, dkv, da1, gdown, dn_sum, dnp,
     qp, op, kp, gp, ggot, q_sum, o_sum, kv_sum, g_sum,
     q_half, q_full, q_pair, o_half, o_full, o_pair, k_half, k_full, k_pair, e_half, e_full, e_pair,
-    m_half, m_full, m_pair, d_half, d_full, d_pair,
+    m_half, m_full, m_pair, d_half, d_full, d_pair, n_half, n_full, n_pair,
     or_half, or_full, or_pair, qr_half, qr_full, qr_pair, kr_half, kr_full, kr_pair,
     sib0, sib1, x0, x1, y0, y1, ag0, ag1, swap0, swap1, local,
 ):
     me = Place()
-    moved = me.c != me.j
-    swapped = {"ctx": me.j, "fsdp": 2 * me.c + me.co}
-    barrier = pltpu.get_barrier_semaphore()
-    others = near(me.across_x) + near(me.across_y) + [me.sibling()]
-    for device in others:
-        pl.semaphore_signal(barrier, 1, device_id=device, device_id_type=MESH)
-
-    @pl.when(moved)
-    def _():
-        pl.semaphore_signal(barrier, 1, device_id=swapped, device_id_type=MESH)
-
-    pl.semaphore_wait(barrier, len(others) + jnp.where(moved, 1, 0))
-
-    dn_move = pltpu.make_async_remote_copy(dn, dnp, swap0, swap1, device_id=swapped, device_id_type=MESH)
-    dn_keep = pltpu.make_async_copy(dn, dnp, local.at[0])
-
-    @pl.when(moved)
-    def _():
-        dn_move.start()
-
-    @pl.when(jnp.logical_not(moved))
-    def _():
-        dn_keep.start()
-
+    greet_all(me)
+    nload = load(gdown_in, gdown, local.at[0])
     own, other = pl.ds(0, 128), pl.ds(128, 128)
     mload = load(mpart_in, mpart, local.at[1])
     a1load = load(a1_in, a1s.at[own], local.at[2])
@@ -766,6 +778,8 @@
     q_job = Scatter(me.across_x, lambda slot: qp.at[slot], 128, q_half, q_full, q_pair, over_x, 1)
     k_job = Scatter(me.across_x, lambda slot: kp.at[slot], 128, k_half, k_full, k_pair, over_x, 2)
     e_job = Scatter(me.across_x, lambda slot: gp.at[slot], 16, e_half, e_full, e_pair, over_x, 3)
+    n_job = Scatter(me.across_x, lambda slot: gdown.at[slot], 352, n_half, n_full, n_pair, over_x, 4)
+    dn_swap = Swap(me, dn_sum, dnp, (swap0, swap1), local.at[8])
     m_job = Scatter(me.across_y, lambda slot: mpart.at[slot], 128, m_half, m_full, m_pair, over_y, 0)
     d_job = Scatter(me.across_y, lambda slot: kvp.at[slot], 128, d_half, d_full, d_pair, over_y, 1)
 
@@ -821,6 +835,8 @@
     att_swap.start()
     a1load.wait()
     a1_swap.start()
+    nload.wait()
+    n_job.start()
     mload.wait()
     m_job.start()
 
@@ -844,6 +860,8 @@
         datts[at] = total.astype(BF)
 
     datt_swap.start()
+    n_job.turn(1)
+    n_job.turn(0)
     for n in range(4):
         wo_load(n).wait()
         part = dot_back(datts[own], stream[n % 2, :, 0:2048]).astype(BF)
@@ -854,24 +872,22 @@
     qkv_load(0).start()
     qkv_load(1).start()
 
-    def chip_of(t):
-        dr = jnp.where(t < 2, 0, jnp.where(t >= 6, 2, 1 + 2 * lax.rem(t, 2)))
-        dp = jnp.where(t < 2, t, jnp.where(t >= 6, t - 6, lax.div(t, 4)))
-        return lax.rem(me.x + dr, 4) * 2 + lax.rem(me.zh + dp, 2)
-
-    def terms(left, right, out):
+    def terms(left, right, out, job):
         @pl.loop(0, 8)
         def _(i):
-            t = 7 - i
-            first = pl.multiple_of((chip_of(t) * 2 + me.co) * 128, 128)
-            out[t] = dot_rows(left[:, pl.ds(first, 128)], right).astype(BF)
-
+            at = pl.multiple_of((chip_of(me, 7 - i) * 2 + me.co) * 128, 128)
+            out[7 - i] = dot_rows(left[:, pl.ds(at, 128)], right[...]).astype(BF)
+
+            @pl.when(i == 1)
+            def _():
+                job.start()
+
+    m_job.turn(1)
     att_swap.wait_recv()
     datt_swap.wait_recv()
-    terms(atts, datts[...], op)
-    o_job.start()
-    m_job.turn(1)
+    terms(atts, datts, op, o_job)
     m_job.turn(0)
+    n_job.pair()
 
     def attend(n, half):
         count = 512 if half == 0 else 640
@@ -912,18 +928,15 @@
 
         @pl.when(n == 0)
         def _():
-            o_job.turn(1)
-            o_job.turn(0)
+            n_job.finish(dn_sum)
+            dn_swap.start()
 
         @pl.when(n == 1)
         def _():
-            m_job.pair()
-
-        @pl.when(n == 2)
-        def _():
-            o_job.pair()
+            o_job.turn(1)
 
     dq_swap.start()
+    o_job.turn(0)
     mate = partner[0]
     for out, base in ((kgrad, 0), (vgrad, 256)):
         for n in range(4):
@@ -936,14 +949,19 @@
                     late = jnp.where(mate == slot, out[n, 512:576, :], jnp.zeros((64, 64), BF))
                 kvp[slot, 64:128, first : first + 64] = late
     d_job.start()
+    m_job.pair()
     a1_swap.wait_recv()
     dq_swap.wait_recv()
-    terms(a1s, dqkvs[:, 0:2048], qp)
-    q_job.start()
+    terms(a1s, dqkvs.at[:, pl.ds(0, 2048)], qp, q_job)
+    m_job.finish(mixed, (h1,))
+    o_job.pair()
     d_job.turn(1)
     d_job.turn(0)
-    m_job.finish(mixed, (h1,))
-    o_job.finish(o_sum)
+    kept = [load(gu, gu_all.at[me.c], local.at[6])]
+    gu_task.start()
+    dn_swap.wait()
+    dn_task.start()
+    kept.append(load(dnp, dn_at(0, 0, 0, 0, None), local.at[7]))
     d_job.pair()
     d_job.finish(dkv)
     for i in range(2):
@@ -952,31 +970,17 @@
         dqkvs[own, 2048 + 128 * i : 2176 + 128 * i] = (block * cosine[...] - turned(block) * sine[...]).astype(BF)
     dqkvs[own, 2304:2560] = dkv[:, 256:512].astype(BF)
     dkv_swap.start()
+    o_job.finish(o_sum)
     o_sums.start()
-    kept = [load(gu, gu_all.at[me.c], local.at[6])]
-    gu_task.start()
-
-    @pl.when(moved)
-    def _():
-        dn_move.wait()
-
-    @pl.when(jnp.logical_not(moved))
-    def _():
-        dn_keep.wait()
-
-    dn_task.start()
-    kept.append(load(dnp, dn_at(0, 0, 0, 0, None), local.at[7]))
-    dkv_swap.wait_recv()
-    terms(a1s, dqkvs[:, 2048:2560], kp)
-    k_job.start()
-    q_job.turn(1)
-    q_job.turn(0)
 
     for n in range(4):
         qkv_load(n).wait()
         da1[:, 512 * n : 512 * n + 512] = dot_back(dqkvs[own], stream[n % 2])
         if n < 2:
             qkv_load(n + 2).start()
+    q_job.turn(1)
+    dkv_swap.wait_recv()
+    terms(a1s, dqkvs.at[:, pl.ds(2048, 512)], kp, k_job)
 
     @pl.loop(0, 8)
     def _(i):
@@ -992,54 +996,59 @@
         gown[i, 0:1, :] = grow[2, :, 128 * i : 128 * i + 128]
         gown[i, 8:9, :] = grow[3, :, 128 * i : 128 * i + 128]
     gain_swap.start()
-    o_sums.turn(1)
-    o_sums.turn(0)
+    gu_task.pair()
+    dn_task.pair()
+    q_job.turn(0)
+    gu_task.turn(0)
+    dn_task.turn(0)
     gain_swap.wait_recv()
     for slot in range(8):
         block = me.fsdp_at(STEPS[slot], PAIRS[slot])
         gp[slot] = gown[block] + gsib[block]
     e_job.start()
-    gu_task.pair()
-    dn_task.pair()
+    o_sums.turn(1)
+    o_sums.turn(0)
+    gu_task.turn(1)
+    dn_task.turn(1)
     o_sums.pair()
     o_sums.finish(o_out.at[own_rows])
     o_spread.start()
-    gu_task.turn(0)
-    dn_task.turn(0)
+    q_job.pair()
     k_job.turn(1)
     k_job.turn(0)
-    q_job.pair()
     e_job.turn(1)
     e_job.turn(0)
-    gu_task.turn(1)
-    dn_task.turn(1)
     o_spread.pair()
     o_spread.turn(0)
     o_spread.turn(1)
+    q_job.finish(q_sum)
+    q_sums.start()
     k_job.pair()
     e_job.pair()
-    q_job.finish(q_sum)
-    q_sums.start()
+    q_sums.turn(1)
+    q_sums.turn(0)
     k_job.finish(kv_sum)
     kv_sums.start()
     e_job.finish(g_sum)
     e_task.start()
     ggot[me.c] = g_sum[...]
-    for job in (q_sums, kv_sums):
-        job.turn(1)
-        job.turn(0)
+    q_sums.pair()
+    kv_sums.turn(1)
+    kv_sums.turn(0)
     e_task.pair()
     e_task.turn(0)
+    q_sums.finish(q_out.at[own_rows])
+    q_spread.start()
     e_task.turn(1)
-    for job, out, task in ((q_sums, q_out, q_spread), (kv_sums, kv_out, kv_spread)):
-        job.pair()
-        job.finish(out.at[own_rows])
-        task.start()
-    for task in (q_spread, kv_spread):
-        task.pair()
-    for task in (q_spread, kv_spread):
-        task.turn(0)
-        task.turn(1)
+    kv_sums.pair()
+    q_spread.pair()
+    q_spread.turn(0)
+    kv_sums.finish(kv_out.at[own_rows])
+    kv_spread.start()
+    q_spread.turn(1)
+    kv_spread.pair()
+    kv_spread.turn(0)
+    kv_spread.turn(1)
     e_task.last(0)
     e_task.last(1)
     total = ggot[0]
@@ -1049,7 +1058,7 @@
     for task in (gu_task, dn_task, o_spread, q_spread, kv_spread):
         task.last(0)
         task.last(1)
-    jobs = (o_job, q_job, k_job, e_job, m_job, d_job, o_sums, q_sums, kv_sums)
+    jobs = (o_job, q_job, k_job, e_job, m_job, d_job, n_job, o_sums, q_sums, kv_sums)
     for job in (*jobs, gu_task, dn_task, e_task, o_spread, q_spread, kv_spread):
         job.end()
     for copy in (att_swap, datt_swap, a1_swap, dq_swap, dkv_swap, gain_swap):
@@ -1058,7 +1067,7 @@
         copy.wait()
 
 
-def back(da2, h1, dy, x, gains, wo, qkv, qst, kst, vst, lse, cosine, sine, bias_p, bias_c, partner, a1, att, mpart, gu, dn):
+def back(da2, h1, dy, x, gains, wo, qkv, qst, kst, vst, lse, cosine, sine, bias_p, bias_c, partner, a1, att, mpart, gu, gdown):
     scratch = [
         pltpu.VMEM((256, 2048), BF),
         pltpu.VMEM((256, 2048), BF),
@@ -1080,6 +1089,8 @@
         pltpu.VMEM((8, 128, 512), BF),
         pltpu.VMEM((128, 512), F32),
         pltpu.VMEM((128, 2048), F32),
+        pltpu.VMEM((8, 352, 256), BF),
+        pltpu.VMEM((352, 256), BF),
         pltpu.VMEM((352, 256), BF),
         pltpu.VMEM((8, 128, 2048), BF),
         pltpu.VMEM((8, 128, 2048), BF),
@@ -1096,17 +1107,18 @@
         *scatter_buffers(16, 128, F32),
         *scatter_buffers(128, 2048),
         *scatter_buffers(128, 512),
+        *scatter_buffers(352, 256),
         *scatter_buffers(16, 2048, cut=True),
         *scatter_buffers(16, 2048, cut=True),
         *scatter_buffers(16, 512, cut=True),
         pltpu.SemaphoreType.DMA((6,)),
         pltpu.SemaphoreType.DMA((6,)),
-        *dma_sems(4, 9),
+        *dma_sems(5, 9),
         *dma_sems(5, 9),
         *dma_sems(6, 9),
         pltpu.SemaphoreType.DMA,
         pltpu.SemaphoreType.DMA,
-        pltpu.SemaphoreType.DMA((8,)),
+        pltpu.SemaphoreType.DMA((9,)),
     ]
     return pl.pallas_call(
         back_kernel,
@@ -1125,7 +1137,31 @@
         scratch_shapes=scratch,
         compiler_params=params(5, 62),
         name="back",
-    )(da2, h1, dy, x, gains, wo, qkv, qst, kst, vst, lse, cosine, sine, bias_p, bias_c, partner, a1, att, mpart, gu, dn)
+    )(da2, h1, dy, x, gains, wo, qkv, qst, kst, vst, lse, cosine, sine, bias_p, bias_c, partner, a1, att, mpart, gu, gdown)
+
+
+def widen_kernel(parts, gate, up):
+    for out, base in ((gate, 0), (up, 768)):
+        for pair in range(4):
+            even = parts[2 * pair, :, base : base + 768].astype(F32)
+            odd = pltpu.roll(parts[2 * pair + 1, :, base : base + 768].astype(F32), 64, 1)
+            first = 1408 * pair
+            out[:, first : first + 640] = even[:, 0:640]
+            out[:, first + 640 : first + 768] = even[:, 640:768] + odd[:, 0:128]
+            out[:, first + 768 : first + 1408] = odd[:, 128:768]
+
+
+def widen(parts):
+    out = jax.ShapeDtypeStruct((128, 5632), F32)
+    block = pl.BlockSpec((16, 5632), lambda i: (i, 0))
+    return pl.pallas_call(
+        widen_kernel,
+        grid=(8,),
+        out_shape=(out, out),
+        in_specs=[pl.BlockSpec((8, 16, 1536), lambda i: (0, i, 0))],
+        out_specs=[block, block],
+        name="widen",
+    )(parts)
 
 
 def tables(position):
@@ -1145,14 +1181,6 @@
     segment = jnp.where(later, 1 + (moment - prompt_len) // cont_len, 0)
     position = jnp.where(later, prompt_len + (moment - prompt_len) % cont_len, moment)
     return (segment, position)
-
-
-def swap_pairs():
-    pairs = []
-    for c in range(8):
-        for f in range(16):
-            pairs.append((c * 16 + f, (f // 2) * 16 + 2 * c + f % 2))
-    return pairs
 
 
 def on_device(
@@ -1181,8 +1209,6 @@
     gains = jnp.concatenate([attn_gain.astype(F32)[None], none, mlp_gain.astype(F32)[None], none])
     qkv = jnp.concatenate([query_weight, key_weight, value_weight], axis=1)
     gu = jnp.concatenate([sliced(gate_weight), sliced(up_weight)], axis=1)
-    dn = lax.dynamic_slice_in_dim(down_weight, c * 256, 256, 1)
-    dn = lax.ppermute(dn, ("ctx", "fsdp"), swap_pairs())
 
     y, zl = c // 2, c % 2
     order = jnp.stack([((y + STEPS[s]) % 4) * 2 + (zl + PAIRS[s]) % 2 for s in range(8)])
@@ -1209,20 +1235,18 @@
     bias_c = jnp.concatenate([bias_c, bias_c], axis=1).astype(F32)
 
     gains_all, qkv_all, wo_all, gu_all, dn_all, dy_all, normed, qst, kst, vst, attended, lse, hidden_state, normed_two = front(
-        tokens[0], gains, qkv, output_weight, gu, dn, cotangent[0], cosine_two, sine_two, bias_p, bias_c, mate[None]
+        tokens[0], gains, qkv, output_weight, gu, down_weight, cotangent[0], cosine_two, sine_two, bias_p, bias_c, mate[None]
     )
     wo_all = wo_all.reshape(2048, 2048)
 
-    grad_normed_two, mixed_parts, gu_sum, dn_sum = feed_forward(normed_two, gu_all, dn_all, dy_all)
+    grad_normed_two, mixed_parts, gu_sum, dn_parts = feed_forward(normed_two, gu_all, dn_all, dy_all)
 
     mixed, tokens_grad, query_grad, kv_grad, o_grad, gain_grads, gu_grads, dn_grad = back(
         grad_normed_two, hidden_state, cotangent[0], tokens[0], gains_all, wo_all, qkv_all, qst, kst, vst, lse,
-        cosine_two, sine_two, bias_p, bias_c, mate[None], normed, attended, mixed_parts, gu_sum, dn_sum,
+        cosine_two, sine_two, bias_p, bias_c, mate[None], normed, attended, mixed_parts, gu_sum, dn_parts,
     )
 
-    def joined(parts):
-        return parts.transpose(1, 0, 2).reshape(parts.shape[1], -1).astype(F32)
-
+    gate_grad, up_grad = widen(gu_grads)
     return (
         mixed[None],
         tokens_grad[None],
@@ -1232,8 +1256,8 @@
         kv_grad[:, 256:].astype(F32),
         o_grad.astype(F32),
         gain_grads[8],
-        joined(gu_grads[:, :, :704]),
-        joined(gu_grads[:, :, 768:1472]),
+        gate_grad,
+        up_grad,
         dn_grad.astype(F32),
     )
 

time: 433 us -> 400 us (0.924)
  Pallas kernels: 392 us -> 376 us
  local copies, waits for them, and re-layouts: 22.4 us -> 9.82 us
    pallas_call x1, Pallas kernels: 139 us -> 122 us  [front(): pl.pallas_call(front_kernel, out_shape=(jax.ShapeDtypeStruct((16, 16, 128...]
    pallas_call x1, Pallas kernels: 111 us -> 94.9 us  [feed_forward(): pl.pallas_call(mlp_kernel, out_shape=(jax.ShapeDtypeStruct((128, 2048), F...]
    pallas_call x1, Pallas kernels: 142 us -> 152 us  [back(): pl.pallas_call(back_kernel, out_shape=(jax.ShapeDtypeStruct((128, 2048),...]
    pallas_call x0 -> x1, Pallas kernels: none -> 6.84 us  [widen(): pl.pallas_call(widen_kernel, grid=(8,), out_shape=(out, out), in_specs=[p...]
    unnamed x44 -> x42, local copies, waits for them, and re-layouts: 11.4 us -> 5.3 us
    convert_element_type x2 -> x0, local copies, waits for them, and re-layouts: 5.74 us -> none  [joined(): return parts.transpose(1, 0, 2).reshape(parts.shape[1], -1).astype(F32)]
  transfers between devices with their start and end apart: 1 -> 0, of which waited for: 0 -> 0; matrix products, arithmetic and copies ran while one was open for 2% -> 0% of each run, Pallas kernels for 0% -> 0%
where the time goes in v4:
time: 400 us
  Pallas kernels  376 us (94%)
  other arithmetic  10.4 us (3%)
  local copies, waits for them, and re-layouts  9.82 us (2%)
    pallas_call x1, Pallas kernels, back(): pl.pallas_call(back_kernel, out_shape=(jax.ShapeDtypeStruct((128, 2048),...  152 us
    pallas_call x1, Pallas kernels, front(): pl.pallas_call(front_kernel, out_shape=(jax.ShapeDtypeStruct((16, 16, 128...  122 us
    pallas_call x1, Pallas kernels, feed_forward(): pl.pallas_call(mlp_kernel, out_shape=(jax.ShapeDtypeStruct((128, 2048), F...  94.9 us

profile of v4, /device:TPU:0, one launch (start us, length us, event | category | flops | bytes accessed | tf_op | source)
XLA Modules:
  0.0 399.5 jit_solution(1081437285103832401)
XLA Ops:
  0.6 0.0 copy-start
  0.8 0.1 stack.53
  0.9 0.1 stack.62
  1.0 0.7 bitcast_convert_fusion
  1.7 0.0 copy-done
  1.7 0.1 constant_dynamic-slice_fusion
  1.8 0.1 copy.25
  1.9 0.1 copy.26
  2.0 0.6 gather_fusion
  2.6 0.1 broadcast_multiply_fusion.1
  2.6 0.6 slice.33
  5.2 0.2 convert_reduce_fusion
  5.4 0.1 mul.82
  5.4 0.7 iota_reduce_fusion
  6.1 0.1 add_compare_fusion
  6.2 0.1 broadcast_in_dim.74
  6.3 0.1 mul.83
  6.4 0.1 fusion.6
  6.5 0.1 le.36
  6.6 0.1 pad_maximum_fusion.5.bias_c
  6.7 0.0 copy-start.4
  6.7 0.0 copy-start.15
  6.7 0.0 copy-start.18
  6.7 0.0 copy-start.19
  6.7 0.1 broadcast_multiply_fusion
  6.8 0.3 sine_multiply_fusion
  7.1 0.1 pad_maximum_fusion.3
  7.2 0.0 copy-start.5
  7.2 0.0 copy-start.6
  7.3 0.1 compare_select_fusion
  7.4 0.1 pad_maximum_fusion.1.bias_p
  7.5 0.0 copy-start.2
  7.5 0.0 copy-start.3
  7.6 0.0 copy-start.9
  7.6 1.3 constant_dynamic-slice_fusion.1
  9.0 0.0 copy-done.15
  9.0 0.0 copy-done.18
  9.0 0.0 copy-done.19
  9.0 0.9 pad_maximum_fusion.qkv_in
  9.9 0.0 copy-done.4
  9.9 0.0 copy-done.5
  9.9 0.0 copy-done.6
  9.9 0.0 copy-done.2
  9.9 0.0 copy-done.3
  9.9 0.0 copy-done.9
  9.9 122.3 %front.1 = (f32[16,16,128]{2,1,0:T(8,128)S(1)}, bf16[2048,2560]{1,0:T(8,128)(2,1)}, bf16[8,2,128,2048]{3,2,1,0:T(8,128)(2,1)}, bf16[2048,1536]{1,0:T(8,128)(2,1)...) custom-call(bf16[128,2048]{1,0:T(8,128)(2,1)S(1)} %bitcast.37, ...), custom_call_target="tpu_custom_call" | custom-call | tf_op jit(solution)/shard_map/front/pallas_call | solution.py:703
  132.2 0.0 copy-start.7
  132.2 0.8 copy-done.7
  133.0 0.8 copy-done.8
  133.8 0.8 copy-done.10
  134.6 0.7 copy-done.11
  135.2 0.6 copy-done.12
  135.8 94.9 %feed_forward.1 = (f32[128,2048]{1,0:T(8,128)}, bf16[8,128,2048]{2,1,0:T(8,128)(2,1)}, bf16[128,1536]{1,0:T(8,128)(2,1)}, bf16[8,352,256]{2,1,0:T(8,128)(2,1)}) custom-call(bf16[128,2048]{1,0:T(8,128)(2,1)} %copy-done.10, bf16[2048,1536]{1,0:T(8,128)(2,1)} %get-tuple-element.42.gu_in, bf16[704,2048]{1,0:T(8,128)(2,1)} %get-tuple-element.43.dn_in, ...), custom_call_target="tpu_custom_call" | custom-call | tf_op jit(solution)/shard_map/feed_forward/pallas_call | solution.py:446
  230.8 152.2 %back.1 = (bf16[128,2048]{1,0:T(8,128)(2,1)}, bf16[128,2048]{1,0:T(8,128)(2,1)}, bf16[128,2048]{1,0:T(8,128)(2,1)}, bf16[128,512]{1,0:T(8,128)(2,1)}, bf16[128,2...) custom-call(f32[128,2048]{1,0:T(8,128)} %get-tuple-element.45.da2, ...), custom_call_target="tpu_custom_call" | custom-call | tf_op jit(solution)/shard_map/back/pallas_call | solution.py:1123
  383.0 0.0 copy-start.14
  383.0 1.3 slice_bitcast_fusion
  384.3 1.6 slice_convert_fusion
  385.8 2.2 convert_element_type.32
  388.1 0.0 copy-done.14
  388.1 1.1 convert_element_type.35
  389.2 1.9 convert_element_type.36
  391.1 6.8 %widen.1 = (f32[128,5632]{1,0:T(8,128)}, f32[128,5632]{1,0:T(8,128)}) custom-call(bf16[8,128,1536]{2,1,0:T(8,128)(2,1)} %get-tuple-element.65.parts), custom_call_target="tpu_custom_call" | custom-call | tf_op jit(solution)/shard_map/widen/pallas_call | solution.py:1157
  397.9 0.8 copy.29
  398.7 0.8 copy.30
  (26 shorter events, 0.2 us)
Async XLA Ops:
  0.6 1.1 copy-start
  6.7 3.2 copy-start.4
  6.7 2.3 copy-start.15
  6.7 2.3 copy-start.18
  6.7 2.3 copy-start.19
  7.2 2.7 copy-start.5
  7.2 2.6 copy-start.6
  7.5 2.4 copy-start.2
  7.5 2.3 copy-start.3
  7.6 2.3 copy-start.9
  132.2 0.8 copy-start.7
  133.0 0.8 copy-start.8
  133.8 0.8 copy-start.10
  134.6 0.7 copy-start.11
  135.2 0.6 copy-start.12
  383.0 5.1 %copy-start.14 = (bf16[128,2048]{1,0:T(8,128)(2,1)S(1)}, bf16[128,2048]{1,0:T(8,128)(2,1)}, u32[]{:S(2)}) copy-start(bf16[128,2048]{1,0:T(8,128)(2,1)} %get-tuple-element.64) | copy-start | bytes 1572868
  385.8 3.3 copy-start.13
  391.1 6.8 %copy-start.17 = (bf16[128,2048]{1,0:T(8,128)(2,1)S(1)}, bf16[128,2048]{1,0:T(8,128)(2,1)}, u32[]{:S(2)}) copy-start(bf16[128,2048]{1,0:T(8,128)(2,1)} %get-tuple-element.59) | copy-start | bytes 1572868
  391.1 7.6 %copy-start.16 = (bf16[128,2048]{1,0:T(8,128)(2,1)S(1)}, bf16[128,2048]{1,0:T(8,128)(2,1)}, u32[]{:S(2)}) copy-start(bf16[128,2048]{1,0:T(8,128)(2,1)} %get-tuple-element.60) | copy-start | bytes 1572868
  391.1 8.4 %copy-start.1 = (s32[16,8,2]{0,2,1:T(2,128)S(1)}, s32[16,8,2]{0,2,1:T(2,128)}, u32[]{:S(2)}) copy-start(s32[16,8,2]{0,2,1:T(2,128)} %param.13) | copy-start | bytes 3076

commit v5 on v4

--- a/solution.py
+++ b/solution.py
@@ -85,9 +85,10 @@
         pl.when(jnp.logical_not(self.moved))(self.keep.wait)
 
 
-def greet_all(me):
+def greet_all(me, plane=False):
     barrier = pltpu.get_barrier_semaphore()
-    others = near(me.across_x) + near(me.across_y) + [me.sibling()]
+    others = near(me.across_x) + [me.sibling()]
+    others += [me.across_y(STEPS[s], PAIRS[s]) for s in range(1, 8)] if plane else near(me.across_y)
     for device in others:
         pl.semaphore_signal(barrier, 1, device_id=device, device_id_type=MESH)
     moved = me.c != me.j
@@ -165,20 +166,13 @@
         for got in ((5, 7) if dp == 0 else (6, 8)):
             self._got(got)
 
+    def sync(self):
+        for copy in self.passed.values():
+            copy.wait()
+
     def end(self):
         for copy in self.copies:
             copy.wait_send()
-        for copy in self.passed.values():
-            copy.wait()
-
-    def all(self):
-        self.start()
-        self.pair()
-        self.turn(0)
-        self.turn(1)
-        self.last(0)
-        self.last(1)
-        self.end()
 
 
 def row_half(half, rows):
@@ -255,6 +249,33 @@
             copy.wait_send()
 
 
+def mirror(slot):
+    return slot_of(-STEPS[slot], PAIRS[slot])
+
+
+class Trade:
+    def __init__(self, dev, what, where, sems, row):
+        self.copies = [
+            pltpu.make_async_remote_copy(
+                what(slot), where(slot), sems[0].at[row, slot], sems[1].at[row, mirror(slot)],
+                device_id=dev(STEPS[slot], PAIRS[slot]), device_id_type=MESH,
+            )
+            for slot in range(1, 8)
+        ]
+
+    def start(self):
+        for copy in self.copies:
+            copy.start()
+
+    def got(self):
+        for copy in self.copies:
+            copy.wait_recv()
+
+    def end(self):
+        for copy in self.copies:
+            copy.wait_send()
+
+
 def scatter_buffers(rows, columns, dtype=BF, cut=False):
     half = (rows, columns // 2) if cut else (rows // 2, columns)
     return [
@@ -287,33 +308,52 @@
 
 
 def mlp_kernel(
-    a2, gu_in, dn_in, dy_in,
+    a2, gu_in, dn_in, dy_in, dy_own,
     da2_out, mpart, gu_out, gdown,
     acts, gu, wd, dy, hid, dgu, dpart,
     d_half, d_full, d_pair,
     gsib, grecv, gown, gd, gdrecv,
     g_half, g_full, g_pair,
-    ag0, ag1, rs0, rs1, sib0, sib1, local,
+    ag0, ag1, dn0, dn1, dp0, dp1, rs0, rs1, sib0, sib1, local,
 ):
     me = Place()
     greet(near(me.across_x) + near(me.across_y) + [me.sibling()])
 
+    def wd_at(dr, dp, er, ep, half):
+        size = 352 if half is None else 176
+        first = me.co * 352 + (0 if half is None else half * size)
+        return wd.at[
+            pl.ds(pl.multiple_of(first, 16), size),
+            pl.ds(pl.multiple_of(me.chip_at(dr, dp) * 256, 256), 256),
+        ]
+
     def acts_at(dr, dp, er, ep, half):
         return acts.at[slot_of(dr - er, dp + ep), row_half(half, 128)]
 
     task = Gather(me.across_y, a2, acts_at, (ag0, ag1), 0)
+    down = Gather(me.across_x, dn_in, wd_at, (dn0, dn1), 0, me.sibling(), (dp0, dp1))
+    down.start()
     task.start()
     loads = [
         pltpu.make_async_copy(gu_in, gu, local.at[0]),
-        pltpu.make_async_copy(dn_in, wd.at[pl.ds(0, 704)], local.at[1]),
-        pltpu.make_async_copy(dy_in, dy, local.at[2]),
+        pltpu.make_async_copy(dn_in, wd_at(0, 0, 0, 0, None), local.at[1]),
+        pltpu.make_async_copy(dy_in.at[pl.ds(1, 7)], dy.at[pl.ds(1, 7)], local.at[2]),
+        pltpu.make_async_copy(dy_own, dy.at[0], local.at[3]),
     ]
     for load in loads:
         load.start()
     acts[0] = a2[...]
     wd[pl.ds(704, 64)] = jnp.zeros((64, 2048), BF)
+    down.turn(0)
+    down.pair()
+    down.last(0)
+    task.turn(0)
+    down.turn(1)
+    task.pair()
     for load in loads:
         load.wait()
+    down.last(1)
+    down.sync()
 
     def group(g):
         at = pl.ds(2 * g, 2)
@@ -336,14 +376,6 @@
 
     @pl.loop(0, 4)
     def _(g):
-        @pl.when(g == 0)
-        def _():
-            task.pair()
-
-        @pl.when(g == 1)
-        def _():
-            task.turn(0)
-
         @pl.when(g == 2)
         def _():
             task.turn(1)
@@ -412,7 +444,7 @@
 
     first.finish(gu_out)
     grad.finish(da2_out)
-    for job in (task, grad, first):
+    for job in (task, down, grad, first):
         job.end()
 
     @pl.loop(0, 8)
@@ -421,7 +453,7 @@
         down_to(t).wait_send()
 
 
-def feed_forward(a2, gu, dn, dy):
+def feed_forward(a2, gu, dn, dy, dy_own):
     scratch = [
         pltpu.VMEM((8, 128, 2048), BF),
         pltpu.VMEM((2048, 1536), BF),
@@ -438,10 +470,12 @@
         pltpu.VMEM((8, 352, 256), BF),
         *scatter_buffers(128, 1536),
         *dma_sems(1, 9),
+        *dma_sems(1, 9),
+        *dma_sems(1, 10),
         *dma_sems(2, 9),
         pltpu.SemaphoreType.DMA((16,)),
         pltpu.SemaphoreType.DMA((16,)),
-        pltpu.SemaphoreType.DMA((3,)),
+        pltpu.SemaphoreType.DMA((4,)),
     ]
     return pl.pallas_call(
         mlp_kernel,
@@ -451,12 +485,12 @@
             jax.ShapeDtypeStruct((128, 1536), BF),
             jax.ShapeDtypeStruct((8, 352, 256), BF),
         ),
-        in_specs=[VMEM, ANY, ANY, ANY],
+        in_specs=[VMEM, ANY, ANY, ANY, ANY],
         out_specs=[VMEM] * 4,
         scratch_shapes=scratch,
         compiler_params=params(4, 62),
         name="feed_forward",
-    )(a2, gu, dn, dy)
+    )(a2, gu, dn, dy, dy_own)
 
 
 def load(src, dst, sem):
@@ -490,15 +524,14 @@
 
 
 def front_kernel(
-    x, gains_in, qkv_in, wo_in, gu_in, dn_in, dy_in, cosine, sine, bias_p, bias_c, partner,
-    gains, qkv_out, wo_out, gu_all, dn_all, dy_all, a1, qst, kst, vst, att, lse, h1, a2,
-    qkv, wo, kv_own, kv, sT, pT, scale, dnp,
+    x, gains_in, q_in, kw_in, wo_in, gu_in, dn_in, dy_in, cosine, sine, bias_p, bias_c, partner,
+    gains, q_out, kw_out, wo_out, gu_all, dn_out, dy_all, a1, qst, kst, vst, att, lse, h1, a2,
+    qw, kw, wo, kv_own, kv, sT, pT, scale, gu_own,
     s0, s1, t0, t1, y0, y1, u0, u1, w0, w1, local,
 ):
     me = Place()
     greet_all(me)
-    swap = Swap(me, dn_in.at[:, pl.ds(pl.multiple_of(me.c * 256, 256), 256)], dnp, (w0, w1), local.at[8])
-    swap.start()
+    swap = Swap(me, dn_in.at[:, pl.ds(pl.multiple_of(me.c * 256, 256), 256)], dn_out, (w0, w1), local.at[10])
 
     def rows_at(ref, rows):
         def loc(dr, dp, er, ep, half):
@@ -511,124 +544,95 @@
     def gains_at(dr, dp, er, ep, half):
         return gains.at[me.fsdp_at(dr, dp), row_half(half, 16)]
 
-    def dn_at(dr, dp, er, ep, half):
-        size = 352 if half is None else 176
-        first = me.co * 352 + (0 if half is None else half * size)
-        return dn_all.at[
-            pl.ds(pl.multiple_of(first, 16), size),
-            pl.ds(pl.multiple_of(me.chip_at(dr, dp) * 256, 256), 256),
-        ]
-
     def slot_at(ref, rows):
         def loc(dr, dp, er, ep, half):
             return ref.at[slot_of(dr - er, dp + ep), row_half(half, rows)]
 
         return loc
 
-    def columns(index):
-        return pl.ds(pl.multiple_of(index * 256, 256), 256)
-
-    def wo_x_at(dr, dp, er, ep, half):
-        return wo.at[me.chip_at(dr, dp), me.co, row_half(half, 128), columns(me.c)]
-
-    def wo_y_at(dr, dp, er, ep, half):
-        chips = pl.ds(0, 8) if half is None else pl.ds(4 * half, 4)
-        return wo.at[chips, me.co, :, columns(me.ctx_at(dr, dp))]
+    def columns(first, index):
+        return pl.ds(pl.multiple_of(first + index * 128, 128), 128)
+
+    def plain(ref, count):
+        def loc(dr, dp, er, ep, half):
+            return ref.at[me.chip_at(dr, dp), me.co, row_half(half, 128), pl.ds(0, count)]
+
+        return loc
+
+    def strip_x(ref, first):
+        def loc(dr, dp, er, ep, half):
+            return ref.at[me.chip_at(dr, dp), me.co, row_half(half, 128), columns(first, me.c)]
+
+        return loc
+
+    def strip_y(ref, first):
+        def loc(dr, dp, er, ep, half):
+            chips = pl.ds(0, 8) if half is None else pl.ds(4 * half, 4)
+            return ref.at[chips, me.co, :, columns(first, me.ctx_at(dr, dp))]
+
+        return loc
 
     def over_x(own, loc, row, both=True):
         return Gather(me.across_x, own, loc, (s0, s1), row, me.sibling() if both else None, (t0, t1))
 
-    wo_own = wo_in.at[:, columns(me.c)]
+    def over_y(loc, row):
+        own = loc(0, 0, 0, 0, None)
+        return Gather(me.across_y, own, loc, (y0, y1), row, me.sibling(), (u0, u1))
+
     g = over_x(gains_in, gains_at, 0)
-    q = over_x(qkv_in, rows_at(qkv, 128), 1)
-    o = over_x(wo_own, wo_x_at, 2, both=False)
-    m = over_x(gu_in, rows_at(gu_all, 128), 3)
-    d = over_x(dnp, dn_at, 4)
-    dy = Gather(me.across_y, dy_in, slot_at(dy_all, 128), (y0, y1), 0)
-    oy = Gather(me.across_y, wo_y_at(0, 0, 0, 0, None), wo_y_at, (y0, y1), 1, me.sibling(), (u0, u1))
-    kv_task = Gather(me.across_y, kv_own, slot_at(kv, 128), (y0, y1), 2)
-    kept = [load(task.own, task.loc(0, 0, 0, 0, None), local.at[i]) for i, task in enumerate((g, q, o, m, dy))]
-
-    g.start()
-    o.start()
-    q.start()
-    dy.start()
-    norm_scale(x, scale)
-    swap.wait()
-    kept.append(load(dnp, d.loc(0, 0, 0, 0, None), local.at[5]))
-    for task in (g, o):
-        task.pair()
-        task.turn(0)
-    dy.pair()
-    dy.turn(0)
-    q.pair()
-    g.turn(1)
-    o.turn(1)
-    q.turn(0)
-    dy.turn(1)
-    q.turn(1)
-    m.start()
-    d.start()
-    for task in (g, o):
-        task.last(0)
-        task.last(1)
-    kept[2].wait()
-    oy.start()
-    dy.last(0)
-    dy.last(1)
-    kept[0].wait()
-    g.end()
-
-    @pl.loop(0, 16)
-    def _(i):
-        at = pl.ds(pl.multiple_of(i * 128, 128), 128)
-        a1[:, at] = (x[:, at].astype(F32) * scale[...] * gains[i, pl.ds(0, 1), :]).astype(BF)
-
-    q.last(0)
-    q.last(1)
-    m.pair()
-    d.pair()
-    oy.pair()
-    kept[1].wait()
-    q.end()
-    saved = [load(qkv, qkv_out, local.at[6])]
-
-    @pl.loop(0, 4)
-    def _(n):
-        raw = dot_in(a1[...], qkv[:, pl.ds(pl.multiple_of(512 * n, 512), 512)])
-        for i in range(4):
+    k = over_x(kw_in, plain(kw, 512), 6)
+    q = over_x(q_in.at[:, pl.ds(0, 1024)], plain(qw, 1024), 1)
+    qx = over_x(q_in.at[:, columns(1024, me.c)], strip_x(qw, 1024), 2, both=False)
+    o = over_x(wo_in.at[:, pl.ds(0, 1024)], plain(wo, 1024), 3)
+    ox = over_x(wo_in.at[:, columns(1024, me.c)], strip_x(wo, 1024), 4, both=False)
+    m = over_x(gu_in, rows_at(gu_all, 128), 5)
+    qy = over_y(strip_y(qw, 1024), 0)
+    oy = over_y(strip_y(wo, 1024), 1)
+    dy = Gather(me.across_y, dy_in, slot_at(dy_all, 128), (y0, y1), 2)
+    kv_task = Gather(me.across_y, kv_own, slot_at(kv, 128), (y0, y1), 3)
+    kept = [load(task.own, task.loc(0, 0, 0, 0, None), local.at[i]) for i, task in enumerate((g, q, qx, o, ox, k))]
+    kept.append(load(gu_in, gu_own, local.at[6]))
+
+    def normed():
+        norm_scale(x, scale)
+        kept[0].wait()
+
+        @pl.loop(0, 16)
+        def _(i):
+            at = pl.ds(pl.multiple_of(i * 128, 128), 128)
+            a1[:, at] = (x[:, at].astype(F32) * scale[...] * gains[i, pl.ds(0, 1), :]).astype(BF)
+
+    def project_kv():
+        kept[5].wait()
+        raw = dot_in(a1[...], kw[...].reshape(2048, 512))
+        for i in range(2):
             part = raw[:, 128 * i : 128 * i + 128]
-            part = ((part * cosine[...] + turned(part) * sine[...]) .astype(BF).astype(F32) * SCALE).astype(BF)
-            for half in (0, 1):
-                for e in (0, 1):
-                    qst[n, half, pl.ds(64 * (2 * i + e), 64), :] = part[64 * half : 64 * half + 64, 64 * e : 64 * e + 64]
-
-    raw = dot_in(a1[...], qkv[:, pl.ds(2048, 512)])
-    for i in range(2):
-        part = raw[:, 128 * i : 128 * i + 128]
-        kv_own[:, 128 * i : 128 * i + 128] = (part * cosine[...] + turned(part) * sine[...]).astype(BF)
-    kv_own[:, 256:] = raw[:, 256:].astype(BF)
-    kv_task.start()
-    kv[0] = kv_own[...]
-    m.turn(0)
-    kv_task.pair()
-    kv_task.turn(0)
-    d.turn(0)
-    kv_task.turn(1)
-    oy.turn(0)
-    kv_task.last(0)
-    kv_task.last(1)
-    kv_task.end()
-
-    mate = partner[0]
-    beside = kv[mate]
-    for out, base in ((kst, 0), (vst, 256)):
-        for n in range(4):
-            first = base + 64 * n
-            for slot in range(8):
-                out[n, pl.ds(64 * slot, 64), :] = kv[slot, 0:64, first : first + 64]
-            out[n, pl.ds(512, 64), :] = beside[64:128, first : first + 64]
-            out[n, pl.ds(576, 64), :] = kv_own[64:128, first : first + 64]
+            kv_own[:, 128 * i : 128 * i + 128] = (part * cosine[...] + turned(part) * sine[...]).astype(BF)
+        kv_own[:, 256:] = raw[:, 256:].astype(BF)
+        kv[0] = kv_own[...]
+
+    def project_q():
+        @pl.loop(0, 4)
+        def _(n):
+            raw = dot_in(a1[...], qw[:, :, :, pl.ds(pl.multiple_of(512 * n, 512), 512)].reshape(2048, 512))
+            for i in range(4):
+                part = raw[:, 128 * i : 128 * i + 128]
+                part = ((part * cosine[...] + turned(part) * sine[...]).astype(BF).astype(F32) * SCALE).astype(BF)
+                for half in (0, 1):
+                    for e in (0, 1):
+                        rows = pl.ds(64 * (2 * i + e), 64)
+                        qst[n, half, rows, :] = part[64 * half : 64 * half + 64, 64 * e : 64 * e + 64]
+
+    def collect_kv():
+        mate = partner[0]
+        beside = kv[mate]
+        for out, base in ((kst, 0), (vst, 256)):
+            for n in range(4):
+                first = base + 64 * n
+                for slot in range(8):
+                    out[n, pl.ds(64 * slot, 64), :] = kv[slot, 0:64, first : first + 64]
+                out[n, pl.ds(512, 64), :] = beside[64:128, first : first + 64]
+                out[n, pl.ds(576, 64), :] = kv_own[64:128, first : first + 64]
 
     def attend(n, half):
         count = 512 if half == 0 else 640
@@ -658,56 +662,137 @@
             first = pl.multiple_of(512 * n + 128 * i, 128)
             att[pl.ds(64 * half, 64), pl.ds(first, 128)] = block.astype(BF)
 
+    def project_o():
+        @pl.loop(0, 4)
+        def _(n):
+            at = pl.ds(pl.multiple_of(512 * n, 512), 512)
+            h1[:, at] = x[:, at].astype(F32) + dot_in(att[...], wo[:, :, :, at].reshape(2048, 512))
+
+    def normed_two():
+        norm_scale(h1, scale)
+
+        @pl.loop(0, 16)
+        def _(i):
+            at = pl.ds(pl.multiple_of(i * 128, 128), 128)
+            a2[:, at] = (h1[:, at] * scale[...] * gains[i, pl.ds(8, 1), :]).astype(BF)
+
+    qx.start()
+    k.start()
+    g.start()
+    ox.start()
+    dy.start()
+    qx.pair()
+    qx.turn(0)
+    k.turn(0)
+    g.pair()
+    qx.turn(1)
+    ox.pair()
+    k.pair()
+    k.last(0)
+    qx.last(0)
+    g.turn(0)
+    g.turn(1)
+    ox.turn(0)
+    qx.last(1)
+    ox.turn(1)
+    kept[2].wait()
+    qy.start()
+    q.start()
+    dy.pair()
+    k.turn(1)
+    o.start()
+    g.last(0)
+    m.start()
+    g.last(1)
+    ox.last(0)
+    k.last(1)
+    ox.last(1)
+    g.sync()
+    qy.pair()
+    k.sync()
+    q.turn(0)
+    normed()
+    project_kv()
+    qy.turn(0)
+    o.turn(0)
+    kept[4].wait()
+    oy.start()
+    o.pair()
+    qy.turn(1)
+    q.pair()
+    kv_task.start()
+    o.last(0)
+    qy.last(0)
+    oy.pair()
+    q.last(0)
+    o.turn(1)
+    q.turn(1)
+    m.pair()
+    kv_task.pair()
+    oy.turn(0)
+    q.last(1)
+    qy.last(1)
+    kv_task.turn(1)
+    kv_task.turn(0)
+    o.last(1)
+    oy.turn(1)
+    m.turn(0)
+    dy.turn(0)
+    dy.turn(1)
+    q.sync()
+    qy.sync()
+    kept[1].wait()
+    kept[6].wait()
+    saved = [load(qw, q_out, local.at[7]), load(kw, kw_out, local.at[8])]
+    saved.append(load(gu_own, m.loc(0, 0, 0, 0, None), local.at[6]))
+    project_q()
+    swap.start()
+    kv_task.last(1)
+    kv_task.last(0)
+    oy.last(0)
+    collect_kv()
+    m.turn(1)
+
     @pl.loop(0, 4)
     def _(n):
         attend(n, 0)
         attend(n, 1)
 
-        @pl.when(n == 0)
-        def _():
-            oy.turn(1)
-            m.turn(1)
-
         @pl.when(n == 1)
         def _():
-            d.turn(1)
-
-    oy.last(0)
-    oy.last(1)
-    o.end()
-    oy.end()
-    saved.append(load(wo, wo_out, local.at[7]))
-
-    @pl.loop(0, 4)
-    def _(n):
-        at = pl.ds(pl.multiple_of(512 * n, 512), 512)
-        h1[:, at] = x[:, at].astype(F32) + dot_in(att[...], wo[:, :, :, at].reshape(2048, 512))
-
-    norm_scale(h1, scale)
-
-    @pl.loop(0, 16)
-    def _(i):
-        at = pl.ds(pl.multiple_of(i * 128, 128), 128)
-        a2[:, at] = (h1[:, at] * scale[...] * gains[i, pl.ds(8, 1), :]).astype(BF)
-
-    for task in (m, d):
-        task.last(0)
-        task.last(1)
-    for task in (m, d, dy):
+            oy.last(1)
+
+        @pl.when(n == 2)
+        def _():
+            o.sync()
+
+    oy.sync()
+    m.last(0)
+    m.last(1)
+    dy.last(0)
+    kept[3].wait()
+    saved.append(load(wo, wo_out, local.at[9]))
+    project_o()
+    normed_two()
+    m.sync()
+    dy.last(1)
+    for task in (g, k, q, qx, o, ox, m, qy, oy, dy, kv_task):
         task.end()
-    for copy in (*kept[3:], *saved):
+    swap.wait()
+    for copy in saved:
         copy.wait()
 
 
-def front(x, gains, qkv, wo, gu, dn, dy, cosine, sine, bias_p, bias_c, partner):
+def front(x, gains, q, kw, wo, gu, dn, dy, cosine, sine, bias_p, bias_c, partner):
     return pl.pallas_call(
         front_kernel,
         out_shape=(
             jax.ShapeDtypeStruct((16, 16, 128), F32),
-            jax.ShapeDtypeStruct((2048, 2560), BF),
+            jax.ShapeDtypeStruct((8, 2, 128, 2048), BF),
+            jax.ShapeDtypeStruct((8, 2, 128, 512), BF),
             jax.ShapeDtypeStruct((8, 2, 128, 2048), BF),
             jax.ShapeDtypeStruct((2048, 1536), BF),
-            jax.ShapeDtypeStruct((704, 2048), BF),
+            jax.ShapeDtypeStruct((352, 256), BF),
             jax.ShapeDtypeStruct((8, 128, 2048), BF),
             jax.ShapeDtypeStruct((128, 2048), BF),
             jax.ShapeDtypeStruct((4, 2, 512, 64), BF),
@@ -718,47 +803,49 @@
             jax.ShapeDtypeStruct((128, 2048), F32),
             jax.ShapeDtypeStruct((128, 2048), BF),
         ),
-        in_specs=[VMEM] + [ANY] * 6 + [VMEM] * 4 + [pl.BlockSpec(memory_space=pltpu.SMEM)],
-        out_specs=[VMEM] + [ANY] * 5 + [VMEM] * 8,
+        in_specs=[VMEM] + [ANY] * 7 + [VMEM] * 4 + [pl.BlockSpec(memory_space=pltpu.SMEM)],
+        out_specs=[VMEM] + [ANY] * 6 + [VMEM] * 8,
         scratch_shapes=[
-            pltpu.VMEM((2048, 2560), BF),
+            pltpu.VMEM((8, 2, 128, 2048), BF),
+            pltpu.VMEM((8, 2, 128, 512), BF),
             pltpu.VMEM((8, 2, 128, 2048), BF),
             pltpu.VMEM((128, 512), BF),
             pltpu.VMEM((8, 128, 512), BF),
             pltpu.VMEM((640, 512), F32),
             pltpu.VMEM((640, 512), BF),
             pltpu.VMEM((128, 1), F32),
-            pltpu.VMEM((352, 256), BF),
-            *dma_sems(5, 9),
-            *dma_sems(5, 10),
-            *dma_sems(3, 9),
+            pltpu.VMEM((128, 1536), BF),
+            *dma_sems(7, 9),
+            *dma_sems(7, 10),
+            *dma_sems(4, 9),
             *dma_sems(2, 10),
             pltpu.SemaphoreType.DMA,
             pltpu.SemaphoreType.DMA,
-            pltpu.SemaphoreType.DMA((9,)),
+            pltpu.SemaphoreType.DMA((11,)),
         ],
-        compiler_params=params(1, 50),
+        compiler_params=params(1, 62),
         name="front",
-    )(x, gains, qkv, wo, gu, dn, dy, cosine, sine, bias_p, bias_c, partner)
+    )(x, gains, q, kw, wo, gu, dn, dy, cosine, sine, bias_p, bias_c, partner)
 
 
 def back_kernel(
-    da2, h1, dy, x, gains, wo_in, qkv_in, qst, kst, vst, lse, cosine, sine, bias_p, bias_c, partner,
+    da2, h1, dy, x, gains, wo_in, q_in, kw_in, qst, kst, vst, lse, cosine, sine, bias_p, bias_c, partner,
     a1_in, att_in, mpart_in, gu, gdown_in,
     mixed, tokens_grad, q_out, kv_out, o_out, gains_out, gu_all, dn_all,
     a1s, atts, dqkvs, datts, grow, dh1, gown, gsib, mpart, stream, dost, sT, dT, pT, dsT,
-    kgrad, vgrad, kvp, dkv, da1, gdown, dn_sum, dnp,
+    kgrad, vgrad, kvp, dkv, da1, gdown, dn_sum, dnp, gu_own,
     qp, op, kp, gp, ggot, q_sum, o_sum, kv_sum, g_sum,
     q_half, q_full, q_pair, o_half, o_full, o_pair, k_half, k_full, k_pair, e_half, e_full, e_pair,
     m_half, m_full, m_pair, d_half, d_full, d_pair, n_half, n_full, n_pair,
-    or_half, or_full, or_pair, qr_half, qr_full, qr_pair, kr_half, kr_full, kr_pair,
-    sib0, sib1, x0, x1, y0, y1, ag0, ag1, swap0, swap1, local,
+    o_got, q_got, k_got,
+    sib0, sib1, x0, x1, y0, y1, ag0, ag1, z0, z1, swap0, swap1, local,
 ):
     me = Place()
-    greet_all(me)
+    greet_all(me, plane=True)
     nload = load(gdown_in, gdown, local.at[0])
     own, other = pl.ds(0, 128), pl.ds(128, 128)
     mload = load(mpart_in, mpart, local.at[1])
+    guload = load(gu, gu_own, local.at[6])
     a1load = load(a1_in, a1s.at[own], local.at[2])
     attload = load(att_in, atts.at[own], local.at[3])
 
@@ -768,12 +855,16 @@
         )
 
     def qkv_load(n):
-        return pltpu.make_async_copy(qkv_in.at[pl.ds(512 * n, 512)], stream.at[n % 2], local.at[4 + n % 2])
+        rows = pl.ds(512 * n, 512)
+        return (
+            pltpu.make_async_copy(q_in.at[rows], stream.at[n % 2, :, pl.ds(0, 2048)], local.at[4 + n % 2]),
+            pltpu.make_async_copy(kw_in.at[rows], stream.at[n % 2, :, pl.ds(2048, 512)], local.at[9 + n % 2]),
+        )
 
     wo_load(0).start()
     wo_load(1).start()
 
-    over_x, over_y, over_ag = (x0, x1), (y0, y1), (ag0, ag1)
+    over_x, over_y, over_ag, over_sum = (x0, x1), (y0, y1), (ag0, ag1), (z0, z1)
     o_job = Scatter(me.across_x, lambda slot: op.at[slot], 128, o_half, o_full, o_pair, over_x, 0)
     q_job = Scatter(me.across_x, lambda slot: qp.at[slot], 128, q_half, q_full, q_pair, over_x, 1)
     k_job = Scatter(me.across_x, lambda slot: kp.at[slot], 128, k_half, k_full, k_pair, over_x, 2)
@@ -793,33 +884,33 @@
         first = pl.multiple_of(me.ctx_at(dr, dp) * 256, 256)
         return dn_all.at[row_half(half, 352), pl.ds(first, 256)]
 
-    gu_task = Gather(me.across_y, gu, at_ctx(gu_all), over_ag, 0)
+    gu_task = Gather(me.across_y, gu_own, at_ctx(gu_all), over_ag, 0)
     dn_task = Gather(me.across_y, dnp, dn_at, over_ag, 1)
-    e_task = Gather(me.across_y, g_sum, at_ctx(ggot), over_ag, 2)
-
-    def sum_over_ctx(total, columns, halves, fulls, paired, row):
-        def part(slot):
-            first = pl.multiple_of(me.ctx_at(STEPS[slot], PAIRS[slot]) * 16, 16)
-            return total.at[pl.ds(first, 16)]
-
-        return Scatter(me.across_y, part, 16, halves, fulls, paired, over_y, row, cut=columns)
-
-    def spread(out, columns, row):
-        def loc(dr, dp, er, ep, half):
-            first = pl.multiple_of(me.ctx_at(dr, dp) * 16, 16)
-            if half is None:
-                return out.at[pl.ds(first, 16)]
-            return out.at[pl.ds(first, 16), pl.ds(half * (columns // 2), columns // 2)]
-
-        return Gather(me.across_y, loc(0, 0, 0, 0, None), loc, over_ag, row)
-
-    o_sums = sum_over_ctx(o_sum, 2048, or_half, or_full, or_pair, 2)
-    q_sums = sum_over_ctx(q_sum, 2048, qr_half, qr_full, qr_pair, 3)
-    kv_sums = sum_over_ctx(kv_sum, 512, kr_half, kr_full, kr_pair, 4)
-    o_spread = spread(o_out, 2048, 3)
-    q_spread = spread(q_out, 2048, 4)
-    kv_spread = spread(kv_out, 512, 5)
-    own_rows = pl.ds(pl.multiple_of(me.c * 16, 16), 16)
+    def block_at(ref, slot):
+        first = pl.multiple_of(me.ctx_at(STEPS[slot], PAIRS[slot]) * 16, 16)
+        return ref.at[pl.ds(first, 16)]
+
+    def sum_over_ctx(total, got, row):
+        return Trade(
+            me.across_y, lambda slot: block_at(total, slot), lambda slot: got.at[mirror(slot)], over_sum, row
+        )
+
+    def spread(out, row):
+        return Trade(me.across_y, lambda slot: block_at(out, 0), lambda slot: block_at(out, 0), over_sum, row)
+
+    def sum_up(total, got, out):
+        value = block_at(total, 0)[...].astype(F32)
+        for slot in range(1, 8):
+            value = value + got[slot].astype(F32)
+        block_at(out, 0)[...] = value.astype(BF)
+
+    o_sums = sum_over_ctx(o_sum, o_got, 0)
+    q_sums = sum_over_ctx(q_sum, q_got, 1)
+    k_sums = sum_over_ctx(kv_sum, k_got, 2)
+    o_spread = spread(o_out, 3)
+    q_spread = spread(q_out, 4)
+    k_spread = spread(kv_out, 5)
+    e_task = Trade(me.across_y, lambda slot: g_sum, lambda slot: ggot.at[me.c], over_sum, 6)
 
     swap = lambda src, dst, index: send(src, dst, (sib0, sib1), index, me.sibling())
     att_swap = swap(atts.at[own], atts.at[other], 0)
@@ -831,46 +922,39 @@
     dkv_swap = swap(dqkvs.at[own, rest], dqkvs.at[other, rest], 4)
     gain_swap = swap(gown, gsib, 5)
 
-    attload.wait()
-    att_swap.start()
-    a1load.wait()
-    a1_swap.start()
-    nload.wait()
-    n_job.start()
-    mload.wait()
-    m_job.start()
-
-    gown[...] = jnp.zeros((16, 16, 128), F32)
     for i in range(16):
         grow[0, :, 128 * i : 128 * i + 128] = gains[i, 0:1, :]
         grow[1, :, 128 * i : 128 * i + 128] = gains[i, 8:9, :]
     grow[2] = jnp.zeros((1, 2048), F32)
     grow[3] = jnp.zeros((1, 2048), F32)
-
-    @pl.loop(0, 8)
-    def _(i):
-        at = pl.ds(pl.multiple_of(16 * i, 16), 16)
-        values, grad = h1[at], da2[at]
-        scale = lax.rsqrt(jnp.mean(values * values, axis=1, keepdims=True) + EPS)
-        grow[3] += jnp.sum(grad * values * scale, axis=0, keepdims=True)
-        grad = grad * grow[1]
-        level = jnp.mean(grad * values, axis=1, keepdims=True) * scale * scale * scale
-        total = dy[at].astype(F32) + scale * grad - values * level
-        dh1[at] = total
-        datts[at] = total.astype(BF)
-
-    datt_swap.start()
-    n_job.turn(1)
-    n_job.turn(0)
-    for n in range(4):
-        wo_load(n).wait()
-        part = dot_back(datts[own], stream[n % 2, :, 0:2048]).astype(BF)
-        for half in (0, 1):
-            pile(dost.at[n, half], part, half)
-        if n < 2:
-            wo_load(n + 2).start()
-    qkv_load(0).start()
-    qkv_load(1).start()
+    kept = []
+
+    def norm_two_back():
+        @pl.loop(0, 8)
+        def _(i):
+            at = pl.ds(pl.multiple_of(16 * i, 16), 16)
+            values, grad = h1[at], da2[at]
+            scale = lax.rsqrt(jnp.mean(values * values, axis=1, keepdims=True) + EPS)
+            grow[3] += jnp.sum(grad * values * scale, axis=0, keepdims=True)
+            grad = grad * grow[1]
+            level = jnp.mean(grad * values, axis=1, keepdims=True) * scale * scale * scale
+            total = dy[at].astype(F32) + scale * grad - values * level
+            dh1[at] = total
+            datts[at] = total.astype(BF)
+
+        datt_swap.start()
+
+    def heads_back():
+        for n in range(4):
+            wo_load(n).wait()
+            part = dot_back(datts[own], stream[n % 2, :, 0:2048]).astype(BF)
+            for half in (0, 1):
+                pile(dost.at[n, half], part, half)
+            if n < 2:
+                wo_load(n + 2).start()
+        for n in range(2):
+            for copy in qkv_load(n):
+                copy.start()
 
     def terms(left, right, out, job):
         @pl.loop(0, 8)
@@ -882,12 +966,86 @@
             def _():
                 job.start()
 
-    m_job.turn(1)
-    att_swap.wait_recv()
-    datt_swap.wait_recv()
-    terms(atts, datts, op, o_job)
-    m_job.turn(0)
-    n_job.pair()
+    def output_terms():
+        att_swap.wait_recv()
+        datt_swap.wait_recv()
+        terms(atts, datts, op, o_job)
+
+    def query_terms():
+        a1_swap.wait_recv()
+        dq_swap.wait_recv()
+        terms(a1s, dqkvs.at[:, pl.ds(0, 2048)], qp, q_job)
+
+    def kv_terms():
+        dkv_swap.wait_recv()
+        terms(a1s, dqkvs.at[:, pl.ds(2048, 512)], kp, k_job)
+
+    def kv_blocks():
+        mate = partner[0]
+        for out, base in ((kgrad, 0), (vgrad, 256)):
+            for n in range(4):
+                first = base + 64 * n
+                for slot in range(8):
+                    kvp[slot, 0:64, first : first + 64] = out[n, 64 * slot : 64 * slot + 64, :]
+                    if slot == 0:
+                        late = out[n, 576:640, :]
+                    else:
+                        late = jnp.where(mate == slot, out[n, 512:576, :], jnp.zeros((64, 64), BF))
+                    kvp[slot, 64:128, first : first + 64] = late
+
+    def kv_back():
+        for i in range(2):
+            at = slice(128 * i, 128 * i + 128)
+            block = dkv[:, at]
+            dqkvs[own, 2048 + 128 * i : 2176 + 128 * i] = (block * cosine[...] - turned(block) * sine[...]).astype(BF)
+        dqkvs[own, 2304:2560] = dkv[:, 256:512].astype(BF)
+        dkv_swap.start()
+
+    def inputs_back():
+        for n in range(4):
+            for copy in qkv_load(n):
+                copy.wait()
+            da1[:, 512 * n : 512 * n + 512] = dot_back(dqkvs[own], stream[n % 2])
+            if n < 2:
+                for copy in qkv_load(n + 2):
+                    copy.start()
+
+    def norm_one_back():
+        @pl.loop(0, 8)
+        def _(i):
+            at = pl.ds(pl.multiple_of(16 * i, 16), 16)
+            values, grad = x[at].astype(F32), da1[at]
+            scale = lax.rsqrt(jnp.mean(values * values, axis=1, keepdims=True) + EPS)
+            grow[2] += jnp.sum(grad * values * scale, axis=0, keepdims=True)
+            grad = grad * grow[0]
+            level = jnp.mean(grad * values, axis=1, keepdims=True) * scale * scale * scale
+            tokens_grad[at] = (dh1[at] + scale * grad - values * level).astype(BF)
+
+        gown[...] = jnp.zeros((16, 16, 128), F32)
+        for i in range(16):
+            gown[i, 0:1, :] = grow[2, :, 128 * i : 128 * i + 128]
+            gown[i, 8:9, :] = grow[3, :, 128 * i : 128 * i + 128]
+        gain_swap.start()
+
+    def gain_terms():
+        gain_swap.wait_recv()
+        for slot in range(8):
+            block = me.fsdp_at(STEPS[slot], PAIRS[slot])
+            gp[slot] = gown[block] + gsib[block]
+
+    def dn_begin():
+        dn_swap.wait()
+        dn_task.start()
+        kept.append(load(dnp, dn_at(0, 0, 0, 0, None), local.at[7]))
+
+    def gu_begin():
+        guload.wait()
+        kept.append(load(gu_own, gu_all.at[me.c], local.at[6]))
+        gu_task.start()
+
+    def e_begin():
+        e_task.start()
+        ggot[me.c] = g_sum[...]
 
     def attend(n, half):
         count = 512 if half == 0 else 640
@@ -918,6 +1076,22 @@
             dqkvs[rows, pl.ds(first, 128)] = block.astype(BF)
         return dot_in(dsT[keys], query), dot_in(pT[keys], out)
 
+    nload.wait()
+    n_job.start()
+    gu_begin()
+    a1load.wait()
+    a1_swap.start()
+    norm_two_back()
+    n_job.turn(1)
+    attload.wait()
+    att_swap.start()
+    n_job.turn(0)
+    mload.wait()
+    m_job.start()
+    output_terms()
+    heads_back()
+    n_job.pair()
+
     @pl.loop(0, 4)
     def _(n):
         key_one, value_one = attend(n, 0)
@@ -928,138 +1102,80 @@
 
         @pl.when(n == 0)
         def _():
+            m_job.turn(1)
+            o_job.turn(1)
+
+        @pl.when(n == 2)
+        def _():
             n_job.finish(dn_sum)
-            dn_swap.start()
-
-        @pl.when(n == 1)
-        def _():
-            o_job.turn(1)
-
+
+    kv_blocks()
+    d_job.start()
+    o_job.turn(0)
+    gu_task.turn(0)
+    m_job.pair()
     dq_swap.start()
-    o_job.turn(0)
-    mate = partner[0]
-    for out, base in ((kgrad, 0), (vgrad, 256)):
-        for n in range(4):
-            first = base + 64 * n
-            for slot in range(8):
-                kvp[slot, 0:64, first : first + 64] = out[n, 64 * slot : 64 * slot + 64, :]
-                if slot == 0:
-                    late = out[n, 576:640, :]
-                else:
-                    late = jnp.where(mate == slot, out[n, 512:576, :], jnp.zeros((64, 64), BF))
-                kvp[slot, 64:128, first : first + 64] = late
-    d_job.start()
-    m_job.pair()
-    a1_swap.wait_recv()
-    dq_swap.wait_recv()
-    terms(a1s, dqkvs.at[:, pl.ds(0, 2048)], qp, q_job)
-    m_job.finish(mixed, (h1,))
+    d_job.turn(1)
+    dn_swap.start()
+    d_job.turn(0)
+    query_terms()
     o_job.pair()
-    d_job.turn(1)
-    d_job.turn(0)
-    kept = [load(gu, gu_all.at[me.c], local.at[6])]
-    gu_task.start()
-    dn_swap.wait()
-    dn_task.start()
-    kept.append(load(dnp, dn_at(0, 0, 0, 0, None), local.at[7]))
+    gu_task.pair()
+    m_job.turn(0)
     d_job.pair()
-    d_job.finish(dkv)
-    for i in range(2):
-        at = slice(128 * i, 128 * i + 128)
-        block = dkv[:, at]
-        dqkvs[own, 2048 + 128 * i : 2176 + 128 * i] = (block * cosine[...] - turned(block) * sine[...]).astype(BF)
-    dqkvs[own, 2304:2560] = dkv[:, 256:512].astype(BF)
-    dkv_swap.start()
+    q_job.turn(1)
+    gu_task.turn(1)
+    dn_begin()
     o_job.finish(o_sum)
     o_sums.start()
-
-    for n in range(4):
-        qkv_load(n).wait()
-        da1[:, 512 * n : 512 * n + 512] = dot_back(dqkvs[own], stream[n % 2])
-        if n < 2:
-            qkv_load(n + 2).start()
-    q_job.turn(1)
-    dkv_swap.wait_recv()
-    terms(a1s, dqkvs.at[:, pl.ds(2048, 512)], kp, k_job)
-
-    @pl.loop(0, 8)
-    def _(i):
-        at = pl.ds(pl.multiple_of(16 * i, 16), 16)
-        values, grad = x[at].astype(F32), da1[at]
-        scale = lax.rsqrt(jnp.mean(values * values, axis=1, keepdims=True) + EPS)
-        grow[2] += jnp.sum(grad * values * scale, axis=0, keepdims=True)
-        grad = grad * grow[0]
-        level = jnp.mean(grad * values, axis=1, keepdims=True) * scale * scale * scale
-        tokens_grad[at] = (dh1[at] + scale * grad - values * level).astype(BF)
-
-    for i in range(16):
-        gown[i, 0:1, :] = grow[2, :, 128 * i : 128 * i + 128]
-        gown[i, 8:9, :] = grow[3, :, 128 * i : 128 * i + 128]
-    gain_swap.start()
-    gu_task.pair()
+    gu_task.last(0)
+    d_job.finish(dkv)
+    kv_back()
+    kv_terms()
+    q_job.turn(0)
+    q_job.pair()
     dn_task.pair()
-    q_job.turn(0)
-    gu_task.turn(0)
+    gu_task.last(1)
+    inputs_back()
+    k_job.turn(1)
+    norm_one_back()
+    o_sums.got()
+    sum_up(o_sum, o_got, o_out)
+    o_spread.start()
+    m_job.finish(mixed, (h1,))
+    k_job.turn(0)
+    gain_terms()
     dn_task.turn(0)
-    gain_swap.wait_recv()
-    for slot in range(8):
-        block = me.fsdp_at(STEPS[slot], PAIRS[slot])
-        gp[slot] = gown[block] + gsib[block]
+    q_job.finish(q_sum)
+    k_job.pair()
+    q_sums.start()
     e_job.start()
-    o_sums.turn(1)
-    o_sums.turn(0)
-    gu_task.turn(1)
+    o_spread.got()
+    k_job.finish(kv_sum)
     dn_task.turn(1)
-    o_sums.pair()
-    o_sums.finish(o_out.at[own_rows])
-    o_spread.start()
-    q_job.pair()
-    k_job.turn(1)
-    k_job.turn(0)
     e_job.turn(1)
+    e_job.pair()
+    k_sums.start()
+    q_sums.got()
+    sum_up(q_sum, q_got, q_out)
+    q_spread.start()
     e_job.turn(0)
-    o_spread.pair()
-    o_spread.turn(0)
-    o_spread.turn(1)
-    q_job.finish(q_sum)
-    q_sums.start()
-    k_job.pair()
-    e_job.pair()
-    q_sums.turn(1)
-    q_sums.turn(0)
-    k_job.finish(kv_sum)
-    kv_sums.start()
     e_job.finish(g_sum)
-    e_task.start()
-    ggot[me.c] = g_sum[...]
-    q_sums.pair()
-    kv_sums.turn(1)
-    kv_sums.turn(0)
-    e_task.pair()
-    e_task.turn(0)
-    q_sums.finish(q_out.at[own_rows])
-    q_spread.start()
-    e_task.turn(1)
-    kv_sums.pair()
-    q_spread.pair()
-    q_spread.turn(0)
-    kv_sums.finish(kv_out.at[own_rows])
-    kv_spread.start()
-    q_spread.turn(1)
-    kv_spread.pair()
-    kv_spread.turn(0)
-    kv_spread.turn(1)
-    e_task.last(0)
-    e_task.last(1)
+    e_begin()
+    dn_task.last(0)
+    dn_task.last(1)
+    k_sums.got()
+    sum_up(kv_sum, k_got, kv_out)
+    k_spread.start()
+    q_spread.got()
+    e_task.got()
+    k_spread.got()
     total = ggot[0]
     for index in range(1, 8):
         total = total + ggot[index]
     gains_out[...] = total
-    for task in (gu_task, dn_task, o_spread, q_spread, kv_spread):
-        task.last(0)
-        task.last(1)
-    jobs = (o_job, q_job, k_job, e_job, m_job, d_job, n_job, o_sums, q_sums, kv_sums)
-    for job in (*jobs, gu_task, dn_task, e_task, o_spread, q_spread, kv_spread):
+    jobs = (o_job, q_job, k_job, e_job, m_job, d_job, n_job, o_sums, q_sums, k_sums)
+    for job in (*jobs, gu_task, dn_task, e_task, o_spread, q_spread, k_spread):
         job.end()
     for copy in (att_swap, datt_swap, a1_swap, dq_swap, dkv_swap, gain_swap):
         copy.wait_send()
@@ -1067,7 +1183,7 @@
         copy.wait()
 
 
-def back(da2, h1, dy, x, gains, wo, qkv, qst, kst, vst, lse, cosine, sine, bias_p, bias_c, partner, a1, att, mpart, gu, gdown):
+def back(da2, h1, dy, x, gains, wo, q, kw, qst, kst, vst, lse, cosine, sine, bias_p, bias_c, partner, a1, att, mpart, gu, gdown):
     scratch = [
         pltpu.VMEM((256, 2048), BF),
         pltpu.VMEM((256, 2048), BF),
@@ -1092,6 +1208,7 @@
         pltpu.VMEM((8, 352, 256), BF),
         pltpu.VMEM((352, 256), BF),
         pltpu.VMEM((352, 256), BF),
+        pltpu.VMEM((128, 1536), BF),
         pltpu.VMEM((8, 128, 2048), BF),
         pltpu.VMEM((8, 128, 2048), BF),
         pltpu.VMEM((8, 128, 512), BF),
@@ -1108,17 +1225,18 @@
         *scatter_buffers(128, 2048),
         *scatter_buffers(128, 512),
         *scatter_buffers(352, 256),
-        *scatter_buffers(16, 2048, cut=True),
-        *scatter_buffers(16, 2048, cut=True),
-        *scatter_buffers(16, 512, cut=True),
+        pltpu.VMEM((8, 16, 2048), BF),
+        pltpu.VMEM((8, 16, 2048), BF),
+        pltpu.VMEM((8, 16, 512), BF),
         pltpu.SemaphoreType.DMA((6,)),
         pltpu.SemaphoreType.DMA((6,)),
         *dma_sems(5, 9),
-        *dma_sems(5, 9),
-        *dma_sems(6, 9),
+        *dma_sems(2, 9),
+        *dma_sems(2, 9),
+        *dma_sems(7, 8),
         pltpu.SemaphoreType.DMA,
         pltpu.SemaphoreType.DMA,
-        pltpu.SemaphoreType.DMA((9,)),
+        pltpu.SemaphoreType.DMA((11,)),
     ]
     return pl.pallas_call(
         back_kernel,
@@ -1132,12 +1250,12 @@
             jax.ShapeDtypeStruct((8, 128, 1536), BF),
             jax.ShapeDtypeStruct((352, 2048), BF),
         ),
-        in_specs=[VMEM] * 5 + [ANY] * 2 + [VMEM] * 8 + [pl.BlockSpec(memory_space=pltpu.SMEM)] + [ANY] * 5,
+        in_specs=[VMEM] * 5 + [ANY] * 3 + [VMEM] * 8 + [pl.BlockSpec(memory_space=pltpu.SMEM)] + [ANY] * 5,
         out_specs=[VMEM] * 6 + [ANY] * 2,
         scratch_shapes=scratch,
         compiler_params=params(5, 62),
         name="back",
-    )(da2, h1, dy, x, gains, wo, qkv, qst, kst, vst, lse, cosine, sine, bias_p, bias_c, partner, a1, att, mpart, gu, gdown)
+    )(da2, h1, dy, x, gains, wo, q, kw, qst, kst, vst, lse, cosine, sine, bias_p, bias_c, partner, a1, att, mpart, gu, gdown)
 
 
 def widen_kernel(parts, gate, up):
@@ -1207,7 +1325,7 @@
 
     none = jnp.zeros((7, 128), F32)
     gains = jnp.concatenate([attn_gain.astype(F32)[None], none, mlp_gain.astype(F32)[None], none])
-    qkv = jnp.concatenate([query_weight, key_weight, value_weight], axis=1)
+    kv_weight = jnp.concatenate([key_weight, value_weight], axis=1)
     gu = jnp.concatenate([sliced(gate_weight), sliced(up_weight)], axis=1)
 
     y, zl = c // 2, c % 2
@@ -1234,15 +1352,17 @@
     bias_p = jnp.concatenate([bias_p, bias_p], axis=1).astype(F32)
     bias_c = jnp.concatenate([bias_c, bias_c], axis=1).astype(F32)
 
-    gains_all, qkv_all, wo_all, gu_all, dn_all, dy_all, normed, qst, kst, vst, attended, lse, hidden_state, normed_two = front(
-        tokens[0], gains, qkv, output_weight, gu, down_weight, cotangent[0], cosine_two, sine_two, bias_p, bias_c, mate[None]
+    gains_all, q_all, kv_all, wo_all, gu_all, dn_all, dy_all, normed, qst, kst, vst, attended, lse, hidden_state, normed_two = front(
+        tokens[0], gains, query_weight, kv_weight, output_weight, gu, down_weight, cotangent[0], cosine_two, sine_two, bias_p, bias_c, mate[None]
     )
     wo_all = wo_all.reshape(2048, 2048)
-
-    grad_normed_two, mixed_parts, gu_sum, dn_parts = feed_forward(normed_two, gu_all, dn_all, dy_all)
+    q_all = q_all.reshape(2048, 2048)
+    kv_all = kv_all.reshape(2048, 512)
+
+    grad_normed_two, mixed_parts, gu_sum, dn_parts = feed_forward(normed_two, gu_all, dn_all, dy_all, cotangent[0])
 
     mixed, tokens_grad, query_grad, kv_grad, o_grad, gain_grads, gu_grads, dn_grad = back(
-        grad_normed_two, hidden_state, cotangent[0], tokens[0], gains_all, wo_all, qkv_all, qst, kst, vst, lse,
+        grad_normed_two, hidden_state, cotangent[0], tokens[0], gains_all, wo_all, q_all, kv_all, qst, kst, vst, lse,
         cosine_two, sine_two, bias_p, bias_c, mate[None], normed, attended, mixed_parts, gu_sum, dn_parts,
     )
 

time: 400 us -> 361 us (0.902)
  Pallas kernels: 376 us -> 335 us
  other arithmetic: 10.4 us -> 15.4 us
    pallas_call x1, Pallas kernels: 122 us -> 99.4 us  [front(): pl.pallas_call(front_kernel, out_shape=(jax.ShapeDtypeStruct((16, 16, 128...]
    pallas_call x1, Pallas kernels: 152 us -> 134 us  [back(): pl.pallas_call(back_kernel, out_shape=(jax.ShapeDtypeStruct((128, 2048),...]
where the time goes in v5:
time: 361 us; the launch traced here: 359 us
  Pallas kernels  335 us (93%)
  other arithmetic  15.4 us (4%)
  local copies, waits for them, and re-layouts  6.04 us (2%)
    pallas_call x1, Pallas kernels, back(): pl.pallas_call(back_kernel, out_shape=(jax.ShapeDtypeStruct((128, 2048),...  134 us
    pallas_call x1, Pallas kernels, front(): pl.pallas_call(front_kernel, out_shape=(jax.ShapeDtypeStruct((16, 16, 128...  99.4 us
    pallas_call x1, Pallas kernels, feed_forward(): pl.pallas_call(mlp_kernel, out_shape=(jax.ShapeDtypeStruct((128, 2048), F...  94.6 us

profile of v5, /device:TPU:0, one launch (start us, length us, event | category | flops | bytes accessed | tf_op | source)
XLA Modules:
  0.0 359.2 jit_solution(14629672338705056228)
XLA Ops:
  0.6 0.0 copy-start
  0.8 0.1 stack.53
  0.9 0.1 stack.62
  1.0 0.7 bitcast_convert_fusion
  1.7 0.6 pad_maximum_fusion.6.gains_in
  2.3 0.0 copy-done
  2.3 0.1 constant_dynamic-slice_fusion
  2.4 0.1 copy.25
  2.5 0.1 copy.26
  2.6 0.6 gather_fusion
  3.1 0.1 broadcast_multiply_fusion.1
  3.2 0.6 slice.33
  5.8 0.2 convert_reduce_fusion
  5.9 0.1 mul.82
  6.0 0.7 iota_reduce_fusion
  6.7 0.1 add_compare_fusion
  6.8 0.1 broadcast_in_dim.74
  6.8 0.1 mul.83
  6.9 0.1 fusion.6
  7.1 0.1 le.36
  7.2 0.7 pad_maximum_fusion.5.bias_c
  7.9 0.1 broadcast_multiply_fusion
  8.0 0.3 sine_multiply_fusion
  8.3 0.8 pad_maximum_fusion.3
  9.0 1.5 pad_maximum_fusion.1.kw_in
  10.6 0.1 compare_select_fusion
  10.7 0.8 pad_maximum_fusion.bias_p
  11.6 1.2 constant_dynamic-slice_fusion.1
  12.8 0.8 fusion.2.gu_in
  13.6 99.4 %front.1 = (f32[16,16,128]{2,1,0:T(8,128)}, bf16[8,2,128,2048]{3,2,1,0:T(8,128)(2,1)}, bf16[8,2,128,512]{3,2,1,0:T(8,128)(2,1)}, bf16[8,2,128,2048]{3,2,1,0:T(8,...) custom-call(bf16[128,2048]{1,0:T(8,128)(2,1)} %bitcast.43, ...), custom_call_target="tpu_custom_call" | custom-call | tf_op jit(solution)/shard_map/front/pallas_call | solution.py:787
  112.9 94.6 %feed_forward.1 = (f32[128,2048]{1,0:T(8,128)}, bf16[8,128,2048]{2,1,0:T(8,128)(2,1)}, bf16[128,1536]{1,0:T(8,128)(2,1)}, bf16[8,352,256]{2,1,0:T(8,128)(2,1)}) custom-call(bf16[128,2048]{1,0:T(8,128)(2,1)} %get-tuple-element.42.a2, bf16[2048,1536]{1,0:T(8,128)(2,1)} %get-tuple-element.43.gu_in, bf16[352,256]{1,0:T(8,128)(2,1)} %get-tuple-element.44.dn_in, ...), custom_call_target="tpu_custom_call" | custom-call | tf_op jit(solution)/shard_map/feed_forward/pallas_call | solution.py:480
  207.5 134.2 %back.1 = (bf16[128,2048]{1,0:T(8,128)(2,1)}, bf16[128,2048]{1,0:T(8,128)(2,1)}, bf16[128,2048]{1,0:T(8,128)(2,1)}, bf16[128,512]{1,0:T(8,128)(2,1)}, bf16[128,2...) custom-call(f32[128,2048]{1,0:T(8,128)} %get-tuple-element.46.da2, ...), custom_call_target="tpu_custom_call" | custom-call | tf_op jit(solution)/shard_map/back/pallas_call | solution.py:1241
  341.7 0.0 copy-start.2
  341.7 1.3 slice_bitcast_fusion
  343.0 1.6 slice_convert_fusion
  344.6 2.1 convert_element_type.32
  346.7 2.1 convert_element_type.35
  348.8 0.0 copy-done.2
  348.8 0.0 copy-start.4
  348.8 0.0 copy-start.1
  348.8 1.9 convert_element_type.36
  350.8 0.0 copy-start.3
  350.8 6.8 %widen.1 = (f32[128,5632]{1,0:T(8,128)}, f32[128,5632]{1,0:T(8,128)}) custom-call(bf16[8,128,1536]{2,1,0:T(8,128)(2,1)} %get-tuple-element.67.parts), custom_call_target="tpu_custom_call" | custom-call | tf_op jit(solution)/shard_map/widen/pallas_call | solution.py:1275
  357.6 0.0 copy-done.4
  357.6 0.8 copy.29
  358.4 0.0 copy-done.3
  358.4 0.8 copy.30
  359.2 0.0 copy-done.1
  (12 shorter events, 0.1 us)
Async XLA Ops:
  0.6 1.7 copy-start
  341.7 7.1 %copy-start.2 = (bf16[352,2048]{1,0:T(8,128)(2,1)S(1)}, bf16[352,2048]{1,0:T(8,128)(2,1)}, u32[]{:S(2)}) copy-start(bf16[352,2048]{1,0:T(8,128)(2,1)} %get-tuple-element.70) | copy-start | bytes 4325380
  348.8 8.7 %copy-start.4 = (bf16[128,2048]{1,0:T(8,128)(2,1)S(1)}, bf16[128,2048]{1,0:T(8,128)(2,1)}, u32[]{:S(2)}) copy-start(bf16[128,2048]{1,0:T(8,128)(2,1)} %get-tuple-element.61) | copy-start | bytes 1572868
  348.8 10.3 %copy-start.1 = (s32[16,8,2]{0,2,1:T(2,128)S(1)}, s32[16,8,2]{0,2,1:T(2,128)}, u32[]{:S(2)}) copy-start(s32[16,8,2]{0,2,1:T(2,128)} %param.13) | copy-start | bytes 3076
  350.8 7.6 %copy-start.3 = (bf16[128,2048]{1,0:T(8,128)(2,1)S(1)}, bf16[128,2048]{1,0:T(8,128)(2,1)}, u32[]{:S(2)}) copy-start(bf16[128,2048]{1,0:T(8,128)(2,1)} %get-tuple-element.62) | copy-start | bytes 1572868

commit v6 on v5

--- a/solution.py
+++ b/solution.py
@@ -307,17 +307,111 @@
     return lax.dot_general(left, right, (((0,), (0,)), ((), ())), preferred_element_type=F32)
 
 
-def mlp_kernel(
-    a2, gu_in, dn_in, dy_in, dy_own,
+def load(src, dst, sem):
+    copy = pltpu.make_async_copy(src, dst, sem)
+    copy.start()
+    return copy
+
+
+def turned(values):
+    lane = lax.broadcasted_iota(jnp.int32, values.shape, 1)
+    low = lax.rem(lane, 64) < 32
+    return jnp.where(low, pltpu.roll(values, 96, 1), pltpu.roll(values, 32, 1))
+
+
+def pile(out, values, half):
+    for h in range(8):
+        out[pl.ds(64 * h, 64), :] = values[64 * half : 64 * half + 64, 64 * h : 64 * h + 64]
+
+
+def unpile(values):
+    flat = values.T
+    return [
+        jnp.concatenate([flat[128 * m : 128 * m + 64], flat[128 * m + 64 : 128 * m + 128]], axis=1)
+        for m in range(4)
+    ]
+
+
+def norm_scale(ref, out):
+    values = ref[...].astype(F32)
+    out[...] = lax.rsqrt(jnp.mean(values * values, axis=1, keepdims=True) + EPS)
+
+
+def place_tables(me, deal, freq, cosine, sine, bias_p, bias_c):
+    def block(slot, part):
+        return deal[(me.f * 8 + me.ctx_at(STEPS[slot], PAIRS[slot])) * 2 + part]
+
+    first, second = block(0, 0), block(0, 1)
+    odd = lax.rem(second, 2)
+    row = lax.broadcasted_iota(jnp.int32, (128, 128), 0)
+    lane = lax.broadcasted_iota(jnp.int32, (128, 128), 1)
+    position = jnp.where(row < 64, first * 64 + row, 448 + odd * 64 + row)
+    angle = position.astype(F32) * freq[...]
+    cosine[...] = jnp.cos(angle)
+    sine[...] = jnp.where(lax.rem(lane, 64) < 32, -jnp.sin(angle), jnp.sin(angle))
+    row, lane = row[:64], lax.rem(lane[:64], 64)
+    mate = jnp.int32(0)
+    for slot in range(8):
+        seen = block(slot, 0) * 64 + row <= first * 64 + lane
+        bias_p[pl.ds(64 * slot, 64), :] = jnp.where(seen, 0.0, -1e30)
+        if slot:
+            mate = mate + jnp.where(block(slot, 1) == second + 1 - 2 * odd, slot, 0)
+    bias_c[pl.ds(0, 64), :] = jnp.where(odd + 0 * row == 1, 0.0, -1e30)
+    bias_c[pl.ds(64, 64), :] = jnp.where(row <= lane, 0.0, -1e30)
+    return mate
+
+
+def find_mate(me, deal):
+    def block(slot):
+        return deal[(me.f * 8 + me.ctx_at(STEPS[slot], PAIRS[slot])) * 2 + 1]
+
+    second = block(0)
+    mate = jnp.int32(0)
+    for slot in range(1, 8):
+        mate = mate + jnp.where(block(slot) == second + 1 - 2 * lax.rem(second, 2), slot, 0)
+    return mate
+
+
+def fore_kernel(
+    x, attn_gain, mlp_gain, deal, freq, q_in, key_in, value_in, wo_in, gate_in, up_in, dn_in, dy_in,
+    gains, q_out, kw_out, wo_out, a1, qst, kst, vst, att, lse, h1, cosine, sine, bias_p, bias_c,
     da2_out, mpart, gu_out, gdown,
-    acts, gu, wd, dy, hid, dgu, dpart,
-    d_half, d_full, d_pair,
-    gsib, grecv, gown, gd, gdrecv,
-    g_half, g_full, g_pair,
-    ag0, ag1, dn0, dn1, dp0, dp1, rs0, rs1, sib0, sib1, local,
+    qw, kw, wo, kv_own, kv, sT, pT, scale, gu_win, dnp, acts, gu, wd, dy, hid, mstage,
+    d_half, d_full, d_pair, grecv, gdrecv, g_half, g_full, g_pair,
+    s0, s1, t0, t1, y0, y1, u0, u1, w0, w1, rs0, rs1, sib0, sib1, local, msem,
 ):
     me = Place()
-    greet(near(me.across_x) + near(me.across_y) + [me.sibling()])
+    greet_all(me)
+    def gains_at(dr, dp, er, ep, half):
+        return gains.at[me.fsdp_at(dr, dp), row_half(half, 16)]
+
+    def slot_at(ref, rows):
+        def loc(dr, dp, er, ep, half):
+            return ref.at[slot_of(dr - er, dp + ep), row_half(half, rows)]
+
+        return loc
+
+    def columns(first, index):
+        return pl.ds(pl.multiple_of(first + index * 128, 128), 128)
+
+    def plain(ref, count):
+        def loc(dr, dp, er, ep, half):
+            return ref.at[me.chip_at(dr, dp), me.co, row_half(half, 128), pl.ds(0, count)]
+
+        return loc
+
+    def strip_x(ref, first):
+        def loc(dr, dp, er, ep, half):
+            return ref.at[me.chip_at(dr, dp), me.co, row_half(half, 128), columns(first, me.c)]
+
+        return loc
+
+    def strip_y(ref, first):
+        def loc(dr, dp, er, ep, half):
+            chips = pl.ds(0, 8) if half is None else pl.ds(4 * half, 4)
+            return ref.at[chips, me.co, :, columns(first, me.ctx_at(dr, dp))]
+
+        return loc
 
     def wd_at(dr, dp, er, ep, half):
         size = 352 if half is None else 176
@@ -327,275 +421,76 @@
             pl.ds(pl.multiple_of(me.chip_at(dr, dp) * 256, 256), 256),
         ]
 
-    def acts_at(dr, dp, er, ep, half):
-        return acts.at[slot_of(dr - er, dp + ep), row_half(half, 128)]
-
-    task = Gather(me.across_y, a2, acts_at, (ag0, ag1), 0)
-    down = Gather(me.across_x, dn_in, wd_at, (dn0, dn1), 0, me.sibling(), (dp0, dp1))
-    down.start()
-    task.start()
+    def gu_at(dr, dp, er, ep, half):
+        size = 128 if half is None else 64
+        first = me.fsdp_at(dr, dp) * 128 + (0 if half is None else half * size)
+        return gu.at[pl.ds(pl.multiple_of(first, size), size)]
+
+    def over_x(own, loc, row, both=True):
+        own = loc(0, 0, 0, 0, None) if own is None else own
+        return Gather(me.across_x, own, loc, (s0, s1), row, me.sibling() if both else None, (t0, t1))
+
+    def over_y(own, loc, row, both=True):
+        own = loc(0, 0, 0, 0, None) if own is None else own
+        return Gather(me.across_y, own, loc, (y0, y1), row, me.sibling() if both else None, (u0, u1))
+
+    g = over_x(None, gains_at, 0)
+    k = over_x(None, plain(kw, 512), 1)
+    q = over_x(q_in.at[:, pl.ds(0, 1024)], plain(qw, 1024), 2)
+    qx = over_x(q_in.at[:, columns(1024, me.c)], strip_x(qw, 1024), 3, both=False)
+    o = over_x(wo_in.at[:, pl.ds(0, 1024)], plain(wo, 1024), 4)
+    ox = over_x(wo_in.at[:, columns(1024, me.c)], strip_x(wo, 1024), 5, both=False)
+    m = over_x(None, gu_at, 6)
+    dn = over_x(dnp, wd_at, 7)
+    qy = over_y(None, strip_y(qw, 1024), 0)
+    oy = over_y(None, strip_y(wo, 1024), 1)
+    dy_task = over_y(dy_in, slot_at(dy, 128), 2, both=False)
+    kv_task = over_y(kv_own, slot_at(kv, 128), 3, both=False)
+    a = over_y(None, slot_at(acts, 128), 4, both=False)
+    swap = Swap(me, dn_in.at[:, pl.ds(pl.multiple_of(me.c * 256, 256), 256)], dnp, (w0, w1), local.at[0])
+
+    own_kw = plain(kw, 512)(0, 0, 0, 0, None)
     loads = [
-        pltpu.make_async_copy(gu_in, gu, local.at[0]),
-        pltpu.make_async_copy(dn_in, wd_at(0, 0, 0, 0, None), local.at[1]),
-        pltpu.make_async_copy(dy_in.at[pl.ds(1, 7)], dy.at[pl.ds(1, 7)], local.at[2]),
-        pltpu.make_async_copy(dy_own, dy.at[0], local.at[3]),
+        load(key_in, own_kw.at[:, pl.ds(0, 256)], local.at[1]),
+        load(value_in, own_kw.at[:, pl.ds(256, 256)], local.at[2]),
     ]
-    for load in loads:
-        load.start()
-    acts[0] = a2[...]
-    wd[pl.ds(704, 64)] = jnp.zeros((64, 2048), BF)
-    down.turn(0)
-    down.pair()
-    down.last(0)
-    task.turn(0)
-    down.turn(1)
-    task.pair()
-    for load in loads:
-        load.wait()
-    down.last(1)
-    down.sync()
-
-    def group(g):
-        at = pl.ds(2 * g, 2)
-        rows = pl.ds(pl.multiple_of(256 * g, 256), 256)
-        for h in range(3):
-            first, second = pl.ds(256 * h, 256), pl.ds(768 + 256 * h, 256)
-            here = acts[at].reshape(256, 2048)
-            gate = dot_in(here, gu[:, first])
-            up = dot_in(here, gu[:, second])
-            back = dot_back(dy[at].reshape(256, 2048), wd[first, :])
-            curve = 1.0 / (1.0 + jnp.exp(-gate))
-            silu = gate * curve
-            hid[rows, first] = (silu * up).astype(BF)
-            dgu[rows, first] = (back * up * (curve + silu * (1.0 - curve))).astype(BF)
-            dgu[rows, second] = (back * silu).astype(BF)
-        for n in range(4):
-            wide = pl.ds(512 * n, 512)
-            mpart[at, :, wide] = dot_in(hid[rows, :], wd[:, wide]).astype(BF).reshape(2, 128, 512)
-            dpart[at, :, wide] = dot_back(dgu[rows, :], gu[wide, :]).astype(BF).reshape(2, 128, 512)
-
-    @pl.loop(0, 4)
-    def _(g):
-        @pl.when(g == 2)
-        def _():
-            task.turn(1)
-
-        @pl.when(g == 3)
-        def _():
-            task.last(0)
-            task.last(1)
-
-        group(g)
-
-    grad = Scatter(me.across_y, lambda slot: dpart.at[slot], 128, d_half, d_full, d_pair, (rs0, rs1), 0)
-    first = Scatter(me.across_x, lambda slot: gown.at[slot], 128, g_half, g_full, g_pair, (rs0, rs1), 1)
-    grad.start()
-
-    def weight_terms(t, core):
-        at = pl.multiple_of((chip_of(me, t) * 2 + core) * 128, 128)
-        left = acts[:, :, pl.ds(at, 128)].reshape(1024, 128)
-        return dot_rows(left, dgu[...])
-
-    def gu_to(t):
-        return send(gsib.at[t], grecv.at[t], (sib0, sib1), 8 + t, me.sibling())
-
-    @pl.loop(0, 8)
-    def _(i):
-        gsib[7 - i] = weight_terms(7 - i, 1 - me.co).astype(BF)
-        gu_to(7 - i).start()
-
-    grad.turn(1)
-
-    @pl.loop(0, 8)
-    def _(i):
-        gu_to(7 - i).wait_recv()
-        gown[7 - i] = (weight_terms(7 - i, me.co) + grecv[7 - i].astype(F32)).astype(BF)
-
-        @pl.when(i == 1)
-        def _():
-            first.start()
-
-    grad.turn(0)
-    first.turn(1)
-
-    def down_to(t):
-        mine = pl.ds(pl.multiple_of((1 - me.co) * 352, 16), 352)
-        return send(gd.at[t, mine], gdrecv.at[t], (sib0, sib1), t, me.sibling())
-
-    @pl.loop(0, 8)
-    def _(t):
-        at = pl.multiple_of(chip_of(me, t) * 256, 256)
-        gd[t] = dot_rows(hid[...], dy[:, :, pl.ds(at, 256)].reshape(1024, 256)).astype(BF)
-        down_to(t).start()
-
-    first.turn(0)
-    grad.pair()
-    first.pair()
-
-    @pl.loop(0, 8)
-    def _(t):
-        down_to(t).wait_recv()
-
-        @pl.loop(0, 22)
+    kept = {task: load(task.own, task.loc(0, 0, 0, 0, None), local.at[3 + i]) for i, task in enumerate((q, qx, o, ox, dy_task))}
+    window = pl.ds(pl.multiple_of(me.y * 1408 + me.zl * 640, 128), 768)
+    loads.append(load(gate_in.at[:, window], gu_win.at[0], local.at[8]))
+    loads.append(load(up_in.at[:, window], gu_win.at[1], local.at[9]))
+    gains[me.f] = jnp.zeros((16, 128), F32)
+    gains[me.f, pl.ds(0, 1), :] = attn_gain[...].astype(F32)
+    gains[me.f, pl.ds(8, 1), :] = mlp_gain[...].astype(F32)
+
+    dpart = wo.at[:, 0]
+    dgu = wo.at[:, 1, :, pl.ds(0, 1536)]
+    gsib = qw.at[:, 0, :, pl.ds(0, 1536)]
+    gown = qw.at[:, 1, :, pl.ds(0, 1536)]
+
+    def gd(t):
+        rows = pl.ds(pl.multiple_of(lax.div(t, 6) * 768, 768), 768)
+        return gu.at[rows, pl.ds(pl.multiple_of(lax.rem(t, 6) * 256, 256), 256)]
+
+    saved = []
+
+    def put_gate_up():
+        loads[2].wait()
+        loads[3].wait()
+
+        @pl.loop(0, 8)
         def _(i):
-            mine = gd[t, pl.ds(pl.multiple_of(me.co * 352 + i * 16, 16), 16)].astype(F32)
-            at = pl.ds(pl.multiple_of(i * 16, 16), 16)
-            gdown[t, at] = (mine + gdrecv[t, at].astype(F32)).astype(BF)
-
-    first.finish(gu_out)
-    grad.finish(da2_out)
-    for job in (task, down, grad, first):
-        job.end()
-
-    @pl.loop(0, 8)
-    def _(t):
-        gu_to(t).wait_send()
-        down_to(t).wait_send()
-
-
-def feed_forward(a2, gu, dn, dy, dy_own):
-    scratch = [
-        pltpu.VMEM((8, 128, 2048), BF),
-        pltpu.VMEM((2048, 1536), BF),
-        pltpu.VMEM((768, 2048), BF),
-        pltpu.VMEM((8, 128, 2048), BF),
-        pltpu.VMEM((1024, 768), BF),
-        pltpu.VMEM((1024, 1536), BF),
-        pltpu.VMEM((8, 128, 2048), BF),
-        *scatter_buffers(128, 2048),
-        pltpu.VMEM((8, 128, 1536), BF),
-        pltpu.VMEM((8, 128, 1536), BF),
-        pltpu.VMEM((8, 128, 1536), BF),
-        pltpu.VMEM((8, 768, 256), BF),
-        pltpu.VMEM((8, 352, 256), BF),
-        *scatter_buffers(128, 1536),
-        *dma_sems(1, 9),
-        *dma_sems(1, 9),
-        *dma_sems(1, 10),
-        *dma_sems(2, 9),
-        pltpu.SemaphoreType.DMA((16,)),
-        pltpu.SemaphoreType.DMA((16,)),
-        pltpu.SemaphoreType.DMA((4,)),
-    ]
-    return pl.pallas_call(
-        mlp_kernel,
-        out_shape=(
-            jax.ShapeDtypeStruct((128, 2048), F32),
-            jax.ShapeDtypeStruct((8, 128, 2048), BF),
-            jax.ShapeDtypeStruct((128, 1536), BF),
-            jax.ShapeDtypeStruct((8, 352, 256), BF),
-        ),
-        in_specs=[VMEM, ANY, ANY, ANY, ANY],
-        out_specs=[VMEM] * 4,
-        scratch_shapes=scratch,
-        compiler_params=params(4, 62),
-        name="feed_forward",
-    )(a2, gu, dn, dy, dy_own)
-
-
-def load(src, dst, sem):
-    copy = pltpu.make_async_copy(src, dst, sem)
-    copy.start()
-    return copy
-
-
-def turned(values):
-    lane = lax.broadcasted_iota(jnp.int32, values.shape, 1)
-    low = lax.rem(lane, 64) < 32
-    return jnp.where(low, pltpu.roll(values, 96, 1), pltpu.roll(values, 32, 1))
-
-
-def pile(out, values, half):
-    for h in range(8):
-        out[pl.ds(64 * h, 64), :] = values[64 * half : 64 * half + 64, 64 * h : 64 * h + 64]
-
-
-def unpile(values):
-    flat = values.T
-    return [
-        jnp.concatenate([flat[128 * m : 128 * m + 64], flat[128 * m + 64 : 128 * m + 128]], axis=1)
-        for m in range(4)
-    ]
-
-
-def norm_scale(ref, out):
-    values = ref[...].astype(F32)
-    out[...] = lax.rsqrt(jnp.mean(values * values, axis=1, keepdims=True) + EPS)
-
-
-def front_kernel(
-    x, gains_in, q_in, kw_in, wo_in, gu_in, dn_in, dy_in, cosine, sine, bias_p, bias_c, partner,
-    gains, q_out, kw_out, wo_out, gu_all, dn_out, dy_all, a1, qst, kst, vst, att, lse, h1, a2,
-    qw, kw, wo, kv_own, kv, sT, pT, scale, gu_own,
-    s0, s1, t0, t1, y0, y1, u0, u1, w0, w1, local,
-):
-    me = Place()
-    greet_all(me)
-    swap = Swap(me, dn_in.at[:, pl.ds(pl.multiple_of(me.c * 256, 256), 256)], dn_out, (w0, w1), local.at[10])
-
-    def rows_at(ref, rows):
-        def loc(dr, dp, er, ep, half):
-            size = rows if half is None else rows // 2
-            first = me.fsdp_at(dr, dp) * rows + (0 if half is None else half * size)
-            return ref.at[pl.ds(pl.multiple_of(first, size), size)]
-
-        return loc
-
-    def gains_at(dr, dp, er, ep, half):
-        return gains.at[me.fsdp_at(dr, dp), row_half(half, 16)]
-
-    def slot_at(ref, rows):
-        def loc(dr, dp, er, ep, half):
-            return ref.at[slot_of(dr - er, dp + ep), row_half(half, rows)]
-
-        return loc
-
-    def columns(first, index):
-        return pl.ds(pl.multiple_of(first + index * 128, 128), 128)
-
-    def plain(ref, count):
-        def loc(dr, dp, er, ep, half):
-            return ref.at[me.chip_at(dr, dp), me.co, row_half(half, 128), pl.ds(0, count)]
-
-        return loc
-
-    def strip_x(ref, first):
-        def loc(dr, dp, er, ep, half):
-            return ref.at[me.chip_at(dr, dp), me.co, row_half(half, 128), columns(first, me.c)]
-
-        return loc
-
-    def strip_y(ref, first):
-        def loc(dr, dp, er, ep, half):
-            chips = pl.ds(0, 8) if half is None else pl.ds(4 * half, 4)
-            return ref.at[chips, me.co, :, columns(first, me.ctx_at(dr, dp))]
-
-        return loc
-
-    def over_x(own, loc, row, both=True):
-        return Gather(me.across_x, own, loc, (s0, s1), row, me.sibling() if both else None, (t0, t1))
-
-    def over_y(loc, row):
-        own = loc(0, 0, 0, 0, None)
-        return Gather(me.across_y, own, loc, (y0, y1), row, me.sibling(), (u0, u1))
-
-    g = over_x(gains_in, gains_at, 0)
-    k = over_x(kw_in, plain(kw, 512), 6)
-    q = over_x(q_in.at[:, pl.ds(0, 1024)], plain(qw, 1024), 1)
-    qx = over_x(q_in.at[:, columns(1024, me.c)], strip_x(qw, 1024), 2, both=False)
-    o = over_x(wo_in.at[:, pl.ds(0, 1024)], plain(wo, 1024), 3)
-    ox = over_x(wo_in.at[:, columns(1024, me.c)], strip_x(wo, 1024), 4, both=False)
-    m = over_x(gu_in, rows_at(gu_all, 128), 5)
-    qy = over_y(strip_y(qw, 1024), 0)
-    oy = over_y(strip_y(wo, 1024), 1)
-    dy = Gather(me.across_y, dy_in, slot_at(dy_all, 128), (y0, y1), 2)
-    kv_task = Gather(me.across_y, kv_own, slot_at(kv, 128), (y0, y1), 3)
-    kept = [load(task.own, task.loc(0, 0, 0, 0, None), local.at[i]) for i, task in enumerate((g, q, qx, o, ox, k))]
-    kept.append(load(gu_in, gu_own, local.at[6]))
+            rows = pl.ds(pl.multiple_of(16 * i, 16), 16)
+            out = pl.ds(pl.multiple_of(me.f * 128 + 16 * i, 16), 16)
+            for w in (0, 1):
+                values = gu_win[w, rows].astype(F32)
+                values = jnp.where(me.zl == 1, pltpu.roll(values, 704, 1), values)
+                lane = lax.broadcasted_iota(jnp.int32, values.shape, 1)
+                gu[out, 768 * w : 768 * w + 768] = jnp.where(lane < 704, values, 0.0).astype(BF)
+
+        wd[pl.ds(704, 64)] = jnp.zeros((64, 2048), BF)
 
     def normed():
         norm_scale(x, scale)
-        kept[0].wait()
 
         @pl.loop(0, 16)
         def _(i):
@@ -603,7 +498,6 @@
             a1[:, at] = (x[:, at].astype(F32) * scale[...] * gains[i, pl.ds(0, 1), :]).astype(BF)
 
     def project_kv():
-        kept[5].wait()
         raw = dot_in(a1[...], kw[...].reshape(2048, 512))
         for i in range(2):
             part = raw[:, 128 * i : 128 * i + 128]
@@ -623,8 +517,7 @@
                         rows = pl.ds(64 * (2 * i + e), 64)
                         qst[n, half, rows, :] = part[64 * half : 64 * half + 64, 64 * e : 64 * e + 64]
 
-    def collect_kv():
-        mate = partner[0]
+    def collect_kv(mate):
         beside = kv[mate]
         for out, base in ((kst, 0), (vst, 256)):
             for n in range(4):
@@ -674,137 +567,282 @@
         @pl.loop(0, 16)
         def _(i):
             at = pl.ds(pl.multiple_of(i * 128, 128), 128)
-            a2[:, at] = (h1[:, at] * scale[...] * gains[i, pl.ds(8, 1), :]).astype(BF)
+            acts[0, :, at] = (h1[:, at] * scale[...] * gains[i, pl.ds(8, 1), :]).astype(BF)
+
+    def mpart_copy(n):
+        return pltpu.make_async_copy(mstage, mpart.at[pl.ds(2 * n, 2)], msem)
+
+    def group(n):
+        at = pl.ds(2 * n, 2)
+        rows = pl.ds(pl.multiple_of(256 * n, 256), 256)
+        for h in range(3):
+            first, second = pl.ds(256 * h, 256), pl.ds(768 + 256 * h, 256)
+            here = acts[at].reshape(256, 2048)
+            gate = dot_in(here, gu[:, first])
+            up = dot_in(here, gu[:, second])
+            back = dot_back(dy[at].reshape(256, 2048), wd[first, :])
+            curve = 1.0 / (1.0 + jnp.exp(-gate))
+            silu = gate * curve
+            hid[rows, first] = (silu * up).astype(BF)
+            dgu[at, :, first] = (back * up * (curve + silu * (1.0 - curve))).astype(BF).reshape(2, 128, 256)
+            dgu[at, :, second] = (back * silu).astype(BF).reshape(2, 128, 256)
+
+        @pl.when(n > 0)
+        def _():
+            mpart_copy(n - 1).wait()
+
+        for i in range(4):
+            wide = pl.ds(512 * i, 512)
+            grads = dgu[at].reshape(256, 1536)
+            dpart[at, :, wide] = dot_back(grads, gu[wide, :]).astype(BF).reshape(2, 128, 512)
+            mstage[:, :, wide] = dot_in(hid[rows, :], wd[:, wide]).astype(BF).reshape(2, 128, 512)
+        mpart_copy(n).start()
+
+    d = Scatter(me.across_y, lambda slot: dpart.at[slot], 128, d_half, d_full, d_pair, (rs0, rs1), 0)
+    gjob = Scatter(me.across_x, lambda slot: gown.at[slot], 128, g_half, g_full, g_pair, (rs0, rs1), 1)
+
+    def weight_terms(t, core):
+        at = pl.multiple_of((chip_of(me, t) * 2 + core) * 128, 128)
+        left = acts[:, :, pl.ds(at, 128)].reshape(1024, 128)
+        return dot_rows(left, dgu[...].reshape(1024, 1536))
+
+    def gu_to(t):
+        return send(gsib.at[t], grecv.at[t], (sib0, sib1), 8 + t, me.sibling())
+
+    def down_to(t):
+        mine = pl.ds(pl.multiple_of((1 - me.co) * 352, 16), 352)
+        return send(gd(t).at[mine], gdrecv.at[t], (sib0, sib1), t, me.sibling())
+
+    def terms_for_sibling():
+        @pl.loop(0, 8)
+        def _(i):
+            gsib[7 - i] = weight_terms(7 - i, 1 - me.co).astype(BF)
+            gu_to(7 - i).start()
+
+    def own_terms(start, stop):
+        @pl.loop(start, stop)
+        def _(i):
+            gu_to(7 - i).wait_recv()
+            gown[7 - i] = (weight_terms(7 - i, me.co) + grecv[7 - i].astype(F32)).astype(BF)
+
+    def down_terms():
+        @pl.loop(0, 8)
+        def _(t):
+            at = pl.multiple_of(chip_of(me, t) * 256, 256)
+            gd(t)[...] = dot_rows(hid[...], dy[:, :, pl.ds(at, 256)].reshape(1024, 256)).astype(BF)
+            down_to(t).start()
+
+    def down_sums():
+        @pl.loop(0, 8)
+        def _(t):
+            down_to(t).wait_recv()
+
+            @pl.loop(0, 22)
+            def _(i):
+                mine = gd(t)[pl.ds(pl.multiple_of(me.co * 352 + i * 16, 16), 16)].astype(F32)
+                at = pl.ds(pl.multiple_of(i * 16, 16), 16)
+                gdown[t, at] = (mine + gdrecv[t, at].astype(F32)).astype(BF)
 
     qx.start()
+    g.start()
+    dy_task.start()
+    ox.start()
+    qx.pair()
+    g.turn(0)
+    qx.turn(0)
+    loads[0].wait()
+    loads[1].wait()
     k.start()
-    g.start()
-    ox.start()
-    dy.start()
-    qx.pair()
-    qx.turn(0)
+    qx.turn(1)
+    qx.last(0)
+    g.pair()
+    q.start()
+    mate = place_tables(me, deal, freq, cosine, sine, bias_p, bias_c)
+    qx.last(1)
+    g.turn(1)
+    g.last(0)
+    kept[qx].wait()
+    qy.start()
+    o.start()
     k.turn(0)
-    g.pair()
-    qx.turn(1)
+    swap.start()
+    dy_task.pair()
+    ox.turn(0)
+    k.pair()
+    qy.turn(0)
+    q.turn(0)
+    g.last(1)
+    k.turn(1)
+    o.turn(0)
+    ox.last(0)
+    qy.pair()
+    k.last(0)
+    g.sync()
+    normed()
     ox.pair()
-    k.pair()
-    k.last(0)
-    qx.last(0)
-    g.turn(0)
-    g.turn(1)
-    ox.turn(0)
-    qx.last(1)
+    swap.wait()
+    kept[dn] = load(dnp, wd_at(0, 0, 0, 0, None), local.at[13])
+    dn.start()
+    k.last(1)
     ox.turn(1)
-    kept[2].wait()
-    qy.start()
-    q.start()
-    dy.pair()
-    k.turn(1)
-    o.start()
-    g.last(0)
-    m.start()
-    g.last(1)
-    ox.last(0)
-    k.last(1)
-    ox.last(1)
-    g.sync()
-    qy.pair()
+    q.pair()
     k.sync()
-    q.turn(0)
-    normed()
     project_kv()
-    qy.turn(0)
-    o.turn(0)
-    kept[4].wait()
-    oy.start()
+    kv_task.start()
     o.pair()
     qy.turn(1)
-    q.pair()
-    kv_task.start()
+    kv_task.pair()
+    ox.last(1)
+    qy.last(0)
+    q.turn(1)
+    qy.last(1)
+    kv_task.turn(0)
+    kept[ox].wait()
+    oy.start()
+    q.last(0)
+    put_gate_up()
+    dn.turn(0)
+    kv_task.last(0)
+    kv_task.turn(1)
+    o.turn(1)
     o.last(0)
-    qy.last(0)
+    q.last(1)
+    dn.pair()
     oy.pair()
-    q.last(0)
-    o.turn(1)
-    q.turn(1)
-    m.pair()
-    kv_task.pair()
+    qy.sync()
+    m.start()
+    q.sync()
+    kept[q].wait()
+    saved.append(load(qw, q_out, local.at[10]))
+    saved.append(load(kw, kw_out, local.at[11]))
+    project_q()
+    kv_task.last(1)
     oy.turn(0)
-    q.last(1)
-    qy.last(1)
-    kv_task.turn(1)
-    kv_task.turn(0)
-    o.last(1)
-    oy.turn(1)
-    m.turn(0)
-    dy.turn(0)
-    dy.turn(1)
-    q.sync()
-    qy.sync()
-    kept[1].wait()
-    kept[6].wait()
-    saved = [load(qw, q_out, local.at[7]), load(kw, kw_out, local.at[8])]
-    saved.append(load(gu_own, m.loc(0, 0, 0, 0, None), local.at[6]))
-    project_q()
-    swap.start()
-    kv_task.last(1)
-    kv_task.last(0)
-    oy.last(0)
-    collect_kv()
-    m.turn(1)
+    collect_kv(mate)
 
     @pl.loop(0, 4)
     def _(n):
         attend(n, 0)
         attend(n, 1)
 
+        @pl.when(n == 0)
+        def _():
+            o.last(1)
+            oy.turn(1)
+            dn.turn(1)
+
         @pl.when(n == 1)
         def _():
-            oy.last(1)
+            dy_task.turn(0)
+            oy.last(0)
+            dy_task.turn(1)
+            dn.last(0)
 
         @pl.when(n == 2)
         def _():
-            o.sync()
-
+            oy.last(1)
+
+    o.sync()
+    m.turn(0)
     oy.sync()
-    m.last(0)
-    m.last(1)
-    dy.last(0)
-    kept[3].wait()
-    saved.append(load(wo, wo_out, local.at[9]))
+    kept[o].wait()
+    saved.append(load(wo, wo_out, local.at[12]))
     project_o()
     normed_two()
+    a.start()
+    m.pair()
+    m.turn(1)
+    m.last(0)
+    dn.last(1)
+    dy_task.last(0)
+    a.pair()
+    dy_task.last(1)
+    m.last(1)
+    a.turn(0)
     m.sync()
-    dy.last(1)
-    for task in (g, k, q, qx, o, ox, m, qy, oy, dy, kv_task):
+    dn.sync()
+
+    for task in (o, ox, oy):
         task.end()
-    swap.wait()
-    for copy in saved:
-        copy.wait()
-
-
-def front(x, gains, q, kw, wo, gu, dn, dy, cosine, sine, bias_p, bias_c, partner):
+    saved[2].wait()
+    kept[dn].wait()
+    kept[dy_task].wait()
+
+    @pl.loop(0, 4)
+    def _(n):
+        group(n)
+
+        @pl.when(n == 0)
+        def _():
+            a.turn(1)
+
+        @pl.when(n == 1)
+        def _():
+            a.last(0)
+
+        @pl.when(n == 2)
+        def _():
+            a.last(1)
+
+    d.start()
+    for task in (q, qx, qy):
+        task.end()
+    saved[0].wait()
+    terms_for_sibling()
+    d.turn(1)
+    own_terms(0, 2)
+    gjob.start()
+    d.turn(0)
+    own_terms(2, 4)
+    gjob.turn(1)
+    d.pair()
+    own_terms(4, 8)
+    m.end()
+    down_terms()
+    gjob.turn(0)
+    gjob.pair()
+    d.finish(da2_out)
+    down_sums()
+    gjob.finish(gu_out)
+    for task in (g, k, dn, dy_task, kv_task, a, d, gjob):
+        task.end()
+    saved[1].wait()
+    mpart_copy(3).wait()
+
+    @pl.loop(0, 8)
+    def _(t):
+        gu_to(t).wait_send()
+        down_to(t).wait_send()
+
+
+def fore(x, attn_gain, mlp_gain, deal, freq, q, key, value, wo, gate, up, dn, dy):
+    shape = jax.ShapeDtypeStruct
+    smem = pl.BlockSpec(memory_space=pltpu.SMEM)
     return pl.pallas_call(
-        front_kernel,
+        fore_kernel,
         out_shape=(
-            jax.ShapeDtypeStruct((16, 16, 128), F32),
-            jax.ShapeDtypeStruct((8, 2, 128, 2048), BF),
-            jax.ShapeDtypeStruct((8, 2, 128, 512), BF),
-            jax.ShapeDtypeStruct((8, 2, 128, 2048), BF),
-            jax.ShapeDtypeStruct((2048, 1536), BF),
-            jax.ShapeDtypeStruct((352, 256), BF),
-            jax.ShapeDtypeStruct((8, 128, 2048), BF),
-            jax.ShapeDtypeStruct((128, 2048), BF),
-            jax.ShapeDtypeStruct((4, 2, 512, 64), BF),
-            jax.ShapeDtypeStruct((4, 640, 64), BF),
-            jax.ShapeDtypeStruct((4, 640, 64), BF),
-            jax.ShapeDtypeStruct((128, 2048), BF),
-            jax.ShapeDtypeStruct((8, 1, 512), F32),
-            jax.ShapeDtypeStruct((128, 2048), F32),
-            jax.ShapeDtypeStruct((128, 2048), BF),
+            shape((16, 16, 128), F32),
+            shape((8, 2, 128, 2048), BF),
+            shape((8, 2, 128, 512), BF),
+            shape((8, 2, 128, 2048), BF),
+            shape((128, 2048), BF),
+            shape((4, 2, 512, 64), BF),
+            shape((4, 640, 64), BF),
+            shape((4, 640, 64), BF),
+            shape((128, 2048), BF),
+            shape((8, 1, 512), F32),
+            shape((128, 2048), F32),
+            shape((128, 128), F32),
+            shape((128, 128), F32),
+            shape((512, 128), F32),
+            shape((128, 128), F32),
+            shape((128, 2048), F32),
+            shape((8, 128, 2048), BF),
+            shape((128, 1536), BF),
+            shape((8, 352, 256), BF),
         ),
-        in_specs=[VMEM] + [ANY] * 7 + [VMEM] * 4 + [pl.BlockSpec(memory_space=pltpu.SMEM)],
-        out_specs=[VMEM] + [ANY] * 6 + [VMEM] * 8,
+        in_specs=[VMEM] * 3 + [smem, VMEM] + [ANY] * 8,
+        out_specs=[VMEM] + [ANY] * 3 + [VMEM] * 12 + [ANY] + [VMEM] * 2,
         scratch_shapes=[
             pltpu.VMEM((8, 2, 128, 2048), BF),
             pltpu.VMEM((8, 2, 128, 512), BF),
@@ -814,22 +852,37 @@
             pltpu.VMEM((640, 512), F32),
             pltpu.VMEM((640, 512), BF),
             pltpu.VMEM((128, 1), F32),
-            pltpu.VMEM((128, 1536), BF),
-            *dma_sems(7, 9),
-            *dma_sems(7, 10),
-            *dma_sems(4, 9),
+            pltpu.VMEM((2, 128, 768), BF),
+            pltpu.VMEM((352, 256), BF),
+            pltpu.VMEM((8, 128, 2048), BF),
+            pltpu.VMEM((2048, 1536), BF),
+            pltpu.VMEM((768, 2048), BF),
+            pltpu.VMEM((8, 128, 2048), BF),
+            pltpu.VMEM((1024, 768), BF),
+            pltpu.VMEM((2, 128, 2048), BF),
+            *scatter_buffers(128, 2048),
+            pltpu.VMEM((8, 128, 1536), BF),
+            pltpu.VMEM((8, 352, 256), BF),
+            *scatter_buffers(128, 1536),
+            *dma_sems(8, 9),
+            *dma_sems(8, 10),
+            *dma_sems(5, 9),
             *dma_sems(2, 10),
             pltpu.SemaphoreType.DMA,
             pltpu.SemaphoreType.DMA,
-            pltpu.SemaphoreType.DMA((11,)),
+            *dma_sems(2, 9),
+            pltpu.SemaphoreType.DMA((16,)),
+            pltpu.SemaphoreType.DMA((16,)),
+            pltpu.SemaphoreType.DMA((14,)),
+            pltpu.SemaphoreType.DMA,
         ],
-        compiler_params=params(1, 62),
-        name="front",
-    )(x, gains, q, kw, wo, gu, dn, dy, cosine, sine, bias_p, bias_c, partner)
+        compiler_params=params(1, 63),
+        name="fore",
+    )(x, attn_gain, mlp_gain, deal, freq, q, key, value, wo, gate, up, dn, dy)
 
 
 def back_kernel(
-    da2, h1, dy, x, gains, wo_in, q_in, kw_in, qst, kst, vst, lse, cosine, sine, bias_p, bias_c, partner,
+    da2, h1, dy, x, gains, wo_in, q_in, kw_in, qst, kst, vst, lse, cosine, sine, bias_p, bias_c, deal,
     a1_in, att_in, mpart_in, gu, gdown_in,
     mixed, tokens_grad, q_out, kv_out, o_out, gains_out, gu_all, dn_all,
     a1s, atts, dqkvs, datts, grow, dh1, gown, gsib, mpart, stream, dost, sT, dT, pT, dsT,
@@ -981,7 +1034,7 @@
         terms(a1s, dqkvs.at[:, pl.ds(2048, 512)], kp, k_job)
 
     def kv_blocks():
-        mate = partner[0]
+        mate = find_mate(me, deal)
         for out, base in ((kgrad, 0), (vgrad, 256)):
             for n in range(4):
                 first = base + 64 * n
@@ -1183,7 +1236,7 @@
         copy.wait()
 
 
-def back(da2, h1, dy, x, gains, wo, q, kw, qst, kst, vst, lse, cosine, sine, bias_p, bias_c, partner, a1, att, mpart, gu, gdown):
+def back(da2, h1, dy, x, gains, wo, q, kw, qst, kst, vst, lse, cosine, sine, bias_p, bias_c, deal, a1, att, mpart, gu, gdown):
     scratch = [
         pltpu.VMEM((256, 2048), BF),
         pltpu.VMEM((256, 2048), BF),
@@ -1255,7 +1308,7 @@
         scratch_shapes=scratch,
         compiler_params=params(5, 62),
         name="back",
-    )(da2, h1, dy, x, gains, wo, q, kw, qst, kst, vst, lse, cosine, sine, bias_p, bias_c, partner, a1, att, mpart, gu, gdown)
+    )(da2, h1, dy, x, gains, wo, q, kw, qst, kst, vst, lse, cosine, sine, bias_p, bias_c, deal, a1, att, mpart, gu, gdown)
 
 
 def widen_kernel(parts, gate, up):
@@ -1280,25 +1333,6 @@
         out_specs=[block, block],
         name="widen",
     )(parts)
-
-
-def tables(position):
-    freq = BASE ** (-(jnp.arange(HEAD_DIM // 2, dtype=jnp.float32) * 2.0) / HEAD_DIM)
-    angle = position.astype(jnp.float32)[:, None] * freq[None, :]
-    angle = jnp.concatenate([angle, angle], axis=-1)
-    return (jnp.cos(angle), jnp.sin(angle))
-
-
-def timeline(table_flat, total_len, row_count):
-    everywhere = jnp.arange(total_len, dtype=jnp.int32)
-    half_len = row_count // 2
-    moment = jnp.repeat(table_flat, half_len) * half_len + everywhere % half_len
-    prompt_len = total_len // 2
-    cont_len = total_len // 8
-    later = moment >= prompt_len
-    segment = jnp.where(later, 1 + (moment - prompt_len) // cont_len, 0)
-    position = jnp.where(later, prompt_len + (moment - prompt_len) % cont_len, moment)
-    return (segment, position)
 
 
 def on_device(
@@ -1315,57 +1349,21 @@
     down_weight,
     cotangent,
 ):
-    row_count = tokens.shape[1]
-    c = lax.axis_index("ctx")
-    f = lax.axis_index("fsdp")
-    full_len = row_count * 8
-
-    def sliced(weight):
-        return jnp.pad(lax.dynamic_slice_in_dim(weight, c * 704, 704, 1), ((0, 0), (0, 64)))
-
-    none = jnp.zeros((7, 128), F32)
-    gains = jnp.concatenate([attn_gain.astype(F32)[None], none, mlp_gain.astype(F32)[None], none])
-    kv_weight = jnp.concatenate([key_weight, value_weight], axis=1)
-    gu = jnp.concatenate([sliced(gate_weight), sliced(up_weight)], axis=1)
-
-    y, zl = c // 2, c % 2
-    order = jnp.stack([((y + STEPS[s]) % 4) * 2 + (zl + PAIRS[s]) % 2 for s in range(8)])
-    deal = jnp.take(lax.dynamic_index_in_dim(block_deal, f, 0, keepdims=False), order, axis=0)
-    mate_block = 8 + (deal[0, 1] - 8 + 1 - 2 * ((deal[0, 1] - 8) % 2))
-    mate = jnp.argmax((deal[:, 1] == mate_block).astype(jnp.int32)).astype(jnp.int32)
-    segment, position = timeline(deal.reshape(-1), full_len, row_count)
-    own_segment, own_position = segment[:row_count], position[:row_count]
-    cosine, sine = tables(own_position)
-    sign = jnp.where(jnp.arange(HEAD_DIM) < 32, -1.0, 1.0)
-    cosine_two = jnp.concatenate([cosine, cosine], axis=1)
-    sine_two = jnp.concatenate([sine * sign, sine * sign], axis=1)
-    prompt_position = position.reshape(8, 2, 64)[:, 0].reshape(512)
-    bias_p = jnp.where(prompt_position[:, None] <= own_position[None, :64], 0.0, -1e30)
-    mate_seen = deal[0, 1] > mate_block
-    step = jnp.arange(64)
-    bias_c = jnp.concatenate(
-        [
-            jnp.broadcast_to(jnp.where(mate_seen, 0.0, -1e30), (64, 64)),
-            jnp.where(step[:, None] <= step[None, :], 0.0, -1e30),
-        ]
+    freq = BASE ** (-(jnp.arange(HEAD_DIM // 2, dtype=F32) * 2.0) / HEAD_DIM)
+    freq = jnp.concatenate([freq] * 4)[None]
+    deal = block_deal.reshape(256)
+    (
+        gains, q_all, kv_all, wo_all, a1, qst, kst, vst, att, lse, h1, cosine, sine, bias_p, bias_c,
+        da2, mixed_parts, gu_sum, dn_parts,
+    ) = fore(
+        tokens[0], attn_gain[None], mlp_gain[None], deal, freq, query_weight, key_weight, value_weight, output_weight,
+        gate_weight, up_weight, down_weight, cotangent[0],
     )
-    bias_p = jnp.concatenate([bias_p, bias_p], axis=1).astype(F32)
-    bias_c = jnp.concatenate([bias_c, bias_c], axis=1).astype(F32)
-
-    gains_all, q_all, kv_all, wo_all, gu_all, dn_all, dy_all, normed, qst, kst, vst, attended, lse, hidden_state, normed_two = front(
-        tokens[0], gains, query_weight, kv_weight, output_weight, gu, down_weight, cotangent[0], cosine_two, sine_two, bias_p, bias_c, mate[None]
+    mixed, tokens_grad, query_grad, kv_grad, o_grad, gain_grads, gu_grads, dn_grad = back(
+        da2, h1, cotangent[0], tokens[0], gains, wo_all.reshape(2048, 2048), q_all.reshape(2048, 2048),
+        kv_all.reshape(2048, 512), qst, kst, vst, lse, cosine, sine, bias_p, bias_c, deal, a1, att, mixed_parts,
+        gu_sum, dn_parts,
     )
-    wo_all = wo_all.reshape(2048, 2048)
-    q_all = q_all.reshape(2048, 2048)
-    kv_all = kv_all.reshape(2048, 512)
-
-    grad_normed_two, mixed_parts, gu_sum, dn_parts = feed_forward(normed_two, gu_all, dn_all, dy_all, cotangent[0])
-
-    mixed, tokens_grad, query_grad, kv_grad, o_grad, gain_grads, gu_grads, dn_grad = back(
-        grad_normed_two, hidden_state, cotangent[0], tokens[0], gains_all, wo_all, q_all, kv_all, qst, kst, vst, lse,
-        cosine_two, sine_two, bias_p, bias_c, mate[None], normed, attended, mixed_parts, gu_sum, dn_parts,
-    )
-
     gate_grad, up_grad = widen(gu_grads)
     return (
         mixed[None],

time: 361 us -> 336 us (0.931)
  Pallas kernels: 335 us -> 322 us
  other arithmetic: 15.4 us -> 8.34 us
    pallas_call x2 -> x1, Pallas kernels: 194 us -> 184 us  [fore(): pl.pallas_call(fore_kernel, out_shape=(shape((16, 16, 128), F32), shape((...]
    concatenate x6 -> x0, other arithmetic: 5.24 us -> none  [the longest x1 1.53 us: on_device(): kv_weight = jnp.concatenate([key_weight, value_weight], axis=1)]
where the time goes in v6:
time: 336 us; the launch traced here: 335 us
  Pallas kernels  322 us (96%)
  other arithmetic  8.34 us (2%)
  local copies, waits for them, and re-layouts  4.43 us (1%)
    pallas_call x1, Pallas kernels, fore(): pl.pallas_call(fore_kernel, out_shape=(shape((16, 16, 128), F32), shape((...  184 us
    pallas_call x1, Pallas kernels, back(): pl.pallas_call(back_kernel, out_shape=(jax.ShapeDtypeStruct((128, 2048),...  131 us
    pallas_call x1, Pallas kernels, widen(): pl.pallas_call(widen_kernel, grid=(8,), out_shape=(out, out), in_specs=[p...  6.8 us

profile of v6, /device:TPU:0, one launch (start us, length us, event | category | flops | bytes accessed | tf_op | source)
XLA Modules:
  0.0 335.1 jit_solution(7001536421678384744)
XLA Ops:
  0.7 0.6 maximum_bitcast_fusion.freq
  1.2 0.8 copy.23
  2.1 0.7 reshape.34.deal
  2.8 183.9 %fore.1 = (f32[16,16,128]{2,1,0:T(8,128)}, bf16[8,2,128,2048]{3,2,1,0:T(8,128)(2,1)}, bf16[8,2,128,512]{3,2,1,0:T(8,128)(2,1)}, bf16[8,2,128,2048]{3,2,1,0:T(8,1...) custom-call(bf16[128,2048]{1,0:T(8,128)(2,1)} %bitcast.17, ...), custom_call_target="tpu_custom_call" | custom-call | tf_op jit(solution)/shard_map/fore/pallas_call | solution.py:821
  186.7 130.9 %back.1 = (bf16[128,2048]{1,0:T(8,128)(2,1)}, bf16[128,2048]{1,0:T(8,128)(2,1)}, bf16[128,2048]{1,0:T(8,128)(2,1)}, bf16[128,512]{1,0:T(8,128)(2,1)}, bf16[128,2...) custom-call(f32[128,2048]{1,0:T(8,128)} %get-tuple-element.40.da2, ...), custom_call_target="tpu_custom_call" | custom-call | tf_op jit(solution)/shard_map/back/pallas_call | solution.py:1294
  317.6 0.0 copy-start
  317.6 1.3 slice_bitcast_fusion
  318.9 1.6 slice_convert_fusion
  320.5 2.1 convert_element_type.15
  322.6 2.1 convert_element_type.18
  324.8 0.0 copy-done
  324.8 0.0 copy-start.2
  324.8 1.9 convert_element_type.19
  326.7 0.0 copy-start.1
  326.7 6.8 %widen.1 = (f32[128,5632]{1,0:T(8,128)}, f32[128,5632]{1,0:T(8,128)}) custom-call(bf16[8,128,1536]{2,1,0:T(8,128)(2,1)} %get-tuple-element.65.parts), custom_call_target="tpu_custom_call" | custom-call | tf_op jit(solution)/shard_map/widen/pallas_call | solution.py:1328
  333.5 0.0 copy-done.2
  333.5 0.8 copy.26
  334.3 0.0 copy-done.1
  334.3 0.8 copy.27
  (1 shorter events, 0.0 us)
Async XLA Ops:
  317.6 7.1 %copy-start = (bf16[352,2048]{1,0:T(8,128)(2,1)S(1)}, bf16[352,2048]{1,0:T(8,128)(2,1)}, u32[]{:S(2)}) copy-start(bf16[352,2048]{1,0:T(8,128)(2,1)} %get-tuple-element.68) | copy-start | bytes 4325380
  324.8 8.7 %copy-start.2 = (bf16[128,2048]{1,0:T(8,128)(2,1)S(1)}, bf16[128,2048]{1,0:T(8,128)(2,1)}, u32[]{:S(2)}) copy-start(bf16[128,2048]{1,0:T(8,128)(2,1)} %get-tuple-element.59) | copy-start | bytes 1572868
  326.7 7.6 %copy-start.1 = (bf16[128,2048]{1,0:T(8,128)(2,1)S(1)}, bf16[128,2048]{1,0:T(8,128)(2,1)}, u32[]{:S(2)}) copy-start(bf16[128,2048]{1,0:T(8,128)(2,1)} %get-tuple-element.60) | copy-start | bytes 1572868

commit v7 on v6

v7 whole, which is shorter than its diff:
```python
import functools

import jax
import jax.numpy as jnp
from jax import lax
from jax.experimental import pallas as pl
from jax.experimental.pallas import tpu as pltpu
from jax.sharding import PartitionSpec as P

MESH = pl.DeviceIdType.MESH
BF = jnp.bfloat16
F32 = jnp.float32
ANY = pl.BlockSpec(memory_space=pl.ANY)
VMEM = pl.BlockSpec(memory_space=pltpu.VMEM)

HEAD_DIM = 64
EPS = 1e-05
SCALE = 0.125
BASE = 10000.0

SLOT = {(0, 0): 0, (0, 1): 1, (1, 0): 2, (3, 0): 3, (1, 1): 4, (3, 1): 5, (2, 0): 6, (2, 1): 7}
STEPS = (0, 0, 1, 3, 1, 3, 2, 2)
PAIRS = (0, 1, 0, 0, 1, 1, 0, 1)


def slot_of(dr, dp):
    return SLOT[(dr % 4, dp % 2)]


class Place:
    def __init__(self):
        self.c = lax.axis_index("ctx")
        self.f = lax.axis_index("fsdp")
        self.y, self.zl = lax.div(self.c, 2), lax.rem(self.c, 2)
        self.j, self.co = lax.div(self.f, 2), lax.rem(self.f, 2)
        self.x, self.zh = lax.div(self.j, 2), lax.rem(self.j, 2)

    def ctx_at(self, dr, dp):
        return lax.rem(self.y + dr % 4, 4) * 2 + lax.rem(self.zl + dp, 2)

    def chip_at(self, dr, dp):
        return lax.rem(self.x + dr % 4, 4) * 2 + lax.rem(self.zh + dp, 2)

    def fsdp_at(self, dr, dp):
        return self.chip_at(dr, dp) * 2 + self.co

    def across_y(self, dr, dp):
        return {"ctx": self.ctx_at(dr, dp), "fsdp": self.f}

    def across_x(self, dr, dp):
        return {"ctx": self.c, "fsdp": self.fsdp_at(dr, dp)}

    def sibling(self):
        return {"ctx": self.c, "fsdp": self.f + 1 - 2 * self.co}


def chip_of(me, t):
    dr = jnp.where(t < 2, 0, jnp.where(t >= 6, 2, 1 + 2 * lax.rem(t, 2)))
    dp = jnp.where(t < 2, t, jnp.where(t >= 6, t - 6, lax.div(t, 4)))
    return lax.rem(me.x + dr, 4) * 2 + lax.rem(me.zh + dp, 2)


def greet(devices):
    barrier = pltpu.get_barrier_semaphore()
    for device in devices:
        pl.semaphore_signal(barrier, 1, device_id=device, device_id_type=MESH)
    pl.semaphore_wait(barrier, len(devices))


class Swap:
    def __init__(self, me, src, dst, sems, local):
        self.moved = me.c != me.j
        self.to = {"ctx": me.j, "fsdp": 2 * me.c + me.co}
        self.copy = pltpu.make_async_remote_copy(
            src, dst, sems[0], sems[1], device_id=self.to, device_id_type=MESH
        )
        self.keep = pltpu.make_async_copy(src, dst, local)

    def start(self):
        pl.when(self.moved)(self.copy.start)
        pl.when(jnp.logical_not(self.moved))(self.keep.start)

    def wait(self):
        pl.when(self.moved)(self.copy.wait)
        pl.when(jnp.logical_not(self.moved))(self.keep.wait)


def greet_all(me, plane=False):
    barrier = pltpu.get_barrier_semaphore()
    others = near(me.across_x) + [me.sibling()]
    others += [me.across_y(STEPS[s], PAIRS[s]) for s in range(1, 8)] if plane else near(me.across_y)
    for device in others:
        pl.semaphore_signal(barrier, 1, device_id=device, device_id_type=MESH)
    moved = me.c != me.j

    @pl.when(moved)
    def _():
        to = {"ctx": me.j, "fsdp": 2 * me.c + me.co}
        pl.semaphore_signal(barrier, 1, device_id=to, device_id_type=MESH)

    pl.semaphore_wait(barrier, len(others) + jnp.where(moved, 1, 0))


def near(dev):
    return [dev(1, 0), dev(-1, 0), dev(0, 1)]


def send(src, dst, sems, index, device):
    return pltpu.make_async_remote_copy(
        src, dst, sems[0].at[index], sems[1].at[index], device_id=device, device_id_type=MESH
    )


class Gather:
    MOVES = (
        ((0, 0), (0, 1), None),
        ((0, 0), (1, 0), None),
        ((0, 0), (-1, 0), None),
        ((0, 1), (1, 0), None),
        ((0, 1), (-1, 0), None),
        ((-1, 0), (1, 0), 0),
        ((-1, 1), (1, 0), 0),
        ((1, 0), (-1, 0), 1),
        ((1, 1), (-1, 0), 1),
    )

    def __init__(self, dev, own, loc, sems, row, sibling=None, sibling_sems=None):
        self.loc = loc
        self.copies = []
        for index, (block, to, half) in enumerate(self.MOVES):
            src = own if block == (0, 0) else loc(*block, 0, 0, half)
            dst = loc(*block, *to, half)
            self.copies.append(send(src, dst, sems, (row, index), dev(*to)))
        self.passed = {}
        if sibling is not None:
            self.passed[9] = send(own, loc(0, 0, 0, 0, None), sibling_sems, (row, 9), sibling)
            for index, ((dr, dp), (er, ep), half) in enumerate(self.MOVES):
                ref = loc(dr - er, dp + ep, 0, 0, half)
                self.passed[index] = send(ref, ref, sibling_sems, (row, index), sibling)
        self.own = own

    def _pass(self, index):
        if self.passed:
            self.passed[index].start()

    def _got(self, index):
        self.copies[index].wait_recv()
        self._pass(index)

    def start(self):
        for index in (0, 1, 2):
            self.copies[index].start()
        self._pass(9)

    def pair(self):
        self._got(0)
        self.copies[3].start()
        self.copies[4].start()

    def turn(self, dp):
        for got, on in (((1, 5), (2, 7)) if dp == 0 else ((3, 6), (4, 8))):
            self._got(got)
            self.copies[on].start()

    def last(self, dp):
        for got in ((5, 7) if dp == 0 else (6, 8)):
            self._got(got)

    def sync(self):
        for copy in self.passed.values():
            copy.wait()

    def end(self):
        for copy in self.copies:
            copy.wait_send()


def row_half(half, rows):
    return pl.ds(0, rows) if half is None else pl.ds(half * (rows // 2), rows // 2)


def add_into(ref, rows, others, step=16):
    step = min(step, rows)

    @pl.loop(0, rows // step)
    def _(i):
        at = pl.ds(pl.multiple_of(i * step, step), step)
        total = ref[at].astype(F32)
        for other in others:
            total = total + other[at].astype(F32)
        ref[at] = total.astype(ref.dtype)


class Scatter:
    def __init__(self, dev, part, rows, halves, fulls, paired, sems, row, cut=None):
        self.part, self.rows, self.cut = part, rows, cut
        self.halves, self.fulls, self.paired = halves, fulls, paired
        self.first, self.second = {}, {}
        for dp in (0, 1):
            for way, sign in ((0, 1), (1, -1)):
                self.first[way, dp] = send(
                    self._half(part(slot_of(2, dp)), way), halves.at[way, dp], sems, (row, way * 2 + dp), dev(sign, 0)
                )
                self.second[way, dp] = send(
                    part(slot_of(sign, dp)), fulls.at[way, dp], sems, (row, 4 + way * 2 + dp), dev(sign, 0)
                )
        self.third = send(part(slot_of(0, 1)), paired, sems, (row, 8), dev(0, 1))

    def _half(self, ref, way):
        if self.cut is None:
            return ref.at[pl.ds(way * (self.rows // 2), self.rows // 2)]
        return ref.at[:, pl.ds(way * (self.cut // 2), self.cut // 2)]

    def start(self):
        for dp in (1, 0):
            for way in (0, 1):
                self.first[way, dp].start()

    def turn(self, dp):
        for way, sign in ((0, 1), (1, -1)):
            self.first[way, dp].wait_recv()
            block = self._half(self.part(slot_of(sign, dp)), way)
            add_into(block, block.shape[0], [self.halves.at[way, dp]])
            self.second[way, dp].start()

    def pair(self):
        for way in (0, 1):
            self.second[way, 1].wait_recv()
        add_into(self.part(slot_of(0, 1)), self.rows, [self.fulls.at[0, 1], self.fulls.at[1, 1]])
        self.third.start()

    def finish(self, out, extra=()):
        for way in (0, 1):
            self.second[way, 0].wait_recv()
        self.third.wait_recv()
        own = self.part(0)
        terms = [own, self.fulls.at[0, 0], self.fulls.at[1, 0], self.paired, *extra]

        @pl.loop(0, self.rows // 16)
        def _(i):
            at = pl.ds(pl.multiple_of(i * 16, 16), 16)
            total = terms[0][at].astype(F32)
            for term in terms[1:]:
                total = total + term[at].astype(F32)
            out[at] = total.astype(out.dtype)

    def end(self):
        for copy in (*self.first.values(), *self.second.values(), self.third):
            copy.wait_send()


def mirror(slot):
    return slot_of(-STEPS[slot], PAIRS[slot])


class Trade:
    def __init__(self, dev, what, where, sems, row):
        self.copies = [
            pltpu.make_async_remote_copy(
                what(slot), where(slot), sems[0].at[row, slot], sems[1].at[row, mirror(slot)],
                device_id=dev(STEPS[slot], PAIRS[slot]), device_id_type=MESH,
            )
            for slot in range(1, 8)
        ]

    def start(self):
        for copy in self.copies:
            copy.start()

    def got(self):
        for copy in self.copies:
            copy.wait_recv()

    def end(self):
        for copy in self.copies:
            copy.wait_send()


def scatter_buffers(rows, columns, dtype=BF, cut=False):
    half = (rows, columns // 2) if cut else (rows // 2, columns)
    return [
        pltpu.VMEM((2, 2, *half), dtype),
        pltpu.VMEM((2, 2, rows, columns), dtype),
        pltpu.VMEM((rows, columns), dtype),
    ]


def dma_sems(rows, count):
    return [pltpu.SemaphoreType.DMA((rows, count)), pltpu.SemaphoreType.DMA((rows, count))]


def params(collective_id, vmem=56):
    return pltpu.CompilerParams(
        collective_id=collective_id, has_side_effects=True, vmem_limit_bytes=vmem << 20
    )


def dot_in(left, right):
    return jnp.dot(left, right, preferred_element_type=F32)


def dot_back(left, right):
    return lax.dot_general(left, right, (((1,), (1,)), ((), ())), preferred_element_type=F32)


def dot_rows(left, right):
    return lax.dot_general(left, right, (((0,), (0,)), ((), ())), preferred_element_type=F32)


def load(src, dst, sem):
    copy = pltpu.make_async_copy(src, dst, sem)
    copy.start()
    return copy


def turned(values):
    lane = lax.broadcasted_iota(jnp.int32, values.shape, 1)
    low = lax.rem(lane, 64) < 32
    return jnp.where(low, pltpu.roll(values, 96, 1), pltpu.roll(values, 32, 1))


def pile(out, values, half):
    for h in range(8):
        out[pl.ds(64 * h, 64), :] = values[64 * half : 64 * half + 64, 64 * h : 64 * h + 64]


def unpile(values):
    flat = values.T
    return [
        jnp.concatenate([flat[128 * m : 128 * m + 64], flat[128 * m + 64 : 128 * m + 128]], axis=1)
        for m in range(4)
    ]


def norm_scale(ref, out):
    values = ref[...].astype(F32)
    out[...] = lax.rsqrt(jnp.mean(values * values, axis=1, keepdims=True) + EPS)


def place_tables(me, deal, freq, cosine, sine, bias_p, bias_c):
    def block(slot, part):
        return deal[(me.f * 8 + me.ctx_at(STEPS[slot], PAIRS[slot])) * 2 + part]

    first, second = block(0, 0), block(0, 1)
    odd = lax.rem(second, 2)
    row = lax.broadcasted_iota(jnp.int32, (128, 128), 0)
    lane = lax.broadcasted_iota(jnp.int32, (128, 128), 1)
    position = jnp.where(row < 64, first * 64 + row, 448 + odd * 64 + row)
    angle = position.astype(F32) * freq[...]
    cosine[...] = jnp.cos(angle)
    sine[...] = jnp.where(lax.rem(lane, 64) < 32, -jnp.sin(angle), jnp.sin(angle))
    row, lane = row[:64], lax.rem(lane[:64], 64)
    mate = jnp.int32(0)
    for slot in range(8):
        seen = block(slot, 0) * 64 + row <= first * 64 + lane
        bias_p[pl.ds(64 * slot, 64), :] = jnp.where(seen, 0.0, -1e30)
        if slot:
            mate = mate + jnp.where(block(slot, 1) == second + 1 - 2 * odd, slot, 0)
    bias_c[pl.ds(0, 64), :] = jnp.where(odd + 0 * row == 1, 0.0, -1e30)
    bias_c[pl.ds(64, 64), :] = jnp.where(row <= lane, 0.0, -1e30)
    return mate


def find_mate(me, deal):
    def block(slot):
        return deal[(me.f * 8 + me.ctx_at(STEPS[slot], PAIRS[slot])) * 2 + 1]

    second = block(0)
    mate = jnp.int32(0)
    for slot in range(1, 8):
        mate = mate + jnp.where(block(slot) == second + 1 - 2 * lax.rem(second, 2), slot, 0)
    return mate


def layer_kernel(
    x, attn_gain, mlp_gain, deal, freq, q_in, key_in, value_in, wo_in, gate_in, up_in, dn_in, dy_in,
    mixed, tokens_grad, q_grad, kv_grad, o_grad, gains_out, gu_all, dn_all,
    q_saved, kw_saved, wo_saved, mpart, m_half, m_full, m_pair,
    gains, a1s, atts, qst, kst, vst, lse, h1, cosine, sine, bias_p, bias_c,
    qw, kw, wo, kv_own, kv, sT, pT, dT, dsT, scale, gu_win, dnp, acts, gu, wd, dy, hid,
    grecv, gdrecv, g_pair, da2, datts, dqkvs, grow, gown_rows, gsib_rows, dn_moved,
    n_half, n_full, n_pair, e_half, e_full, e_pair, gp, ggot, g_sum, o_got, q_got, k_got,
    s0, s1, t0, t1, y0, y1, u0, u1, r0, r1, z0, z1, c0, c1, w0, w1, v0, v1, credit, local,
):
    me = Place()
    greet_all(me, plane=True)
    own, other = pl.ds(0, 128), pl.ds(128, 128)
    slots = iter(range(64))

    def load(src, dst):
        copy = pltpu.make_async_copy(src, dst, local.at[next(slots)])
        copy.start()
        return copy

    def later(src, dst):
        return pltpu.make_async_copy(src, dst, local.at[next(slots)])

    def aligned(index, step):
        return index if isinstance(index, int) else pl.multiple_of(index, step)

    def gains_at(dr, dp, er, ep, half):
        return gains.at[me.fsdp_at(dr, dp), row_half(half, 16)]

    def slot_at(ref, rows):
        def loc(dr, dp, er, ep, half):
            return ref.at[slot_of(dr - er, dp + ep), row_half(half, rows)]

        return loc

    def acts_at(dr, dp, er, ep, half):
        slot = slot_of(dr - er, dp + ep)
        return acts.at[slot // 2, slot % 2, row_half(half, 128)]

    def columns(first, index):
        return pl.ds(pl.multiple_of(first + index * 128, 128), 128)

    def plain(ref, count):
        def loc(dr, dp, er, ep, half):
            return ref.at[me.chip_at(dr, dp), me.co, row_half(half, 128), pl.ds(0, count)]

        return loc

    def strip_x(ref, first):
        def loc(dr, dp, er, ep, half):
            return ref.at[me.chip_at(dr, dp), me.co, row_half(half, 128), columns(first, me.c)]

        return loc

    def strip_y(ref, first):
        def loc(dr, dp, er, ep, half):
            chips = pl.ds(0, 8) if half is None else pl.ds(4 * half, 4)
            return ref.at[chips, me.co, :, columns(first, me.ctx_at(dr, dp))]

        return loc

    def wd_at(dr, dp, er, ep, half):
        size = 352 if half is None else 176
        first = me.co * 352 + (0 if half is None else half * size)
        return wd.at[
            pl.ds(pl.multiple_of(first, 16), size),
            pl.ds(pl.multiple_of(me.chip_at(dr, dp) * 256, 256), 256),
        ]

    def gu_at(dr, dp, er, ep, half):
        size = 128 if half is None else 64
        first = me.fsdp_at(dr, dp) * 128 + (0 if half is None else half * size)
        return gu.at[pl.ds(pl.multiple_of(first, size), size)]

    def over_x(own, loc, row, both=True):
        own = loc(0, 0, 0, 0, None) if own is None else own
        return Gather(me.across_x, own, loc, (s0, s1), row, me.sibling() if both else None, (t0, t1))

    def over_y(own, loc, row, both=True):
        own = loc(0, 0, 0, 0, None) if own is None else own
        return Gather(me.across_y, own, loc, (y0, y1), row, me.sibling() if both else None, (u0, u1))

    g = over_x(None, gains_at, 0)
    k = over_x(None, plain(kw, 512), 1)
    q = over_x(q_in.at[:, pl.ds(0, 1024)], plain(qw, 1024), 2)
    qx = over_x(q_in.at[:, columns(1024, me.c)], strip_x(qw, 1024), 3, both=False)
    o = over_x(wo_in.at[:, pl.ds(0, 1024)], plain(wo, 1024), 4)
    ox = over_x(wo_in.at[:, columns(1024, me.c)], strip_x(wo, 1024), 5, both=False)
    m = over_x(None, gu_at, 6)
    dn = over_x(dnp, wd_at, 7)
    qy = over_y(None, strip_y(qw, 1024), 0)
    oy = over_y(None, strip_y(wo, 1024), 1)
    dy_task = over_y(dy_in, slot_at(dy, 128), 2, both=False)
    kv_task = over_y(kv_own, slot_at(kv, 128), 3, both=False)
    a = over_y(None, acts_at, 4, both=False)
    swap = Swap(me, dn_in.at[:, pl.ds(pl.multiple_of(me.c * 256, 256), 256)], dnp, (w0, w1), local.at[next(slots)])

    own_kw = plain(kw, 512)(0, 0, 0, 0, None)
    loads = [load(key_in, own_kw.at[:, pl.ds(0, 256)]), load(value_in, own_kw.at[:, pl.ds(256, 256)])]
    kept = {task: load(task.own, task.loc(0, 0, 0, 0, None)) for task in (q, qx, o, ox, dy_task)}
    window = pl.ds(pl.multiple_of(me.y * 1408 + me.zl * 640, 128), 768)
    loads.append(load(gate_in.at[:, window], gu_win.at[0]))
    loads.append(load(up_in.at[:, window], gu_win.at[1]))
    gains[me.f] = jnp.zeros((16, 128), F32)
    gains[me.f, pl.ds(0, 1), :] = attn_gain[...].astype(F32)
    gains[me.f, pl.ds(8, 1), :] = mlp_gain[...].astype(F32)

    dpart = op = wo.at[:, 0]
    qp = wo.at[:, 1]
    dgu = wo.at[:, 1, :, pl.ds(0, 1536)]
    kvp = kv

    def gsib(t):
        return gu.at[pl.ds(aligned(128 * t, 128), 128)]

    def gown(t):
        return gu.at[pl.ds(aligned(1024 + 128 * t, 128), 128)]

    def kp(t):
        return gu.at[pl.ds(aligned(128 * t, 128), 128), pl.ds(0, 512)]

    def gd(t):
        return wd.at[:, pl.ds(aligned(256 * t, 256), 256)]

    def gd_own(t):
        return gd(t).at[pl.ds(pl.multiple_of(me.co * 352, 16), 352)]

    def dost(n, half):
        return grecv.at[pl.ds(0, 4), :, pl.ds(pl.multiple_of(512 + 128 * (2 * n + half), 128), 128)]

    saved = []

    def put_gate_up():
        loads[2].wait()
        loads[3].wait()

        @pl.loop(0, 8)
        def _(i):
            rows = pl.ds(pl.multiple_of(16 * i, 16), 16)
            out = pl.ds(pl.multiple_of(me.f * 128 + 16 * i, 16), 16)
            for w in (0, 1):
                values = gu_win[w, rows].astype(F32)
                values = jnp.where(me.zl == 1, pltpu.roll(values, 704, 1), values)
                lane = lax.broadcasted_iota(jnp.int32, values.shape, 1)
                gu[out, 768 * w : 768 * w + 768] = jnp.where(lane < 704, values, 0.0).astype(BF)

        wd[pl.ds(704, 64)] = jnp.zeros((64, 2048), BF)

    def normed():
        norm_scale(x, scale)

        @pl.loop(0, 16)
        def _(i):
            at = pl.ds(pl.multiple_of(i * 128, 128), 128)
            a1s[own, at] = (x[:, at].astype(F32) * scale[...] * gains[i, pl.ds(0, 1), :]).astype(BF)

    def project_kv():
        raw = dot_in(a1s[own], kw[...].reshape(2048, 512))
        for i in range(2):
            part = raw[:, 128 * i : 128 * i + 128]
            kv_own[:, 128 * i : 128 * i + 128] = (part * cosine[...] + turned(part) * sine[...]).astype(BF)
        kv_own[:, 256:] = raw[:, 256:].astype(BF)
        kv[0] = kv_own[...]

    def project_q():
        @pl.loop(0, 4)
        def _(n):
            raw = dot_in(a1s[own], qw[:, :, :, pl.ds(pl.multiple_of(512 * n, 512), 512)].reshape(2048, 512))
            for i in range(4):
                part = raw[:, 128 * i : 128 * i + 128]
                part = ((part * cosine[...] + turned(part) * sine[...]).astype(BF).astype(F32) * SCALE).astype(BF)
                for half in (0, 1):
                    for e in (0, 1):
                        rows = pl.ds(64 * (2 * i + e), 64)
                        qst[n, half, rows, :] = part[64 * half : 64 * half + 64, 64 * e : 64 * e + 64]

    def collect_kv(mate):
        beside = kv[mate]
        for out, base in ((kst, 0), (vst, 256)):
            for n in range(4):
                first = base + 64 * n
                for slot in range(8):
                    out[n, pl.ds(64 * slot, 64), :] = kv[slot, 0:64, first : first + 64]
                out[n, pl.ds(512, 64), :] = beside[64:128, first : first + 64]
                out[n, pl.ds(576, 64), :] = kv_own[64:128, first : first + 64]

    def attend(n, half):
        count = 512 if half == 0 else 640
        keys = pl.ds(0, count)
        sT[keys] = dot_back(kst[n, keys, :], qst[n, half])
        for i in range(4):
            at = pl.ds(128 * i, 128)
            if half == 0:
                scores = sT[keys, at] + bias_p[...]
                peak = jnp.max(scores, axis=0, keepdims=True)
                raised = jnp.exp(scores - peak)
                total = jnp.sum(raised, axis=0, keepdims=True)
                pT[keys, at] = (raised * (1.0 / total)).astype(BF)
            else:
                first = sT[0:512, at]
                rest = sT[512:640, at] + bias_c[...]
                peak = jnp.maximum(
                    jnp.max(first, axis=0, keepdims=True), jnp.max(rest, axis=0, keepdims=True)
                )
                first = jnp.exp(first - peak)
                rest = jnp.exp(rest - peak)
                total = jnp.sum(first, axis=0, keepdims=True) + jnp.sum(rest, axis=0, keepdims=True)
                pT[0:512, at] = (first * (1.0 / total)).astype(BF)
                pT[512:640, at] = (rest * (1.0 / total)).astype(BF)
            lse[2 * n + half, :, at] = peak + jnp.log(total)
        for i, block in enumerate(unpile(dot_rows(vst[n, keys, :], pT[keys]))):
            first = pl.multiple_of(512 * n + 128 * i, 128)
            atts[pl.ds(64 * half, 64), pl.ds(first, 128)] = block.astype(BF)

    def project_o():
        @pl.loop(0, 4)
        def _(n):
            at = pl.ds(pl.multiple_of(512 * n, 512), 512)
            h1[:, at] = x[:, at].astype(F32) + dot_in(atts[own], wo[:, :, :, at].reshape(2048, 512))

    def normed_two():
        norm_scale(h1, scale)

        @pl.loop(0, 16)
        def _(i):
            at = pl.ds(pl.multiple_of(i * 128, 128), 128)
            acts[0, 0, :, at] = (h1[:, at] * scale[...] * gains[i, pl.ds(8, 1), :]).astype(BF)

    def mpart_copy(n):
        return [
            pltpu.make_async_copy(
                kv.at[pl.ds(2 * i, 2)], mpart.at[pl.ds(2 * n, 2), :, pl.ds(512 * i, 512)], local.at[60 + i]
            )
            for i in range(4)
        ]

    def group(n):
        at = pl.ds(2 * n, 2)
        rows = pl.ds(pl.multiple_of(256 * n, 256), 256)
        for h in range(3):
            first, second = pl.ds(256 * h, 256), pl.ds(768 + 256 * h, 256)
            here = acts[n].reshape(256, 2048)
            gate = dot_in(here, gu[:, first])
            up = dot_in(here, gu[:, second])
            back = dot_back(dy[at].reshape(256, 2048), wd[first, :])
            curve = 1.0 / (1.0 + jnp.exp(-gate))
            silu = gate * curve
            hid[rows, first] = (silu * up).astype(BF)
            dgu[at, :, first] = (back * up * (curve + silu * (1.0 - curve))).astype(BF).reshape(2, 128, 256)
            dgu[at, :, second] = (back * silu).astype(BF).reshape(2, 128, 256)

        @pl.when(n > 0)
        def _():
            for copy in mpart_copy(n - 1):
                copy.wait()

        for i in range(4):
            wide = pl.ds(512 * i, 512)
            grads = dgu[at].reshape(256, 1536)
            dpart[at, :, wide] = dot_back(grads, gu[wide, :]).astype(BF).reshape(2, 128, 512)
            kv[pl.ds(2 * i, 2)] = dot_in(hid[rows, :], wd[:, wide]).astype(BF).reshape(2, 128, 512)
        for copy in mpart_copy(n):
            copy.start()

    class Views:
        def __init__(self, pick):
            self.pick = pick

        @property
        def at(self):
            return self

        def __getitem__(self, index):
            return self.pick(index)

    def scatter(dev, part, place, columns, row, pair=None):
        wide = pl.ds(0, columns)
        halves = Views(lambda index: place.at[4 + index[0], pl.ds(64 * index[1], 64), wide])
        fulls = Views(lambda index: place.at[2 * index[0] + index[1], :, wide])
        paired = place.at[6, :, wide] if pair is None else pair
        return Scatter(dev, part, 128, halves, fulls, paired, (r0, r1), row)

    first_bay, second_bay = qw.at[:, 0], qw.at[:, 1]
    d = scatter(me.across_y, lambda slot: dpart.at[slot], second_bay, 2048, 0)
    gjob = scatter(me.across_x, gown, first_bay, 1536, 1, g_pair)
    n_job = Scatter(me.across_x, gd_own, 352, n_half, n_full, n_pair, (r0, r1), 2)
    o_job = scatter(me.across_x, lambda slot: op.at[slot], first_bay, 2048, 3)
    q_job = scatter(me.across_x, lambda slot: qp.at[slot], second_bay, 2048, 4)
    k_job = scatter(me.across_x, kp, kw.at[:, 0], 512, 5)
    e_job = Scatter(me.across_x, lambda slot: gp.at[slot], 16, e_half, e_full, e_pair, (r0, r1), 6)
    d_job = scatter(me.across_y, lambda slot: kvp.at[slot], kw.at[:, 1], 512, 7)

    def weight_terms(t, core):
        at = pl.multiple_of((chip_of(me, t) * 2 + core) * 128, 128)
        left = acts[:, :, :, pl.ds(at, 128)].reshape(1024, 128)
        return dot_rows(left, dgu[...].reshape(1024, 1536))

    def gu_to(t):
        return send(gsib(t), grecv.at[t], (c0, c1), 8 + t, me.sibling())

    def down_to(t):
        mine = pl.ds(pl.multiple_of((1 - me.co) * 352, 16), 352)
        return send(gd(t).at[mine], gdrecv.at[t], (c0, c1), t, me.sibling())

    def terms_for_sibling(start):
        @pl.loop(start, start + 2)
        def _(i):
            gsib(7 - i)[...] = weight_terms(7 - i, 1 - me.co).astype(BF)
            gu_to(7 - i).start()

    def sibling_has_terms():
        @pl.loop(0, 8)
        def _(t):
            gu_to(t).wait_send()

    def own_terms(start):
        @pl.loop(start, start + 2)
        def _(i):
            gu_to(7 - i).wait_recv()
            gown(7 - i)[...] = (weight_terms(7 - i, me.co) + grecv[7 - i].astype(F32)).astype(BF)

    def down_terms():
        @pl.loop(0, 8)
        def _(t):
            at = pl.multiple_of(chip_of(me, t) * 256, 256)
            gd(t)[...] = dot_rows(hid[...], dy[:, :, pl.ds(at, 256)].reshape(1024, 256)).astype(BF)
            down_to(t).start()

    def down_sums():
        @pl.loop(0, 8)
        def _(t):
            down_to(t).wait_recv()

            @pl.loop(0, 22)
            def _(i):
                at = pl.ds(pl.multiple_of(i * 16, 16), 16)
                mine = gd(t).at[pl.ds(pl.multiple_of(me.co * 352 + i * 16, 16), 16)]
                mine[...] = (mine[...].astype(F32) + gdrecv[t, at].astype(F32)).astype(BF)

    m_first, m_second = {}, {}
    for dp in (0, 1):
        for way, sign in ((0, 1), (1, -1)):
            m_first[way, dp] = send(
                mpart.at[slot_of(2, dp), pl.ds(64 * way, 64)], m_half.at[way, dp], (r0, r1), (8, way * 2 + dp),
                me.across_y(sign, 0),
            )
            m_second[way, dp] = send(
                dy.at[1 + 2 * way + dp], m_full.at[way, dp], (r0, r1), (8, 4 + way * 2 + dp), me.across_y(sign, 0)
            )
    m_third = send(dy.at[5], m_pair, (r0, r1), (8, 8), me.across_y(0, 1))

    def m_start():
        dy_task.end()
        for copy in mpart_copy(3):
            copy.wait()
        for dp in (1, 0):
            for way in (0, 1):
                m_first[way, dp].start()

    m_parts = {(way, dp): later(mpart.at[slot_of(1 - 2 * way, dp)], dy.at[1 + 2 * way + dp]) for way in (0, 1) for dp in (0, 1)}
    m_halves = {(way, dp): later(m_half.at[way, dp], dy.at[6 + way, pl.ds(0, 64)]) for way in (0, 1) for dp in (0, 1)}
    m_fulls = {(way, dp): later(m_full.at[way, dp], dy.at[6 + way]) for way in (0, 1) for dp in (0, 1)}
    m_mine, m_near, m_last = later(mpart.at[0], dy.at[1]), later(mpart.at[1], dy.at[5]), later(m_pair, dy.at[2])
    m_out = later(dy.at[1], mixed)

    def m_turn(dp):
        for way in (0, 1):
            m_parts[way, dp].start()
        for way in (0, 1):
            m_first[way, dp].wait_recv()
            m_halves[way, dp].start()
        for way in (0, 1):
            m_parts[way, dp].wait()
            m_halves[way, dp].wait()
            add_into(dy.at[1 + 2 * way + dp, pl.ds(64 * way, 64)], 64, [dy.at[6 + way, pl.ds(0, 64)]])
            m_second[way, dp].start()

    def m_pair_up():
        m_near.start()
        for way in (0, 1):
            m_second[way, 1].wait_recv()
            m_fulls[way, 1].start()
        m_near.wait()
        for way in (0, 1):
            m_fulls[way, 1].wait()
        add_into(dy.at[5], 128, [dy.at[6], dy.at[7]])
        m_third.start()

    def m_finish():
        for dp in (0, 1):
            m_second[0, dp].wait_send()
        m_mine.start()
        for way in (0, 1):
            m_second[way, 0].wait_recv()
            m_fulls[way, 0].start()
        m_third.wait_recv()
        m_last.start()
        m_mine.wait()
        for way in (0, 1):
            m_fulls[way, 0].wait()
        m_last.wait()

        @pl.loop(0, 8)
        def _(i):
            at = pl.ds(pl.multiple_of(i * 16, 16), 16)
            total = h1[at]
            for slot in (1, 2, 6, 7):
                total = total + dy[slot, at].astype(F32)
            dy[1, at] = total.astype(BF)

        m_out.start()

    def wo_load(n):
        return pltpu.make_async_copy(
            wo_saved.at[pl.ds(2 * n, 2)], acts.at[pl.ds(2 * (n % 2), 2)], local.at[56 + n % 2]
        )

    def q_load(n):
        return pltpu.make_async_copy(q_saved.at[pl.ds(2 * n, 2)], acts.at[pl.ds(2 * (n % 2), 2)], local.at[58 + n % 2])

    def kw_load():
        return [
            load(kw_saved.at[chip], grecv.at[pl.ds(2 * (chip % 4), 2), :, pl.ds(512 * (chip // 4), 512)])
            for chip in range(8)
        ]

    def at_ctx(ref):
        def loc(dr, dp, er, ep, half):
            return ref.at[me.ctx_at(dr, dp), row_half(half, ref.shape[1])]

        return loc

    def dn_at(dr, dp, er, ep, half):
        first = pl.multiple_of(me.ctx_at(dr, dp) * 256, 256)
        return dn_all.at[row_half(half, 352), pl.ds(first, 256)]

    gu_task = over_y(gown(0), at_ctx(gu_all), 5, both=False)
    dn_task = over_y(dn_moved, dn_at, 6, both=False)
    dn_swap = Swap(me, gd_own(0), dn_moved, (v0, v1), local.at[next(slots)])
    gu_keep = later(gown(0), gu_all.at[me.c])
    dn_keep = later(dn_moved, dn_at(0, 0, 0, 0, None))
    dn_local = later(dnp, wd_at(0, 0, 0, 0, None))
    tokens_out = later(datts.at[own], tokens_grad)

    def block_at(ref, slot):
        first = pl.multiple_of(me.ctx_at(STEPS[slot], PAIRS[slot]) * 16, 16)
        return ref.at[pl.ds(first, 16)]

    def sum_over_ctx(total, got, row):
        return Trade(
            me.across_y, lambda slot: block_at(total, slot), lambda slot: got.at[mirror(slot)], (z0, z1), row
        )

    def spread(out, row):
        return Trade(me.across_y, lambda slot: block_at(out, 0), lambda slot: block_at(out, 0), (z0, z1), row)

    def sum_up(total, got, out):
        value = block_at(total, 0)[...].astype(F32)
        for slot in range(1, 8):
            value = value + got[slot].astype(F32)
        block_at(out, 0)[...] = value.astype(BF)

    o_sum, q_sum, kv_sum = op.at[0], qp.at[0], kp(0)
    o_sums = sum_over_ctx(o_sum, o_got, 0)
    q_sums = sum_over_ctx(q_sum, q_got, 1)
    k_sums = sum_over_ctx(kv_sum, k_got, 2)
    o_spread = spread(o_grad, 3)
    q_spread = spread(q_grad, 4)
    k_spread = spread(kv_grad, 5)
    e_task = Trade(me.across_y, lambda slot: g_sum, lambda slot: ggot.at[me.c], (z0, z1), 6)

    def to_sibling(src, dst, index):
        return send(src, dst, (c0, c1), 16 + index, me.sibling())

    att_swap = to_sibling(atts.at[own], atts.at[other], 0)
    datt_swap = to_sibling(datts.at[own], datts.at[other], 1)
    a1_swap = to_sibling(a1s.at[own], a1s.at[other], 2)
    queries, rest = pl.ds(0, 2048), pl.ds(2048, 512)
    dq_swap = to_sibling(dqkvs.at[own, queries], dqkvs.at[other, queries], 3)
    dkv_swap = to_sibling(dqkvs.at[own, rest], dqkvs.at[other, rest], 4)
    gain_swap = to_sibling(gown_rows, gsib_rows, 5)

    def norm_two_back():
        for i in range(16):
            grow[0, :, 128 * i : 128 * i + 128] = gains[i, 0:1, :]
            grow[1, :, 128 * i : 128 * i + 128] = gains[i, 8:9, :]
        grow[2] = jnp.zeros((1, 2048), F32)
        grow[3] = jnp.zeros((1, 2048), F32)

        @pl.loop(0, 8)
        def _(i):
            at = pl.ds(pl.multiple_of(16 * i, 16), 16)
            values, grad = h1[at], da2[at]
            scale = lax.rsqrt(jnp.mean(values * values, axis=1, keepdims=True) + EPS)
            grow[3] += jnp.sum(grad * values * scale, axis=0, keepdims=True)
            grad = grad * grow[1]
            level = jnp.mean(grad * values, axis=1, keepdims=True) * scale * scale * scale
            total = dy[0, at].astype(F32) + scale * grad - values * level
            da2[at] = total
            datts[at] = total.astype(BF)

        datt_swap.start()

    def heads_back():
        for n in range(4):
            wo_load(n).wait()
            part = dot_back(datts[own], acts[2 * (n % 2) : 2 * (n % 2) + 2].reshape(512, 2048)).astype(BF)
            for half in (0, 1):
                place = dost(n, half)
                for h in range(8):
                    place[h // 2, pl.ds(64 * (h % 2), 64), pl.ds(0, 64)] = part[
                        64 * half : 64 * half + 64, 64 * h : 64 * h + 64
                    ]
            if n < 2:
                wo_load(n + 2).start()
        for n in range(2):
            q_load(n).start()

    def terms(left, right, out, job):
        @pl.loop(0, 8)
        def _(i):
            at = pl.multiple_of((chip_of(me, 7 - i) * 2 + me.co) * 128, 128)
            out(7 - i)[...] = dot_rows(left[:, pl.ds(at, 128)], right[...]).astype(BF)

            @pl.when(i == 1)
            def _():
                job.start()

    def output_terms():
        att_swap.wait_recv()
        datt_swap.wait_recv()
        pl.semaphore_wait(credit, 3)
        terms(atts, datts, lambda t: op.at[t], o_job)

    def query_terms():
        a1_swap.wait_recv()
        dq_swap.wait_recv()
        terms(a1s, dqkvs.at[:, pl.ds(0, 2048)], lambda t: qp.at[t], q_job)

    def kv_terms():
        dkv_swap.wait_recv()
        terms(a1s, dqkvs.at[:, pl.ds(2048, 512)], kp, k_job)

    def kv_blocks(mate):
        for part, base in ((0, 0), (64, 256)):
            for n in range(4):
                first = base + 64 * n
                block = grecv[0:5, :, 128 * n : 128 * n + 128].reshape(640, 128)[:, part : part + 64]
                for slot in range(8):
                    kvp[slot, 0:64, first : first + 64] = block[64 * slot : 64 * slot + 64]
                    if slot == 0:
                        late = block[576:640]
                    else:
                        late = jnp.where(mate == slot, block[512:576], jnp.zeros((64, 64), BF))
                    kvp[slot, 64:128, first : first + 64] = late

    def kv_back():
        for i in range(2):
            at = slice(128 * i, 128 * i + 128)
            block = sT[512:640, at]
            dqkvs[own, 2048 + 128 * i : 2176 + 128 * i] = (block * cosine[...] - turned(block) * sine[...]).astype(BF)
        dqkvs[own, 2304:2560] = sT[512:640, 256:512].astype(BF)
        dkv_swap.start()

    def inputs_back():
        for copy in kw_back:
            copy.wait()
        for n in range(4):
            q_load(n).wait()
            block = dot_back(dqkvs[own, queries], acts[2 * (n % 2) : 2 * (n % 2) + 2].reshape(512, 2048))
            four, wide = pl.ds(4 * (n % 2), 4), pl.ds(512 * (n // 2), 512)
            block = block + dot_back(dqkvs[own, rest], grecv[four, :, wide].reshape(512, 512))
            sT[pl.ds(128 * n, 128)] = block
            if n < 2:
                q_load(n + 2).start()

    def norm_one_back():
        datt_swap.wait_send()

        @pl.loop(0, 8)
        def _(i):
            at = pl.ds(pl.multiple_of(16 * i, 16), 16)
            values = x[at].astype(F32)
            grad = jnp.concatenate([sT[pl.ds(pl.multiple_of(128 * n + 16 * i, 16), 16)] for n in range(4)], axis=1)
            scale = lax.rsqrt(jnp.mean(values * values, axis=1, keepdims=True) + EPS)
            grow[2] += jnp.sum(grad * values * scale, axis=0, keepdims=True)
            grad = grad * grow[0]
            level = jnp.mean(grad * values, axis=1, keepdims=True) * scale * scale * scale
            datts[at] = (da2[at] + scale * grad - values * level).astype(BF)

        tokens_out.start()

        gown_rows[...] = jnp.zeros((16, 16, 128), F32)
        for i in range(16):
            gown_rows[i, 0:1, :] = grow[2, :, 128 * i : 128 * i + 128]
            gown_rows[i, 8:9, :] = grow[3, :, 128 * i : 128 * i + 128]
        gain_swap.start()

    def gain_terms():
        gain_swap.wait_recv()
        for slot in range(8):
            block = me.fsdp_at(STEPS[slot], PAIRS[slot])
            gp[slot] = gown_rows[block] + gsib_rows[block]

    def dn_begin():
        dn_swap.wait()
        dn_task.start()
        dn_keep.start()

    def gu_begin():
        gu_keep.start()
        gu_task.start()

    def e_begin():
        e_task.start()
        ggot[me.c] = g_sum[...]

    def attend_back(n, half):
        count = 512 if half == 0 else 640
        keys = pl.ds(0, count)
        key, query, out = kst[n, keys, :], qst[n, half], dost(n, half)[...].reshape(512, 128)[:, 0:64]
        sT[keys] = dot_back(key, query)
        dT[keys] = dot_back(vst[n, keys, :], out)
        for i in range(4):
            at = pl.ds(128 * i, 128)
            parts = []
            for first, size in ((0, 512), (512, 128))[: 1 + half]:
                scores = sT[first : first + size, at]
                if half == 0:
                    scores = scores + bias_p[...]
                elif first:
                    scores = scores + bias_c[...]
                probs = jnp.exp(scores - lse[2 * n + half, :, at])
                grad = dT[first : first + size, at]
                parts.append((first, size, probs, grad))
            level = sum(jnp.sum(probs * grad, axis=0, keepdims=True) for _, _, probs, grad in parts)
            for first, size, probs, grad in parts:
                pT[first : first + size, at] = probs.astype(BF)
                dsT[first : first + size, at] = (probs * (grad - level)).astype(BF)
        rows = slice(64 * half, 64 * half + 64)
        for i, block in enumerate(unpile(dot_rows(key, dsT[keys]) * SCALE)):
            block = block * cosine[rows] - turned(block) * sine[rows]
            first = pl.multiple_of(512 * n + 128 * i, 128)
            dqkvs[rows, pl.ds(first, 128)] = block.astype(BF)
        return dot_in(dsT[keys], query), dot_in(pT[keys], out)

    def keep_kv_grads(n, one, two):
        keys = jnp.concatenate([one[0] + two[0][0:512], two[0][512:640]], axis=0)
        values = jnp.concatenate([one[1] + two[1][0:512], two[1][512:640]], axis=0)
        both = jnp.concatenate([keys, values], axis=1).astype(BF)
        grecv[pl.ds(0, 5), :, pl.ds(pl.multiple_of(128 * n, 128), 128)] = both.reshape(5, 128, 128)

    qx.start()
    dy_task.start()
    ox.start()
    g.start()
    loads[0].wait()
    loads[1].wait()
    k.start()
    mate = place_tables(me, deal, freq, cosine, sine, bias_p, bias_c)
    qx.turn(0)
    ox.turn(0)
    qx.pair()
    k.turn(0)
    qx.turn(1)
    q.start()
    g.turn(0)
    qx.last(1)
    qx.last(0)
    kept[qx].wait()
    qy.start()
    g.pair()
    dy_task.pair()
    q.turn(0)
    g.turn(1)
    k.pair()
    ox.pair()
    k.turn(1)
    o.start()
    q.last(0)
    ox.turn(1)
    ox.last(0)
    swap.start()
    g.last(0)
    qy.turn(0)
    qy.pair()
    g.last(1)
    k.last(0)
    put_gate_up()
    k.last(1)
    q.pair()
    g.sync()
    normed()
    k.sync()
    ox.last(1)
    o.pair()
    project_kv()
    kv_task.start()
    o.turn(0)
    qy.last(0)
    qy.turn(1)
    kv_task.pair()
    kept[ox].wait()
    oy.start()
    q.turn(1)
    swap.wait()
    dn_local.start()
    dn.start()
    qy.last(1)
    m.start()
    kv_task.turn(0)
    q.last(1)
    qy.sync()
    kv_task.turn(1)
    oy.pair()
    kv_task.last(0)
    q.sync()
    kept[q].wait()
    saved.append(load(qw, q_saved))
    saved.append(load(kw, kw_saved))
    project_q()
    o.turn(1)
    kv_task.last(1)
    oy.turn(0)
    collect_kv(mate)
    a1_swap.start()

    @pl.loop(0, 4)
    def _(n):
        attend(n, 0)
        attend(n, 1)

        @pl.when(n == 0)
        def _():
            o.last(0)
            dn.turn(0)
            oy.turn(1)
            dn.pair()

        @pl.when(n == 1)
        def _():
            dy_task.turn(0)
            oy.last(0)

        @pl.when(n == 2)
        def _():
            o.last(1)
            oy.last(1)
            m.pair()

    dy_task.turn(1)
    o.sync()
    oy.sync()
    kept[o].wait()
    saved.append(load(wo, wo_saved))
    project_o()
    normed_two()
    for task in (k, q, qx, qy):
        task.end()
    saved[0].wait()
    saved[1].wait()
    a.start()
    m.turn(0)
    dy_task.last(1)
    dy_task.last(0)
    m.turn(1)
    dn.last(0)
    dn.turn(1)
    a.pair()
    a.turn(0)
    dn.last(1)
    m.last(1)
    m.last(0)
    m.sync()
    dn.sync()

    for task in (o, ox, oy, kv_task):
        task.end()
    saved[2].wait()
    dn_local.wait()
    kept[dy_task].wait()

    @pl.loop(0, 4)
    def _(n):
        group(n)

        @pl.when(n == 0)
        def _():
            a.turn(1)

        @pl.when(n == 2)
        def _():
            a.last(0)
            att_swap.start()
            a.last(1)

    d.start()
    m.end()
    terms_for_sibling(0)
    dn.end()
    down_terms()
    d.turn(1)
    own_terms(0)
    gjob.start()
    terms_for_sibling(2)
    terms_for_sibling(4)
    own_terms(2)
    terms_for_sibling(6)
    down_sums()
    n_job.start()
    d.turn(0)
    own_terms(4)
    gjob.turn(1)
    m_start()
    own_terms(6)
    a.end()
    wo_load(0).start()
    wo_load(1).start()
    d.pair()
    n_job.turn(1)
    gjob.pair()
    gjob.turn(0)
    d.finish(da2)
    n_job.turn(0)
    norm_two_back()
    m_turn(1)
    gjob.finish(gown(0))
    for device in near(me.across_x):
        pl.semaphore_signal(credit, 1, device_id=device, device_id_type=MESH)
    gu_begin()
    d.end()
    output_terms()
    m_turn(0)
    heads_back()

    @pl.loop(0, 4)
    def _(n):
        one, two = attend_back(n, 0), attend_back(n, 1)
        keep_kv_grads(n, one, two)

        @pl.when(n == 0)
        def _():
            o_job.turn(1)
            n_job.pair()

        @pl.when(n == 1)
        def _():
            m_pair_up()

    dq_swap.start()
    o_job.turn(0)
    kv_blocks(mate)
    kw_back = kw_load()
    d_job.start()
    n_job.finish(gd_own(0))
    dn_swap.start()
    o_job.pair()
    gu_task.turn(0)
    d_job.turn(1)
    d_job.turn(0)
    query_terms()
    gu_task.pair()
    d_job.pair()
    o_job.finish(o_sum)
    d_job.finish(sT.at[pl.ds(512, 128)])
    o_sums.start()
    q_job.turn(1)
    m_finish()
    dn_begin()
    kv_back()
    o_sums.got()
    gu_task.turn(1)
    sum_up(o_sum, o_got, o_grad)
    sibling_has_terms()
    kv_terms()
    o_spread.start()
    k_job.turn(1)
    q_job.turn(0)
    dn_task.pair()
    q_job.pair()
    dn_task.turn(0)
    gu_task.last(0)
    k_job.turn(0)
    inputs_back()
    norm_one_back()
    k_job.pair()
    gain_terms()
    dn_task.turn(1)
    q_job.finish(q_sum)
    q_sums.start()
    k_job.finish(kv_sum)
    e_job.start()
    dn_task.last(0)
    e_job.turn(1)
    dn_task.last(1)
    e_job.pair()
    k_sums.start()
    e_job.turn(0)
    q_sums.got()
    sum_up(q_sum, q_got, q_grad)
    q_spread.start()
    e_job.finish(g_sum)
    k_sums.got()
    sum_up(kv_sum, k_got, kv_grad)
    gu_task.last(1)
    k_spread.start()
    o_spread.got()
    e_begin()
    k_spread.got()
    q_spread.got()
    e_task.got()
    total = ggot[0]
    for index in range(1, 8):
        total = total + ggot[index]
    gains_out[...] = total
    for job in (g, gjob, n_job, o_job, q_job, k_job, e_job, d_job, gu_task, dn_task):
        job.end()
    for job in (o_sums, q_sums, k_sums, o_spread, q_spread, k_spread, e_task):
        job.end()
    for copy in (*m_first.values(), m_second[1, 0], m_second[1, 1], m_third):
        copy.wait_send()
    m_out.wait()
    tokens_out.wait()
    gu_keep.wait()
    dn_keep.wait()
    for copy in (att_swap, a1_swap, dq_swap, dkv_swap, gain_swap):
        copy.wait_send()

    @pl.loop(0, 8)
    def _(t):
        down_to(t).wait_send()


def layer(x, attn_gain, mlp_gain, deal, freq, q, key, value, wo, gate, up, dn, dy):
    shape = jax.ShapeDtypeStruct
    smem = pl.BlockSpec(memory_space=pltpu.SMEM)
    vmem = pltpu.VMEM
    outs = pl.pallas_call(
        layer_kernel,
        out_shape=(
            shape((128, 2048), BF),
            shape((128, 2048), BF),
            shape((128, 2048), BF),
            shape((128, 512), BF),
            shape((128, 2048), BF),
            shape((16, 128), F32),
            shape((8, 128, 1536), BF),
            shape((352, 2048), BF),
            shape((8, 2, 128, 2048), BF),
            shape((8, 2, 128, 512), BF),
            shape((8, 2, 128, 2048), BF),
            shape((8, 128, 2048), BF),
            shape((2, 2, 64, 2048), BF),
            shape((2, 2, 128, 2048), BF),
            shape((128, 2048), BF),
        ),
        in_specs=[VMEM] * 3 + [smem, VMEM] + [ANY] * 8,
        out_specs=[ANY] * 2 + [VMEM] * 4 + [ANY] * 9,
        scratch_shapes=[
            vmem((16, 16, 128), F32),
            vmem((256, 2048), BF),
            vmem((256, 2048), BF),
            vmem((4, 2, 512, 64), BF),
            vmem((4, 640, 64), BF),
            vmem((4, 640, 64), BF),
            vmem((8, 1, 512), F32),
            vmem((128, 2048), F32),
            vmem((128, 128), F32),
            vmem((128, 128), F32),
            vmem((512, 128), F32),
            vmem((128, 128), F32),
            vmem((8, 2, 128, 2048), BF),
            vmem((8, 2, 128, 512), BF),
            vmem((8, 2, 128, 2048), BF),
            vmem((128, 512), BF),
            vmem((8, 128, 512), BF),
            vmem((640, 512), F32),
            vmem((640, 512), BF),
            vmem((640, 512), F32),
            vmem((640, 512), BF),
            vmem((128, 1), F32),
            vmem((2, 128, 768), BF),
            vmem((352, 256), BF),
            vmem((4, 2, 128, 2048), BF),
            vmem((2048, 1536), BF),
            vmem((768, 2048), BF),
            vmem((8, 128, 2048), BF),
            vmem((1024, 768), BF),
            vmem((8, 128, 1536), BF),
            vmem((8, 352, 256), BF),
            vmem((128, 1536), BF),
            vmem((128, 2048), F32),
            vmem((256, 2048), BF),
            vmem((256, 2560), BF),
            vmem((4, 1, 2048), F32),
            vmem((16, 16, 128), F32),
            vmem((16, 16, 128), F32),
            vmem((352, 256), BF),
            *scatter_buffers(352, 256),
            *scatter_buffers(16, 128, F32),
            vmem((8, 16, 128), F32),
            vmem((8, 16, 128), F32),
            vmem((16, 128), F32),
            vmem((8, 16, 2048), BF),
            vmem((8, 16, 2048), BF),
            vmem((8, 16, 512), BF),
            *dma_sems(8, 9),
            *dma_sems(8, 10),
            *dma_sems(7, 9),
            *dma_sems(2, 10),
            *dma_sems(9, 9),
            *dma_sems(7, 8),
            pltpu.SemaphoreType.DMA((22,)),
            pltpu.SemaphoreType.DMA((22,)),
            pltpu.SemaphoreType.DMA,
            pltpu.SemaphoreType.DMA,
            pltpu.SemaphoreType.DMA,
            pltpu.SemaphoreType.DMA,
            pltpu.SemaphoreType.REGULAR,
            pltpu.SemaphoreType.DMA((64,)),
        ],
        compiler_params=params(1, 63),
        name="layer",
    )(x, attn_gain, mlp_gain, deal, freq, q, key, value, wo, gate, up, dn, dy)
    return outs[:8]


def widen_kernel(parts, gate, up):
    for out, base in ((gate, 0), (up, 768)):
        for pair in range(4):
            even = parts[2 * pair, :, base : base + 768].astype(F32)
            odd = pltpu.roll(parts[2 * pair + 1, :, base : base + 768].astype(F32), 64, 1)
            first = 1408 * pair
            out[:, first : first + 640] = even[:, 0:640]
            out[:, first + 640 : first + 768] = even[:, 640:768] + odd[:, 0:128]
            out[:, first + 768 : first + 1408] = odd[:, 128:768]


def widen(parts):
    out = jax.ShapeDtypeStruct((128, 5632), F32)
    block = pl.BlockSpec((16, 5632), lambda i: (i, 0))
    return pl.pallas_call(
        widen_kernel,
        grid=(8,),
        out_shape=(out, out),
        in_specs=[pl.BlockSpec((8, 16, 1536), lambda i: (0, i, 0))],
        out_specs=[block, block],
        name="widen",
    )(parts)


def on_device(
    tokens,
    block_deal,
    attn_gain,
    query_weight,
    key_weight,
    value_weight,
    output_weight,
    mlp_gain,
    gate_weight,
    up_weight,
    down_weight,
    cotangent,
):
    freq = BASE ** (-(jnp.arange(HEAD_DIM // 2, dtype=F32) * 2.0) / HEAD_DIM)
    freq = jnp.concatenate([freq] * 4)[None]
    deal = block_deal.reshape(256)
    mixed, tokens_grad, query_grad, kv_grad, o_grad, gain_grads, gu_grads, dn_grad = layer(
        tokens[0], attn_gain[None], mlp_gain[None], deal, freq, query_weight, key_weight, value_weight, output_weight,
        gate_weight, up_weight, down_weight, cotangent[0],
    )
    gate_grad, up_grad = widen(gu_grads)
    return (
        mixed[None],
        tokens_grad[None],
        gain_grads[0],
        query_grad.astype(F32),
        kv_grad[:, :256].astype(F32),
        kv_grad[:, 256:].astype(F32),
        o_grad.astype(F32),
        gain_grads[8],
        gate_grad,
        up_grad,
        dn_grad.astype(F32),
    )


def solution(mesh):
    held = P("fsdp", "ctx", None)
    rows = P("fsdp", None)
    return jax.shard_map(
        on_device,
        mesh=mesh,
        in_specs=(held, P(), P("fsdp"), rows, rows, rows, rows, P("fsdp"), rows, rows, rows, held),
        out_specs=(held, held, P("fsdp"), rows, rows, rows, rows, P("fsdp"), rows, rows, rows),
        check_vma=False,
    )
```

time: 336 us -> 315 us (0.938)
  Pallas kernels: 322 us -> 299 us
    pallas_call x2 -> x1, Pallas kernels: 315 us -> 292 us  [layer(): pl.pallas_call(layer_kernel, out_shape=(shape((128, 2048), BF), shape((12...]
where the time goes in v7:
time: 315 us; the launch traced here: 313 us
  Pallas kernels  299 us (95%)
  other arithmetic  8.34 us (3%)
  local copies, waits for them, and re-layouts  4.43 us (1%)
    pallas_call x1, Pallas kernels, layer(): pl.pallas_call(layer_kernel, out_shape=(shape((128, 2048), BF), shape((12...  292 us
    pallas_call x1, Pallas kernels, widen(): pl.pallas_call(widen_kernel, grid=(8,), out_shape=(out, out), in_specs=[p...  6.8 us

profile of v7, /device:TPU:0, one launch (start us, length us, event | category | flops | bytes accessed | tf_op | source)
XLA Modules:
  0.0 312.7 jit_solution(837462524176443614)
XLA Ops:
  0.7 0.6 maximum_bitcast_fusion.freq
  1.2 0.8 copy.23
  2.1 0.7 reshape.25.deal
  2.8 292.5 %layer.1 = (bf16[128,2048]{1,0:T(8,128)(2,1)}, bf16[128,2048]{1,0:T(8,128)(2,1)}, bf16[128,2048]{1,0:T(8,128)(2,1)}, bf16[128,512]{1,0:T(8,128)(2,1)}, bf16[128,...) custom-call(bf16[128,2048]{1,0:T(8,128)(2,1)} %bitcast.12, ...), custom_call_target="tpu_custom_call" | custom-call | tf_op jit(solution)/shard_map/layer/pallas_call | solution.py:1312
  295.3 0.0 copy-start
  295.3 1.3 slice_bitcast_fusion
  296.6 1.6 slice_convert_fusion
  298.2 2.1 convert_element_type.15
  300.3 2.1 convert_element_type.18
  302.4 0.0 copy-done
  302.4 0.0 copy-start.2
  302.4 1.9 convert_element_type.19
  304.3 0.0 copy-start.1
  304.3 6.8 %widen.1 = (f32[128,5632]{1,0:T(8,128)}, f32[128,5632]{1,0:T(8,128)}) custom-call(bf16[8,128,1536]{2,1,0:T(8,128)(2,1)} %get-tuple-element.27.parts), custom_call_target="tpu_custom_call" | custom-call | tf_op jit(solution)/shard_map/widen/pallas_call | solution.py:1416
  311.1 0.0 copy-done.2
  311.1 0.8 copy.26
  311.9 0.0 copy-done.1
  311.9 0.8 copy.27
  (1 shorter events, 0.0 us)
Async XLA Ops:
  295.3 7.1 %copy-start = (bf16[352,2048]{1,0:T(8,128)(2,1)S(1)}, bf16[352,2048]{1,0:T(8,128)(2,1)}, u32[]{:S(2)}) copy-start(bf16[352,2048]{1,0:T(8,128)(2,1)} %get-tuple-element.30) | copy-start | bytes 4325380
  302.4 8.7 %copy-start.2 = (bf16[128,2048]{1,0:T(8,128)(2,1)S(1)}, bf16[128,2048]{1,0:T(8,128)(2,1)}, u32[]{:S(2)}) copy-start(bf16[128,2048]{1,0:T(8,128)(2,1)} %get-tuple-element.21) | copy-start | bytes 1572868
  304.3 7.6 %copy-start.1 = (bf16[128,2048]{1,0:T(8,128)(2,1)S(1)}, bf16[128,2048]{1,0:T(8,128)(2,1)}, u32[]{:S(2)}) copy-start(bf16[128,2048]{1,0:T(8,128)(2,1)} %get-tuple-element.22) | copy-start | bytes 1572868

commit v8 on v7

--- a/solution.py
+++ b/solution.py
@@ -6,6 +6,7 @@
 from jax.experimental import pallas as pl
 from jax.experimental.pallas import tpu as pltpu
 from jax.sharding import PartitionSpec as P
+import numpy as np
 
 MESH = pl.DeviceIdType.MESH
 BF = jnp.bfloat16
@@ -169,6 +170,39 @@
     def sync(self):
         for copy in self.passed.values():
             copy.wait()
+
+    def end(self):
+        for copy in self.copies:
+            copy.wait_send()
+
+
+class RingFirst:
+    MOVES = (
+        ((0, 0), (0, 1), None),
+        ((0, 0), (1, 0), None),
+        ((0, 0), (-1, 0), None),
+        ((-1, 0), (1, 0), 0),
+        ((1, 0), (-1, 0), 1),
+        ((-1, 0), (0, 1), None),
+        ((1, 0), (0, 1), None),
+        ((2, 0), (0, 1), 0),
+        ((2, 0), (0, 1), 1),
+    )
+
+    def __init__(self, dev, own, loc, sems, row):
+        self.own, self.loc = own, loc
+        self.copies = []
+        for index, (block, to, half) in enumerate(self.MOVES):
+            src = own if block == (0, 0) else loc(*block, 0, 0, half)
+            self.copies.append(send(src, loc(*block, *to, half), sems, (row, index), dev(*to)))
+
+    def go(self, *indices):
+        for index in indices:
+            self.copies[index].start()
+
+    def got(self, *indices):
+        for index in indices:
+            self.copies[index].wait_recv()
 
     def end(self):
         for copy in self.copies:
@@ -464,7 +498,7 @@
     dn = over_x(dnp, wd_at, 7)
     qy = over_y(None, strip_y(qw, 1024), 0)
     oy = over_y(None, strip_y(wo, 1024), 1)
-    dy_task = over_y(dy_in, slot_at(dy, 128), 2, both=False)
+    dy_task = RingFirst(me.across_y, dy_in, slot_at(dy, 128), (y0, y1), 2)
     kv_task = over_y(kv_own, slot_at(kv, 128), 3, both=False)
     a = over_y(None, acts_at, 4, both=False)
     swap = Swap(me, dn_in.at[:, pl.ds(pl.multiple_of(me.c * 256, 256), 256)], dnp, (w0, w1), local.at[next(slots)])
@@ -634,6 +668,32 @@
             dpart[at, :, wide] = dot_back(grads, gu[wide, :]).astype(BF).reshape(2, 128, 512)
             kv[pl.ds(2 * i, 2)] = dot_in(hid[rows, :], wd[:, wide]).astype(BF).reshape(2, 128, 512)
         for copy in mpart_copy(n):
+            copy.start()
+
+    def group_half(slot):
+        rows = pl.ds(128 * slot, 128)
+        here = acts[slot // 2, slot % 2]
+        for h in range(3):
+            first, second = pl.ds(256 * h, 256), pl.ds(768 + 256 * h, 256)
+            gate = dot_in(here, gu[:, first])
+            up = dot_in(here, gu[:, second])
+            back = dot_back(dy[slot], wd[first, :])
+            curve = 1.0 / (1.0 + jnp.exp(-gate))
+            silu = gate * curve
+            hid[rows, first] = (silu * up).astype(BF)
+            dgu[slot, :, first] = (back * up * (curve + silu * (1.0 - curve))).astype(BF)
+            dgu[slot, :, second] = (back * silu).astype(BF)
+        for i in range(4):
+            wide = pl.ds(512 * i, 512)
+            dpart[slot, :, wide] = dot_back(dgu[slot], gu[wide, :]).astype(BF)
+
+    def group_out():
+        for copy in mpart_copy(2):
+            copy.wait()
+        for i in range(4):
+            wide = pl.ds(512 * i, 512)
+            kv[pl.ds(2 * i, 2)] = dot_in(hid[pl.ds(768, 256), :], wd[:, wide]).astype(BF).reshape(2, 128, 512)
+        for copy in mpart_copy(3):
             copy.start()
 
     class Views:
@@ -1025,79 +1085,87 @@
         grecv[pl.ds(0, 5), :, pl.ds(pl.multiple_of(128 * n, 128), 128)] = both.reshape(5, 128, 128)
 
     qx.start()
-    dy_task.start()
-    ox.start()
     g.start()
     loads[0].wait()
     loads[1].wait()
     k.start()
-    mate = place_tables(me, deal, freq, cosine, sine, bias_p, bias_c)
+    dy_task.go(1, 2)
+    ox.start()
+    qx.pair()
     qx.turn(0)
+    q.start()
+    qx.turn(1)
+    qx.last(0)
+    put_gate_up()
+    g.pair()
+    ox.pair()
+    swap.start()
+    k.pair()
+    k.turn(0)
     ox.turn(0)
-    qx.pair()
-    k.turn(0)
-    qx.turn(1)
-    q.start()
-    g.turn(0)
     qx.last(1)
-    qx.last(0)
     kept[qx].wait()
     qy.start()
-    g.pair()
-    dy_task.pair()
     q.turn(0)
+    g.turn(0)
+    k.turn(1)
     g.turn(1)
-    k.pair()
-    ox.pair()
-    k.turn(1)
+    ox.turn(1)
     o.start()
-    q.last(0)
-    ox.turn(1)
     ox.last(0)
-    swap.start()
+    mate = place_tables(me, deal, freq, cosine, sine, bias_p, bias_c)
+    q.pair()
+    qy.pair()
+    k.last(0)
+    g.last(1)
     g.last(0)
-    qy.turn(0)
-    qy.pair()
-    g.last(1)
-    k.last(0)
-    put_gate_up()
-    k.last(1)
-    q.pair()
-    g.sync()
-    normed()
-    k.sync()
     ox.last(1)
-    o.pair()
-    project_kv()
-    kv_task.start()
-    o.turn(0)
-    qy.last(0)
-    qy.turn(1)
-    kv_task.pair()
-    kept[ox].wait()
-    oy.start()
-    q.turn(1)
     swap.wait()
     dn_local.start()
     dn.start()
+    k.last(1)
+    qy.turn(0)
+    o.pair()
+    kept[ox].wait()
+    oy.start()
+    qy.turn(1)
+    g.sync()
+    q.last(0)
+    normed()
+    qy.last(0)
+    k.sync()
+    project_kv()
+    q.turn(1)
+    kv_task.start()
+    dy_task.go(0)
+    kv_task.pair()
+    o.turn(0)
+    kv_task.turn(0)
     qy.last(1)
+    oy.pair()
+    o.turn(1)
+    q.last(1)
     m.start()
-    kv_task.turn(0)
-    q.last(1)
+    kv_task.turn(1)
+    dn.pair()
+    oy.turn(0)
+    o.last(0)
     qy.sync()
-    kv_task.turn(1)
-    oy.pair()
-    kv_task.last(0)
     q.sync()
     kept[q].wait()
     saved.append(load(qw, q_saved))
     saved.append(load(kw, kw_saved))
     project_q()
-    o.turn(1)
+    o.last(1)
+    dn.turn(0)
+    oy.turn(1)
+    dy_task.got(1, 2)
+    dy_task.go(3, 4)
+    dy_task.go(5)
+    kv_task.last(0)
     kv_task.last(1)
-    oy.turn(0)
+    dy_task.got(0)
     collect_kv(mate)
-    a1_swap.start()
 
     @pl.loop(0, 4)
     def _(n):
@@ -1106,24 +1174,14 @@
 
         @pl.when(n == 0)
         def _():
-            o.last(0)
-            dn.turn(0)
-            oy.turn(1)
-            dn.pair()
+            o.sync()
+            oy.last(0)
 
         @pl.when(n == 1)
         def _():
-            dy_task.turn(0)
-            oy.last(0)
-
-        @pl.when(n == 2)
-        def _():
-            o.last(1)
             oy.last(1)
             m.pair()
 
-    dy_task.turn(1)
-    o.sync()
     oy.sync()
     kept[o].wait()
     saved.append(load(wo, wo_saved))
@@ -1134,17 +1192,18 @@
     saved[0].wait()
     saved[1].wait()
     a.start()
+    dy_task.go(6)
     m.turn(0)
-    dy_task.last(1)
-    dy_task.last(0)
     m.turn(1)
+    dy_task.got(3, 4)
+    dy_task.go(7, 8)
+    m.last(0)
+    dn.turn(1)
     dn.last(0)
-    dn.turn(1)
     a.pair()
+    m.last(1)
     a.turn(0)
     dn.last(1)
-    m.last(1)
-    m.last(0)
     m.sync()
     dn.sync()
 
@@ -1154,58 +1213,60 @@
     dn_local.wait()
     kept[dy_task].wait()
 
-    @pl.loop(0, 4)
+    @pl.loop(0, 3)
     def _(n):
         group(n)
 
-        @pl.when(n == 0)
+        @pl.when(n == 1)
         def _():
             a.turn(1)
-
-        @pl.when(n == 2)
-        def _():
-            a.last(0)
-            att_swap.start()
-            a.last(1)
-
+            dy_task.got(5, 6)
+
+    a.last(0)
+    group_half(6)
+    dy_task.got(7, 8)
+    a.last(1)
+    group_half(7)
     d.start()
     m.end()
     terms_for_sibling(0)
+    terms_for_sibling(2)
+    own_terms(0)
+    terms_for_sibling(4)
+    d.turn(1)
+    group_out()
+    gjob.start()
     dn.end()
     down_terms()
-    d.turn(1)
-    own_terms(0)
-    gjob.start()
-    terms_for_sibling(2)
-    terms_for_sibling(4)
+    d.turn(0)
     own_terms(2)
+    own_terms(4)
+    down_sums()
+    att_swap.start()
+    n_job.start()
+    gjob.turn(1)
     terms_for_sibling(6)
-    down_sums()
-    n_job.start()
-    d.turn(0)
-    own_terms(4)
-    gjob.turn(1)
+    d.pair()
+    gjob.turn(0)
+    n_job.turn(0)
+    n_job.turn(1)
     m_start()
     own_terms(6)
     a.end()
     wo_load(0).start()
     wo_load(1).start()
-    d.pair()
-    n_job.turn(1)
     gjob.pair()
-    gjob.turn(0)
     d.finish(da2)
-    n_job.turn(0)
+    m_turn(1)
     norm_two_back()
-    m_turn(1)
     gjob.finish(gown(0))
     for device in near(me.across_x):
         pl.semaphore_signal(credit, 1, device_id=device, device_id_type=MESH)
     gu_begin()
     d.end()
     output_terms()
-    m_turn(0)
     heads_back()
+    m_pair_up()
 
     @pl.loop(0, 4)
     def _(n):
@@ -1214,75 +1275,76 @@
 
         @pl.when(n == 0)
         def _():
+            gu_task.pair()
+            a1_swap.start()
             o_job.turn(1)
-            n_job.pair()
 
         @pl.when(n == 1)
         def _():
-            m_pair_up()
-
-    dq_swap.start()
-    o_job.turn(0)
+            o_job.turn(0)
+
     kv_blocks(mate)
     kw_back = kw_load()
+    gu_task.turn(0)
     d_job.start()
+    n_job.pair()
+    dq_swap.start()
+    gu_task.turn(1)
+    o_job.pair()
+    d_job.turn(1)
+    query_terms()
     n_job.finish(gd_own(0))
     dn_swap.start()
-    o_job.pair()
-    gu_task.turn(0)
-    d_job.turn(1)
     d_job.turn(0)
-    query_terms()
-    gu_task.pair()
     d_job.pair()
     o_job.finish(o_sum)
+    dn_begin()
+    gu_task.last(0)
+    q_job.turn(1)
     d_job.finish(sT.at[pl.ds(512, 128)])
     o_sums.start()
-    q_job.turn(1)
-    m_finish()
-    dn_begin()
     kv_back()
-    o_sums.got()
-    gu_task.turn(1)
-    sum_up(o_sum, o_got, o_grad)
+    inputs_back()
+    dn_task.pair()
+    norm_one_back()
     sibling_has_terms()
     kv_terms()
+    o_sums.got()
+    sum_up(o_sum, o_got, o_grad)
     o_spread.start()
+    dn_task.turn(0)
+    m_turn(0)
+    gain_terms()
+    e_job.start()
     k_job.turn(1)
+    q_job.pair()
+    e_job.turn(1)
     q_job.turn(0)
-    dn_task.pair()
-    q_job.pair()
-    dn_task.turn(0)
-    gu_task.last(0)
+    e_job.pair()
+    k_job.pair()
     k_job.turn(0)
-    inputs_back()
-    norm_one_back()
-    k_job.pair()
-    gain_terms()
+    e_job.turn(0)
     dn_task.turn(1)
     q_job.finish(q_sum)
     q_sums.start()
+    e_job.finish(g_sum)
     k_job.finish(kv_sum)
-    e_job.start()
-    dn_task.last(0)
-    e_job.turn(1)
-    dn_task.last(1)
-    e_job.pair()
+    m_finish()
     k_sums.start()
-    e_job.turn(0)
+    e_begin()
     q_sums.got()
     sum_up(q_sum, q_got, q_grad)
     q_spread.start()
-    e_job.finish(g_sum)
+    dn_task.last(0)
+    o_spread.got()
     k_sums.got()
+    dn_task.last(1)
     sum_up(kv_sum, k_got, kv_grad)
+    k_spread.start()
+    e_task.got()
+    q_spread.got()
     gu_task.last(1)
-    k_spread.start()
-    o_spread.got()
-    e_begin()
     k_spread.got()
-    q_spread.got()
-    e_task.got()
     total = ggot[0]
     for index in range(1, 8):
         total = total + ggot[index]
@@ -1399,28 +1461,103 @@
     return outs[:8]
 
 
-def widen_kernel(parts, gate, up):
-    for out, base in ((gate, 0), (up, 768)):
-        for pair in range(4):
-            even = parts[2 * pair, :, base : base + 768].astype(F32)
-            odd = pltpu.roll(parts[2 * pair + 1, :, base : base + 768].astype(F32), 64, 1)
-            first = 1408 * pair
-            out[:, first : first + 640] = even[:, 0:640]
-            out[:, first + 640 : first + 768] = even[:, 640:768] + odd[:, 0:128]
-            out[:, first + 768 : first + 1408] = odd[:, 128:768]
-
-
-def widen(parts):
-    out = jax.ShapeDtypeStruct((128, 5632), F32)
-    block = pl.BlockSpec((16, 5632), lambda i: (i, 0))
+def finish_kernel(
+    mixed_in, tokens_in, q_in, kv_in, o_in, gu_in, dn_in,
+    mixed, tokens_grad, q_out, key_out, value_out, o_out, gate_out, up_out, dn_out,
+    b_mixed, b_tokens, b_q, b_kv, b_o, b_gu, b_dn, f_q, f_key, f_value, f_o, f_gate, f_up, f_dn, sems,
+):
+    slots = iter(range(24))
+
+    def move(src, dst):
+        return pltpu.make_async_copy(src, dst, sems.at[next(slots)])
+
+    loads = [
+        move(src, dst)
+        for src, dst in (
+            (gu_in.at[pl.ds(0, 4)], b_gu.at[pl.ds(0, 4)]), (gu_in.at[pl.ds(4, 4)], b_gu.at[pl.ds(4, 4)]), (dn_in, b_dn),
+            (q_in, b_q), (o_in, b_o), (kv_in, b_kv), (mixed_in, b_mixed), (tokens_in, b_tokens),
+        )
+    ]
+    for copy in loads:
+        copy.start()
+    stores = []
+
+    def store(src, dst):
+        copy = move(src, dst)
+        copy.start()
+        stores.append(copy)
+
+    def widen(pair):
+        first = 1408 * pair
+
+        @pl.loop(0, 8)
+        def _(i):
+            rows = pl.ds(pl.multiple_of(16 * i, 16), 16)
+            for out, base in ((f_gate, 0), (f_up, 768)):
+                even = b_gu[2 * pair, rows, base : base + 768].astype(F32)
+                odd = pltpu.roll(b_gu[2 * pair + 1, rows, base : base + 768].astype(F32), 64, 1)
+                out[rows, first : first + 640] = even[:, 0:640]
+                out[rows, first + 640 : first + 768] = even[:, 640:768] + odd[:, 0:128]
+                out[rows, first + 768 : first + 1408] = odd[:, 128:768]
+
+    for half in (0, 1):
+        loads[half].wait()
+        widen(2 * half)
+        widen(2 * half + 1)
+        wide = pl.ds(2816 * half, 2816)
+        store(f_gate.at[:, wide], gate_out.at[:, wide])
+        store(f_up.at[:, wide], up_out.at[:, wide])
+
+    def cast(src, dst, rows):
+        @pl.loop(0, rows // 32)
+        def _(i):
+            at = pl.ds(pl.multiple_of(32 * i, 32), 32)
+            dst[at] = src[at].astype(F32)
+
+    loads[2].wait()
+    cast(b_dn, f_dn, 352)
+    store(f_dn, dn_out)
+    loads[3].wait()
+    cast(b_q, f_q, 128)
+    store(f_q, q_out)
+    loads[4].wait()
+    cast(b_o, f_o, 128)
+    store(f_o, o_out)
+    loads[5].wait()
+    f_key[...] = b_kv[:, 0:256].astype(F32)
+    f_value[...] = b_kv[:, 256:512].astype(F32)
+    store(f_key, key_out)
+    store(f_value, value_out)
+    loads[6].wait()
+    store(b_mixed, mixed)
+    loads[7].wait()
+    store(b_tokens, tokens_grad)
+    for copy in stores:
+        copy.wait()
+
+
+def finish(mixed, tokens_grad, q, kv, o, gu, dn):
+    shape, vmem = jax.ShapeDtypeStruct, pltpu.VMEM
+    wholes = [(128, 2048), (128, 256), (128, 256), (128, 2048), (128, 5632), (128, 5632), (352, 2048)]
     return pl.pallas_call(
-        widen_kernel,
-        grid=(8,),
-        out_shape=(out, out),
-        in_specs=[pl.BlockSpec((8, 16, 1536), lambda i: (0, i, 0))],
-        out_specs=[block, block],
-        name="widen",
-    )(parts)
+        finish_kernel,
+        out_shape=(shape((128, 2048), BF), shape((128, 2048), BF), *[shape(dims, F32) for dims in wholes]),
+        in_specs=[ANY] * 7,
+        out_specs=[ANY] * 9,
+        scratch_shapes=[
+            vmem((128, 2048), BF),
+            vmem((128, 2048), BF),
+            vmem((128, 2048), BF),
+            vmem((128, 512), BF),
+            vmem((128, 2048), BF),
+            vmem((8, 128, 1536), BF),
+            vmem((352, 2048), BF),
+            *[vmem(dims, F32) for dims in wholes],
+            pltpu.SemaphoreType.DMA((24,)),
+        ],
+        compiler_params=pltpu.CompilerParams(vmem_limit_bytes=62 << 20),
+        name="finish",
+    )(mixed, tokens_grad, q, kv, o, gu, dn)
 
 
 def on_device(
@@ -1437,27 +1574,15 @@
     down_weight,
     cotangent,
 ):
-    freq = BASE ** (-(jnp.arange(HEAD_DIM // 2, dtype=F32) * 2.0) / HEAD_DIM)
-    freq = jnp.concatenate([freq] * 4)[None]
+    freq = BASE ** (-(np.arange(HEAD_DIM // 2, dtype=np.float32) * 2.0) / HEAD_DIM)
+    freq = np.concatenate([freq] * 4)[None].astype(np.float32)
     deal = block_deal.reshape(256)
     mixed, tokens_grad, query_grad, kv_grad, o_grad, gain_grads, gu_grads, dn_grad = layer(
         tokens[0], attn_gain[None], mlp_gain[None], deal, freq, query_weight, key_weight, value_weight, output_weight,
         gate_weight, up_weight, down_weight, cotangent[0],
     )
-    gate_grad, up_grad = widen(gu_grads)
-    return (
-        mixed[None],
-        tokens_grad[None],
-        gain_grads[0],
-        query_grad.astype(F32),
-        kv_grad[:, :256].astype(F32),
-        kv_grad[:, 256:].astype(F32),
-        o_grad.astype(F32),
-        gain_grads[8],
-        gate_grad,
-        up_grad,
-        dn_grad.astype(F32),
-    )
+    mixed, tokens_grad, *grads = finish(mixed, tokens_grad, query_grad, kv_grad, o_grad, gu_grads, dn_grad)
+    return (mixed[None], tokens_grad[None], gain_grads[0], *grads[:4], gain_grads[8], *grads[4:])
 
 
 def solution(mesh):

time: 315 us -> 311 us (0.987)
  other arithmetic: 8.34 us -> 0 us
  Pallas kernels: 299 us -> 303 us
    convert_element_type x4 -> x0, other arithmetic: 7.74 us -> none  [the longest x1 2.12 us: on_device(): query_grad.astype(F32)]
where the time goes in v8:
time: 311 us; the launch traced here: 307 us
  Pallas kernels  303 us (97%)
    pallas_call x1, Pallas kernels, layer(): pl.pallas_call(layer_kernel, out_shape=(shape((128, 2048), BF), shape((12...  296 us
    pallas_call x1, Pallas kernels, finish(): pl.pallas_call(finish_kernel, out_shape=(shape((128, 2048), BF), shape((1...  7.73 us

profile of v8, /device:TPU:0, one launch (start us, length us, event | category | flops | bytes accessed | tf_op | source)
XLA Modules:
  0.0 306.9 jit_solution(2179390095782966310)
XLA Ops:
  0.6 0.8 copy.24
  1.5 0.7 reshape.25.deal
  2.2 295.6 %layer.1 = (bf16[128,2048]{1,0:T(8,128)(2,1)}, bf16[128,2048]{1,0:T(8,128)(2,1)}, bf16[128,2048]{1,0:T(8,128)(2,1)}, bf16[128,512]{1,0:T(8,128)(2,1)}, bf16[128,...) custom-call(bf16[128,2048]{1,0:T(8,128)(2,1)} %bitcast.10, ...), custom_call_target="tpu_custom_call" | custom-call | tf_op jit(solution)/shard_map/layer/pallas_call | solution.py:1374
  297.8 1.2 slice_bitcast_fusion
  299.0 7.7 %finish.1 = (bf16[128,2048]{1,0:T(8,128)(2,1)}, bf16[128,2048]{1,0:T(8,128)(2,1)}, f32[128,2048]{1,0:T(8,128)}, f32[128,256]{1,0:T(8,128)}, f32[128,256]{1,0:T(8...) custom-call(bf16[128,2048]{1,0:T(8,128)(2,1)} %get-tuple-element.28.mixed_in, ...), custom_call_target="tpu_custom_call" | custom-call | tf_op jit(solution)/shard_map/finish/pallas_call | solution.py:1542

commit v9 on v8

--- a/solution.py
+++ b/solution.py
@@ -373,7 +373,7 @@
 
 def place_tables(me, deal, freq, cosine, sine, bias_p, bias_c):
     def block(slot, part):
-        return deal[(me.f * 8 + me.ctx_at(STEPS[slot], PAIRS[slot])) * 2 + part]
+        return deal[me.f, me.ctx_at(STEPS[slot], PAIRS[slot]), part]
 
     first, second = block(0, 0), block(0, 1)
     odd = lax.rem(second, 2)
@@ -395,22 +395,11 @@
     return mate
 
 
-def find_mate(me, deal):
-    def block(slot):
-        return deal[(me.f * 8 + me.ctx_at(STEPS[slot], PAIRS[slot])) * 2 + 1]
-
-    second = block(0)
-    mate = jnp.int32(0)
-    for slot in range(1, 8):
-        mate = mate + jnp.where(block(slot) == second + 1 - 2 * lax.rem(second, 2), slot, 0)
-    return mate
-
-
 def layer_kernel(
-    x, attn_gain, mlp_gain, deal, freq, q_in, key_in, value_in, wo_in, gate_in, up_in, dn_in, dy_in,
+    x_in, attn_gain, mlp_gain, deal, freq, q_in, key_in, value_in, wo_in, gate_in, up_in, dn_in, dy_in,
     mixed, tokens_grad, q_grad, kv_grad, o_grad, gains_out, gu_all, dn_all,
     q_saved, kw_saved, wo_saved, mpart, m_half, m_full, m_pair,
-    gains, a1s, atts, qst, kst, vst, lse, h1, cosine, sine, bias_p, bias_c,
+    x, gains, a1s, atts, qst, kst, vst, lse, h1, cosine, sine, bias_p, bias_c,
     qw, kw, wo, kv_own, kv, sT, pT, dT, dsT, scale, gu_win, dnp, acts, gu, wd, dy, hid,
     grecv, gdrecv, g_pair, da2, datts, dqkvs, grow, gown_rows, gsib_rows, dn_moved,
     n_half, n_full, n_pair, e_half, e_full, e_pair, gp, ggot, g_sum, o_got, q_got, k_got,
@@ -498,12 +487,13 @@
     dn = over_x(dnp, wd_at, 7)
     qy = over_y(None, strip_y(qw, 1024), 0)
     oy = over_y(None, strip_y(wo, 1024), 1)
-    dy_task = RingFirst(me.across_y, dy_in, slot_at(dy, 128), (y0, y1), 2)
+    dy_task = over_y(dy_in, slot_at(dy, 128), 2, both=False)
     kv_task = over_y(kv_own, slot_at(kv, 128), 3, both=False)
     a = over_y(None, acts_at, 4, both=False)
     swap = Swap(me, dn_in.at[:, pl.ds(pl.multiple_of(me.c * 256, 256), 256)], dnp, (w0, w1), local.at[next(slots)])
 
     own_kw = plain(kw, 512)(0, 0, 0, 0, None)
+    x_load = load(x_in, x)
     loads = [load(key_in, own_kw.at[:, pl.ds(0, 256)]), load(value_in, own_kw.at[:, pl.ds(256, 256)])]
     kept = {task: load(task.own, task.loc(0, 0, 0, 0, None)) for task in (q, qx, o, ox, dy_task)}
     window = pl.ds(pl.multiple_of(me.y * 1408 + me.zl * 640, 128), 768)
@@ -718,8 +708,8 @@
     d = scatter(me.across_y, lambda slot: dpart.at[slot], second_bay, 2048, 0)
     gjob = scatter(me.across_x, gown, first_bay, 1536, 1, g_pair)
     n_job = Scatter(me.across_x, gd_own, 352, n_half, n_full, n_pair, (r0, r1), 2)
-    o_job = scatter(me.across_x, lambda slot: op.at[slot], first_bay, 2048, 3)
-    q_job = scatter(me.across_x, lambda slot: qp.at[slot], second_bay, 2048, 4)
+    o_job = scatter(me.across_x, lambda slot: op.at[slot], second_bay, 2048, 3)
+    q_job = scatter(me.across_x, lambda slot: qp.at[slot], first_bay, 2048, 4)
     k_job = scatter(me.across_x, kp, kw.at[:, 0], 512, 5)
     e_job = Scatter(me.across_x, lambda slot: gp.at[slot], 16, e_half, e_full, e_pair, (r0, r1), 6)
     d_job = scatter(me.across_y, lambda slot: kvp.at[slot], kw.at[:, 1], 512, 7)
@@ -1085,87 +1075,87 @@
         grecv[pl.ds(0, 5), :, pl.ds(pl.multiple_of(128 * n, 128), 128)] = both.reshape(5, 128, 128)
 
     qx.start()
-    g.start()
+    ox.start()
+    dy_task.start()
     loads[0].wait()
     loads[1].wait()
     k.start()
-    dy_task.go(1, 2)
-    ox.start()
+    qx.turn(0)
+    ox.pair()
+    ox.turn(0)
+    ox.turn(1)
+    g.start()
     qx.pair()
-    qx.turn(0)
+    qx.last(0)
+    ox.last(1)
+    ox.last(0)
+    g.turn(0)
+    k.turn(0)
+    kept[ox].wait()
+    oy.start()
+    qx.turn(1)
     q.start()
-    qx.turn(1)
-    qx.last(0)
-    put_gate_up()
-    g.pair()
-    ox.pair()
+    k.last(0)
+    qx.last(1)
     swap.start()
-    k.pair()
-    k.turn(0)
-    ox.turn(0)
-    qx.last(1)
     kept[qx].wait()
     qy.start()
+    g.pair()
+    k.pair()
+    oy.turn(0)
     q.turn(0)
-    g.turn(0)
+    oy.pair()
     k.turn(1)
     g.turn(1)
-    ox.turn(1)
+    g.last(0)
     o.start()
-    ox.last(0)
+    g.last(1)
+    qy.turn(0)
     mate = place_tables(me, deal, freq, cosine, sine, bias_p, bias_c)
     q.pair()
+    k.last(1)
+    g.sync()
+    k.sync()
+    x_load.wait()
+    normed()
+    oy.turn(1)
+    q.last(0)
+    project_kv()
+    kv_task.start()
+    oy.last(0)
+    o.turn(0)
     qy.pair()
-    k.last(0)
-    g.last(1)
-    g.last(0)
-    ox.last(1)
+    put_gate_up()
+    q.turn(1)
+    o.pair()
+    kv_task.pair()
+    oy.last(1)
     swap.wait()
     dn_local.start()
     dn.start()
-    k.last(1)
-    qy.turn(0)
-    o.pair()
-    kept[ox].wait()
-    oy.start()
+    kv_task.turn(0)
     qy.turn(1)
-    g.sync()
-    q.last(0)
-    normed()
+    q.last(1)
+    kv_task.turn(1)
     qy.last(0)
-    k.sync()
-    project_kv()
-    q.turn(1)
-    kv_task.start()
-    dy_task.go(0)
-    kv_task.pair()
-    o.turn(0)
-    kv_task.turn(0)
+    o.turn(1)
+    m.start()
+    dy_task.pair()
+    o.last(0)
+    oy.sync()
+    dy_task.turn(0)
+    kv_task.last(1)
     qy.last(1)
-    oy.pair()
-    o.turn(1)
-    q.last(1)
-    m.start()
-    kv_task.turn(1)
+    dn.turn(0)
+    kv_task.last(0)
+    q.sync()
     dn.pair()
-    oy.turn(0)
-    o.last(0)
+    collect_kv(mate)
     qy.sync()
-    q.sync()
     kept[q].wait()
     saved.append(load(qw, q_saved))
     saved.append(load(kw, kw_saved))
     project_q()
-    o.last(1)
-    dn.turn(0)
-    oy.turn(1)
-    dy_task.got(1, 2)
-    dy_task.go(3, 4)
-    dy_task.go(5)
-    kv_task.last(0)
-    kv_task.last(1)
-    dy_task.got(0)
-    collect_kv(mate)
 
     @pl.loop(0, 4)
     def _(n):
@@ -1174,37 +1164,37 @@
 
         @pl.when(n == 0)
         def _():
-            o.sync()
-            oy.last(0)
-
-        @pl.when(n == 1)
+            o.last(1)
+
+        @pl.when(n == 2)
         def _():
-            oy.last(1)
-            m.pair()
-
-    oy.sync()
+            dy_task.turn(1)
+
+    m.pair()
+    o.sync()
     kept[o].wait()
     saved.append(load(wo, wo_saved))
     project_o()
+    a1_swap.start()
     normed_two()
     for task in (k, q, qx, qy):
         task.end()
     saved[0].wait()
     saved[1].wait()
+    m.turn(0)
     a.start()
-    dy_task.go(6)
-    m.turn(0)
+    dy_task.last(0)
     m.turn(1)
-    dy_task.got(3, 4)
-    dy_task.go(7, 8)
+    dy_task.last(1)
     m.last(0)
     dn.turn(1)
     dn.last(0)
     a.pair()
+    att_swap.start()
     m.last(1)
-    a.turn(0)
     dn.last(1)
     m.sync()
+    a.turn(0)
     dn.sync()
 
     for task in (o, ox, oy, kv_task):
@@ -1220,11 +1210,9 @@
         @pl.when(n == 1)
         def _():
             a.turn(1)
-            dy_task.got(5, 6)
 
     a.last(0)
     group_half(6)
-    dy_task.got(7, 8)
     a.last(1)
     group_half(7)
     d.start()
@@ -1232,41 +1220,40 @@
     terms_for_sibling(0)
     terms_for_sibling(2)
     own_terms(0)
+    gjob.start()
     terms_for_sibling(4)
+    own_terms(2)
     d.turn(1)
+    terms_for_sibling(6)
+    own_terms(4)
+    gjob.turn(1)
     group_out()
-    gjob.start()
     dn.end()
     down_terms()
-    d.turn(0)
-    own_terms(2)
-    own_terms(4)
-    down_sums()
-    att_swap.start()
-    n_job.start()
-    gjob.turn(1)
-    terms_for_sibling(6)
-    d.pair()
-    gjob.turn(0)
-    n_job.turn(0)
-    n_job.turn(1)
-    m_start()
     own_terms(6)
     a.end()
     wo_load(0).start()
     wo_load(1).start()
-    gjob.pair()
+    d.turn(0)
+    down_sums()
+    n_job.start()
+    d.pair()
+    n_job.turn(1)
+    gjob.turn(0)
+    n_job.turn(0)
+    m_start()
+    n_job.pair()
     d.finish(da2)
-    m_turn(1)
     norm_two_back()
-    gjob.finish(gown(0))
     for device in near(me.across_x):
         pl.semaphore_signal(credit, 1, device_id=device, device_id_type=MESH)
-    gu_begin()
+    m_turn(1)
+    gjob.pair()
     d.end()
     output_terms()
+    n_job.finish(gd_own(0))
+    dn_swap.start()
     heads_back()
-    m_pair_up()
 
     @pl.loop(0, 4)
     def _(n):
@@ -1275,9 +1262,10 @@
 
         @pl.when(n == 0)
         def _():
-            gu_task.pair()
-            a1_swap.start()
+            dn_begin()
+            gjob.finish(gown(0))
             o_job.turn(1)
+            gu_begin()
 
         @pl.when(n == 1)
         def _():
@@ -1285,65 +1273,63 @@
 
     kv_blocks(mate)
     kw_back = kw_load()
+    d_job.start()
+    dn_task.pair()
+    d_job.turn(1)
+    o_job.pair()
+    d_job.turn(0)
     gu_task.turn(0)
-    d_job.start()
-    n_job.pair()
     dq_swap.start()
-    gu_task.turn(1)
-    o_job.pair()
-    d_job.turn(1)
     query_terms()
-    n_job.finish(gd_own(0))
-    dn_swap.start()
-    d_job.turn(0)
     d_job.pair()
+    gu_task.pair()
+    m_pair_up()
+    m_turn(0)
     o_job.finish(o_sum)
-    dn_begin()
-    gu_task.last(0)
+    d_job.finish(sT.at[pl.ds(512, 128)])
+    kv_back()
+    o_sums.start()
     q_job.turn(1)
-    d_job.finish(sT.at[pl.ds(512, 128)])
-    o_sums.start()
-    kv_back()
     inputs_back()
-    dn_task.pair()
     norm_one_back()
     sibling_has_terms()
     kv_terms()
+    gain_terms()
+    gu_task.last(0)
+    e_job.start()
+    q_job.turn(0)
+    q_job.pair()
+    gu_task.turn(1)
+    m_finish()
+    e_job.turn(1)
+    k_job.turn(1)
     o_sums.got()
     sum_up(o_sum, o_got, o_grad)
+    dn_task.turn(0)
     o_spread.start()
-    dn_task.turn(0)
-    m_turn(0)
-    gain_terms()
-    e_job.start()
-    k_job.turn(1)
-    q_job.pair()
-    e_job.turn(1)
-    q_job.turn(0)
+    dn_task.turn(1)
+    q_job.finish(q_sum)
+    k_job.turn(0)
+    gu_task.last(1)
     e_job.pair()
     k_job.pair()
-    k_job.turn(0)
+    q_sums.start()
     e_job.turn(0)
-    dn_task.turn(1)
-    q_job.finish(q_sum)
-    q_sums.start()
+    dn_task.last(1)
     e_job.finish(g_sum)
     k_job.finish(kv_sum)
-    m_finish()
+    dn_task.last(0)
+    e_begin()
     k_sums.start()
-    e_begin()
     q_sums.got()
     sum_up(q_sum, q_got, q_grad)
     q_spread.start()
-    dn_task.last(0)
     o_spread.got()
     k_sums.got()
-    dn_task.last(1)
     sum_up(kv_sum, k_got, kv_grad)
     k_spread.start()
     e_task.got()
     q_spread.got()
-    gu_task.last(1)
     k_spread.got()
     total = ggot[0]
     for index in range(1, 8):
@@ -1390,9 +1376,10 @@
             shape((2, 2, 128, 2048), BF),
             shape((128, 2048), BF),
         ),
-        in_specs=[VMEM] * 3 + [smem, VMEM] + [ANY] * 8,
+        in_specs=[ANY] + [VMEM] * 2 + [smem, VMEM] + [ANY] * 8,
         out_specs=[ANY] * 2 + [VMEM] * 4 + [ANY] * 9,
         scratch_shapes=[
+            vmem((128, 2048), BF),
             vmem((16, 16, 128), F32),
             vmem((256, 2048), BF),
             vmem((256, 2048), BF),
@@ -1462,8 +1449,8 @@
 
 
 def finish_kernel(
-    mixed_in, tokens_in, q_in, kv_in, o_in, gu_in, dn_in,
-    mixed, tokens_grad, q_out, key_out, value_out, o_out, gate_out, up_out, dn_out,
+    mixed_in, tokens_in, q_in, kv_in, o_in, gu_in, dn_in, gains,
+    mixed, tokens_grad, q_out, key_out, value_out, o_out, gate_out, up_out, dn_out, first_gain, second_gain,
     b_mixed, b_tokens, b_q, b_kv, b_o, b_gu, b_dn, f_q, f_key, f_value, f_o, f_gate, f_up, f_dn, sems,
 ):
     slots = iter(range(24))
@@ -1474,8 +1461,8 @@
     loads = [
         move(src, dst)
         for src, dst in (
-            (gu_in.at[pl.ds(0, 4)], b_gu.at[pl.ds(0, 4)]), (gu_in.at[pl.ds(4, 4)], b_gu.at[pl.ds(4, 4)]), (dn_in, b_dn),
-            (q_in, b_q), (o_in, b_o), (kv_in, b_kv), (mixed_in, b_mixed), (tokens_in, b_tokens),
+            (q_in, b_q), (o_in, b_o), (dn_in, b_dn), (gu_in.at[pl.ds(0, 4)], b_gu.at[pl.ds(0, 4)]),
+            (gu_in.at[pl.ds(4, 4)], b_gu.at[pl.ds(4, 4)]), (kv_in, b_kv), (mixed_in, b_mixed), (tokens_in, b_tokens),
         )
     ]
     for copy in loads:
@@ -1500,29 +1487,27 @@
                 out[rows, first + 640 : first + 768] = even[:, 640:768] + odd[:, 0:128]
                 out[rows, first + 768 : first + 1408] = odd[:, 128:768]
 
-    for half in (0, 1):
-        loads[half].wait()
-        widen(2 * half)
-        widen(2 * half + 1)
-        wide = pl.ds(2816 * half, 2816)
-        store(f_gate.at[:, wide], gate_out.at[:, wide])
-        store(f_up.at[:, wide], up_out.at[:, wide])
-
     def cast(src, dst, rows):
         @pl.loop(0, rows // 32)
         def _(i):
             at = pl.ds(pl.multiple_of(32 * i, 32), 32)
             dst[at] = src[at].astype(F32)
 
-    loads[2].wait()
-    cast(b_dn, f_dn, 352)
-    store(f_dn, dn_out)
-    loads[3].wait()
-    cast(b_q, f_q, 128)
-    store(f_q, q_out)
-    loads[4].wait()
-    cast(b_o, f_o, 128)
-    store(f_o, o_out)
+    for index, src, dst, out, rows in (
+        (0, b_q, f_q, q_out, 128), (1, b_o, f_o, o_out, 128), (2, b_dn, f_dn, dn_out, 352)
+    ):
+        loads[index].wait()
+        cast(src, dst, rows)
+        store(dst, out)
+    for half in (0, 1):
+        loads[3 + half].wait()
+        for pair in (2 * half, 2 * half + 1):
+            widen(pair)
+            wide = pl.ds(1408 * pair, 1408)
+            store(f_gate.at[:, wide], gate_out.at[:, wide])
+            store(f_up.at[:, wide], up_out.at[:, wide])
+    first_gain[...] = gains[0:1, :]
+    second_gain[...] = gains[8:9, :]
     loads[5].wait()
     f_key[...] = b_kv[:, 0:256].astype(F32)
     f_value[...] = b_kv[:, 256:512].astype(F32)
@@ -1536,14 +1521,14 @@
         copy.wait()
 
 
-def finish(mixed, tokens_grad, q, kv, o, gu, dn):
+def finish(mixed, tokens_grad, q, kv, o, gu, dn, gains):
     shape, vmem = jax.ShapeDtypeStruct, pltpu.VMEM
     wholes = [(128, 2048), (128, 256), (128, 256), (128, 2048), (128, 5632), (128, 5632), (352, 2048)]
     return pl.pallas_call(
         finish_kernel,
-        out_shape=(shape((128, 2048), BF), shape((128, 2048), BF), *[shape(dims, F32) for dims in wholes]),
-        in_specs=[ANY] * 7,
-        out_specs=[ANY] * 9,
+        out_shape=(shape((128, 2048), BF), shape((128, 2048), BF), *[shape(dims, F32) for dims in (*wholes, (1, 128), (1, 128))]),
+        in_specs=[ANY] * 7 + [VMEM],
+        out_specs=[ANY] * 9 + [VMEM] * 2,
         scratch_shapes=[
             vmem((128, 2048), BF),
             vmem((128, 2048), BF),
@@ -1557,7 +1542,7 @@
         ],
         compiler_params=pltpu.CompilerParams(vmem_limit_bytes=62 << 20),
         name="finish",
-    )(mixed, tokens_grad, q, kv, o, gu, dn)
+    )(mixed, tokens_grad, q, kv, o, gu, dn, gains)
 
 
 def on_device(
@@ -1576,13 +1561,14 @@
 ):
     freq = BASE ** (-(np.arange(HEAD_DIM // 2, dtype=np.float32) * 2.0) / HEAD_DIM)
     freq = np.concatenate([freq] * 4)[None].astype(np.float32)
-    deal = block_deal.reshape(256)
     mixed, tokens_grad, query_grad, kv_grad, o_grad, gain_grads, gu_grads, dn_grad = layer(
-        tokens[0], attn_gain[None], mlp_gain[None], deal, freq, query_weight, key_weight, value_weight, output_weight,
+        tokens[0], attn_gain[None], mlp_gain[None], block_deal, freq, query_weight, key_weight, value_weight, output_weight,
         gate_weight, up_weight, down_weight, cotangent[0],
     )
-    mixed, tokens_grad, *grads = finish(mixed, tokens_grad, query_grad, kv_grad, o_grad, gu_grads, dn_grad)
-    return (mixed[None], tokens_grad[None], gain_grads[0], *grads[:4], gain_grads[8], *grads[4:])
+    mixed, tokens_grad, *grads, first_gain, second_gain = finish(
+        mixed, tokens_grad, query_grad, kv_grad, o_grad, gu_grads, dn_grad, gain_grads
+    )
+    return (mixed[None], tokens_grad[None], first_gain[0], *grads[:4], second_gain[0], *grads[4:])
 
 
 def solution(mesh):

time: 311 us -> 311 us (level)
  no operation moved by 1% of the time
where the time goes in v9:
time: 311 us; the launch traced here: 308 us
  Pallas kernels  305 us (98%)
    pallas_call x1, Pallas kernels, layer(): pl.pallas_call(layer_kernel, out_shape=(shape((128, 2048), BF), shape((12...  297 us
    pallas_call x1, Pallas kernels, finish(): pl.pallas_call(finish_kernel, out_shape=(shape((128, 2048), BF), shape((1...  8.24 us

profile of v9, /device:TPU:0, one launch (start us, length us, event | category | flops | bytes accessed | tf_op | source)
XLA Modules:
  0.0 307.5 jit_solution(1424669906409454830)
XLA Ops:
  0.6 1.4 copy.24.deal
  2.1 297.0 %layer.1 = (bf16[128,2048]{1,0:T(8,128)(2,1)}, bf16[128,2048]{1,0:T(8,128)(2,1)}, bf16[128,2048]{1,0:T(8,128)(2,1)}, bf16[128,512]{1,0:T(8,128)(2,1)}, bf16[128,...) custom-call(bf16[128,2048]{1,0:T(8,128)(2,1)} %bitcast.8, ...), custom_call_target="tpu_custom_call" | custom-call | tf_op jit(solution)/shard_map/layer/pallas_call | solution.py:1360
  299.1 8.2 %finish.1 = (bf16[128,2048]{1,0:T(8,128)(2,1)}, bf16[128,2048]{1,0:T(8,128)(2,1)}, f32[128,2048]{1,0:T(8,128)}, f32[128,256]{1,0:T(8,128)}, f32[128,256]{1,0:T(8...) custom-call(bf16[128,2048]{1,0:T(8,128)(2,1)} %get-tuple-element.30., ...), custom_call_target="tpu_custom_call" | custom-call | tf_op jit(solution)/shard_map/finish/pallas_call | solution.py:1527

commit v10 on v9

--- a/solution.py
+++ b/solution.py
@@ -1075,87 +1075,81 @@
         grecv[pl.ds(0, 5), :, pl.ds(pl.multiple_of(128 * n, 128), 128)] = both.reshape(5, 128, 128)
 
     qx.start()
-    ox.start()
     dy_task.start()
+    g.start()
     loads[0].wait()
     loads[1].wait()
     k.start()
+    g.turn(0)
     qx.turn(0)
-    ox.pair()
-    ox.turn(0)
-    ox.turn(1)
-    g.start()
     qx.pair()
+    ox.start()
     qx.last(0)
-    ox.last(1)
-    ox.last(0)
-    g.turn(0)
-    k.turn(0)
-    kept[ox].wait()
-    oy.start()
     qx.turn(1)
-    q.start()
-    k.last(0)
+    o.start()
+    swap.start()
     qx.last(1)
-    swap.start()
     kept[qx].wait()
     qy.start()
+    mate = place_tables(me, deal, freq, cosine, sine, bias_p, bias_c)
+    q.start()
     g.pair()
+    dy_task.pair()
     k.pair()
-    oy.turn(0)
-    q.turn(0)
-    oy.pair()
-    k.turn(1)
+    qy.turn(0)
     g.turn(1)
     g.last(0)
-    o.start()
+    k.turn(0)
+    ox.turn(0)
+    k.turn(1)
+    q.turn(0)
+    ox.pair()
     g.last(1)
-    qy.turn(0)
-    mate = place_tables(me, deal, freq, cosine, sine, bias_p, bias_c)
-    q.pair()
+    k.last(0)
+    qy.pair()
     k.last(1)
+    o.pair()
+    ox.turn(1)
     g.sync()
     k.sync()
     x_load.wait()
     normed()
-    oy.turn(1)
-    q.last(0)
     project_kv()
+    qy.last(0)
+    ox.last(0)
     kv_task.start()
-    oy.last(0)
-    o.turn(0)
-    qy.pair()
-    put_gate_up()
-    q.turn(1)
-    o.pair()
-    kv_task.pair()
-    oy.last(1)
+    q.pair()
+    ox.last(1)
+    qy.turn(1)
     swap.wait()
     dn_local.start()
     dn.start()
+    kv_task.pair()
+    kept[ox].wait()
+    oy.start()
     kv_task.turn(0)
-    qy.turn(1)
+    q.turn(1)
+    o.turn(0)
+    qy.last(1)
+    kv_task.turn(1)
+    o.turn(1)
+    put_gate_up()
+    qy.sync()
+    m.start()
     q.last(1)
-    kv_task.turn(1)
-    qy.last(0)
-    o.turn(1)
-    m.start()
-    dy_task.pair()
-    o.last(0)
-    oy.sync()
-    dy_task.turn(0)
-    kv_task.last(1)
-    qy.last(1)
-    dn.turn(0)
+    q.last(0)
+    oy.pair()
+    q.sync()
+    oy.turn(0)
     kv_task.last(0)
-    q.sync()
-    dn.pair()
-    collect_kv(mate)
-    qy.sync()
     kept[q].wait()
     saved.append(load(qw, q_saved))
     saved.append(load(kw, kw_saved))
     project_q()
+    kv_task.last(1)
+    collect_kv(mate)
+    a1_swap.start()
+    o.last(1)
 
     @pl.loop(0, 4)
     def _(n):
@@ -1164,37 +1158,45 @@
 
         @pl.when(n == 0)
         def _():
-            o.last(1)
+            oy.turn(1)
+            dn.turn(0)
+            dn.pair()
+            o.last(0)
+
+        @pl.when(n == 1)
+        def _():
+            dy_task.turn(0)
+            oy.last(0)
 
         @pl.when(n == 2)
         def _():
             dy_task.turn(1)
-
-    m.pair()
+            oy.last(1)
+            m.pair()
+
     o.sync()
+    oy.sync()
     kept[o].wait()
     saved.append(load(wo, wo_saved))
     project_o()
-    a1_swap.start()
     normed_two()
     for task in (k, q, qx, qy):
         task.end()
     saved[0].wait()
     saved[1].wait()
+    a.start()
     m.turn(0)
-    a.start()
-    dy_task.last(0)
+    dn.last(0)
     m.turn(1)
-    dy_task.last(1)
+    dn.turn(1)
+    m.last(1)
     m.last(0)
-    dn.turn(1)
-    dn.last(0)
     a.pair()
-    att_swap.start()
-    m.last(1)
     dn.last(1)
     m.sync()
-    a.turn(0)
+    att_swap.start()
+    dy_task.last(1)
+    dy_task.last(0)
     dn.sync()
 
     for task in (o, ox, oy, kv_task):
@@ -1206,6 +1208,10 @@
     @pl.loop(0, 3)
     def _(n):
         group(n)
+
+        @pl.when(n == 0)
+        def _():
+            a.turn(0)
 
         @pl.when(n == 1)
         def _():
@@ -1222,38 +1228,38 @@
     own_terms(0)
     gjob.start()
     terms_for_sibling(4)
+    terms_for_sibling(6)
+    d.turn(1)
     own_terms(2)
-    d.turn(1)
-    terms_for_sibling(6)
     own_terms(4)
+    group_out()
     gjob.turn(1)
-    group_out()
     dn.end()
     down_terms()
-    own_terms(6)
-    a.end()
-    wo_load(0).start()
-    wo_load(1).start()
-    d.turn(0)
     down_sums()
     n_job.start()
+    d.turn(0)
     d.pair()
     n_job.turn(1)
     gjob.turn(0)
     n_job.turn(0)
     m_start()
+    own_terms(6)
+    a.end()
+    wo_load(0).start()
+    wo_load(1).start()
     n_job.pair()
     d.finish(da2)
     norm_two_back()
     for device in near(me.across_x):
         pl.semaphore_signal(credit, 1, device_id=device, device_id_type=MESH)
+    gjob.pair()
     m_turn(1)
-    gjob.pair()
     d.end()
     output_terms()
-    n_job.finish(gd_own(0))
-    dn_swap.start()
     heads_back()
+    gjob.finish(gown(0))
+    gu_begin()
 
     @pl.loop(0, 4)
     def _(n):
@@ -1262,74 +1268,74 @@
 
         @pl.when(n == 0)
         def _():
-            dn_begin()
-            gjob.finish(gown(0))
             o_job.turn(1)
-            gu_begin()
-
-        @pl.when(n == 1)
+            m_pair_up()
+
+        @pl.when(n == 2)
         def _():
+            gu_task.pair()
             o_job.turn(0)
 
     kv_blocks(mate)
     kw_back = kw_load()
+    dq_swap.start()
     d_job.start()
-    dn_task.pair()
+    n_job.finish(gd_own(0))
+    dn_swap.start()
+    o_job.pair()
+    query_terms()
+    gu_task.turn(0)
     d_job.turn(1)
-    o_job.pair()
     d_job.turn(0)
-    gu_task.turn(0)
-    dq_swap.start()
-    query_terms()
+    gu_task.last(0)
+    gu_task.turn(1)
     d_job.pair()
-    gu_task.pair()
-    m_pair_up()
-    m_turn(0)
     o_job.finish(o_sum)
+    o_sums.start()
+    q_job.turn(1)
     d_job.finish(sT.at[pl.ds(512, 128)])
     kv_back()
-    o_sums.start()
-    q_job.turn(1)
+    m_turn(0)
+    dn_begin()
     inputs_back()
-    norm_one_back()
+    o_sums.got()
+    sum_up(o_sum, o_got, o_grad)
     sibling_has_terms()
     kv_terms()
+    o_spread.start()
+    q_job.pair()
+    dn_task.pair()
+    gu_task.last(1)
+    k_job.turn(1)
+    q_job.turn(0)
+    m_finish()
+    norm_one_back()
     gain_terms()
-    gu_task.last(0)
+    dn_task.turn(0)
+    k_job.turn(0)
+    k_job.pair()
     e_job.start()
-    q_job.turn(0)
-    q_job.pair()
-    gu_task.turn(1)
-    m_finish()
-    e_job.turn(1)
-    k_job.turn(1)
-    o_sums.got()
-    sum_up(o_sum, o_got, o_grad)
-    dn_task.turn(0)
-    o_spread.start()
     dn_task.turn(1)
     q_job.finish(q_sum)
-    k_job.turn(0)
-    gu_task.last(1)
-    e_job.pair()
-    k_job.pair()
     q_sums.start()
     e_job.turn(0)
-    dn_task.last(1)
-    e_job.finish(g_sum)
+    e_job.turn(1)
     k_job.finish(kv_sum)
+    e_job.pair()
+    k_sums.start()
     dn_task.last(0)
-    e_begin()
-    k_sums.start()
     q_sums.got()
     sum_up(q_sum, q_got, q_grad)
     q_spread.start()
-    o_spread.got()
+    e_job.finish(g_sum)
+    e_begin()
     k_sums.got()
     sum_up(kv_sum, k_got, kv_grad)
     k_spread.start()
+    o_spread.got()
+    q_spread.got()
     e_task.got()
-    q_spread.got()
+    dn_task.last(1)
     k_spread.got()
     total = ggot[0]
     for index in range(1, 8):

time: 311 us -> 302 us (0.971)
  Pallas kernels: 305 us -> 299 us
    pallas_call x1, Pallas kernels: 297 us -> 291 us  [layer(): pl.pallas_call(layer_kernel, out_shape=(shape((128, 2048), BF), shape((12...]
where the time goes in v10:
time: 302 us; the launch traced here: 301 us
  Pallas kernels  299 us (99%)
    pallas_call x1, Pallas kernels, layer(): pl.pallas_call(layer_kernel, out_shape=(shape((128, 2048), BF), shape((12...  291 us
    pallas_call x1, Pallas kernels, finish(): pl.pallas_call(finish_kernel, out_shape=(shape((128, 2048), BF), shape((1...  8.24 us

profile of v10, /device:TPU:0, one launch (start us, length us, event | category | flops | bytes accessed | tf_op | source)
XLA Modules:
  0.0 301.1 jit_solution(4295612546669762470)
XLA Ops:
  0.6 1.4 copy.24.deal
  2.1 290.6 %layer.1 = (bf16[128,2048]{1,0:T(8,128)(2,1)}, bf16[128,2048]{1,0:T(8,128)(2,1)}, bf16[128,2048]{1,0:T(8,128)(2,1)}, bf16[128,512]{1,0:T(8,128)(2,1)}, bf16[128,...) custom-call(bf16[128,2048]{1,0:T(8,128)(2,1)} %bitcast.8, ...), custom_call_target="tpu_custom_call" | custom-call | tf_op jit(solution)/shard_map/layer/pallas_call | solution.py:1366
  292.7 8.2 %finish.1 = (bf16[128,2048]{1,0:T(8,128)(2,1)}, bf16[128,2048]{1,0:T(8,128)(2,1)}, f32[128,2048]{1,0:T(8,128)}, f32[128,256]{1,0:T(8,128)}, f32[128,256]{1,0:T(8...) custom-call(bf16[128,2048]{1,0:T(8,128)(2,1)} %get-tuple-element.30., ...), custom_call_target="tpu_custom_call" | custom-call | tf_op jit(solution)/shard_map/finish/pallas_call | solution.py:1533

commit v11 on v10

--- a/solution.py
+++ b/solution.py
@@ -373,7 +373,7 @@
 
 def place_tables(me, deal, freq, cosine, sine, bias_p, bias_c):
     def block(slot, part):
-        return deal[me.f, me.ctx_at(STEPS[slot], PAIRS[slot]), part]
+        return deal[me.ctx_at(STEPS[slot], PAIRS[slot]), part, me.f]
 
     first, second = block(0, 0), block(0, 1)
     odd = lax.rem(second, 2)
@@ -507,6 +507,7 @@
     qp = wo.at[:, 1]
     dgu = wo.at[:, 1, :, pl.ds(0, 1536)]
     kvp = kv
+    packed = gu.at[pl.ds(1024, 128), pl.ds(0, 1408)]
 
     def gsib(t):
         return gu.at[pl.ds(aligned(128 * t, 128), 128)]
@@ -858,10 +859,10 @@
         first = pl.multiple_of(me.ctx_at(dr, dp) * 256, 256)
         return dn_all.at[row_half(half, 352), pl.ds(first, 256)]
 
-    gu_task = over_y(gown(0), at_ctx(gu_all), 5, both=False)
+    gu_task = over_y(packed, at_ctx(gu_all), 5, both=False)
     dn_task = over_y(dn_moved, dn_at, 6, both=False)
     dn_swap = Swap(me, gd_own(0), dn_moved, (v0, v1), local.at[next(slots)])
-    gu_keep = later(gown(0), gu_all.at[me.c])
+    gu_keep = later(packed, gu_all.at[me.c])
     dn_keep = later(dn_moved, dn_at(0, 0, 0, 0, None))
     dn_local = later(dnp, wd_at(0, 0, 0, 0, None))
     tokens_out = later(datts.at[own], tokens_grad)
@@ -1032,6 +1033,7 @@
         dn_keep.start()
 
     def gu_begin():
+        pack()
         gu_keep.start()
         gu_task.start()
 
@@ -1067,6 +1069,16 @@
             first = pl.multiple_of(512 * n + 128 * i, 128)
             dqkvs[rows, pl.ds(first, 128)] = block.astype(BF)
         return dot_in(dsT[keys], query), dot_in(pT[keys], out)
+
+    def pack():
+        @pl.loop(0, 8)
+        def _(i):
+            here = pl.ds(pl.multiple_of(1024 + 16 * i, 16), 16)
+            gate = gu[here, 0:768].astype(F32)
+            up = pltpu.roll(gu[here, 768:1536].astype(F32), 64, 1)
+            gu[here, 0:640] = gate[:, 0:640].astype(BF)
+            gu[here, 640:768] = (gate[:, 640:768] + up[:, 0:128]).astype(BF)
+            gu[here, 768:1408] = up[:, 128:768].astype(BF)
 
     def keep_kv_grads(n, one, two):
         keys = jnp.concatenate([one[0] + two[0][0:512], two[0][512:640]], axis=0)
@@ -1372,7 +1384,7 @@
             shape((128, 512), BF),
             shape((128, 2048), BF),
             shape((16, 128), F32),
-            shape((8, 128, 1536), BF),
+            shape((8, 128, 1408), BF),
             shape((352, 2048), BF),
             shape((8, 2, 128, 2048), BF),
             shape((8, 2, 128, 512), BF),
@@ -1486,11 +1498,14 @@
         @pl.loop(0, 8)
         def _(i):
             rows = pl.ds(pl.multiple_of(16 * i, 16), 16)
-            for out, base in ((f_gate, 0), (f_up, 768)):
+            lane = lax.broadcasted_iota(jnp.int32, (16, 128), 1)
+            for out, base, turn in ((f_gate, 0, (0, 64)), (f_up, 640, (704, 0))):
                 even = b_gu[2 * pair, rows, base : base + 768].astype(F32)
-                odd = pltpu.roll(b_gu[2 * pair + 1, rows, base : base + 768].astype(F32), 64, 1)
+                odd = b_gu[2 * pair + 1, rows, base : base + 768].astype(F32)
+                even = pltpu.roll(even, turn[0], 1) if turn[0] else even
+                odd = pltpu.roll(odd, turn[1], 1) if turn[1] else odd
                 out[rows, first : first + 640] = even[:, 0:640]
-                out[rows, first + 640 : first + 768] = even[:, 640:768] + odd[:, 0:128]
+                out[rows, first + 640 : first + 768] = jnp.where(lane < 64, even[:, 640:768], odd[:, 0:128])
                 out[rows, first + 768 : first + 1408] = odd[:, 128:768]
 
     def cast(src, dst, rows):
@@ -1541,7 +1556,7 @@
             vmem((128, 2048), BF),
             vmem((128, 512), BF),
             vmem((128, 2048), BF),
-            vmem((8, 128, 1536), BF),
+            vmem((8, 128, 1408), BF),
             vmem((352, 2048), BF),
             *[vmem(dims, F32) for dims in wholes],
             pltpu.SemaphoreType.DMA((24,)),
@@ -1568,7 +1583,7 @@
     freq = BASE ** (-(np.arange(HEAD_DIM // 2, dtype=np.float32) * 2.0) / HEAD_DIM)
     freq = np.concatenate([freq] * 4)[None].astype(np.float32)
     mixed, tokens_grad, query_grad, kv_grad, o_grad, gain_grads, gu_grads, dn_grad = layer(
-        tokens[0], attn_gain[None], mlp_gain[None], block_deal, freq, query_weight, key_weight, value_weight, output_weight,
+        tokens[0], attn_gain[None], mlp_gain[None], block_deal.transpose(1, 2, 0), freq, query_weight, key_weight, value_weight, output_weight,
         gate_weight, up_weight, down_weight, cotangent[0],
     )
     mixed, tokens_grad, *grads, first_gain, second_gain = finish(

time: 302 us -> 296 us (0.980)
  Pallas kernels: 299 us -> 295 us
    pallas_call x1, Pallas kernels: 291 us -> 287 us  [layer(): pl.pallas_call(layer_kernel, out_shape=(shape((128, 2048), BF), shape((12...]
where the time goes in v11:
time: 296 us
  Pallas kernels  295 us (100%)
    pallas_call x1, Pallas kernels, layer(): pl.pallas_call(layer_kernel, out_shape=(shape((128, 2048), BF), shape((12...  287 us
    pallas_call x1, Pallas kernels, finish(): pl.pallas_call(finish_kernel, out_shape=(shape((128, 2048), BF), shape((1...  7.97 us

profile of v11, /device:TPU:0, one launch (start us, length us, event | category | flops | bytes accessed | tf_op | source)
XLA Modules:
  0.0 295.9 jit_solution(11643325386215559749)
XLA Ops:
  0.6 287.1 %layer.1 = (bf16[128,2048]{1,0:T(8,128)(2,1)}, bf16[128,2048]{1,0:T(8,128)(2,1)}, bf16[128,2048]{1,0:T(8,128)(2,1)}, bf16[128,512]{1,0:T(8,128)(2,1)}, bf16[128,...) custom-call(bf16[128,2048]{1,0:T(8,128)(2,1)} %bitcast.9, ...), custom_call_target="tpu_custom_call" | custom-call | tf_op jit(solution)/shard_map/layer/pallas_call | solution.py:1378
  287.8 8.0 %finish.1 = (bf16[128,2048]{1,0:T(8,128)(2,1)}, bf16[128,2048]{1,0:T(8,128)(2,1)}, f32[128,2048]{1,0:T(8,128)}, f32[128,256]{1,0:T(8,128)}, f32[128,256]{1,0:T(8...) custom-call(bf16[128,2048]{1,0:T(8,128)(2,1)} %get-tuple-element.30., ...), custom_call_target="tpu_custom_call" | custom-call | tf_op jit(solution)/shard_map/finish/pallas_call | solution.py:1548

commit v12 on v11

--- a/solution.py
+++ b/solution.py
@@ -1088,80 +1088,80 @@
 
     qx.start()
     dy_task.start()
-    g.start()
     loads[0].wait()
     loads[1].wait()
     k.start()
-    g.turn(0)
+    qx.pair()
     qx.turn(0)
-    qx.pair()
     ox.start()
+    put_gate_up()
+    k.turn(0)
+    qx.turn(1)
+    g.start()
+    q.start()
     qx.last(0)
-    qx.turn(1)
-    o.start()
-    swap.start()
     qx.last(1)
     kept[qx].wait()
     qy.start()
-    mate = place_tables(me, deal, freq, cosine, sine, bias_p, bias_c)
-    q.start()
-    g.pair()
+    g.turn(0)
+    o.start()
     dy_task.pair()
     k.pair()
+    swap.start()
+    k.last(0)
+    ox.pair()
+    mate = place_tables(me, deal, freq, cosine, sine, bias_p, bias_c)
+    g.last(0)
+    g.pair()
+    ox.turn(0)
+    q.turn(0)
+    k.turn(1)
+    g.turn(1)
     qy.turn(0)
-    g.turn(1)
-    g.last(0)
-    k.turn(0)
-    ox.turn(0)
-    k.turn(1)
-    q.turn(0)
-    ox.pair()
+    q.pair()
+    swap.wait()
+    dn_local.start()
+    dn.start()
+    ox.last(0)
+    qy.pair()
     g.last(1)
-    k.last(0)
-    qy.pair()
     k.last(1)
-    o.pair()
-    ox.turn(1)
     g.sync()
     k.sync()
+    ox.turn(1)
     x_load.wait()
     normed()
     project_kv()
+    q.turn(1)
+    kv_task.start()
+    qy.turn(1)
+    o.pair()
+    kv_task.pair()
+    q.last(0)
+    ox.last(1)
+    q.last(1)
+    dn.pair()
     qy.last(0)
-    ox.last(0)
-    kv_task.start()
-    q.pair()
-    ox.last(1)
-    qy.turn(1)
-    swap.wait()
-    dn_local.start()
-    dn.start()
-    kv_task.pair()
     kept[ox].wait()
     oy.start()
+    qy.last(1)
+    o.turn(1)
     kv_task.turn(0)
-    q.turn(1)
+    kv_task.turn(1)
     o.turn(0)
-    qy.last(1)
-    kv_task.turn(1)
-    o.turn(1)
-    put_gate_up()
+    q.sync()
+    dn.turn(1)
+    oy.pair()
     qy.sync()
-    m.start()
-    q.last(1)
-    q.last(0)
-    oy.pair()
-    q.sync()
-    oy.turn(0)
-    kv_task.last(0)
     kept[q].wait()
     saved.append(load(qw, q_saved))
     saved.append(load(kw, kw_saved))
     project_q()
+    oy.turn(0)
+    m.start()
     kv_task.last(1)
+    kv_task.last(0)
     collect_kv(mate)
-    a1_swap.start()
-    o.last(1)
 
     @pl.loop(0, 4)
     def _(n):
@@ -1170,23 +1170,25 @@
 
         @pl.when(n == 0)
         def _():
-            oy.turn(1)
-            dn.turn(0)
-            dn.pair()
             o.last(0)
 
         @pl.when(n == 1)
         def _():
+            oy.turn(1)
+            o.last(1)
+            a1_swap.start()
             dy_task.turn(0)
+            dn.last(1)
             oy.last(0)
 
         @pl.when(n == 2)
         def _():
+            oy.last(1)
             dy_task.turn(1)
-            oy.last(1)
             m.pair()
-
-    o.sync()
+            o.sync()
+            dn.turn(0)
+
     oy.sync()
     kept[o].wait()
     saved.append(load(wo, wo_saved))
@@ -1198,17 +1200,13 @@
     saved[1].wait()
     a.start()
     m.turn(0)
+    m.turn(1)
+    m.last(0)
     dn.last(0)
-    m.turn(1)
-    dn.turn(1)
+    a.pair()
     m.last(1)
-    m.last(0)
-    a.pair()
-    dn.last(1)
     m.sync()
-    att_swap.start()
-    dy_task.last(1)
-    dy_task.last(0)
+    a.turn(0)
     dn.sync()
 
     for task in (o, ox, oy, kv_task):
@@ -1221,14 +1219,12 @@
     def _(n):
         group(n)
 
-        @pl.when(n == 0)
-        def _():
-            a.turn(0)
-
         @pl.when(n == 1)
         def _():
+            dy_task.last(0)
             a.turn(1)
 
+    dy_task.last(1)
     a.last(0)
     group_half(6)
     a.last(1)
@@ -1237,30 +1233,30 @@
     m.end()
     terms_for_sibling(0)
     terms_for_sibling(2)
+    terms_for_sibling(4)
     own_terms(0)
     gjob.start()
-    terms_for_sibling(4)
-    terms_for_sibling(6)
+    own_terms(2)
     d.turn(1)
-    own_terms(2)
+    group_out()
     own_terms(4)
-    group_out()
     gjob.turn(1)
+    att_swap.start()
+    d.turn(0)
+    m_start()
     dn.end()
     down_terms()
+    gjob.turn(0)
+    terms_for_sibling(6)
     down_sums()
-    n_job.start()
-    d.turn(0)
     d.pair()
-    n_job.turn(1)
-    gjob.turn(0)
-    n_job.turn(0)
-    m_start()
     own_terms(6)
     a.end()
     wo_load(0).start()
     wo_load(1).start()
-    n_job.pair()
+    n_job.start()
+    n_job.turn(1)
+    n_job.turn(0)
     d.finish(da2)
     norm_two_back()
     for device in near(me.across_x):
@@ -1269,9 +1265,8 @@
     m_turn(1)
     d.end()
     output_terms()
+    n_job.pair()
     heads_back()
-    gjob.finish(gown(0))
-    gu_begin()
 
     @pl.loop(0, 4)
     def _(n):
@@ -1280,74 +1275,76 @@
 
         @pl.when(n == 0)
         def _():
+            gjob.finish(gown(0))
+            gu_begin()
             o_job.turn(1)
+
+        @pl.when(n == 1)
+        def _():
             m_pair_up()
-
-        @pl.when(n == 2)
-        def _():
-            gu_task.pair()
-            o_job.turn(0)
-
+            m_turn(0)
+
+    n_job.finish(gd_own(0))
+    dq_swap.start()
+    o_job.turn(0)
+    o_job.pair()
     kv_blocks(mate)
     kw_back = kw_load()
-    dq_swap.start()
     d_job.start()
-    n_job.finish(gd_own(0))
+    query_terms()
+    d_job.turn(1)
+    gu_task.turn(0)
     dn_swap.start()
-    o_job.pair()
-    query_terms()
-    gu_task.turn(0)
-    d_job.turn(1)
+    d_job.pair()
     d_job.turn(0)
-    gu_task.last(0)
-    gu_task.turn(1)
-    d_job.pair()
     o_job.finish(o_sum)
+    dn_begin()
+    q_job.turn(1)
     o_sums.start()
-    q_job.turn(1)
     d_job.finish(sT.at[pl.ds(512, 128)])
     kv_back()
-    m_turn(0)
-    dn_begin()
     inputs_back()
+    dn_task.pair()
+    gu_task.pair()
+    sibling_has_terms()
+    kv_terms()
+    norm_one_back()
     o_sums.got()
     sum_up(o_sum, o_got, o_grad)
-    sibling_has_terms()
-    kv_terms()
     o_spread.start()
+    gain_terms()
+    e_job.start()
+    k_job.turn(1)
     q_job.pair()
-    dn_task.pair()
-    gu_task.last(1)
-    k_job.turn(1)
+    dn_task.turn(1)
+    gu_task.last(0)
+    dn_task.turn(0)
+    e_job.turn(1)
     q_job.turn(0)
-    m_finish()
-    norm_one_back()
-    gain_terms()
-    dn_task.turn(0)
+    gu_task.turn(1)
     k_job.turn(0)
     k_job.pair()
-    e_job.start()
-    dn_task.turn(1)
+    e_job.pair()
     q_job.finish(q_sum)
     q_sums.start()
+    m_finish()
+    k_job.finish(kv_sum)
     e_job.turn(0)
-    e_job.turn(1)
-    k_job.finish(kv_sum)
-    e_job.pair()
+    e_job.finish(g_sum)
+    gu_task.last(1)
+    dn_task.last(0)
+    e_begin()
+    dn_task.last(1)
     k_sums.start()
-    dn_task.last(0)
     q_sums.got()
     sum_up(q_sum, q_got, q_grad)
     q_spread.start()
-    e_job.finish(g_sum)
-    e_begin()
     k_sums.got()
     sum_up(kv_sum, k_got, kv_grad)
     k_spread.start()
     o_spread.got()
     q_spread.got()
     e_task.got()
-    dn_task.last(1)
     k_spread.got()
     total = ggot[0]
     for index in range(1, 8):
@@ -1471,7 +1468,7 @@
     mixed, tokens_grad, q_out, key_out, value_out, o_out, gate_out, up_out, dn_out, first_gain, second_gain,
     b_mixed, b_tokens, b_q, b_kv, b_o, b_gu, b_dn, f_q, f_key, f_value, f_o, f_gate, f_up, f_dn, sems,
 ):
-    slots = iter(range(24))
+    slots = iter(range(28))
 
     def move(src, dst):
         return pltpu.make_async_copy(src, dst, sems.at[next(slots)])
@@ -1479,8 +1476,8 @@
     loads = [
         move(src, dst)
         for src, dst in (
-            (q_in, b_q), (o_in, b_o), (dn_in, b_dn), (gu_in.at[pl.ds(0, 4)], b_gu.at[pl.ds(0, 4)]),
-            (gu_in.at[pl.ds(4, 4)], b_gu.at[pl.ds(4, 4)]), (kv_in, b_kv), (mixed_in, b_mixed), (tokens_in, b_tokens),
+            *[(gu_in.at[pl.ds(2 * pair, 2)], b_gu.at[pl.ds(2 * pair, 2)]) for pair in range(4)],
+            (dn_in, b_dn), (q_in, b_q), (o_in, b_o), (kv_in, b_kv), (mixed_in, b_mixed), (tokens_in, b_tokens),
         )
     ]
     for copy in loads:
@@ -1514,29 +1511,28 @@
             at = pl.ds(pl.multiple_of(32 * i, 32), 32)
             dst[at] = src[at].astype(F32)
 
+    for pair in range(4):
+        loads[pair].wait()
+        widen(pair)
+        wide = pl.ds(1408 * pair, 1408)
+        store(f_gate.at[:, wide], gate_out.at[:, wide])
+        store(f_up.at[:, wide], up_out.at[:, wide])
     for index, src, dst, out, rows in (
-        (0, b_q, f_q, q_out, 128), (1, b_o, f_o, o_out, 128), (2, b_dn, f_dn, dn_out, 352)
+        (4, b_dn, f_dn, dn_out, 352), (5, b_q, f_q, q_out, 128), (6, b_o, f_o, o_out, 128)
     ):
         loads[index].wait()
         cast(src, dst, rows)
         store(dst, out)
-    for half in (0, 1):
-        loads[3 + half].wait()
-        for pair in (2 * half, 2 * half + 1):
-            widen(pair)
-            wide = pl.ds(1408 * pair, 1408)
-            store(f_gate.at[:, wide], gate_out.at[:, wide])
-            store(f_up.at[:, wide], up_out.at[:, wide])
     first_gain[...] = gains[0:1, :]
     second_gain[...] = gains[8:9, :]
-    loads[5].wait()
+    loads[7].wait()
     f_key[...] = b_kv[:, 0:256].astype(F32)
     f_value[...] = b_kv[:, 256:512].astype(F32)
     store(f_key, key_out)
     store(f_value, value_out)
-    loads[6].wait()
+    loads[8].wait()
     store(b_mixed, mixed)
-    loads[7].wait()
+    loads[9].wait()
     store(b_tokens, tokens_grad)
     for copy in stores:
         copy.wait()
@@ -1559,7 +1555,7 @@
             vmem((8, 128, 1408), BF),
             vmem((352, 2048), BF),
             *[vmem(dims, F32) for dims in wholes],
-            pltpu.SemaphoreType.DMA((24,)),
+            pltpu.SemaphoreType.DMA((28,)),
         ],
         compiler_params=pltpu.CompilerParams(vmem_limit_bytes=62 << 20),
         name="finish",

time: 296 us -> 299 us (1.010)
  no operation moved by 1% of the time
where the time goes in v12:
time: 299 us; the launch traced here: 298 us
  Pallas kernels  297 us (99%)
    pallas_call x1, Pallas kernels, layer(): pl.pallas_call(layer_kernel, out_shape=(shape((128, 2048), BF), shape((12...  289 us
    pallas_call x1, Pallas kernels, finish(): pl.pallas_call(finish_kernel, out_shape=(shape((128, 2048), BF), shape((1...  8.22 us

profile of v12, /device:TPU:0, one launch (start us, length us, event | category | flops | bytes accessed | tf_op | source)
XLA Modules:
  0.0 298.0 jit_solution(3055600905552546582)
XLA Ops:
  0.6 289.0 %layer.1 = (bf16[128,2048]{1,0:T(8,128)(2,1)}, bf16[128,2048]{1,0:T(8,128)(2,1)}, bf16[128,2048]{1,0:T(8,128)(2,1)}, bf16[128,512]{1,0:T(8,128)(2,1)}, bf16[128,...) custom-call(bf16[128,2048]{1,0:T(8,128)(2,1)} %bitcast.9, ...), custom_call_target="tpu_custom_call" | custom-call | tf_op jit(solution)/shard_map/layer/pallas_call | solution.py:1375
  289.6 8.2 %finish.1 = (bf16[128,2048]{1,0:T(8,128)(2,1)}, bf16[128,2048]{1,0:T(8,128)(2,1)}, f32[128,2048]{1,0:T(8,128)}, f32[128,256]{1,0:T(8,128)}, f32[128,256]{1,0:T(8...) custom-call(bf16[128,2048]{1,0:T(8,128)(2,1)} %get-tuple-element.30., ...), custom_call_target="tpu_custom_call" | custom-call | tf_op jit(solution)/shard_map/finish/pallas_call | solution.py:1544
